TPU v7x, 512 devices: a whole 4x4x16 slice. The times are simulated.
512 devices in a mesh: dp: 64 (over x_lo, z, core), mp: 8 (over y, x_hi).
Axes of the slice: x: 4 (x_hi: 2, x_lo: 2; x = x_hi * 2 + x_lo), y: 4, z: 16, core: 2. Of those that a mesh axis runs over, the one named last changes fastest.
Arguments:
- image_features: bfloat16 [8192, 1536], P('dp', 'mp'), may hold values from -6 to 6
- text_features: bfloat16 [8192, 1536], P('dp', 'mp'), may hold values from -6 to 6
- image_weight: bfloat16 [1536, 1536], P('mp'), may hold values from -1.5 to 1.5
- text_weight: bfloat16 [1536, 1536], P('mp'), may hold values from -1.5 to 1.5
- logit_scale: float32 [1], replicated, may hold values from 8 to 16
- logit_bias: float32 [1], replicated, may hold values from -5 to -3.5
- loss_cotangent: float32 [1], replicated, may hold values from 20 to 40
Outputs:
- image_input_grad: float32 [8192, 1536], P('dp', 'mp')
- text_input_grad: float32 [8192, 1536], P('dp', 'mp')
- image_weight_grad: float32 [1536, 1536], P('mp')
- text_weight_grad: float32 [1536, 1536], P('mp')
All inputs are finite; a program needn't handle non-finite values.
Results may differ from a plain program's by a relative error of at most 0.018.
Values may be sent and summed in bfloat16 or wider, within the bound.
No kernel may reach another device: no remote copies, remote signals or barrier semaphores. Data moves between devices by JAX's collectives and lax.ppermute only.
A program may use at most 64 MiB of HBM per device.

v0:
```python
import jax
import jax.numpy as jnp
from jax import lax
from jax.sharding import PartitionSpec as P


def from_behind(value, axis, by):
    devices = lax.axis_size(axis)
    return lax.ppermute(value, axis, [(i, (i + by) % devices) for i in range(devices)])


def unit_rows(heads):
    values = heads.astype(jnp.float32)
    norm = jnp.sqrt(jnp.sum(values * values, axis=1, keepdims=True) + 1e-06)
    return (values / norm, norm)


def head_back(unit, norm, grads):
    inner = jnp.sum(unit * grads, axis=1, keepdims=True)
    return ((grads - unit * inner) / norm).astype(jnp.bfloat16)


def on_device(
    image_features,
    text_features,
    image_weight,
    text_weight,
    logit_scale,
    logit_bias,
    loss_cotangent,
):
    member = lax.axis_index("mp")
    place = lax.axis_index("dp")
    dp_count = lax.axis_size("dp")
    scale = logit_scale[0]
    shift_bias = logit_bias[0]
    factor = loss_cotangent[0] * scale
    pair_rows = image_features.shape[0]
    share = pair_rows // lax.axis_size("mp")
    embed_width = image_weight.shape[1]
    image_part = image_features
    text_part = text_features
    both_heads = lax.psum_scatter(
        jnp.concatenate(
            (
                jnp.dot(image_part, image_weight, preferred_element_type=jnp.float32),
                jnp.dot(text_part, text_weight, preferred_element_type=jnp.float32),
            ),
            axis=1,
        ),
        "mp",
        scatter_dimension=0,
        tiled=True,
    )
    image_heads = both_heads[:, :embed_width].astype(jnp.bfloat16)
    text_heads = both_heads[:, embed_width:].astype(jnp.bfloat16)
    image_unit, image_norm = unit_rows(image_heads)
    text_unit, text_norm = unit_rows(text_heads)
    image_own = image_unit.astype(jnp.bfloat16)
    image_embed = lax.all_gather(image_own, "mp", axis=0, tiled=True)
    text_embed = text_unit.astype(jnp.bfloat16)
    text_rows = jnp.arange(share, dtype=jnp.int32)[:, None] + member * share
    image_rows = jnp.arange(pair_rows, dtype=jnp.int32)[None, :]

    def contribute_rows(block, anchor, text_local):
        scores = (
            scale * jnp.einsum("se,pe->sp", block, image_embed, preferred_element_type=jnp.float32)
            + shift_bias
        )
        positive = ((text_local == image_rows) & (anchor == place)).astype(jnp.float32)
        coeff = (factor * (jax.nn.sigmoid(scores) - positive)).astype(jnp.bfloat16)
        text_part = jnp.dot(coeff, image_embed, preferred_element_type=jnp.float32)
        image_part = jnp.einsum("sp,se->pe", coeff, block, preferred_element_type=jnp.float32)
        return (image_part, text_part)

    def contribute(block, anchor):
        return contribute_rows(block, anchor, text_rows)

    image_first, text_first = contribute(text_embed, place)

    def step_one(turn, carry):
        block, grads, image_sum = carry
        block = from_behind(block, "dp", 1)
        grads = from_behind(grads, "dp", 1)
        image_part, text_part = contribute(block, (place - turn) % dp_count)
        return (block, grads + text_part, image_sum + image_part)

    block, grads, image_sum = lax.fori_loop(
        1, dp_count, step_one, (text_embed, text_first, image_first)
    )
    text_grad_embed = from_behind(grads.astype(jnp.bfloat16), "dp", 1).astype(grads.dtype)
    image_share = lax.psum_scatter(
        image_sum.astype(jnp.bfloat16), "mp", scatter_dimension=0, tiled=True
    ).astype(jnp.float32)
    image_grad_heads = head_back(image_unit, image_norm, image_share)
    text_grad_heads = head_back(text_unit, text_norm, text_grad_embed)
    image_grad_rows, text_grad_rows = (
        lax.all_gather(image_grad_heads, "mp", axis=0, tiled=True),
        lax.all_gather(text_grad_heads, "mp", axis=0, tiled=True),
    )
    image_input_grad = jnp.dot(image_grad_rows, image_weight.T, preferred_element_type=jnp.float32)
    text_input_grad = jnp.dot(text_grad_rows, text_weight.T, preferred_element_type=jnp.float32)
    image_weight_part = jnp.dot(
        image_features.T, image_grad_rows, preferred_element_type=jnp.float32
    )
    text_weight_part = jnp.dot(text_features.T, text_grad_rows, preferred_element_type=jnp.float32)
    image_weight_grad, text_weight_grad = lax.psum((image_weight_part, text_weight_part), "dp")
    return (image_input_grad, text_input_grad, image_weight_grad, text_weight_grad)


def solution(mesh):
    return jax.shard_map(
        on_device,
        mesh=mesh,
        in_specs=(P("dp", "mp"), P("dp", "mp"), P("mp", None), P("mp", None), P(), P(), P()),
        out_specs=(P("dp", "mp"), P("dp", "mp"), P("mp", None), P("mp", None)),
        check_vma=False,
    )
```

profile of v0, /device:TPU:1, one launch (start us, length us, event | category | flops | bytes accessed | tf_op | source)
XLA Modules:
  0.0 1372.0 jit_solution(778636685503183836)
XLA Ops:
  12.3 92.9 %reduce-scatter.3.cloned.1.call-done = f32[16,3072]{1,0:T(8,128)} async-done(((f32[128,3072]{1,0:T(8,128)}), f32[16,3072]{1,0:T(8,128)}) %reduce-scatter.3.cloned.1.call-update) | async-done | bytes 196624 | tf_op jit(solution)/shard_map/reduce_scatter | solution.py:43
  106.4 29.6 %all_gather.9 = bf16[128,1536]{1,0:T(8,128)(2,1)S(1)} all-gather(bf16[16,1536]{1,0:T(8,128)(2,1)S(1)} %get-tuple-element.324), channel_id=1, replica_groups=mesh['dp'=64,'mp'=8] {'mp'}, dimensions={0}, use_global_device_ids=true | all-gather | bytes 442368 | tf_op jit(solution)/shard_map/all_gather | solution.py:60
  136.7 641.0 %while.20 = (s32[]{:T(128)}, bf16[16,1536]{1,0:T(8,128)(2,1)S(1)}, f32[16,1536]{1,0:T(8,128)S(1)}, f32[128,1536]{1,0:T(8,128)S(1)}, f32[]{:T(128)}, /*index=5*/f...) while((s32[]{:T(128)}, bf16[16,1536]{1,0:T(8,128)(2,1)S(1)}, ...), condition=%wide.region_4.5_spmd.clone, body=%wide.region_3.4_spmd.clone.sunk | while | flops 19118112 | bytes 3355112 | solution.py:88
  136.7 10.8 collective-permute-start
  183.5 4.1 collective-permute-done
  193.7 4.1 collective-permute-done
  203.8 4.1 collective-permute-done
  214.0 4.1 collective-permute-done
  224.1 4.1 collective-permute-done
  234.2 4.1 collective-permute-done
  244.4 4.1 collective-permute-done
  254.5 4.1 collective-permute-done
  264.6 4.1 collective-permute-done
  274.8 4.1 collective-permute-done
  284.9 4.1 collective-permute-done
  295.1 4.1 collective-permute-done
  305.2 4.1 collective-permute-done
  315.3 4.1 collective-permute-done
  325.5 4.1 collective-permute-done
  335.6 4.1 collective-permute-done
  345.7 4.1 collective-permute-done
  355.9 4.1 collective-permute-done
  366.0 4.1 collective-permute-done
  376.2 4.1 collective-permute-done
  386.3 4.1 collective-permute-done
  396.4 4.1 collective-permute-done
  406.6 4.1 collective-permute-done
  416.7 4.1 collective-permute-done
  426.8 4.1 collective-permute-done
  437.0 4.1 collective-permute-done
  447.1 4.1 collective-permute-done
  457.3 4.1 collective-permute-done
  467.4 4.1 collective-permute-done
  477.5 4.1 collective-permute-done
  487.7 4.1 collective-permute-done
  497.8 4.1 collective-permute-done
  507.9 4.1 collective-permute-done
  518.1 4.1 collective-permute-done
  528.2 4.1 collective-permute-done
  538.4 4.1 collective-permute-done
  548.5 4.1 collective-permute-done
  558.6 4.1 collective-permute-done
  568.8 4.1 collective-permute-done
  578.9 4.1 collective-permute-done
  589.0 4.1 collective-permute-done
  599.2 4.1 collective-permute-done
  609.3 4.1 collective-permute-done
  619.5 4.1 collective-permute-done
  639.7 4.1 collective-permute-done
  649.9 4.1 collective-permute-done
  660.0 4.1 collective-permute-done
  670.1 4.1 collective-permute-done
  690.4 4.1 collective-permute-done
  710.7 4.1 collective-permute-done
  720.8 4.1 collective-permute-done
  731.0 4.1 collective-permute-done
  741.1 4.1 collective-permute-done
  761.4 4.1 collective-permute-done
  771.5 4.1 collective-permute-done
  780.6 6.0 collective-permute-done.2
  786.6 69.0 %reduce-scatter.5.cloned.1.call-done = bf16[16,1536]{1,0:T(8,128)(2,1)} async-done(((bf16[128,1536]{1,0:T(8,128)(2,1)}), bf16[16,1536]{1,0:T(8,128)(2,1)}) %reduce-scatter.5.cloned.1.call-update) | async-done | bytes 49168 | tf_op jit(solution)/shard_map/reduce_scatter | solution.py:92
  857.5 29.6 %all_gather.11 = bf16[128,1536]{1,0:T(8,128)(2,1)S(1)} all-gather(bf16[16,1536]{1,0:T(8,128)(2,1)S(1)} %get-tuple-element.322), channel_id=1, replica_groups=mesh['dp'=64,'mp'=8] {'mp'}, dimensions={0}, use_global_device_ids=true | all-gather | bytes 442368 | tf_op jit(solution)/shard_map/all_gather | solution.py:99
  887.1 29.7 %all_gather.10 = bf16[128,1536]{1,0:T(8,128)(2,1)S(1)} all-gather(bf16[16,1536]{1,0:T(8,128)(2,1)S(1)} %get-tuple-element.323), channel_id=1, replica_groups=mesh['dp'=64,'mp'=8] {'mp'}, dimensions={0}, use_global_device_ids=true | all-gather | bytes 442368 | tf_op jit(solution)/shard_map/all_gather | solution.py:98
  921.4 440.6 %all-reduce.3.cloned.1.call-done = (f32[192,1536]{1,0:T(8,128)}, f32[192,1536]{1,0:T(8,128)}) async-done(((f32[192,1536]{1,0:T(8,128)}, f32[192,1536]{1,0:T(8,128)}), (f32[192,1536]{1,0:T(8,128)}, f32[192,1536]{1,0:T(8,128)})) %all-reduce.3.cloned.1.call-update) | async-done | bytes 2359312 | tf_op jit(solution)/shard_map/psum | solution.py:107
  (549 shorter events, 419.1 us)
Async XLA Ops:
  7.2 98.1 %reduce-scatter.3.cloned.1.call-start = ((), (), s32[]{:S(2)}) async-start(), calls=%async_computation.2 | async-start | bytes 1769472 | tf_op jit(solution)/shard_map/reduce_scatter | solution.py:43
  10.3 845.3 %reduce-scatter.5.cloned.1.call-start = ((), (), s32[]{:S(2)}) async-start(), calls=%async_computation.3 | async-start | bytes 442368 | tf_op jit(solution)/shard_map/reduce_scatter | solution.py:92
  136.7 12.8 collective-permute-start
  179.7 8.0 collective-permute-start
  181.6 8.0 collective-permute-start.1
  191.7 8.0 collective-permute-start.1
  201.9 8.0 collective-permute-start.1
  212.0 8.0 collective-permute-start.1
  222.1 8.0 collective-permute-start.1
  232.3 8.0 collective-permute-start.1
  242.4 8.0 collective-permute-start.1
  252.5 8.0 collective-permute-start.1
  262.7 8.0 collective-permute-start.1
  272.8 8.0 collective-permute-start.1
  283.0 8.0 collective-permute-start.1
  293.1 8.0 collective-permute-start.1
  303.2 8.0 collective-permute-start.1
  313.4 8.0 collective-permute-start.1
  323.5 8.0 collective-permute-start.1
  333.6 8.0 collective-permute-start.1
  343.8 8.0 collective-permute-start.1
  353.9 8.0 collective-permute-start.1
  364.1 8.0 collective-permute-start.1
  374.2 8.0 collective-permute-start.1
  384.3 8.0 collective-permute-start.1
  394.5 8.0 collective-permute-start.1
  404.6 8.0 collective-permute-start.1
  414.7 8.0 collective-permute-start.1
  424.9 8.0 collective-permute-start.1
  435.0 8.0 collective-permute-start.1
  445.2 8.0 collective-permute-start.1
  455.3 8.0 collective-permute-start.1
  465.4 8.0 collective-permute-start.1
  475.6 8.0 collective-permute-start.1
  485.7 8.0 collective-permute-start.1
  495.8 8.0 collective-permute-start.1
  506.0 8.0 collective-permute-start.1
  516.1 8.0 collective-permute-start.1
  526.3 8.0 collective-permute-start.1
  536.4 8.0 collective-permute-start.1
  546.5 8.0 collective-permute-start.1
  556.7 8.0 collective-permute-start.1
  566.8 8.0 collective-permute-start.1
  576.9 8.0 collective-permute-start.1
  587.1 8.0 collective-permute-start.1
  597.2 8.0 collective-permute-start.1
  607.4 8.0 collective-permute-start.1
  617.5 8.0 collective-permute-start.1
  627.6 8.0 collective-permute-start.1
  637.8 8.0 collective-permute-start.1
  647.9 8.0 collective-permute-start.1
  658.0 8.0 collective-permute-start.1
  668.2 8.0 collective-permute-start.1
  678.3 8.0 collective-permute-start.1
  688.4 8.0 collective-permute-start.1
  698.6 8.0 collective-permute-start.1
  708.7 8.0 collective-permute-start.1
  718.9 8.0 collective-permute-start.1
  729.0 8.0 collective-permute-start.1
  739.1 8.0 collective-permute-start.1
  749.3 8.0 collective-permute-start.1
  759.4 8.0 collective-permute-start.1
  769.5 8.0 collective-permute-start.1
  778.6 583.4 %all-reduce.3.cloned.1.call-start = ((), (), s32[]{:S(2)}) async-start(), calls=%async_computation.4 | async-start | bytes 4718592 | tf_op jit(solution)/shard_map/psum | solution.py:107
  (71 other events, 658.4 us)
Sparse Core Ops, SparseCore 0:
  12.6 92.6 reduce-scatter.2
  778.7 76.8 reduce-scatter.4
  919.6 442.3 all-reduce.2
where the time goes:
time: 1380 us; the launch traced here: 1370 us
  waiting for transfers between devices  864 us (63%)
  starting transfers between devices  257 us (19%)
  matrix products  131 us (9%)
  blocking collectives  88.9 us (6%)
  between operations  15.8 us (1%)
    psum x1, waiting for transfers between devices, on_device(): lax.psum((image_weight_part, text_weight_part), 'dp')  441 us
    ppermute x127, waiting for transfers between devices, from_behind(): lax.ppermute(value, axis, [(i, (i + by) % devices) for i in range(devices)])  262 us
    ppermute x127, starting transfers between devices, from_behind(): lax.ppermute(value, axis, [(i, (i + by) % devices) for i in range(devices)])  257 us
    dot_general x64, matrix products, contribute_rows(): jnp.einsum('se,pe->sp', block, image_embed, preferred_element_type=jnp.fl...  95.5 us
    reduce_scatter x1, waiting for transfers between devices, on_device(): lax.psum_scatter(jnp.concatenate((jnp.dot(image_part, image_weight, prefe...  92.9 us
    reduce_scatter x1, waiting for transfers between devices, on_device(): lax.psum_scatter(image_sum.astype(jnp.bfloat16), 'mp', scatter_dimension=...  69 us
    all_gather x1, blocking collectives, on_device(): lax.all_gather(image_grad_heads, 'mp', axis=0, tiled=True)  29.7 us
    all_gather x1, blocking collectives, on_device(): image_embed = lax.all_gather(image_own, 'mp', axis=0, tiled=True)  29.6 us
  transfers between devices with their start and end apart: 130, of which 126 were waited for; matrix products, arithmetic and copies ran while one was open for 9% of the time, Pallas kernels for 0%

commit v1 on v0

v1 whole, which is shorter than its diff:
```python
import jax
import jax.numpy as jnp
from jax import lax
from jax.sharding import Mesh, PartitionSpec as P

BF16 = jnp.bfloat16
F32 = jnp.float32

PARTS = {"xl": 2, "zh": 4, "zl": 4, "c": 2, "y": 4, "xh": 2}
DP = ("xl", "zh", "zl", "c")
MP = ("y", "xh")


def count(axes):
    axes = (axes,) if isinstance(axes, str) else axes
    n = 1
    for axis in axes:
        n *= PARTS[axis]
    return n


def exchange(blocks, axes):
    return lax.all_to_all(blocks, axes, split_axis=0, concat_axis=0, tiled=True)


def gather(rows, axes):
    n = count(axes)
    return exchange(jnp.broadcast_to(rows[None], (n,) + rows.shape), axes)


def scatter_sum(blocks, axes):
    return jnp.sum(exchange(blocks.astype(BF16), axes).astype(F32), axis=0)


def split_rows(value, n):
    return value.reshape((n, value.shape[0] // n) + value.shape[1:])


def merge_rows(value):
    return value.reshape((-1,) + value.shape[2:])


def unit_rows(heads):
    values = heads.astype(F32)
    norm = jnp.sqrt(jnp.sum(values * values, axis=1, keepdims=True) + 1e-06)
    return (values / norm, norm)


def head_back(unit, norm, grads):
    inner = jnp.sum(unit * grads, axis=1, keepdims=True)
    return ((grads - unit * inner) / norm).astype(BF16)


def on_device(
    image_features,
    text_features,
    image_weight,
    text_weight,
    logit_scale,
    logit_bias,
    loss_cotangent,
):
    at = {axis: lax.axis_index(axis) for axis in PARTS}
    scale = logit_scale[0]
    shift_bias = logit_bias[0]
    factor = loss_cotangent[0] * scale
    embed_width = image_weight.shape[1]
    members = count(MP)
    share = image_features.shape[0] // members

    with jax.named_scope("heads"):
        partial_heads = jnp.concatenate(
            (
                jnp.dot(image_features, image_weight, preferred_element_type=F32).astype(BF16),
                jnp.dot(text_features, text_weight, preferred_element_type=F32).astype(BF16),
            ),
            axis=1,
        )
        both_heads = scatter_sum(split_rows(partial_heads, members), MP).astype(BF16)
        image_unit, image_norm = unit_rows(both_heads[:, :embed_width])
        text_unit, text_norm = unit_rows(both_heads[:, embed_width:])

    with jax.named_scope("gather_texts"):
        texts = merge_rows(gather(text_unit.astype(BF16), "zh"))
        texts = merge_rows(gather(texts, ("xh", "xl")))
        texts = merge_rows(gather(texts, "c"))
    with jax.named_scope("gather_images"):
        images = merge_rows(gather(image_unit.astype(BF16), "zl"))
        images = merge_rows(gather(images, "y"))

    with jax.named_scope("pairs"):
        image_base = (at["y"] * 4 + at["zl"]) * share
        text_base = (((at["c"] * 2 + at["xh"]) * 2 + at["xl"]) * 4 + at["zh"]) * share
        text_at = jnp.arange(texts.shape[0], dtype=jnp.int32)[:, None] - text_base
        image_at = jnp.arange(images.shape[0], dtype=jnp.int32)[None, :] - image_base
        positive = (text_at == image_at) & (text_at >= 0) & (text_at < share)
        scores = (
            scale * jnp.einsum("te,ie->ti", texts, images, preferred_element_type=F32) + shift_bias
        )
        coeff = (factor * (jax.nn.sigmoid(scores) - positive.astype(F32))).astype(BF16)
        text_part = jnp.dot(coeff, images, preferred_element_type=F32)
        image_part = jnp.einsum("ti,te->ie", coeff, texts, preferred_element_type=F32)

    with jax.named_scope("sum_texts"):
        text_part = scatter_sum(split_rows(text_part, count("c")), "c")
        text_part = scatter_sum(split_rows(text_part, count(("xh", "xl"))), ("xh", "xl"))
        text_grads = scatter_sum(split_rows(text_part, count("zh")), "zh")
    with jax.named_scope("sum_images"):
        image_part = scatter_sum(split_rows(image_part, count("y")), "y")
        image_grads = scatter_sum(split_rows(image_part, count("zl")), "zl")

    with jax.named_scope("head_grads"):
        grads = jnp.stack(
            (
                head_back(image_unit, image_norm, image_grads),
                head_back(text_unit, text_norm, text_grads),
            )
        )
        rows = gather(grads, MP)
        image_rows = merge_rows(rows[:, 0])
        text_rows = merge_rows(rows[:, 1])

    with jax.named_scope("input_grads"):
        image_input_grad = jnp.dot(image_rows, image_weight.T, preferred_element_type=F32)
        text_input_grad = jnp.dot(text_rows, text_weight.T, preferred_element_type=F32)
    with jax.named_scope("weight_grads"):
        part = jnp.stack(
            (
                jnp.dot(image_features.T, image_rows, preferred_element_type=F32).astype(BF16),
                jnp.dot(text_features.T, text_rows, preferred_element_type=F32).astype(BF16),
            )
        )
        width = part.shape[1]
        part = part.reshape(2, 2, width // 2, embed_width).swapaxes(0, 1)
        part = scatter_sum(part, "c")
        part = scatter_sum(part, "xl")
        part = scatter_sum(split_rows(part, 4), "zl")
        part = part.reshape(width // 8, 4, embed_width // 4).swapaxes(0, 1)
        part = scatter_sum(part, "zh").astype(BF16)
        part = gather(part, "zh").swapaxes(0, 1).reshape(width // 8, embed_width)
        part = merge_rows(gather(part, "zl"))
        part = gather(part, "xl")
        part = gather(part, "c").swapaxes(0, 1).reshape(2, width, embed_width)
        weight_grads = part.astype(F32)
    return (image_input_grad, text_input_grad, weight_grads[0], weight_grads[1])


def solution(mesh):
    fine = Mesh(mesh.devices.reshape(tuple(PARTS.values())), tuple(PARTS))
    return jax.shard_map(
        on_device,
        mesh=fine,
        in_specs=(P(DP, MP), P(DP, MP), P(MP, None), P(MP, None), P(), P(), P()),
        out_specs=(P(DP, MP), P(DP, MP), P(MP, None), P(MP, None)),
        check_vma=False,
    )
```

time: 1380 us -> 278 us (0.20)
  waiting for transfers between devices: 864 us -> 47.7 us
  starting transfers between devices: 257 us -> 25.9 us
  matrix products: 131 us -> 9.7 us
  blocking collectives: 88.9 us -> 176 us
    psum x1 -> x0, waiting for transfers between devices: 441 us -> none  [on_device(): lax.psum((image_weight_part, text_weight_part), 'dp')]
    ppermute x127 -> x0, waiting for transfers between devices: 262 us -> none  [from_behind(): lax.ppermute(value, axis, [(i, (i + by) % devices) for i in range(devices)])]
    ppermute x127 -> x0, starting transfers between devices: 257 us -> none  [from_behind(): lax.ppermute(value, axis, [(i, (i + by) % devices) for i in range(devices)])]
    all_to_all x0 -> x13, blocking collectives: none -> 176 us  [exchange(): return lax.all_to_all(blocks, axes, split_axis=0, concat_axis=0, tiled=True)]
    reduce_scatter x2 -> x0, waiting for transfers between devices: 162 us -> none  [the longest x1 92.9 us: on_device(): lax.psum_scatter(jnp.concatenate((jnp.dot(image_part, image_weight, prefe...]
    dot_general x198 -> x9, matrix products: 131 us -> 9.7 us  [the longest x1 1.72 us: on_device(): text_part = jnp.dot(coeff, images, preferred_element_type=F32)]
    all_gather x3 -> x0, blocking collectives: 88.9 us -> none  [the longest x1 29.7 us: on_device(): lax.all_gather(image_grad_heads, 'mp', axis=0, tiled=True)]
    all_to_all x0 -> x7, waiting for transfers between devices: none -> 47.7 us  [exchange(): return lax.all_to_all(blocks, axes, split_axis=0, concat_axis=0, tiled=True)]
  transfers between devices with their start and end apart: 130 -> 7, of which waited for: 126 -> 7; matrix products, arithmetic and copies ran while one was open for 9% -> 3% of each run, Pallas kernels for 0% -> 0%
where the time goes in v1:
time: 278 us; the launch traced here: 276 us
  blocking collectives  176 us (63%)
  waiting for transfers between devices  47.7 us (17%)
  starting transfers between devices  25.9 us (9%)
  matrix products  9.7 us (3%)
  other arithmetic  7.38 us (3%)
  local copies, waits for them, and re-layouts  6.4 us (2%)
  between operations  2.89 us (1%)
    all_to_all x13, blocking collectives, exchange(): return lax.all_to_all(blocks, axes, split_axis=0, concat_axis=0, tiled=True)  176 us
    all_to_all x7, waiting for transfers between devices, exchange(): return lax.all_to_all(blocks, axes, split_axis=0, concat_axis=0, tiled=True)  47.7 us
    all_to_all x7, starting transfers between devices, exchange(): return lax.all_to_all(blocks, axes, split_axis=0, concat_axis=0, tiled=True)  25.9 us
  transfers between devices with their start and end apart: 7, of which 7 were waited for; matrix products, arithmetic and copies ran while one was open for 3% of the time, Pallas kernels for 0%

profile of v1, /device:TPU:1, one launch (start us, length us, event | category | flops | bytes accessed | tf_op | source)
XLA Modules:
  0.0 276.3 jit_solution(18298224094345055510)
XLA Ops:
  0.6 0.0 copy-start
  0.6 1.1 copy-done
  1.7 1.1 convolution_convert_fusion.5
  2.8 1.4 convolution_convert_fusion.4
  4.2 0.1 pad_maximum_fusion
  4.3 19.4 %all_to_all.100 = bf16[8,16,3072]{2,1,0:T(8,128)(2,1)S(1)} all-to-all(bf16[8,16,3072]{2,1,0:T(8,128)(2,1)S(1)} %bitcast.80), channel_id=1, replica_groups=mesh['xl'=2,'zh'=4,'zl'=4,'c'=2,'y'=4,'xh'=2] {'y','xh'}, dimensions={0} | all-to-all | bytes 1572864 | tf_op jit(solution)/shard_map/heads/all_to_all | solution.py:23
  23.6 0.1 reduce_sum.150
  23.8 0.1 fusion.8
  23.9 0.1 fusion.14
  24.0 12.5 %all_to_all.101 = bf16[4,16,1536]{2,1,0:T(8,128)(2,1)S(1)} all-to-all(bf16[4,16,1536]{2,1,0:T(8,128)(2,1)S(1)} %broadcast_in_dim.35), channel_id=1, replica_groups=mesh['xl'=2,'zh'=4,'zl'=4,'c'=2,'y'=4,'xh'=2] {'zl'}, dimensions={0} | all-to-all | bytes 393216 | tf_op jit(solution)/shard_map/gather_images/all_to_all | solution.py:23
  36.6 24.9 %all_to_all.102 = bf16[4,16,1536]{2,1,0:T(8,128)(2,1)S(1)} all-to-all(bf16[4,16,1536]{2,1,0:T(8,128)(2,1)S(1)} %broadcast_in_dim.30), channel_id=1, replica_groups=mesh['xl'=2,'zh'=4,'zl'=4,'c'=2,'y'=4,'xh'=2] {'zh'}, dimensions={0} | all-to-all | bytes 393216 | tf_op jit(solution)/shard_map/gather_texts/all_to_all | solution.py:23
  61.5 0.1 broadcast_in_dim.32
  61.5 10.7 %all_to_all.103 = bf16[4,64,1536]{2,1,0:T(8,128)(2,1)S(1)} all-to-all(bf16[4,64,1536]{2,1,0:T(8,128)(2,1)S(1)} %broadcast_in_dim.32), channel_id=1, replica_groups=mesh['xl'=2,'zh'=4,'zl'=4,'c'=2,'y'=4,'xh'=2] {'xh','xl'}, dimensions={0} | all-to-all | bytes 1572864 | tf_op jit(solution)/shard_map/gather_texts/all_to_all | solution.py:23
  72.3 0.9 broadcast_in_dim.37
  73.2 3.5 %all-to-all-start.5 = ((bf16[4,64,1536]{2,1,0:T(8,128)(2,1)}), bf16[4,64,1536]{2,1,0:T(8,128)(2,1)S(1)}, u32[]{:S(2)}, u32[]{:S(2)}) async-start(bf16[4,64,1536]{2,1,0:T(8,128)(2,1)} %broadcast_in_dim.37), calls=%async_computation.5 | async-start | bytes 1572864 | tf_op jit(solution)/shard_map/gather_images/all_to_all | solution.py:23
  78.7 6.3 %all-to-all-done.5 = bf16[4,64,1536]{2,1,0:T(8,128)(2,1)S(1)} async-done(((bf16[4,64,1536]{2,1,0:T(8,128)(2,1)}), bf16[4,64,1536]{2,1,0:T(8,128)(2,1)S(1)}, u32[]{:S(2)}, u32[]{:S(2)}) %all-to-all-start.5) | async-done | bytes 786464 | tf_op jit(solution)/shard_map/gather_images/all_to_all | solution.py:23
  85.0 0.1 broadcast_in_dim.34
  85.1 12.6 %all_to_all.104 = bf16[2,256,1536]{2,1,0:T(8,128)(2,1)S(1)} all-to-all(bf16[2,256,1536]{2,1,0:T(8,128)(2,1)S(1)} %broadcast_in_dim.34), channel_id=1, replica_groups=mesh['xl'=2,'zh'=4,'zl'=4,'c'=2,'y'=4,'xh'=2] {'c'}, dimensions={0} | all-to-all | bytes 3145728 | tf_op jit(solution)/shard_map/gather_texts/all_to_all | solution.py:23
  97.7 1.6 fusion.6
  99.3 1.1 copy.21
  100.4 1.3 multiply_convert_fusion
  101.7 1.7 convolution_convert_fusion
  103.4 5.0 %all-to-all-start.8 = ((bf16[2,256,1536]{2,1,0:T(8,128)(2,1)}), bf16[2,256,1536]{2,1,0:T(8,128)(2,1)}, u32[]{:S(2)}, u32[]{:S(2)}) async-start(bf16[2,256,1536]{2,1,0:T(8,128)(2,1)} %convolution_convert_fusion), calls=%async_computation.8 | async-start | bytes 3145728 | tf_op jit(solution)/shard_map/sum_texts/all_to_all | solution.py:23
  108.4 1.5 convolution_convert_fusion.1
  109.8 0.8 all-to-all-done.8
  110.6 3.5 %all-to-all-start.6 = ((bf16[4,64,1536]{2,1,0:T(8,128)(2,1)}), bf16[4,64,1536]{2,1,0:T(8,128)(2,1)S(1)}, u32[]{:S(2)}, u32[]{:S(2)}) async-start(bf16[4,64,1536]{2,1,0:T(8,128)(2,1)} %convolution_convert_fusion.1), calls=%async_computation.6 | async-start | bytes 1572864 | tf_op jit(solution)/shard_map/sum_images/all_to_all | solution.py:23
  114.1 2.8 %reduce_sum.156 = bf16[256,1536]{1,0:T(8,128)(2,1)} reduce(bf16[2,256,1536]{2,1,0:T(8,128)(2,1)} %all-to-all-done.8, bf16[]{:T(256)} %constant.35.clone.1), dimensions={0}, to_apply=%region_6.0 | reduce | flops 393216 | bytes 2359298 | tf_op jit(solution)/shard_map/sum_texts/reduce_sum | solution.py:32
  116.9 9.2 %all-to-all-done.6 = bf16[4,64,1536]{2,1,0:T(8,128)(2,1)S(1)} async-done(((bf16[4,64,1536]{2,1,0:T(8,128)(2,1)}), bf16[4,64,1536]{2,1,0:T(8,128)(2,1)S(1)}, u32[]{:S(2)}, u32[]{:S(2)}) %all-to-all-start.6) | async-done | bytes 786464 | tf_op jit(solution)/shard_map/sum_images/all_to_all | solution.py:23
  126.1 3.5 %all-to-all-start.9 = ((bf16[4,64,1536]{2,1,0:T(8,128)(2,1)}), bf16[4,64,1536]{2,1,0:T(8,128)(2,1)S(1)}, u32[]{:S(2)}, u32[]{:S(2)}) async-start(bf16[4,64,1536]{2,1,0:T(8,128)(2,1)} %bitcast.16), calls=%async_computation.9 | async-start | bytes 1572864 | tf_op jit(solution)/shard_map/sum_texts/all_to_all | solution.py:23
  129.6 0.8 reduce_sum.153
  130.5 10.3 %all-to-all-done.9 = bf16[4,64,1536]{2,1,0:T(8,128)(2,1)S(1)} async-done(((bf16[4,64,1536]{2,1,0:T(8,128)(2,1)}), bf16[4,64,1536]{2,1,0:T(8,128)(2,1)S(1)}, u32[]{:S(2)}, u32[]{:S(2)}) %all-to-all-start.9) | async-done | bytes 786464 | tf_op jit(solution)/shard_map/sum_texts/all_to_all | solution.py:23
  140.7 3.6 %all-to-all-start.7 = ((bf16[4,16,1536]{2,1,0:T(8,128)(2,1)}), bf16[4,16,1536]{2,1,0:T(8,128)(2,1)S(1)}, u32[]{:S(2)}, u32[]{:S(2)}) async-start(bf16[4,16,1536]{2,1,0:T(8,128)(2,1)} %bitcast.12), calls=%async_computation.7 | async-start | bytes 393216 | tf_op jit(solution)/shard_map/sum_images/all_to_all | solution.py:23
  144.3 0.8 reduce_sum.157
  145.2 4.3 %all-to-all-done.7 = bf16[4,16,1536]{2,1,0:T(8,128)(2,1)S(1)} async-done(((bf16[4,16,1536]{2,1,0:T(8,128)(2,1)}), bf16[4,16,1536]{2,1,0:T(8,128)(2,1)S(1)}, u32[]{:S(2)}, u32[]{:S(2)}) %all-to-all-start.7) | async-done | bytes 196640 | tf_op jit(solution)/shard_map/sum_images/all_to_all | solution.py:23
  149.4 3.4 %all-to-all-start.10 = ((bf16[4,16,1536]{2,1,0:T(8,128)(2,1)}), bf16[4,16,1536]{2,1,0:T(8,128)(2,1)S(1)}, u32[]{:S(2)}, u32[]{:S(2)}) async-start(bf16[4,16,1536]{2,1,0:T(8,128)(2,1)} %bitcast.17), calls=%async_computation.10 | async-start | bytes 393216 | tf_op jit(solution)/shard_map/sum_texts/all_to_all | solution.py:23
  152.9 13.0 %all-to-all-done.10 = bf16[4,16,1536]{2,1,0:T(8,128)(2,1)S(1)} async-done(((bf16[4,16,1536]{2,1,0:T(8,128)(2,1)}), bf16[4,16,1536]{2,1,0:T(8,128)(2,1)S(1)}, u32[]{:S(2)}, u32[]{:S(2)}) %all-to-all-start.10) | async-done | bytes 196640 | tf_op jit(solution)/shard_map/sum_texts/all_to_all | solution.py:23
  165.9 0.2 multiply_reduce_fusion.1
  166.1 0.1 fusion.9
  166.2 0.1 broadcast_in_dim.38
  166.3 0.0 copy-start.2
  166.3 13.0 %all_to_all.105 = bf16[8,2,16,1536]{3,2,1,0:T(8,128)(2,1)S(1)} all-to-all(bf16[8,2,16,1536]{3,2,1,0:T(8,128)(2,1)S(1)} %broadcast_in_dim.38), channel_id=1, replica_groups=mesh['xl'=2,'zh'=4,'zl'=4,'c'=2,'y'=4,'xh'=2] {'y','xh'}, dimensions={0} | all-to-all | bytes 1572864 | tf_op jit(solution)/shard_map/head_grads/all_to_all | solution.py:23
  179.3 0.1 fusion.16
  179.4 0.0 copy-done.2
  179.4 0.3 convolution_convert_fusion.2
  179.7 0.4 copy-done.3
  180.1 0.3 convolution_convert_fusion.3
  180.4 0.1 maximum_bitcast_fusion
  180.5 11.4 %all_to_all.106 = bf16[2,2,96,1536]{3,2,1,0:T(8,128)(2,1)S(1)} all-to-all(bf16[2,2,96,1536]{3,2,1,0:T(8,128)(2,1)S(1)} %maximum_bitcast_fusion), channel_id=1, replica_groups=mesh['xl'=2,'zh'=4,'zl'=4,'c'=2,'y'=4,'xh'=2] {'c'}, dimensions={0} | all-to-all | bytes 2359296 | tf_op jit(solution)/shard_map/weight_grads/all_to_all | solution.py:23
  192.0 0.2 reduce_sum.160
  192.2 10.8 %all_to_all.107 = bf16[2,96,1536]{2,1,0:T(8,128)(2,1)S(1)} all-to-all(bf16[2,96,1536]{2,1,0:T(8,128)(2,1)S(1)} %reduce_sum.160), channel_id=1, replica_groups=mesh['xl'=2,'zh'=4,'zl'=4,'c'=2,'y'=4,'xh'=2] {'xl'}, dimensions={0} | all-to-all | bytes 1179648 | tf_op jit(solution)/shard_map/weight_grads/all_to_all | solution.py:23
  203.1 0.1 reduce_sum.161
  203.2 10.5 %all_to_all.108 = bf16[4,24,1536]{2,1,0:T(8,128)(2,1)S(1)} all-to-all(bf16[4,24,1536]{2,1,0:T(8,128)(2,1)S(1)} %bitcast.86), channel_id=1, replica_groups=mesh['xl'=2,'zh'=4,'zl'=4,'c'=2,'y'=4,'xh'=2] {'zl'}, dimensions={0} | all-to-all | bytes 589824 | tf_op jit(solution)/shard_map/weight_grads/all_to_all | solution.py:23
  213.8 15.1 %all_to_all.109 = bf16[4,24,384]{2,1,0:T(8,128)(2,1)S(1)} all-to-all(bf16[4,24,384]{2,1,0:T(8,128)(2,1)S(1)} %copy.24), channel_id=1, replica_groups=mesh['xl'=2,'zh'=4,'zl'=4,'c'=2,'y'=4,'xh'=2] {'zh'}, dimensions={0} | all-to-all | bytes 147456 | tf_op jit(solution)/shard_map/weight_grads/all_to_all | solution.py:23
  228.9 14.2 %all_to_all.110 = bf16[4,24,384]{2,1,0:T(8,128)(2,1)S(1)} all-to-all(bf16[4,24,384]{2,1,0:T(8,128)(2,1)S(1)} %broadcast_in_dim.39), channel_id=1, replica_groups=mesh['xl'=2,'zh'=4,'zl'=4,'c'=2,'y'=4,'xh'=2] {'zh'}, dimensions={0} | all-to-all | bytes 147456 | tf_op jit(solution)/shard_map/weight_grads/all_to_all | solution.py:23
  243.1 10.2 %all_to_all.111 = bf16[4,24,1536]{2,1,0:T(8,128)(2,1)S(1)} all-to-all(bf16[4,24,1536]{2,1,0:T(8,128)(2,1)S(1)} %broadcast_in_dim.82), channel_id=1, replica_groups=mesh['xl'=2,'zh'=4,'zl'=4,'c'=2,'y'=4,'xh'=2] {'zl'}, dimensions={0} | all-to-all | bytes 589824 | tf_op jit(solution)/shard_map/weight_grads/all_to_all | solution.py:23
  253.3 0.9 broadcast_in_dim.84
  254.2 3.5 %all-to-all-start.18 = ((bf16[2,96,1536]{2,1,0:T(8,128)(2,1)}), bf16[2,96,1536]{2,1,0:T(8,128)(2,1)S(1)}, u32[]{:S(2)}, u32[]{:S(2)}) async-start(bf16[2,96,1536]{2,1,0:T(8,128)(2,1)} %broadcast_in_dim.84), calls=%async_computation.18 | async-start | bytes 1179648 | tf_op jit(solution)/shard_map/weight_grads/all_to_all | solution.py:23
  257.7 1.0 fusion.17
  258.7 1.0 fusion.18
  259.6 3.8 %all-to-all-done.18 = bf16[2,96,1536]{2,1,0:T(8,128)(2,1)S(1)} async-done(((bf16[2,96,1536]{2,1,0:T(8,128)(2,1)}), bf16[2,96,1536]{2,1,0:T(8,128)(2,1)S(1)}, u32[]{:S(2)}, u32[]{:S(2)}) %all-to-all-start.18) | async-done | bytes 589856 | tf_op jit(solution)/shard_map/weight_grads/all_to_all | solution.py:23
  263.5 0.1 broadcast_in_dim.85
  263.6 10.9 %all_to_all.112 = bf16[2,2,96,1536]{3,2,1,0:T(8,128)(2,1)S(1)} all-to-all(bf16[2,2,96,1536]{3,2,1,0:T(8,128)(2,1)S(1)} %broadcast_in_dim.85), channel_id=1, replica_groups=mesh['xl'=2,'zh'=4,'zl'=4,'c'=2,'y'=4,'xh'=2] {'c'}, dimensions={0} | all-to-all | bytes 2359296 | tf_op jit(solution)/shard_map/weight_grads/all_to_all | solution.py:23
  274.4 0.3 convert_bitcast_fusion
  274.7 1.6 fusion.15
  (19 shorter events, 0.3 us)
Async XLA Ops:
  0.6 1.1 copy-start
  73.2 11.8 %all-to-all-start.5 = ((bf16[4,64,1536]{2,1,0:T(8,128)(2,1)}), bf16[4,64,1536]{2,1,0:T(8,128)(2,1)S(1)}, u32[]{:S(2)}, u32[]{:S(2)}) async-start(bf16[4,64,1536]{2,1,0:T(8,128)(2,1)} %broadcast_in_dim.37), calls=%async_computation.5 | async-start | bytes 1572864 | tf_op jit(solution)/shard_map/gather_images/all_to_all | solution.py:23
  103.4 7.2 %all-to-all-start.8 = ((bf16[2,256,1536]{2,1,0:T(8,128)(2,1)}), bf16[2,256,1536]{2,1,0:T(8,128)(2,1)}, u32[]{:S(2)}, u32[]{:S(2)}) async-start(bf16[2,256,1536]{2,1,0:T(8,128)(2,1)} %convolution_convert_fusion), calls=%async_computation.8 | async-start | bytes 3145728 | tf_op jit(solution)/shard_map/sum_texts/all_to_all | solution.py:23
  110.6 15.5 %all-to-all-start.6 = ((bf16[4,64,1536]{2,1,0:T(8,128)(2,1)}), bf16[4,64,1536]{2,1,0:T(8,128)(2,1)S(1)}, u32[]{:S(2)}, u32[]{:S(2)}) async-start(bf16[4,64,1536]{2,1,0:T(8,128)(2,1)} %convolution_convert_fusion.1), calls=%async_computation.6 | async-start | bytes 1572864 | tf_op jit(solution)/shard_map/sum_images/all_to_all | solution.py:23
  126.1 14.6 %all-to-all-start.9 = ((bf16[4,64,1536]{2,1,0:T(8,128)(2,1)}), bf16[4,64,1536]{2,1,0:T(8,128)(2,1)S(1)}, u32[]{:S(2)}, u32[]{:S(2)}) async-start(bf16[4,64,1536]{2,1,0:T(8,128)(2,1)} %bitcast.16), calls=%async_computation.9 | async-start | bytes 1572864 | tf_op jit(solution)/shard_map/sum_texts/all_to_all | solution.py:23
  140.7 8.7 %all-to-all-start.7 = ((bf16[4,16,1536]{2,1,0:T(8,128)(2,1)}), bf16[4,16,1536]{2,1,0:T(8,128)(2,1)S(1)}, u32[]{:S(2)}, u32[]{:S(2)}) async-start(bf16[4,16,1536]{2,1,0:T(8,128)(2,1)} %bitcast.12), calls=%async_computation.7 | async-start | bytes 393216 | tf_op jit(solution)/shard_map/sum_images/all_to_all | solution.py:23
  149.4 16.4 %all-to-all-start.10 = ((bf16[4,16,1536]{2,1,0:T(8,128)(2,1)}), bf16[4,16,1536]{2,1,0:T(8,128)(2,1)S(1)}, u32[]{:S(2)}, u32[]{:S(2)}) async-start(bf16[4,16,1536]{2,1,0:T(8,128)(2,1)} %bitcast.17), calls=%async_computation.10 | async-start | bytes 393216 | tf_op jit(solution)/shard_map/sum_texts/all_to_all | solution.py:23
  166.3 13.1 %copy-start.2 = (bf16[128,192]{0,1:T(8,128)(2,1)S(1)}, bf16[128,192]{0,1:T(8,128)(2,1)}, u32[]{:S(2)}) copy-start(bf16[128,192]{0,1:T(8,128)(2,1)} %param.8) | copy-start | bytes 147460
  179.3 0.8 copy-start.3
  253.3 5.3 %copy-start.1 = (bf16[192,1536]{1,0:T(8,128)(2,1)S(1)}, bf16[192,1536]{1,0:T(8,128)(2,1)}, u32[]{:S(2)}) copy-start(bf16[192,1536]{1,0:T(8,128)(2,1)} %param.10) | copy-start | bytes 1769476
  254.2 9.3 %all-to-all-start.18 = ((bf16[2,96,1536]{2,1,0:T(8,128)(2,1)}), bf16[2,96,1536]{2,1,0:T(8,128)(2,1)S(1)}, u32[]{:S(2)}, u32[]{:S(2)}) async-start(bf16[2,96,1536]{2,1,0:T(8,128)(2,1)} %broadcast_in_dim.84), calls=%async_computation.18 | async-start | bytes 1179648 | tf_op jit(solution)/shard_map/weight_grads/all_to_all | solution.py:23

commit v2 on v1

--- a/solution.py
+++ b/solution.py
@@ -30,6 +30,25 @@
 
 def scatter_sum(blocks, axes):
     return jnp.sum(exchange(blocks.astype(BF16), axes).astype(F32), axis=0)
+
+
+def shifted(value, axis, by):
+    n = PARTS[axis]
+    return lax.ppermute(value, axis, [(i, (i + by) % n) for i in range(n)])
+
+
+def ring_gather(rows, axis):
+    n = PARTS[axis]
+    return jnp.concatenate([rows] + [shifted(rows, axis, n - k) for k in range(1, n)], axis=0)
+
+
+def ring_scatter_sum(total, axis):
+    n = PARTS[axis]
+    blocks = split_rows(total, n)
+    own = blocks[0]
+    for k in range(1, n):
+        own = own + shifted(blocks[k].astype(BF16), axis, k).astype(F32)
+    return own
 
 
 def split_rows(value, n):
@@ -83,31 +102,36 @@
     with jax.named_scope("gather_texts"):
         texts = merge_rows(gather(text_unit.astype(BF16), "zh"))
         texts = merge_rows(gather(texts, ("xh", "xl")))
-        texts = merge_rows(gather(texts, "c"))
+        other_texts = shifted(texts, "c", 1)
     with jax.named_scope("gather_images"):
-        images = merge_rows(gather(image_unit.astype(BF16), "zl"))
-        images = merge_rows(gather(images, "y"))
+        images = ring_gather(ring_gather(image_unit.astype(BF16), "zl"), "y")
+
+    def coefficients(block, positive):
+        scores = (
+            scale * jnp.einsum("te,ie->ti", block, images, preferred_element_type=F32) + shift_bias
+        )
+        return (factor * (jax.nn.sigmoid(scores) - positive)).astype(BF16)
 
     with jax.named_scope("pairs"):
-        image_base = (at["y"] * 4 + at["zl"]) * share
-        text_base = (((at["c"] * 2 + at["xh"]) * 2 + at["xl"]) * 4 + at["zh"]) * share
+        text_base = ((at["xh"] * 2 + at["xl"]) * 4 + at["zh"]) * share
         text_at = jnp.arange(texts.shape[0], dtype=jnp.int32)[:, None] - text_base
-        image_at = jnp.arange(images.shape[0], dtype=jnp.int32)[None, :] - image_base
-        positive = (text_at == image_at) & (text_at >= 0) & (text_at < share)
-        scores = (
-            scale * jnp.einsum("te,ie->ti", texts, images, preferred_element_type=F32) + shift_bias
-        )
-        coeff = (factor * (jax.nn.sigmoid(scores) - positive.astype(F32))).astype(BF16)
+        image_at = jnp.arange(images.shape[0], dtype=jnp.int32)[None, :]
+        positive = (text_at == image_at) & (image_at < share)
+        coeff = coefficients(texts, positive.astype(F32))
+        other_coeff = coefficients(other_texts, 0.0)
+        other_part = jnp.dot(other_coeff, images, preferred_element_type=F32)
         text_part = jnp.dot(coeff, images, preferred_element_type=F32)
         image_part = jnp.einsum("ti,te->ie", coeff, texts, preferred_element_type=F32)
+        image_part = image_part + jnp.einsum(
+            "ti,te->ie", other_coeff, other_texts, preferred_element_type=F32
+        )
 
     with jax.named_scope("sum_texts"):
-        text_part = scatter_sum(split_rows(text_part, count("c")), "c")
+        text_part = text_part + shifted(other_part.astype(BF16), "c", 1).astype(F32)
         text_part = scatter_sum(split_rows(text_part, count(("xh", "xl"))), ("xh", "xl"))
         text_grads = scatter_sum(split_rows(text_part, count("zh")), "zh")
     with jax.named_scope("sum_images"):
-        image_part = scatter_sum(split_rows(image_part, count("y")), "y")
-        image_grads = scatter_sum(split_rows(image_part, count("zl")), "zl")
+        image_grads = ring_scatter_sum(ring_scatter_sum(image_part, "y"), "zl")
 
     with jax.named_scope("head_grads"):
         grads = jnp.stack(
@@ -124,25 +148,37 @@
         image_input_grad = jnp.dot(image_rows, image_weight.T, preferred_element_type=F32)
         text_input_grad = jnp.dot(text_rows, text_weight.T, preferred_element_type=F32)
     with jax.named_scope("weight_grads"):
-        part = jnp.stack(
-            (
-                jnp.dot(image_features.T, image_rows, preferred_element_type=F32).astype(BF16),
-                jnp.dot(text_features.T, text_rows, preferred_element_type=F32).astype(BF16),
+        half = image_features.shape[1] // 2
+
+        def half_part(core):
+            return jnp.stack(
+                [
+                    jnp.dot(
+                        lax.dynamic_slice_in_dim(features, core * half, half, 1).T,
+                        rows,
+                        preferred_element_type=F32,
+                    )
+                    for features, rows in (
+                        (image_features, image_rows),
+                        (text_features, text_rows),
+                    )
+                ]
             )
+
+        other = shifted(half_part(1 - at["c"]).astype(BF16), "c", 1)
+        part = half_part(at["c"]) + other.astype(F32)
+        part = scatter_sum(part.reshape(8, half // 4, embed_width), ("xl", "zl"))
+        part = jnp.sum(gather(part.astype(BF16), "zh").astype(F32), axis=0).astype(BF16)
+        part = gather(part, ("xl", "zl")).reshape(2, half, embed_width)
+        other = shifted(part, "c", 1)
+        first = at["c"] == 0
+        image_weight_grad, text_weight_grad = (
+            jnp.concatenate(
+                (jnp.where(first, mine, theirs), jnp.where(first, theirs, mine)), axis=0
+            ).astype(F32)
+            for mine, theirs in zip(part, other)
         )
-        width = part.shape[1]
-        part = part.reshape(2, 2, width // 2, embed_width).swapaxes(0, 1)
-        part = scatter_sum(part, "c")
-        part = scatter_sum(part, "xl")
-        part = scatter_sum(split_rows(part, 4), "zl")
-        part = part.reshape(width // 8, 4, embed_width // 4).swapaxes(0, 1)
-        part = scatter_sum(part, "zh").astype(BF16)
-        part = gather(part, "zh").swapaxes(0, 1).reshape(width // 8, embed_width)
-        part = merge_rows(gather(part, "zl"))
-        part = gather(part, "xl")
-        part = gather(part, "c").swapaxes(0, 1).reshape(2, width, embed_width)
-        weight_grads = part.astype(F32)
-    return (image_input_grad, text_input_grad, weight_grads[0], weight_grads[1])
+    return (image_input_grad, text_input_grad, image_weight_grad, text_weight_grad)
 
 
 def solution(mesh):

time: 278 us -> 230 us (0.83)
  blocking collectives: 176 us -> 45.1 us
  starting transfers between devices: 25.9 us -> 114 us
    all_to_all x13 -> x2, blocking collectives: 176 us -> 45.1 us  [exchange(): return lax.all_to_all(blocks, axes, split_axis=0, concat_axis=0, tiled=True)]
    ppermute x0 -> x16, starting transfers between devices: none -> 61.9 us  [shifted(): return lax.ppermute(value, axis, [(i, (i + by) % n) for i in range(n)])]
    all_to_all x7, starting transfers between devices: 25.9 us -> 52.5 us  [exchange(): return lax.all_to_all(blocks, axes, split_axis=0, concat_axis=0, tiled=True)]
    all_to_all x7, waiting for transfers between devices: 47.7 us -> 41.4 us  [exchange(): return lax.all_to_all(blocks, axes, split_axis=0, concat_axis=0, tiled=True)]
    reduce_sum x10 -> x4, other arithmetic: 5 us -> 1.04 us  [scatter_sum(): return jnp.sum(exchange(blocks.astype(BF16), axes).astype(F32), axis=0)]
    ppermute x0 -> x16, waiting for transfers between devices: none -> 3.9 us  [shifted(): return lax.ppermute(value, axis, [(i, (i + by) % n) for i in range(n)])]
  transfers between devices with their start and end apart: 7 -> 23, of which waited for: 7 -> 11; matrix products, arithmetic and copies ran while one was open for 3% -> 4% of each run, Pallas kernels for 0% -> 0%
where the time goes in v2:
time: 230 us; the launch traced here: 229 us
  starting transfers between devices  114 us (50%)
  waiting for transfers between devices  45.3 us (20%)
  blocking collectives  45.1 us (20%)
  matrix products  9.46 us (4%)
  other arithmetic  6.31 us (3%)
  local copies, waits for them, and re-layouts  5.59 us (2%)
  between operations  3.07 us (1%)
    ppermute x16, starting transfers between devices, shifted(): return lax.ppermute(value, axis, [(i, (i + by) % n) for i in range(n)])  61.9 us
    all_to_all x7, starting transfers between devices, exchange(): return lax.all_to_all(blocks, axes, split_axis=0, concat_axis=0, tiled=True)  52.5 us
    all_to_all x2, blocking collectives, exchange(): return lax.all_to_all(blocks, axes, split_axis=0, concat_axis=0, tiled=True)  45.1 us
    all_to_all x7, waiting for transfers between devices, exchange(): return lax.all_to_all(blocks, axes, split_axis=0, concat_axis=0, tiled=True)  41.4 us
  transfers between devices with their start and end apart: 23, of which 11 were waited for; matrix products, arithmetic and copies ran while one was open for 4% of the time, Pallas kernels for 0%

profile of v2, /device:TPU:1, one launch (start us, length us, event | category | flops | bytes accessed | tf_op | source)
XLA Modules:
  0.0 229.2 jit_solution(5678203308441172730)
XLA Ops:
  0.6 1.4 convolution_convert_fusion.1
  2.1 1.1 convolution_convert_fusion.2
  3.2 1.0 pad_maximum_fusion
  4.2 7.5 %all-to-all-start = ((bf16[8,16,3072]{2,1,0:T(8,128)(2,1)}), bf16[8,16,3072]{2,1,0:T(8,128)(2,1)S(1)}, u32[]{:S(2)}, u32[]{:S(2)}) async-start(bf16[8,16,3072]{2,1,0:T(8,128)(2,1)} %bitcast.2), calls=%async_computation | async-start | bytes 1572864 | tf_op jit(solution)/shard_map/heads/all_to_all | solution.py:23
  11.6 11.2 %all-to-all-done = bf16[8,16,3072]{2,1,0:T(8,128)(2,1)S(1)} async-done(((bf16[8,16,3072]{2,1,0:T(8,128)(2,1)}), bf16[8,16,3072]{2,1,0:T(8,128)(2,1)S(1)}, u32[]{:S(2)}, u32[]{:S(2)}) %all-to-all-start) | async-done | bytes 786464 | tf_op jit(solution)/shard_map/heads/all_to_all | solution.py:23
  23.0 0.1 fusion.23
  23.2 0.7 broadcast_in_dim.12
  23.9 16.8 %all-to-all-start.1 = ((bf16[4,16,1536]{2,1,0:T(8,128)(2,1)}), bf16[4,16,1536]{2,1,0:T(8,128)(2,1)S(1)}, u32[]{:S(2)}, u32[]{:S(2)}) async-start(bf16[4,16,1536]{2,1,0:T(8,128)(2,1)} %broadcast_in_dim.12), calls=%async_computation.1 | async-start | bytes 393216 | tf_op jit(solution)/shard_map/gather_texts/all_to_all | solution.py:23
  40.8 3.5 %collective-permute-start = (bf16[16,1536]{1,0:T(8,128)(2,1)S(1)}, bf16[16,1536]{1,0:T(8,128)(2,1)S(1)}, u32[]{:S(2)}, u32[]{:S(2)}) collective-permute-start(bf16[16,1536]{1,0:T(8,128)(2,1)S(1)} %get-tuple-element.11), channel_id=1, source_target_pairs={{0,48},{16,0},{32,16},{48,32},{1,49},{17,1},{33,17},{49,33},{2,50}... | collective-permute-start | bytes 147464 | tf_op jit(solution)/shard_map/gather_images/ppermute | solution.py:37
  44.3 2.2 collective-permute-start.1
  46.5 2.7 %collective-permute-start.2 = (bf16[16,1536]{1,0:T(8,128)(2,1)S(1)}, bf16[16,1536]{1,0:T(8,128)(2,1)S(1)}, u32[]{:S(2)}, u32[]{:S(2)}) collective-permute-start(bf16[16,1536]{1,0:T(8,128)(2,1)S(1)} %get-tuple-element.11), channel_id=1, source_target_pairs={{0,16},{16,32},{32,48},{48,0},{1,17},{17,33},{33,49},{49,1},{2,18}... | collective-permute-start | bytes 147464 | tf_op jit(solution)/shard_map/gather_images/ppermute | solution.py:37
  51.1 2.2 all-to-all-done.1
  53.4 0.9 broadcast_in_dim.14
  54.3 3.5 %all-to-all-start.2 = ((bf16[4,64,1536]{2,1,0:T(8,128)(2,1)}), bf16[4,64,1536]{2,1,0:T(8,128)(2,1)S(1)}, u32[]{:S(2)}, u32[]{:S(2)}) async-start(bf16[4,64,1536]{2,1,0:T(8,128)(2,1)} %broadcast_in_dim.14), calls=%async_computation.2 | async-start | bytes 1572864 | tf_op jit(solution)/shard_map/gather_texts/all_to_all | solution.py:23
  57.9 2.8 %collective-permute-start.3 = (bf16[64,1536]{1,0:T(8,128)(2,1)S(1)}, bf16[64,1536]{1,0:T(8,128)(2,1)S(1)}, u32[]{:S(2)}, u32[]{:S(2)}) collective-permute-start(bf16[64,1536]{1,0:T(8,128)(2,1)S(1)} %pad_maximum_fusion.2), channel_id=1, source_target_pairs={{0,6},{2,0},{4,2},{6,4},{1,7},{3,1},{5,3},{7,5},{8,14},{10,8},{12,... | collective-permute-start | bytes 589832 | tf_op jit(solution)/shard_map/gather_images/ppermute | solution.py:37
  60.7 2.9 %collective-permute-start.4 = (bf16[64,1536]{1,0:T(8,128)(2,1)S(1)}, bf16[64,1536]{1,0:T(8,128)(2,1)S(1)}, u32[]{:S(2)}, u32[]{:S(2)}) collective-permute-start(bf16[64,1536]{1,0:T(8,128)(2,1)S(1)} %pad_maximum_fusion.2), channel_id=1, source_target_pairs={{0,4},{2,6},{4,0},{6,2},{1,5},{3,7},{5,1},{7,3},{8,12},{10,14},{12... | collective-permute-start | bytes 589832 | tf_op jit(solution)/shard_map/gather_images/ppermute | solution.py:37
  63.5 1.9 collective-permute-start.5
  65.5 0.6 all-to-all-done.2
  66.1 10.2 %collective-permute-start.6 = (bf16[256,1536]{1,0:T(8,128)(2,1)S(1)}, bf16[256,1536]{1,0:T(8,128)(2,1)S(1)}, u32[]{:S(2)}, u32[]{:S(2)}) collective-permute-start(bf16[256,1536]{1,0:T(8,128)(2,1)S(1)} %bitcast.78), channel_id=1, source_target_pairs={{0,8},{8,0},{1,9},{9,1},{2,10},{10,2},{3,11},{11,3},{4,12},{12,4},... | collective-permute-start | bytes 2359304 | tf_op jit(solution)/shard_map/gather_texts/ppermute | solution.py:37
  76.5 1.8 collective-permute-done.6
  78.3 0.4 fusion.17
  78.7 0.4 convolution_convert_fusion
  79.1 2.8 %collective-permute-start.13 = (bf16[256,1536]{1,0:T(8,128)(2,1)S(1)}, bf16[256,1536]{1,0:T(8,128)(2,1)S(1)}, u32[]{:S(2)}, u32[]{:S(2)}) collective-permute-start(bf16[256,1536]{1,0:T(8,128)(2,1)S(1)} %convolution_convert_fusion), channel_id=1, source_target_pairs={{0,8},{8,0},{1,9},{9,1},{2,10},{10,2},{3,11},{11,3},{4,12},{12,4},... | collective-permute-start | bytes 2359304 | tf_op jit(solution)/shard_map/sum_texts/ppermute | solution.py:37
  81.9 0.4 fusion.18
  82.3 0.4 fusion.46
  82.7 1.3 fusion.45
  84.0 1.3 fusion
  85.3 4.5 %all-to-all-start.3 = ((bf16[4,64,1536]{2,1,0:T(8,128)(2,1)}), bf16[4,64,1536]{2,1,0:T(8,128)(2,1)S(1)}, u32[]{:S(2)}, u32[]{:S(2)}) async-start(bf16[4,64,1536]{2,1,0:T(8,128)(2,1)} %bitcast.7), calls=%async_computation.3 | async-start | bytes 1572864 | tf_op jit(solution)/shard_map/sum_texts/all_to_all | solution.py:23
  89.7 1.9 fusion.42
  91.7 1.9 collective-permute-start.7
  93.6 4.8 %collective-permute-start.8 = (bf16[64,1536]{1,0:T(8,128)(2,1)}, bf16[64,1536]{1,0:T(8,128)(2,1)S(1)}, u32[]{:S(2)}, u32[]{:S(2)}) collective-permute-start(bf16[64,1536]{1,0:T(8,128)(2,1)} %get-tuple-element.20), channel_id=1, source_target_pairs={{0,4},{2,6},{4,0},{6,2},{1,5},{3,7},{5,1},{7,3},{8,12},{10,14},{12... | collective-permute-start | bytes 589832 | tf_op jit(solution)/shard_map/sum_images/ppermute | solution.py:37
  98.4 2.8 %collective-permute-start.9 = (bf16[64,1536]{1,0:T(8,128)(2,1)}, bf16[64,1536]{1,0:T(8,128)(2,1)}, u32[]{:S(2)}, u32[]{:S(2)}) collective-permute-start(bf16[64,1536]{1,0:T(8,128)(2,1)} %get-tuple-element.19), channel_id=1, source_target_pairs={{0,6},{2,0},{4,2},{6,4},{1,7},{3,1},{5,3},{7,5},{8,14},{10,8},{12,... | collective-permute-start | bytes 589832 | tf_op jit(solution)/shard_map/sum_images/ppermute | solution.py:37
  101.2 0.5 all-to-all-done.3
  101.7 0.8 reduce_sum.97
  102.5 6.4 %all-to-all-start.4 = ((bf16[4,16,1536]{2,1,0:T(8,128)(2,1)}), bf16[4,16,1536]{2,1,0:T(8,128)(2,1)S(1)}, u32[]{:S(2)}, u32[]{:S(2)}) async-start(bf16[4,16,1536]{2,1,0:T(8,128)(2,1)} %bitcast.8), calls=%async_computation.4 | async-start | bytes 393216 | tf_op jit(solution)/shard_map/sum_texts/all_to_all | solution.py:23
  108.9 1.0 fusion.38
  109.9 3.5 %collective-permute-start.10 = (bf16[16,1536]{1,0:T(8,128)(2,1)S(1)}, bf16[16,1536]{1,0:T(8,128)(2,1)S(1)}, u32[]{:S(2)}, u32[]{:S(2)}) collective-permute-start(bf16[16,1536]{1,0:T(8,128)(2,1)S(1)} %get-tuple-element.25), channel_id=1, source_target_pairs={{0,16},{16,32},{32,48},{48,0},{1,17},{17,33},{33,49},{49,1},{2,18}... | collective-permute-start | bytes 147464 | tf_op jit(solution)/shard_map/sum_images/ppermute | solution.py:37
  113.5 3.1 %collective-permute-start.11 = (bf16[16,1536]{1,0:T(8,128)(2,1)S(1)}, bf16[16,1536]{1,0:T(8,128)(2,1)S(1)}, u32[]{:S(2)}, u32[]{:S(2)}) collective-permute-start(bf16[16,1536]{1,0:T(8,128)(2,1)S(1)} %get-tuple-element.27), channel_id=1, source_target_pairs={{0,32},{16,48},{32,0},{48,16},{1,33},{17,49},{33,1},{49,17},{2,34}... | collective-permute-start | bytes 147464 | tf_op jit(solution)/shard_map/sum_images/ppermute | solution.py:37
  116.6 3.3 %collective-permute-start.12 = (bf16[16,1536]{1,0:T(8,128)(2,1)S(1)}, bf16[16,1536]{1,0:T(8,128)(2,1)S(1)}, u32[]{:S(2)}, u32[]{:S(2)}) collective-permute-start(bf16[16,1536]{1,0:T(8,128)(2,1)S(1)} %get-tuple-element.26), channel_id=1, source_target_pairs={{0,48},{16,0},{32,16},{48,32},{1,49},{17,1},{33,17},{49,33},{2,50}... | collective-permute-start | bytes 147464 | tf_op jit(solution)/shard_map/sum_images/ppermute | solution.py:37
  119.8 2.1 all-to-all-done.4
  122.0 0.3 collective-permute-done.12
  122.3 0.2 multiply_reduce_fusion.1
  122.5 0.1 fusion.26
  122.7 1.0 broadcast_in_dim.15
  123.6 5.8 %all-to-all-start.5 = ((bf16[8,2,16,1536]{3,2,1,0:T(8,128)(2,1)}), bf16[8,2,16,1536]{3,2,1,0:T(8,128)(2,1)S(1)}, u32[]{:S(2)}, u32[]{:S(2)}) async-start(bf16[8,2,16,1536]{3,2,1,0:T(8,128)(2,1)} %broadcast_in_dim.15), calls=%async_computation.5 | async-start | bytes 1572864 | tf_op jit(solution)/shard_map/head_grads/all_to_all | solution.py:23
  129.5 10.4 %all-to-all-done.5 = bf16[8,2,16,1536]{3,2,1,0:T(8,128)(2,1)S(1)} async-done(((bf16[8,2,16,1536]{3,2,1,0:T(8,128)(2,1)}), bf16[8,2,16,1536]{3,2,1,0:T(8,128)(2,1)S(1)}, u32[]{:S(2)}, u32[]{:S(2)}) %all-to-all-start.5) | async-done | bytes 786464 | tf_op jit(solution)/shard_map/head_grads/all_to_all | solution.py:23
  140.0 0.2 fusion.1
  140.2 0.2 fusion.2
  140.5 9.1 %collective-permute-start.14 = (bf16[2,96,1536]{2,1,0:T(8,128)(2,1)S(1)}, bf16[2,96,1536]{2,1,0:T(8,128)(2,1)S(1)}, u32[]{:S(2)}, u32[]{:S(2)}) collective-permute-start(bf16[2,96,1536]{2,1,0:T(8,128)(2,1)S(1)} %pad_maximum_fusion.1), channel_id=1, source_target_pairs={{0,8},{8,0},{1,9},{9,1},{2,10},{10,2},{3,11},{11,3},{4,12},{12,4},... | collective-permute-start | bytes 1769480 | tf_op jit(solution)/shard_map/weight_grads/ppermute | solution.py:37
  149.6 0.2 convolution_bitcast_fusion
  149.8 0.2 convolution_bitcast_fusion.1
  150.1 1.2 collective-permute-done.14
  151.3 19.1 %all_to_all.45 = bf16[8,24,1536]{2,1,0:T(8,128)(2,1)S(1)} all-to-all(bf16[8,24,1536]{2,1,0:T(8,128)(2,1)S(1)} %bitcast.82), channel_id=1, replica_groups=mesh['xl'=2,'zh'=4,'zl'=4,'c'=2,'y'=4,'xh'=2] {'xl','zl'}, dimensions={0} | all-to-all | bytes 1179648 | tf_op jit(solution)/shard_map/weight_grads/all_to_all | solution.py:23
  170.6 25.9 %all_to_all.46 = bf16[4,24,1536]{2,1,0:T(8,128)(2,1)S(1)} all-to-all(bf16[4,24,1536]{2,1,0:T(8,128)(2,1)S(1)} %broadcast_in_dim.16), channel_id=1, replica_groups=mesh['xl'=2,'zh'=4,'zl'=4,'c'=2,'y'=4,'xh'=2] {'zh'}, dimensions={0} | all-to-all | bytes 589824 | tf_op jit(solution)/shard_map/weight_grads/all_to_all | solution.py:23
  196.5 0.9 broadcast_in_dim.17
  197.4 8.1 %all-to-all-start.8 = ((bf16[8,24,1536]{2,1,0:T(8,128)(2,1)}), bf16[8,24,1536]{2,1,0:T(8,128)(2,1)S(1)}, u32[]{:S(2)}, u32[]{:S(2)}) async-start(bf16[8,24,1536]{2,1,0:T(8,128)(2,1)} %broadcast_in_dim.17), calls=%async_computation.8 | async-start | bytes 1179648 | tf_op jit(solution)/shard_map/weight_grads/all_to_all | solution.py:23
  205.5 1.0 fusion.47
  206.4 14.2 %all-to-all-done.8 = bf16[8,24,1536]{2,1,0:T(8,128)(2,1)S(1)} async-done(((bf16[8,24,1536]{2,1,0:T(8,128)(2,1)}), bf16[8,24,1536]{2,1,0:T(8,128)(2,1)S(1)}, u32[]{:S(2)}, u32[]{:S(2)}) %all-to-all-start.8) | async-done | bytes 589856 | tf_op jit(solution)/shard_map/weight_grads/all_to_all | solution.py:23
  220.7 4.5 %collective-permute-start.15 = (bf16[2,96,1536]{2,1,0:T(8,128)(2,1)S(1)}, bf16[2,96,1536]{2,1,0:T(8,128)(2,1)S(1)}, u32[]{:S(2)}, u32[]{:S(2)}) collective-permute-start(bf16[2,96,1536]{2,1,0:T(8,128)(2,1)S(1)} %bitcast.81), channel_id=1, source_target_pairs={{0,8},{8,0},{1,9},{9,1},{2,10},{10,2},{3,11},{11,3},{4,12},{12,4},... | collective-permute-start | bytes 1769480 | tf_op jit(solution)/shard_map/weight_grads/ppermute | solution.py:37
  225.2 1.0 fusion.48
  226.2 0.6 collective-permute-done.15
  226.8 0.1 bitcast_select_fusion.1
  226.9 1.1 maximum_convert_fusion.1
  228.0 1.1 maximum_convert_fusion
  (43 shorter events, 0.9 us)
Async XLA Ops:
  0.6 1.5 copy-start
  4.2 18.7 %all-to-all-start = ((bf16[8,16,3072]{2,1,0:T(8,128)(2,1)}), bf16[8,16,3072]{2,1,0:T(8,128)(2,1)S(1)}, u32[]{:S(2)}, u32[]{:S(2)}) async-start(bf16[8,16,3072]{2,1,0:T(8,128)(2,1)} %bitcast.2), calls=%async_computation | async-start | bytes 1572864 | tf_op jit(solution)/shard_map/heads/all_to_all | solution.py:23
  23.9 29.5 %all-to-all-start.1 = ((bf16[4,16,1536]{2,1,0:T(8,128)(2,1)}), bf16[4,16,1536]{2,1,0:T(8,128)(2,1)S(1)}, u32[]{:S(2)}, u32[]{:S(2)}) async-start(bf16[4,16,1536]{2,1,0:T(8,128)(2,1)} %broadcast_in_dim.12), calls=%async_computation.1 | async-start | bytes 393216 | tf_op jit(solution)/shard_map/gather_texts/all_to_all | solution.py:23
  40.8 17.0 %collective-permute-start = (bf16[16,1536]{1,0:T(8,128)(2,1)S(1)}, bf16[16,1536]{1,0:T(8,128)(2,1)S(1)}, u32[]{:S(2)}, u32[]{:S(2)}) collective-permute-start(bf16[16,1536]{1,0:T(8,128)(2,1)S(1)} %get-tuple-element.11), channel_id=1, source_target_pairs={{0,48},{16,0},{32,16},{48,32},{1,49},{17,1},{33,17},{49,33},{2,50}... | collective-permute-start | bytes 147464 | tf_op jit(solution)/shard_map/gather_images/ppermute | solution.py:37
  44.3 13.5 %collective-permute-start.1 = (bf16[16,1536]{1,0:T(8,128)(2,1)S(1)}, bf16[16,1536]{1,0:T(8,128)(2,1)S(1)}, u32[]{:S(2)}, u32[]{:S(2)}) collective-permute-start(bf16[16,1536]{1,0:T(8,128)(2,1)S(1)} %get-tuple-element.11), channel_id=1, source_target_pairs={{0,32},{16,48},{32,0},{48,16},{1,33},{17,49},{33,1},{49,17},{2,34}... | collective-permute-start | bytes 147464 | tf_op jit(solution)/shard_map/gather_images/ppermute | solution.py:37
  46.5 11.3 %collective-permute-start.2 = (bf16[16,1536]{1,0:T(8,128)(2,1)S(1)}, bf16[16,1536]{1,0:T(8,128)(2,1)S(1)}, u32[]{:S(2)}, u32[]{:S(2)}) collective-permute-start(bf16[16,1536]{1,0:T(8,128)(2,1)S(1)} %get-tuple-element.11), channel_id=1, source_target_pairs={{0,16},{16,32},{32,48},{48,0},{1,17},{17,33},{33,49},{49,1},{2,18}... | collective-permute-start | bytes 147464 | tf_op jit(solution)/shard_map/gather_images/ppermute | solution.py:37
  54.3 11.8 %all-to-all-start.2 = ((bf16[4,64,1536]{2,1,0:T(8,128)(2,1)}), bf16[4,64,1536]{2,1,0:T(8,128)(2,1)S(1)}, u32[]{:S(2)}, u32[]{:S(2)}) async-start(bf16[4,64,1536]{2,1,0:T(8,128)(2,1)} %broadcast_in_dim.14), calls=%async_computation.2 | async-start | bytes 1572864 | tf_op jit(solution)/shard_map/gather_texts/all_to_all | solution.py:23
  57.9 18.5 %collective-permute-start.3 = (bf16[64,1536]{1,0:T(8,128)(2,1)S(1)}, bf16[64,1536]{1,0:T(8,128)(2,1)S(1)}, u32[]{:S(2)}, u32[]{:S(2)}) collective-permute-start(bf16[64,1536]{1,0:T(8,128)(2,1)S(1)} %pad_maximum_fusion.2), channel_id=1, source_target_pairs={{0,6},{2,0},{4,2},{6,4},{1,7},{3,1},{5,3},{7,5},{8,14},{10,8},{12,... | collective-permute-start | bytes 589832 | tf_op jit(solution)/shard_map/gather_images/ppermute | solution.py:37
  60.7 15.8 %collective-permute-start.4 = (bf16[64,1536]{1,0:T(8,128)(2,1)S(1)}, bf16[64,1536]{1,0:T(8,128)(2,1)S(1)}, u32[]{:S(2)}, u32[]{:S(2)}) collective-permute-start(bf16[64,1536]{1,0:T(8,128)(2,1)S(1)} %pad_maximum_fusion.2), channel_id=1, source_target_pairs={{0,4},{2,6},{4,0},{6,2},{1,5},{3,7},{5,1},{7,3},{8,12},{10,14},{12... | collective-permute-start | bytes 589832 | tf_op jit(solution)/shard_map/gather_images/ppermute | solution.py:37
  63.5 12.9 %collective-permute-start.5 = (bf16[64,1536]{1,0:T(8,128)(2,1)S(1)}, bf16[64,1536]{1,0:T(8,128)(2,1)S(1)}, u32[]{:S(2)}, u32[]{:S(2)}) collective-permute-start(bf16[64,1536]{1,0:T(8,128)(2,1)S(1)} %pad_maximum_fusion.2), channel_id=1, source_target_pairs={{0,2},{2,4},{4,6},{6,0},{1,3},{3,5},{5,7},{7,1},{8,10},{10,12},{12... | collective-permute-start | bytes 589832 | tf_op jit(solution)/shard_map/gather_images/ppermute | solution.py:37
  66.1 12.1 %collective-permute-start.6 = (bf16[256,1536]{1,0:T(8,128)(2,1)S(1)}, bf16[256,1536]{1,0:T(8,128)(2,1)S(1)}, u32[]{:S(2)}, u32[]{:S(2)}) collective-permute-start(bf16[256,1536]{1,0:T(8,128)(2,1)S(1)} %bitcast.78), channel_id=1, source_target_pairs={{0,8},{8,0},{1,9},{9,1},{2,10},{10,2},{3,11},{11,3},{4,12},{12,4},... | collective-permute-start | bytes 2359304 | tf_op jit(solution)/shard_map/gather_texts/ppermute | solution.py:37
  79.1 4.9 %collective-permute-start.13 = (bf16[256,1536]{1,0:T(8,128)(2,1)S(1)}, bf16[256,1536]{1,0:T(8,128)(2,1)S(1)}, u32[]{:S(2)}, u32[]{:S(2)}) collective-permute-start(bf16[256,1536]{1,0:T(8,128)(2,1)S(1)} %convolution_convert_fusion), channel_id=1, source_target_pairs={{0,8},{8,0},{1,9},{9,1},{2,10},{10,2},{3,11},{11,3},{4,12},{12,4},... | collective-permute-start | bytes 2359304 | tf_op jit(solution)/shard_map/sum_texts/ppermute | solution.py:37
  85.3 16.4 %all-to-all-start.3 = ((bf16[4,64,1536]{2,1,0:T(8,128)(2,1)}), bf16[4,64,1536]{2,1,0:T(8,128)(2,1)S(1)}, u32[]{:S(2)}, u32[]{:S(2)}) async-start(bf16[4,64,1536]{2,1,0:T(8,128)(2,1)} %bitcast.7), calls=%async_computation.3 | async-start | bytes 1572864 | tf_op jit(solution)/shard_map/sum_texts/all_to_all | solution.py:23
  91.7 17.2 %collective-permute-start.7 = (bf16[64,1536]{1,0:T(8,128)(2,1)}, bf16[64,1536]{1,0:T(8,128)(2,1)S(1)}, u32[]{:S(2)}, u32[]{:S(2)}) collective-permute-start(bf16[64,1536]{1,0:T(8,128)(2,1)} %get-tuple-element.18), channel_id=1, source_target_pairs={{0,2},{2,4},{4,6},{6,0},{1,3},{3,5},{5,7},{7,1},{8,10},{10,12},{12... | collective-permute-start | bytes 589832 | tf_op jit(solution)/shard_map/sum_images/ppermute | solution.py:37
  93.6 15.3 %collective-permute-start.8 = (bf16[64,1536]{1,0:T(8,128)(2,1)}, bf16[64,1536]{1,0:T(8,128)(2,1)S(1)}, u32[]{:S(2)}, u32[]{:S(2)}) collective-permute-start(bf16[64,1536]{1,0:T(8,128)(2,1)} %get-tuple-element.20), channel_id=1, source_target_pairs={{0,4},{2,6},{4,0},{6,2},{1,5},{3,7},{5,1},{7,3},{8,12},{10,14},{12... | collective-permute-start | bytes 589832 | tf_op jit(solution)/shard_map/sum_images/ppermute | solution.py:37
  98.4 10.5 %collective-permute-start.9 = (bf16[64,1536]{1,0:T(8,128)(2,1)}, bf16[64,1536]{1,0:T(8,128)(2,1)}, u32[]{:S(2)}, u32[]{:S(2)}) collective-permute-start(bf16[64,1536]{1,0:T(8,128)(2,1)} %get-tuple-element.19), channel_id=1, source_target_pairs={{0,6},{2,0},{4,2},{6,4},{1,7},{3,1},{5,3},{7,5},{8,14},{10,8},{12,... | collective-permute-start | bytes 589832 | tf_op jit(solution)/shard_map/sum_images/ppermute | solution.py:37
  102.5 19.4 %all-to-all-start.4 = ((bf16[4,16,1536]{2,1,0:T(8,128)(2,1)}), bf16[4,16,1536]{2,1,0:T(8,128)(2,1)S(1)}, u32[]{:S(2)}, u32[]{:S(2)}) async-start(bf16[4,16,1536]{2,1,0:T(8,128)(2,1)} %bitcast.8), calls=%async_computation.4 | async-start | bytes 393216 | tf_op jit(solution)/shard_map/sum_texts/all_to_all | solution.py:23
  109.9 12.0 %collective-permute-start.10 = (bf16[16,1536]{1,0:T(8,128)(2,1)S(1)}, bf16[16,1536]{1,0:T(8,128)(2,1)S(1)}, u32[]{:S(2)}, u32[]{:S(2)}) collective-permute-start(bf16[16,1536]{1,0:T(8,128)(2,1)S(1)} %get-tuple-element.25), channel_id=1, source_target_pairs={{0,16},{16,32},{32,48},{48,0},{1,17},{17,33},{33,49},{49,1},{2,18}... | collective-permute-start | bytes 147464 | tf_op jit(solution)/shard_map/sum_images/ppermute | solution.py:37
  113.5 8.5 %collective-permute-start.11 = (bf16[16,1536]{1,0:T(8,128)(2,1)S(1)}, bf16[16,1536]{1,0:T(8,128)(2,1)S(1)}, u32[]{:S(2)}, u32[]{:S(2)}) collective-permute-start(bf16[16,1536]{1,0:T(8,128)(2,1)S(1)} %get-tuple-element.27), channel_id=1, source_target_pairs={{0,32},{16,48},{32,0},{48,16},{1,33},{17,49},{33,1},{49,17},{2,34}... | collective-permute-start | bytes 147464 | tf_op jit(solution)/shard_map/sum_images/ppermute | solution.py:37
  116.6 5.8 %collective-permute-start.12 = (bf16[16,1536]{1,0:T(8,128)(2,1)S(1)}, bf16[16,1536]{1,0:T(8,128)(2,1)S(1)}, u32[]{:S(2)}, u32[]{:S(2)}) collective-permute-start(bf16[16,1536]{1,0:T(8,128)(2,1)S(1)} %get-tuple-element.26), channel_id=1, source_target_pairs={{0,48},{16,0},{32,16},{48,32},{1,49},{17,1},{33,17},{49,33},{2,50}... | collective-permute-start | bytes 147464 | tf_op jit(solution)/shard_map/sum_images/ppermute | solution.py:37
  123.6 16.3 %all-to-all-start.5 = ((bf16[8,2,16,1536]{3,2,1,0:T(8,128)(2,1)}), bf16[8,2,16,1536]{3,2,1,0:T(8,128)(2,1)S(1)}, u32[]{:S(2)}, u32[]{:S(2)}) async-start(bf16[8,2,16,1536]{3,2,1,0:T(8,128)(2,1)} %broadcast_in_dim.15), calls=%async_computation.5 | async-start | bytes 1572864 | tf_op jit(solution)/shard_map/head_grads/all_to_all | solution.py:23
  129.5 10.5 %copy-start.3 = (bf16[128,192]{0,1:T(8,128)(2,1)S(1)}, bf16[128,192]{0,1:T(8,128)(2,1)}, u32[]{:S(2)}) copy-start(bf16[128,192]{0,1:T(8,128)(2,1)} %param.7) | copy-start | bytes 147460
  129.5 10.8 %copy-start.2 = (bf16[128,192]{0,1:T(8,128)(2,1)S(1)}, bf16[128,192]{0,1:T(8,128)(2,1)}, u32[]{:S(2)}) copy-start(bf16[128,192]{0,1:T(8,128)(2,1)} %param.8) | copy-start | bytes 147460
  140.5 10.7 %collective-permute-start.14 = (bf16[2,96,1536]{2,1,0:T(8,128)(2,1)S(1)}, bf16[2,96,1536]{2,1,0:T(8,128)(2,1)S(1)}, u32[]{:S(2)}, u32[]{:S(2)}) collective-permute-start(bf16[2,96,1536]{2,1,0:T(8,128)(2,1)S(1)} %pad_maximum_fusion.1), channel_id=1, source_target_pairs={{0,8},{8,0},{1,9},{9,1},{2,10},{10,2},{3,11},{11,3},{4,12},{12,4},... | collective-permute-start | bytes 1769480 | tf_op jit(solution)/shard_map/weight_grads/ppermute | solution.py:37
  197.4 27.7 %copy-start.1 = (bf16[192,1536]{1,0:T(8,128)(2,1)S(1)}, bf16[192,1536]{1,0:T(8,128)(2,1)}, u32[]{:S(2)}) copy-start(bf16[192,1536]{1,0:T(8,128)(2,1)} %param.10) | copy-start | bytes 1769476
  197.4 23.3 %all-to-all-start.8 = ((bf16[8,24,1536]{2,1,0:T(8,128)(2,1)}), bf16[8,24,1536]{2,1,0:T(8,128)(2,1)S(1)}, u32[]{:S(2)}, u32[]{:S(2)}) async-start(bf16[8,24,1536]{2,1,0:T(8,128)(2,1)} %broadcast_in_dim.17), calls=%async_computation.8 | async-start | bytes 1179648 | tf_op jit(solution)/shard_map/weight_grads/all_to_all | solution.py:23
  220.7 6.1 %collective-permute-start.15 = (bf16[2,96,1536]{2,1,0:T(8,128)(2,1)S(1)}, bf16[2,96,1536]{2,1,0:T(8,128)(2,1)S(1)}, u32[]{:S(2)}, u32[]{:S(2)}) collective-permute-start(bf16[2,96,1536]{2,1,0:T(8,128)(2,1)S(1)} %bitcast.81), channel_id=1, source_target_pairs={{0,8},{8,0},{1,9},{9,1},{2,10},{10,2},{3,11},{11,3},{4,12},{12,4},... | collective-permute-start | bytes 1769480 | tf_op jit(solution)/shard_map/weight_grads/ppermute | solution.py:37

commit v3 on v2

v3 whole, which is shorter than its diff:
```python
import jax
import jax.numpy as jnp
from jax import lax
from jax.sharding import Mesh, PartitionSpec as P

BF16 = jnp.bfloat16
F32 = jnp.float32

PARTS = {"xl": 2, "zh": 4, "zl": 4, "c": 2, "y": 4, "xh": 2}
DP = ("xl", "zh", "zl", "c")
MP = ("y", "xh")


def count(axes):
    axes = (axes,) if isinstance(axes, str) else axes
    n = 1
    for axis in axes:
        n *= PARTS[axis]
    return n


def exchange(blocks, axes):
    return lax.all_to_all(blocks, axes, split_axis=0, concat_axis=0, tiled=True)


def gather(rows, axes):
    n = count(axes)
    return exchange(jnp.broadcast_to(rows[None], (n,) + rows.shape), axes)


def scatter_sum(blocks, axes):
    return jnp.sum(exchange(blocks.astype(BF16), axes).astype(F32), axis=0)


def shifted(value, axis, by):
    n = PARTS[axis]
    return lax.ppermute(value, axis, [(i, (i + by) % n) for i in range(n)])


def ring_gather(rows, axis):
    n = PARTS[axis]
    return jnp.concatenate([rows] + [shifted(rows, axis, n - k) for k in range(1, n)], axis=0)


def ring_scatter_sum(total, axis):
    n = PARTS[axis]
    blocks = split_rows(total, n)
    own = blocks[0]
    for k in range(1, n):
        own = own + shifted(blocks[k].astype(BF16), axis, k).astype(F32)
    return own


def split_rows(value, n):
    return value.reshape((n, value.shape[0] // n) + value.shape[1:])


def merge_rows(value):
    return value.reshape((-1,) + value.shape[2:])


def unit_rows(heads):
    values = heads.astype(F32)
    norm = jnp.sqrt(jnp.sum(values * values, axis=1, keepdims=True) + 1e-06)
    return ((values / norm).astype(BF16), norm)


def columns(value, start, size):
    return lax.dynamic_slice_in_dim(value, start, size, value.ndim - 1)


def on_device(
    image_features,
    text_features,
    image_weight,
    text_weight,
    logit_scale,
    logit_bias,
    loss_cotangent,
):
    at = {axis: lax.axis_index(axis) for axis in PARTS}
    core, side = at["c"], at["xl"]
    scale = logit_scale[0]
    shift_bias = logit_bias[0]
    factor = loss_cotangent[0] * scale
    width, embed_width = image_weight.shape
    half, quarter = embed_width // 2, embed_width // 4
    members = count(MP)
    share = image_features.shape[0] // members

    with jax.named_scope("heads"):
        partial_heads = jnp.concatenate(
            (
                jnp.dot(image_features, image_weight, preferred_element_type=F32).astype(BF16),
                jnp.dot(text_features, text_weight, preferred_element_type=F32).astype(BF16),
            ),
            axis=1,
        )
        both_heads = scatter_sum(split_rows(partial_heads, members), MP).astype(BF16)

    with jax.named_scope("gather_features"):
        features = jnp.stack((image_features, text_features))
        features = jnp.stack((features, shifted(features, "c", 1)))
        other_features = shifted(features, "xl", 1)

        def ordered(mine, theirs):
            both = jnp.stack((mine, theirs), axis=1)
            both = both.reshape(2, 2, members, share, width).transpose(2, 0, 1, 3, 4)
            return both.reshape(-1, width)

        image_rows = ordered(features[:, 0], other_features[:, 0])
        first = side == 0
        text_rows = ordered(
            jnp.where(first, features[:, 1], other_features[:, 1]),
            jnp.where(first, other_features[:, 1], features[:, 1]),
        )

    with jax.named_scope("gather_texts"):
        texts = merge_rows(gather(both_heads[:, embed_width:], "zh"))
        texts = merge_rows(gather(texts, ("xh", "xl")))
        other_texts = shifted(texts, "c", 1)
    with jax.named_scope("gather_images"):
        images = ring_gather(ring_gather(both_heads[:, :embed_width], "zl"), "y")

    with jax.named_scope("pairs"):
        image_embed, image_norm = unit_rows(images)

        def coefficients(block, positive):
            embed, norm = unit_rows(block)
            dots = jnp.einsum("te,ie->ti", embed, image_embed, preferred_element_type=F32)
            coeff = factor * (jax.nn.sigmoid(scale * dots + shift_bias) - positive)
            coeff = coeff.astype(BF16)
            return (embed, norm, coeff, coeff.astype(F32) * dots)

        text_base = ((at["xh"] * 2 + side) * 4 + at["zh"]) * share
        text_at = jnp.arange(texts.shape[0], dtype=jnp.int32)[:, None] - text_base
        image_at = jnp.arange(images.shape[0], dtype=jnp.int32)[None, :]
        positive = (text_at == image_at) & (image_at < share)
        embed, norm, coeff, along = coefficients(texts, positive.astype(F32))
        other_embed, other_norm, other_coeff, other_along = coefficients(other_texts, 0.0)

        def projected(total, heads, norm, along):
            return ((total - heads.astype(F32) * (along / norm)) / norm).astype(BF16)

        def text_half(which):
            embeds = columns(image_embed, which * half, half)
            return [
                projected(
                    jnp.dot(part, embeds, preferred_element_type=F32),
                    columns(heads, which * half, half),
                    norms,
                    jnp.sum(toward, axis=1, keepdims=True),
                )
                for part, heads, norms, toward in (
                    (coeff, texts, norm, along),
                    (other_coeff, other_texts, other_norm, other_along),
                )
            ]

        sent = jnp.stack(text_half(1 - core)[::-1])
        kept = jnp.stack(text_half(core))
        image_part = jnp.einsum("ti,te->ie", coeff, embed, preferred_element_type=F32)
        image_part = image_part + jnp.einsum(
            "ti,te->ie", other_coeff, other_embed, preferred_element_type=F32
        )
        image_along = jnp.sum(along, axis=0) + jnp.sum(other_along, axis=0)
        image_part = projected(image_part, images, image_norm, image_along[:, None])

    with jax.named_scope("sum_texts"):
        text_part = kept.astype(F32) + shifted(sent, "c", 1).astype(F32)
        text_part = text_part.astype(BF16).reshape(2, 2, 2, 4 * share, 2, quarter)
        text_part = text_part.transpose(1, 4, 0, 2, 3, 5).reshape(4, 16 * share, quarter)
        text_part = scatter_sum(text_part, ("xh", "xl")).astype(BF16)
        text_part = text_part.reshape(4, 4, share, quarter).swapaxes(0, 1)
        text_grads = scatter_sum(text_part.reshape(4, 4 * share, quarter), "zh").astype(BF16)
    with jax.named_scope("sum_images"):
        image_grads = ring_scatter_sum(ring_scatter_sum(image_part, "y"), "zl").astype(BF16)
        theirs = shifted(columns(image_grads, (1 - core) * half, half), "c", 1)
        image_grads = jnp.stack((columns(image_grads, core * half, half), theirs))
        theirs = shifted(columns(image_grads, (1 - side) * quarter, quarter), "xl", 1)
        image_grads = jnp.stack((columns(image_grads, side * quarter, quarter), theirs), axis=1)

    with jax.named_scope("head_grads"):
        grads = jnp.stack((image_grads.reshape(4 * share, quarter), text_grads))
        grads = gather(grads, MP)
        image_grads, text_grads = merge_rows(grads[:, 0]), merge_rows(grads[:, 1])

    with jax.named_scope("weight_grads"):
        part = jnp.stack(
            [
                jnp.dot(rows.T, grads, preferred_element_type=F32)
                .astype(BF16)
                .reshape(4, width // 4, quarter)
                for rows, grads in ((image_rows, image_grads), (text_rows, text_grads))
            ],
            axis=1,
        )
        part = scatter_sum(part, "zl").astype(BF16)
        part = jnp.sum(gather(part, "zh").astype(F32), axis=0).astype(BF16)
        part = gather(part, ("xl", "zl")).reshape(2, 4, 2, width // 4, quarter)
        part = part.transpose(2, 1, 3, 0, 4).reshape(2, width, half)
        other = shifted(part, "c", 1)
        image_weight_grad, text_weight_grad = (
            jnp.concatenate(
                (jnp.where(core == 0, mine, theirs), jnp.where(core == 0, theirs, mine)), axis=1
            ).astype(F32)
            for mine, theirs in zip(part, other)
        )

    with jax.named_scope("input_grads"):
        start = core * half + side * quarter
        image_input, text_input = (
            jnp.dot(grads, columns(weight, start, quarter).T, preferred_element_type=F32).reshape(
                members, 2, 2, share, width
            )
            for grads, weight in ((image_grads, image_weight), (text_grads, text_weight))
        )
        text_input = jnp.where(first, text_input, text_input[:, :, ::-1])
        inputs = jnp.stack((image_input, text_input))
        inputs = inputs[:, :, 0] + shifted(inputs[:, :, 1].astype(BF16), "c", 1).astype(F32)
        inputs = inputs[:, :, 0] + shifted(inputs[:, :, 1].astype(BF16), "xl", 1).astype(F32)
        inputs = inputs.reshape(2, members * share, width)
    return (inputs[0], inputs[1], image_weight_grad, text_weight_grad)


def solution(mesh):
    fine = Mesh(mesh.devices.reshape(tuple(PARTS.values())), tuple(PARTS))
    return jax.shard_map(
        on_device,
        mesh=fine,
        in_specs=(P(DP, MP), P(DP, MP), P(MP, None), P(MP, None), P(), P(), P()),
        out_specs=(P(DP, MP), P(DP, MP), P(MP, None), P(MP, None)),
        check_vma=False,
    )
```

time: 230 us -> 243 us (1.057)
  starting transfers between devices: 114 us -> 128 us
  blocking collectives: 45.1 us -> 38.1 us
  waiting for transfers between devices: 45.3 us -> 39.7 us
  local copies, waits for them, and re-layouts: 5.59 us -> 10.2 us
  matrix products: 9.46 us -> 13.3 us
    all_to_all x7, waiting for transfers between devices: 41.4 us -> 22 us  [exchange(): return lax.all_to_all(blocks, axes, split_axis=0, concat_axis=0, tiled=True)]
    ppermute x16 -> x21, waiting for transfers between devices: 3.9 us -> 17.7 us  [shifted(): return lax.ppermute(value, axis, [(i, (i + by) % n) for i in range(n)])]
    ppermute x16 -> x21, starting transfers between devices: 61.9 us -> 74.3 us  [shifted(): return lax.ppermute(value, axis, [(i, (i + by) % n) for i in range(n)])]
    all_to_all x2, blocking collectives: 45.1 us -> 38.1 us  [exchange(): return lax.all_to_all(blocks, axes, split_axis=0, concat_axis=0, tiled=True)]
    dot_general x12, matrix products: 6.94 us -> 10.7 us  [the longest x4 4.25 us: text_half(): jnp.dot(part, embeds, preferred_element_type=F32)]
    unnamed x13 -> x21, local copies, waits for them, and re-layouts: 0.07 us -> 2.69 us
  transfers between devices with their start and end apart: 23 -> 28, of which waited for: 11 -> 10; matrix products, arithmetic and copies ran while one was open for 4% -> 8% of each run, Pallas kernels for 0% -> 0%
where the time goes in v3:
time: 243 us; the launch traced here: 242 us
  starting transfers between devices  128 us (53%)
  waiting for transfers between devices  39.7 us (16%)
  blocking collectives  38.1 us (16%)
  matrix products  13.3 us (5%)
  local copies, waits for them, and re-layouts  10.2 us (4%)
  other arithmetic  8.5 us (3%)
  between operations  3.41 us (1%)
    ppermute x21, starting transfers between devices, shifted(): return lax.ppermute(value, axis, [(i, (i + by) % n) for i in range(n)])  74.3 us
    all_to_all x7, starting transfers between devices, exchange(): return lax.all_to_all(blocks, axes, split_axis=0, concat_axis=0, tiled=True)  54.1 us
    all_to_all x2, blocking collectives, exchange(): return lax.all_to_all(blocks, axes, split_axis=0, concat_axis=0, tiled=True)  38.1 us
    all_to_all x7, waiting for transfers between devices, exchange(): return lax.all_to_all(blocks, axes, split_axis=0, concat_axis=0, tiled=True)  22 us
    ppermute x21, waiting for transfers between devices, shifted(): return lax.ppermute(value, axis, [(i, (i + by) % n) for i in range(n)])  17.7 us
  transfers between devices with their start and end apart: 28, of which 10 were waited for; matrix products, arithmetic and copies ran while one was open for 8% of the time, Pallas kernels for 0%

profile of v3, /device:TPU:1, one launch (start us, length us, event | category | flops | bytes accessed | tf_op | source)
XLA Modules:
  0.0 241.5 jit_solution(11865843568623315998)
XLA Ops:
  0.6 1.4 convolution_convert_fusion
  2.1 1.1 convolution_convert_fusion.1
  3.2 1.0 pad_maximum_fusion
  4.2 7.5 %all-to-all-start = ((bf16[8,16,3072]{2,1,0:T(8,128)(2,1)}), bf16[8,16,3072]{2,1,0:T(8,128)(2,1)S(1)}, u32[]{:S(2)}, u32[]{:S(2)}) async-start(bf16[8,16,3072]{2,1,0:T(8,128)(2,1)} %bitcast.2), calls=%async_computation | async-start | bytes 1572864 | tf_op jit(solution)/shard_map/heads/all_to_all | solution.py:23
  11.6 11.2 %all-to-all-done = bf16[8,16,3072]{2,1,0:T(8,128)(2,1)S(1)} async-done(((bf16[8,16,3072]{2,1,0:T(8,128)(2,1)}), bf16[8,16,3072]{2,1,0:T(8,128)(2,1)S(1)}, u32[]{:S(2)}, u32[]{:S(2)}) %all-to-all-start) | async-done | bytes 786464 | tf_op jit(solution)/shard_map/heads/all_to_all | solution.py:23
  23.0 8.2 %collective-permute-start = (bf16[16,1536]{1,0:T(8,128)(2,1)S(1)}, bf16[16,1536]{1,0:T(8,128)(2,1)S(1)}, u32[]{:S(2)}, u32[]{:S(2)}) collective-permute-start(bf16[16,1536]{1,0:T(8,128)(2,1)S(1)} %get-tuple-element.55), channel_id=1, source_target_pairs={{0,48},{16,0},{32,16},{48,32},{1,49},{17,1},{33,17},{49,33},{2,50}... | collective-permute-start | bytes 147464 | tf_op jit(solution)/shard_map/gather_images/ppermute | solution.py:37
  31.2 1.9 collective-permute-start.1
  33.1 2.2 collective-permute-start.2
  37.3 0.7 broadcast_in_dim.12
  38.0 12.8 %all-to-all-start.1 = ((bf16[4,16,1536]{2,1,0:T(8,128)(2,1)}), bf16[4,16,1536]{2,1,0:T(8,128)(2,1)S(1)}, u32[]{:S(2)}, u32[]{:S(2)}) async-start(bf16[4,16,1536]{2,1,0:T(8,128)(2,1)} %broadcast_in_dim.12), calls=%async_computation.1 | async-start | bytes 393216 | tf_op jit(solution)/shard_map/gather_texts/all_to_all | solution.py:23
  50.9 2.8 %collective-permute-start.3 = (bf16[64,1536]{1,0:T(8,128)(2,1)S(1)}, bf16[64,1536]{1,0:T(8,128)(2,1)S(1)}, u32[]{:S(2)}, u32[]{:S(2)}) collective-permute-start(bf16[64,1536]{1,0:T(8,128)(2,1)S(1)} %pad_maximum_fusion.6), channel_id=1, source_target_pairs={{0,6},{2,0},{4,2},{6,4},{1,7},{3,1},{5,3},{7,5},{8,14},{10,8},{12,... | collective-permute-start | bytes 589832 | tf_op jit(solution)/shard_map/gather_images/ppermute | solution.py:37
  53.7 2.2 collective-permute-start.4
  55.9 2.5 %collective-permute-start.5 = (bf16[64,1536]{1,0:T(8,128)(2,1)S(1)}, bf16[64,1536]{1,0:T(8,128)(2,1)S(1)}, u32[]{:S(2)}, u32[]{:S(2)}) collective-permute-start(bf16[64,1536]{1,0:T(8,128)(2,1)S(1)} %pad_maximum_fusion.6), channel_id=1, source_target_pairs={{0,2},{2,4},{4,6},{6,0},{1,3},{3,5},{5,7},{7,1},{8,10},{10,12},{12... | collective-permute-start | bytes 589832 | tf_op jit(solution)/shard_map/gather_images/ppermute | solution.py:37
  58.4 3.4 %collective-permute-done.4 = bf16[64,1536]{1,0:T(8,128)(2,1)S(1)} collective-permute-done((bf16[64,1536]{1,0:T(8,128)(2,1)S(1)}, bf16[64,1536]{1,0:T(8,128)(2,1)S(1)}, u32[]{:S(2)}, u32[]{:S(2)}) %collective-permute-start.4) | collective-permute-done | bytes 196640 | tf_op jit(solution)/shard_map/gather_images/ppermute | solution.py:37
  61.9 2.6 %collective-permute-done.5 = bf16[64,1536]{1,0:T(8,128)(2,1)S(1)} collective-permute-done((bf16[64,1536]{1,0:T(8,128)(2,1)S(1)}, bf16[64,1536]{1,0:T(8,128)(2,1)S(1)}, u32[]{:S(2)}, u32[]{:S(2)}) %collective-permute-start.5) | collective-permute-done | bytes 196640 | tf_op jit(solution)/shard_map/gather_images/ppermute | solution.py:37
  64.8 0.9 broadcast_in_dim.14
  65.7 6.0 %all-to-all-start.2 = ((bf16[4,64,1536]{2,1,0:T(8,128)(2,1)}), bf16[4,64,1536]{2,1,0:T(8,128)(2,1)S(1)}, u32[]{:S(2)}, u32[]{:S(2)}) async-start(bf16[4,64,1536]{2,1,0:T(8,128)(2,1)} %broadcast_in_dim.14), calls=%async_computation.2 | async-start | bytes 1572864 | tf_op jit(solution)/shard_map/gather_texts/all_to_all | solution.py:23
  71.7 1.2 fusion.6
  72.9 8.6 %all-to-all-done.2 = bf16[4,64,1536]{2,1,0:T(8,128)(2,1)S(1)} async-done(((bf16[4,64,1536]{2,1,0:T(8,128)(2,1)}), bf16[4,64,1536]{2,1,0:T(8,128)(2,1)S(1)}, u32[]{:S(2)}, u32[]{:S(2)}) %all-to-all-start.2) | async-done | bytes 786464 | tf_op jit(solution)/shard_map/gather_texts/all_to_all | solution.py:23
  81.5 5.4 %collective-permute-start.6 = (bf16[256,1536]{1,0:T(8,128)(2,1)S(1)}, bf16[256,1536]{1,0:T(8,128)(2,1)}, u32[]{:S(2)}, u32[]{:S(2)}) collective-permute-start(bf16[256,1536]{1,0:T(8,128)(2,1)S(1)} %bitcast.136), channel_id=1, source_target_pairs={{0,8},{8,0},{1,9},{9,1},{2,10},{10,2},{3,11},{11,3},{4,12},{12,4},... | collective-permute-start | bytes 2359304 | tf_op jit(solution)/shard_map/gather_texts/ppermute | solution.py:37
  87.4 0.9 copy-done.1
  88.3 0.5 fusion.34
  88.9 1.4 fusion.12
  90.6 0.4 fusion.68
  91.0 1.4 fusion.3
  92.4 1.7 fusion.36
  94.1 1.3 fusion.19
  95.5 1.9 collective-permute-start.15
  97.4 1.8 fusion.2
  99.2 1.9 collective-permute-start.7
  101.2 2.9 %collective-permute-start.8 = (bf16[64,1536]{1,0:T(8,128)(2,1)S(1)}, bf16[64,1536]{1,0:T(8,128)(2,1)}, u32[]{:S(2)}, u32[]{:S(2)}) collective-permute-start(bf16[64,1536]{1,0:T(8,128)(2,1)S(1)} %get-tuple-element.39), channel_id=1, source_target_pairs={{0,4},{2,6},{4,0},{6,2},{1,5},{3,7},{5,1},{7,3},{8,12},{10,14},{12... | collective-permute-start | bytes 589832 | tf_op jit(solution)/shard_map/sum_images/ppermute | solution.py:37
  104.1 3.6 %collective-permute-start.9 = (bf16[64,1536]{1,0:T(8,128)(2,1)S(1)}, bf16[64,1536]{1,0:T(8,128)(2,1)}, u32[]{:S(2)}, u32[]{:S(2)}) collective-permute-start(bf16[64,1536]{1,0:T(8,128)(2,1)S(1)} %get-tuple-element.38), channel_id=1, source_target_pairs={{0,6},{2,0},{4,2},{6,4},{1,7},{3,1},{5,3},{7,5},{8,14},{10,8},{12,... | collective-permute-start | bytes 589832 | tf_op jit(solution)/shard_map/sum_images/ppermute | solution.py:37
  107.7 1.3 fusion.18
  109.4 1.0 copy.56
  110.4 3.5 %all-to-all-start.3 = ((bf16[4,256,384]{2,1,0:T(8,128)(2,1)}), bf16[4,256,384]{2,1,0:T(8,128)(2,1)S(1)}, u32[]{:S(2)}, u32[]{:S(2)}) async-start(bf16[4,256,384]{2,1,0:T(8,128)(2,1)} %bitcast.16), calls=%async_computation.3 | async-start | bytes 1572864 | tf_op jit(solution)/shard_map/sum_texts/all_to_all | solution.py:23
  113.9 0.9 collective-permute-done.9
  114.8 1.2 fusion.61
  116.1 3.5 %collective-permute-start.10 = (bf16[16,1536]{1,0:T(8,128)(2,1)S(1)}, bf16[16,1536]{1,0:T(8,128)(2,1)S(1)}, u32[]{:S(2)}, u32[]{:S(2)}) collective-permute-start(bf16[16,1536]{1,0:T(8,128)(2,1)S(1)} %get-tuple-element.50), channel_id=1, source_target_pairs={{0,16},{16,32},{32,48},{48,0},{1,17},{17,33},{33,49},{49,1},{2,18}... | collective-permute-start | bytes 147464 | tf_op jit(solution)/shard_map/sum_images/ppermute | solution.py:37
  119.7 3.1 %collective-permute-start.11 = (bf16[16,1536]{1,0:T(8,128)(2,1)S(1)}, bf16[16,1536]{1,0:T(8,128)(2,1)S(1)}, u32[]{:S(2)}, u32[]{:S(2)}) collective-permute-start(bf16[16,1536]{1,0:T(8,128)(2,1)S(1)} %get-tuple-element.52), channel_id=1, source_target_pairs={{0,32},{16,48},{32,0},{48,16},{1,33},{17,49},{33,1},{49,17},{2,34}... | collective-permute-start | bytes 147464 | tf_op jit(solution)/shard_map/sum_images/ppermute | solution.py:37
  122.7 3.1 %collective-permute-start.12 = (bf16[16,1536]{1,0:T(8,128)(2,1)S(1)}, bf16[16,1536]{1,0:T(8,128)(2,1)S(1)}, u32[]{:S(2)}, u32[]{:S(2)}) collective-permute-start(bf16[16,1536]{1,0:T(8,128)(2,1)S(1)} %get-tuple-element.51), channel_id=1, source_target_pairs={{0,48},{16,0},{32,16},{48,32},{1,49},{17,1},{33,17},{49,33},{2,50}... | collective-permute-start | bytes 147464 | tf_op jit(solution)/shard_map/sum_images/ppermute | solution.py:37
  126.0 0.7 copy.57
  126.7 11.2 %all-to-all-start.4 = ((bf16[4,64,384]{2,1,0:T(8,128)(2,1)}), bf16[4,64,384]{2,1,0:T(8,128)(2,1)S(1)}, u32[]{:S(2)}, u32[]{:S(2)}) async-start(bf16[4,64,384]{2,1,0:T(8,128)(2,1)} %bitcast.19), calls=%async_computation.4 | async-start | bytes 393216 | tf_op jit(solution)/shard_map/sum_texts/all_to_all | solution.py:23
  138.0 4.6 %collective-permute-start.13 = (bf16[16,768]{1,0:T(8,128)(2,1)S(1)}, bf16[16,768]{1,0:T(8,128)(2,1)S(1)}, u32[]{:S(2)}, u32[]{:S(2)}) collective-permute-start(bf16[16,768]{1,0:T(8,128)(2,1)S(1)} %get-tuple-element.60), channel_id=1, source_target_pairs={{0,8},{8,0},{1,9},{9,1},{2,10},{10,2},{3,11},{11,3},{4,12},{12,4},... | collective-permute-start | bytes 73736 | tf_op jit(solution)/shard_map/sum_images/ppermute | solution.py:37
  142.9 0.6 collective-permute-done.13
  143.5 2.2 collective-permute-start.14
  145.7 2.5 %collective-permute-start.18 = (bf16[2,128,192]{2,1,0:T(8,128)(2,1)S(1)}, bf16[2,128,192]{2,1,0:T(8,128)(2,1)S(1)}, u32[]{:S(2)}, u32[]{:S(2)}) collective-permute-start(bf16[2,128,192]{2,1,0:T(8,128)(2,1)S(1)} %get-tuple-element.54), channel_id=1, source_target_pairs={{0,8},{8,0},{1,9},{9,1},{2,10},{10,2},{3,11},{11,3},{4,12},{12,4},... | collective-permute-start | bytes 294920 | tf_op jit(solution)/shard_map/gather_features/ppermute | solution.py:37
  148.4 2.2 all-to-all-done.4
  150.6 1.0 broadcast_in_dim.15
  151.6 5.7 %all-to-all-start.5 = ((bf16[8,2,64,384]{3,2,1,0:T(8,128)(2,1)}), bf16[8,2,64,384]{3,2,1,0:T(8,128)(2,1)S(1)}, u32[]{:S(2)}, u32[]{:S(2)}) async-start(bf16[8,2,64,384]{3,2,1,0:T(8,128)(2,1)} %broadcast_in_dim.15), calls=%async_computation.5 | async-start | bytes 1572864 | tf_op jit(solution)/shard_map/head_grads/all_to_all | solution.py:23
  157.3 2.8 %collective-permute-start.19 = (bf16[2,2,128,192]{3,2,1,0:T(8,128)(2,1)S(1)}, bf16[2,2,128,192]{3,2,1,0:T(8,128)(2,1)S(1)}, u32[]{:S(2)}, u32[]{:S(2)}) collective-permute-start(bf16[2,2,128,192]{3,2,1,0:T(8,128)(2,1)S(1)} %pad_maximum_fusion.3), channel_id=1, source_target_pairs={{0,256},{256,0},{1,257},{257,1},{2,258},{258,2},{3,259},{259,3},{4... | collective-permute-start | bytes 589832 | tf_op jit(solution)/shard_map/gather_features/ppermute | solution.py:37
  160.2 8.9 %collective-permute-done.19 = bf16[2,2,128,192]{3,2,1,0:T(8,128)(2,1)S(1)} collective-permute-done((bf16[2,2,128,192]{3,2,1,0:T(8,128)(2,1)S(1)}, bf16[2,2,128,192]{3,2,1,0:T(8,128)(2,1)S(1)}, u32[]{:S(2)}, u32[]{:S(2)}) %collective-permute-start.19) | collective-permute-done | bytes 196640 | tf_op jit(solution)/shard_map/gather_features/ppermute | solution.py:37
  170.0 13.5 %all_to_all.45 = bf16[4,2,48,384]{3,2,1,0:T(8,128)(2,1)S(1)} all-to-all(bf16[4,2,48,384]{3,2,1,0:T(8,128)(2,1)S(1)} %pad_maximum_fusion.4), channel_id=1, replica_groups=mesh['xl'=2,'zh'=4,'zl'=4,'c'=2,'y'=4,'xh'=2] {'zl'}, dimensions={0} | all-to-all | bytes 589824 | tf_op jit(solution)/shard_map/weight_grads/all_to_all | solution.py:23
  183.6 24.6 %all_to_all.46 = bf16[4,2,48,384]{3,2,1,0:T(8,128)(2,1)S(1)} all-to-all(bf16[4,2,48,384]{3,2,1,0:T(8,128)(2,1)S(1)} %broadcast_in_dim.16), channel_id=1, replica_groups=mesh['xl'=2,'zh'=4,'zl'=4,'c'=2,'y'=4,'xh'=2] {'zh'}, dimensions={0} | all-to-all | bytes 589824 | tf_op jit(solution)/shard_map/weight_grads/all_to_all | solution.py:23
  208.3 0.9 broadcast_in_dim.17
  209.1 7.5 %all-to-all-start.8 = ((bf16[8,2,48,384]{3,2,1,0:T(8,128)(2,1)}), bf16[8,2,48,384]{3,2,1,0:T(8,128)(2,1)S(1)}, u32[]{:S(2)}, u32[]{:S(2)}) async-start(bf16[8,2,48,384]{3,2,1,0:T(8,128)(2,1)} %broadcast_in_dim.17), calls=%async_computation.8 | async-start | bytes 1179648 | tf_op jit(solution)/shard_map/weight_grads/all_to_all | solution.py:23
  216.9 1.2 fusion.37
  218.2 6.0 %collective-permute-start.16 = (bf16[2,8,2,16,192]{4,3,2,1,0:T(8,128)(2,1)S(1)}, bf16[2,8,2,16,192]{4,3,2,1,0:T(8,128)(2,1)S(1)}, u32[]{:S(2)}, u32[]{:S(2)}) collective-permute-start(bf16[2,8,2,16,192]{4,3,2,1,0:T(8,128)(2,1)S(1)} %fusion.30), channel_id=1, source_target_pairs={{0,8},{8,0},{1,9},{9,1},{2,10},{10,2},{3,11},{11,3},{4,12},{12,4},... | collective-permute-start | bytes 589832 | tf_op jit(solution)/shard_map/input_grads/ppermute | solution.py:37
  224.2 1.1 collective-permute-done.16
  225.5 3.6 %collective-permute-start.17 = (bf16[2,8,16,192]{3,2,1,0:T(8,128)(2,1)S(1)}, bf16[2,8,16,192]{3,2,1,0:T(8,128)(2,1)S(1)}, u32[]{:S(2)}, u32[]{:S(2)}) collective-permute-start(bf16[2,8,16,192]{3,2,1,0:T(8,128)(2,1)S(1)} %fusion.42), channel_id=1, source_target_pairs={{0,256},{256,0},{1,257},{257,1},{2,258},{258,2},{3,259},{259,3},{4... | collective-permute-start | bytes 294920 | tf_op jit(solution)/shard_map/input_grads/ppermute | solution.py:37
  229.2 0.6 copy.67
  230.2 7.2 %collective-permute-start.20 = (bf16[2,192,768]{2,1,0:T(8,128)(2,1)S(1)}, bf16[2,192,768]{2,1,0:T(8,128)(2,1)S(1)}, u32[]{:S(2)}, u32[]{:S(2)}) collective-permute-start(bf16[2,192,768]{2,1,0:T(8,128)(2,1)S(1)} %reshape.175), channel_id=1, source_target_pairs={{0,8},{8,0},{1,9},{9,1},{2,10},{10,2},{3,11},{11,3},{4,12},{12,4},... | collective-permute-start | bytes 1769480 | tf_op jit(solution)/shard_map/weight_grads/ppermute | solution.py:37
  237.5 0.7 copy.69
  238.2 0.7 copy.70
  239.8 1.7 maximum_convert_fusion
  (94 shorter events, 5.4 us)
Async XLA Ops:
  0.6 1.5 copy-start
  4.2 18.7 %all-to-all-start = ((bf16[8,16,3072]{2,1,0:T(8,128)(2,1)}), bf16[8,16,3072]{2,1,0:T(8,128)(2,1)S(1)}, u32[]{:S(2)}, u32[]{:S(2)}) async-start(bf16[8,16,3072]{2,1,0:T(8,128)(2,1)} %bitcast.2), calls=%async_computation | async-start | bytes 1572864 | tf_op jit(solution)/shard_map/heads/all_to_all | solution.py:23
  23.0 27.8 %collective-permute-start = (bf16[16,1536]{1,0:T(8,128)(2,1)S(1)}, bf16[16,1536]{1,0:T(8,128)(2,1)S(1)}, u32[]{:S(2)}, u32[]{:S(2)}) collective-permute-start(bf16[16,1536]{1,0:T(8,128)(2,1)S(1)} %get-tuple-element.55), channel_id=1, source_target_pairs={{0,48},{16,0},{32,16},{48,32},{1,49},{17,1},{33,17},{49,33},{2,50}... | collective-permute-start | bytes 147464 | tf_op jit(solution)/shard_map/gather_images/ppermute | solution.py:37
  31.2 19.6 %collective-permute-start.1 = (bf16[16,1536]{1,0:T(8,128)(2,1)S(1)}, bf16[16,1536]{1,0:T(8,128)(2,1)S(1)}, u32[]{:S(2)}, u32[]{:S(2)}) collective-permute-start(bf16[16,1536]{1,0:T(8,128)(2,1)S(1)} %get-tuple-element.55), channel_id=1, source_target_pairs={{0,32},{16,48},{32,0},{48,16},{1,33},{17,49},{33,1},{49,17},{2,34}... | collective-permute-start | bytes 147464 | tf_op jit(solution)/shard_map/gather_images/ppermute | solution.py:37
  33.1 17.7 %collective-permute-start.2 = (bf16[16,1536]{1,0:T(8,128)(2,1)S(1)}, bf16[16,1536]{1,0:T(8,128)(2,1)S(1)}, u32[]{:S(2)}, u32[]{:S(2)}) collective-permute-start(bf16[16,1536]{1,0:T(8,128)(2,1)S(1)} %get-tuple-element.55), channel_id=1, source_target_pairs={{0,16},{16,32},{32,48},{48,0},{1,17},{17,33},{33,49},{49,1},{2,18}... | collective-permute-start | bytes 147464 | tf_op jit(solution)/shard_map/gather_images/ppermute | solution.py:37
  38.0 26.8 %all-to-all-start.1 = ((bf16[4,16,1536]{2,1,0:T(8,128)(2,1)}), bf16[4,16,1536]{2,1,0:T(8,128)(2,1)S(1)}, u32[]{:S(2)}, u32[]{:S(2)}) async-start(bf16[4,16,1536]{2,1,0:T(8,128)(2,1)} %broadcast_in_dim.12), calls=%async_computation.1 | async-start | bytes 393216 | tf_op jit(solution)/shard_map/gather_texts/all_to_all | solution.py:23
  50.9 7.5 %collective-permute-start.3 = (bf16[64,1536]{1,0:T(8,128)(2,1)S(1)}, bf16[64,1536]{1,0:T(8,128)(2,1)S(1)}, u32[]{:S(2)}, u32[]{:S(2)}) collective-permute-start(bf16[64,1536]{1,0:T(8,128)(2,1)S(1)} %pad_maximum_fusion.6), channel_id=1, source_target_pairs={{0,6},{2,0},{4,2},{6,4},{1,7},{3,1},{5,3},{7,5},{8,14},{10,8},{12,... | collective-permute-start | bytes 589832 | tf_op jit(solution)/shard_map/gather_images/ppermute | solution.py:37
  53.7 8.2 %collective-permute-start.4 = (bf16[64,1536]{1,0:T(8,128)(2,1)S(1)}, bf16[64,1536]{1,0:T(8,128)(2,1)S(1)}, u32[]{:S(2)}, u32[]{:S(2)}) collective-permute-start(bf16[64,1536]{1,0:T(8,128)(2,1)S(1)} %pad_maximum_fusion.6), channel_id=1, source_target_pairs={{0,4},{2,6},{4,0},{6,2},{1,5},{3,7},{5,1},{7,3},{8,12},{10,14},{12... | collective-permute-start | bytes 589832 | tf_op jit(solution)/shard_map/gather_images/ppermute | solution.py:37
  55.9 8.7 %collective-permute-start.5 = (bf16[64,1536]{1,0:T(8,128)(2,1)S(1)}, bf16[64,1536]{1,0:T(8,128)(2,1)S(1)}, u32[]{:S(2)}, u32[]{:S(2)}) collective-permute-start(bf16[64,1536]{1,0:T(8,128)(2,1)S(1)} %pad_maximum_fusion.6), channel_id=1, source_target_pairs={{0,2},{2,4},{4,6},{6,0},{1,3},{3,5},{5,7},{7,1},{8,10},{10,12},{12... | collective-permute-start | bytes 589832 | tf_op jit(solution)/shard_map/gather_images/ppermute | solution.py:37
  65.7 15.7 %all-to-all-start.2 = ((bf16[4,64,1536]{2,1,0:T(8,128)(2,1)}), bf16[4,64,1536]{2,1,0:T(8,128)(2,1)S(1)}, u32[]{:S(2)}, u32[]{:S(2)}) async-start(bf16[4,64,1536]{2,1,0:T(8,128)(2,1)} %broadcast_in_dim.14), calls=%async_computation.2 | async-start | bytes 1572864 | tf_op jit(solution)/shard_map/gather_texts/all_to_all | solution.py:23
  81.5 9.5 %collective-permute-start.6 = (bf16[256,1536]{1,0:T(8,128)(2,1)S(1)}, bf16[256,1536]{1,0:T(8,128)(2,1)}, u32[]{:S(2)}, u32[]{:S(2)}) collective-permute-start(bf16[256,1536]{1,0:T(8,128)(2,1)S(1)} %bitcast.136), channel_id=1, source_target_pairs={{0,8},{8,0},{1,9},{9,1},{2,10},{10,2},{3,11},{11,3},{4,12},{12,4},... | collective-permute-start | bytes 2359304 | tf_op jit(solution)/shard_map/gather_texts/ppermute | solution.py:37
  87.2 1.1 copy-start.1
  88.9 1.4 copy-start.2
  95.5 13.5 %collective-permute-start.15 = (bf16[2,256,768]{2,1,0:T(8,128)(2,1)S(1)}, bf16[2,256,768]{2,1,0:T(8,128)(2,1)S(1)}, u32[]{:S(2)}, u32[]{:S(2)}) collective-permute-start(bf16[2,256,768]{2,1,0:T(8,128)(2,1)S(1)} %pad_maximum_fusion.1), channel_id=1, source_target_pairs={{0,8},{8,0},{1,9},{9,1},{2,10},{10,2},{3,11},{11,3},{4,12},{12,4},... | collective-permute-start | bytes 2359304 | tf_op jit(solution)/shard_map/sum_texts/ppermute | solution.py:37
  99.2 14.7 %collective-permute-start.7 = (bf16[64,1536]{1,0:T(8,128)(2,1)S(1)}, bf16[64,1536]{1,0:T(8,128)(2,1)}, u32[]{:S(2)}, u32[]{:S(2)}) collective-permute-start(bf16[64,1536]{1,0:T(8,128)(2,1)S(1)} %get-tuple-element.37), channel_id=1, source_target_pairs={{0,2},{2,4},{4,6},{6,0},{1,3},{3,5},{5,7},{7,1},{8,10},{10,12},{12... | collective-permute-start | bytes 589832 | tf_op jit(solution)/shard_map/sum_images/ppermute | solution.py:37
  101.2 12.8 %collective-permute-start.8 = (bf16[64,1536]{1,0:T(8,128)(2,1)S(1)}, bf16[64,1536]{1,0:T(8,128)(2,1)}, u32[]{:S(2)}, u32[]{:S(2)}) collective-permute-start(bf16[64,1536]{1,0:T(8,128)(2,1)S(1)} %get-tuple-element.39), channel_id=1, source_target_pairs={{0,4},{2,6},{4,0},{6,2},{1,5},{3,7},{5,1},{7,3},{8,12},{10,14},{12... | collective-permute-start | bytes 589832 | tf_op jit(solution)/shard_map/sum_images/ppermute | solution.py:37
  104.1 10.8 %collective-permute-start.9 = (bf16[64,1536]{1,0:T(8,128)(2,1)S(1)}, bf16[64,1536]{1,0:T(8,128)(2,1)}, u32[]{:S(2)}, u32[]{:S(2)}) collective-permute-start(bf16[64,1536]{1,0:T(8,128)(2,1)S(1)} %get-tuple-element.38), channel_id=1, source_target_pairs={{0,6},{2,0},{4,2},{6,4},{1,7},{3,1},{5,3},{7,5},{8,14},{10,8},{12,... | collective-permute-start | bytes 589832 | tf_op jit(solution)/shard_map/sum_images/ppermute | solution.py:37
  110.4 15.5 %all-to-all-start.3 = ((bf16[4,256,384]{2,1,0:T(8,128)(2,1)}), bf16[4,256,384]{2,1,0:T(8,128)(2,1)S(1)}, u32[]{:S(2)}, u32[]{:S(2)}) async-start(bf16[4,256,384]{2,1,0:T(8,128)(2,1)} %bitcast.16), calls=%async_computation.3 | async-start | bytes 1572864 | tf_op jit(solution)/shard_map/sum_texts/all_to_all | solution.py:23
  116.1 26.6 %copy-start.3 = (bf16[128,192]{0,1:T(8,128)(2,1)S(1)}, bf16[128,192]{0,1:T(8,128)(2,1)}, u32[]{:S(2)}) copy-start(bf16[128,192]{0,1:T(8,128)(2,1)} %param.7) | copy-start | bytes 147460
  116.1 26.7 %copy-start.4 = (bf16[128,192]{0,1:T(8,128)(2,1)S(1)}, bf16[128,192]{0,1:T(8,128)(2,1)}, u32[]{:S(2)}) copy-start(bf16[128,192]{0,1:T(8,128)(2,1)} %param.8) | copy-start | bytes 147460
  116.1 21.8 %collective-permute-start.10 = (bf16[16,1536]{1,0:T(8,128)(2,1)S(1)}, bf16[16,1536]{1,0:T(8,128)(2,1)S(1)}, u32[]{:S(2)}, u32[]{:S(2)}) collective-permute-start(bf16[16,1536]{1,0:T(8,128)(2,1)S(1)} %get-tuple-element.50), channel_id=1, source_target_pairs={{0,16},{16,32},{32,48},{48,0},{1,17},{17,33},{33,49},{49,1},{2,18}... | collective-permute-start | bytes 147464 | tf_op jit(solution)/shard_map/sum_images/ppermute | solution.py:37
  119.7 18.3 %collective-permute-start.11 = (bf16[16,1536]{1,0:T(8,128)(2,1)S(1)}, bf16[16,1536]{1,0:T(8,128)(2,1)S(1)}, u32[]{:S(2)}, u32[]{:S(2)}) collective-permute-start(bf16[16,1536]{1,0:T(8,128)(2,1)S(1)} %get-tuple-element.52), channel_id=1, source_target_pairs={{0,32},{16,48},{32,0},{48,16},{1,33},{17,49},{33,1},{49,17},{2,34}... | collective-permute-start | bytes 147464 | tf_op jit(solution)/shard_map/sum_images/ppermute | solution.py:37
  122.7 15.2 %collective-permute-start.12 = (bf16[16,1536]{1,0:T(8,128)(2,1)S(1)}, bf16[16,1536]{1,0:T(8,128)(2,1)S(1)}, u32[]{:S(2)}, u32[]{:S(2)}) collective-permute-start(bf16[16,1536]{1,0:T(8,128)(2,1)S(1)} %get-tuple-element.51), channel_id=1, source_target_pairs={{0,48},{16,0},{32,16},{48,32},{1,49},{17,1},{33,17},{49,33},{2,50}... | collective-permute-start | bytes 147464 | tf_op jit(solution)/shard_map/sum_images/ppermute | solution.py:37
  126.7 23.8 %all-to-all-start.4 = ((bf16[4,64,384]{2,1,0:T(8,128)(2,1)}), bf16[4,64,384]{2,1,0:T(8,128)(2,1)S(1)}, u32[]{:S(2)}, u32[]{:S(2)}) async-start(bf16[4,64,384]{2,1,0:T(8,128)(2,1)} %bitcast.19), calls=%async_computation.4 | async-start | bytes 393216 | tf_op jit(solution)/shard_map/sum_texts/all_to_all | solution.py:23
  138.0 5.5 %collective-permute-start.13 = (bf16[16,768]{1,0:T(8,128)(2,1)S(1)}, bf16[16,768]{1,0:T(8,128)(2,1)S(1)}, u32[]{:S(2)}, u32[]{:S(2)}) collective-permute-start(bf16[16,768]{1,0:T(8,128)(2,1)S(1)} %get-tuple-element.60), channel_id=1, source_target_pairs={{0,8},{8,0},{1,9},{9,1},{2,10},{10,2},{3,11},{11,3},{4,12},{12,4},... | collective-permute-start | bytes 73736 | tf_op jit(solution)/shard_map/sum_images/ppermute | solution.py:37
  143.5 4.9 %collective-permute-start.14 = (bf16[2,16,384]{2,1,0:T(8,128)(2,1)S(1)}, bf16[2,16,384]{2,1,0:T(8,128)(2,1)S(1)}, u32[]{:S(2)}, u32[]{:S(2)}) collective-permute-start(bf16[2,16,384]{2,1,0:T(8,128)(2,1)S(1)} %get-tuple-element.59), channel_id=1, source_target_pairs={{0,256},{256,0},{1,257},{257,1},{2,258},{258,2},{3,259},{259,3},{4... | collective-permute-start | bytes 73736 | tf_op jit(solution)/shard_map/sum_images/ppermute | solution.py:37
  145.7 11.6 %collective-permute-start.18 = (bf16[2,128,192]{2,1,0:T(8,128)(2,1)S(1)}, bf16[2,128,192]{2,1,0:T(8,128)(2,1)S(1)}, u32[]{:S(2)}, u32[]{:S(2)}) collective-permute-start(bf16[2,128,192]{2,1,0:T(8,128)(2,1)S(1)} %get-tuple-element.54), channel_id=1, source_target_pairs={{0,8},{8,0},{1,9},{9,1},{2,10},{10,2},{3,11},{11,3},{4,12},{12,4},... | collective-permute-start | bytes 294920 | tf_op jit(solution)/shard_map/gather_features/ppermute | solution.py:37
  151.6 17.7 %all-to-all-start.5 = ((bf16[8,2,64,384]{3,2,1,0:T(8,128)(2,1)}), bf16[8,2,64,384]{3,2,1,0:T(8,128)(2,1)S(1)}, u32[]{:S(2)}, u32[]{:S(2)}) async-start(bf16[8,2,64,384]{3,2,1,0:T(8,128)(2,1)} %broadcast_in_dim.15), calls=%async_computation.5 | async-start | bytes 1572864 | tf_op jit(solution)/shard_map/head_grads/all_to_all | solution.py:23
  157.3 11.7 %collective-permute-start.19 = (bf16[2,2,128,192]{3,2,1,0:T(8,128)(2,1)S(1)}, bf16[2,2,128,192]{3,2,1,0:T(8,128)(2,1)S(1)}, u32[]{:S(2)}, u32[]{:S(2)}) collective-permute-start(bf16[2,2,128,192]{3,2,1,0:T(8,128)(2,1)S(1)} %pad_maximum_fusion.3), channel_id=1, source_target_pairs={{0,256},{256,0},{1,257},{257,1},{2,258},{258,2},{3,259},{259,3},{4... | collective-permute-start | bytes 589832 | tf_op jit(solution)/shard_map/gather_features/ppermute | solution.py:37
  209.1 20.0 %all-to-all-start.8 = ((bf16[8,2,48,384]{3,2,1,0:T(8,128)(2,1)}), bf16[8,2,48,384]{3,2,1,0:T(8,128)(2,1)S(1)}, u32[]{:S(2)}, u32[]{:S(2)}) async-start(bf16[8,2,48,384]{3,2,1,0:T(8,128)(2,1)} %broadcast_in_dim.17), calls=%async_computation.8 | async-start | bytes 1179648 | tf_op jit(solution)/shard_map/weight_grads/all_to_all | solution.py:23
  218.2 7.1 %collective-permute-start.16 = (bf16[2,8,2,16,192]{4,3,2,1,0:T(8,128)(2,1)S(1)}, bf16[2,8,2,16,192]{4,3,2,1,0:T(8,128)(2,1)S(1)}, u32[]{:S(2)}, u32[]{:S(2)}) collective-permute-start(bf16[2,8,2,16,192]{4,3,2,1,0:T(8,128)(2,1)S(1)} %fusion.30), channel_id=1, source_target_pairs={{0,8},{8,0},{1,9},{9,1},{2,10},{10,2},{3,11},{11,3},{4,12},{12,4},... | collective-permute-start | bytes 589832 | tf_op jit(solution)/shard_map/input_grads/ppermute | solution.py:37
  225.5 11.9 %collective-permute-start.17 = (bf16[2,8,16,192]{3,2,1,0:T(8,128)(2,1)S(1)}, bf16[2,8,16,192]{3,2,1,0:T(8,128)(2,1)S(1)}, u32[]{:S(2)}, u32[]{:S(2)}) collective-permute-start(bf16[2,8,16,192]{3,2,1,0:T(8,128)(2,1)S(1)} %fusion.42), channel_id=1, source_target_pairs={{0,256},{256,0},{1,257},{257,1},{2,258},{258,2},{3,259},{259,3},{4... | collective-permute-start | bytes 294920 | tf_op jit(solution)/shard_map/input_grads/ppermute | solution.py:37
  230.2 9.6 %collective-permute-start.20 = (bf16[2,192,768]{2,1,0:T(8,128)(2,1)S(1)}, bf16[2,192,768]{2,1,0:T(8,128)(2,1)S(1)}, u32[]{:S(2)}, u32[]{:S(2)}) collective-permute-start(bf16[2,192,768]{2,1,0:T(8,128)(2,1)S(1)} %reshape.175), channel_id=1, source_target_pairs={{0,8},{8,0},{1,9},{9,1},{2,10},{10,2},{3,11},{11,3},{4,12},{12,4},... | collective-permute-start | bytes 1769480 | tf_op jit(solution)/shard_map/weight_grads/ppermute | solution.py:37

commit v4 on v3

--- a/solution.py
+++ b/solution.py
@@ -37,18 +37,25 @@
     return lax.ppermute(value, axis, [(i, (i + by) % n) for i in range(n)])
 
 
+def opposite(value):
+    pairs = [(i, 3 - i) for i in range(4)]
+    return lax.ppermute(value, ("xl", "c"), pairs)
+
+
 def ring_gather(rows, axis):
     n = PARTS[axis]
     return jnp.concatenate([rows] + [shifted(rows, axis, n - k) for k in range(1, n)], axis=0)
 
 
-def ring_scatter_sum(total, axis):
-    n = PARTS[axis]
-    blocks = split_rows(total, n)
-    own = blocks[0]
-    for k in range(1, n):
-        own = own + shifted(blocks[k].astype(BF16), axis, k).astype(F32)
-    return own
+def ring_scatter(total, axis):
+    blocks = split_rows(total, PARTS[axis])
+    return [blocks[0]] + [
+        shifted(blocks[k].astype(BF16), axis, k) for k in range(1, PARTS[axis])
+    ]
+
+
+def added(terms):
+    return sum(term.astype(F32) for term in terms)
 
 
 def split_rows(value, n):
@@ -98,6 +105,8 @@
         )
         both_heads = scatter_sum(split_rows(partial_heads, members), MP).astype(BF16)
 
+    together = lax.optimization_barrier
+
     with jax.named_scope("gather_features"):
         features = jnp.stack((image_features, text_features))
         features = jnp.stack((features, shifted(features, "c", 1)))
@@ -115,12 +124,14 @@
             jnp.where(first, other_features[:, 1], features[:, 1]),
         )
 
-    with jax.named_scope("gather_texts"):
-        texts = merge_rows(gather(both_heads[:, embed_width:], "zh"))
-        texts = merge_rows(gather(texts, ("xh", "xl")))
+    with jax.named_scope("gather"):
+        both_heads, image_rows, text_rows = together((both_heads, image_rows, text_rows))
+        texts, images = together((both_heads[:, embed_width:], both_heads[:, :embed_width]))
+        texts, images = together((merge_rows(gather(texts, "zh")), ring_gather(images, "zl")))
+        texts, images = together(
+            (merge_rows(gather(texts, ("xh", "xl"))), ring_gather(images, "y"))
+        )
         other_texts = shifted(texts, "c", 1)
-    with jax.named_scope("gather_images"):
-        images = ring_gather(ring_gather(both_heads[:, :embed_width], "zl"), "y")
 
     with jax.named_scope("pairs"):
         image_embed, image_norm = unit_rows(images)
@@ -159,26 +170,34 @@
 
         sent = jnp.stack(text_half(1 - core)[::-1])
         kept = jnp.stack(text_half(core))
+    with jax.named_scope("sum"):
+        text_part = kept.astype(F32) + shifted(sent, "c", 1).astype(F32)
+        text_part = text_part.astype(BF16).reshape(2, 2, 2, 4 * share, 2, quarter)
+        text_part = text_part.transpose(1, 4, 0, 2, 3, 5).reshape(4, 16 * share, quarter)
+        text_part, coeff, other_coeff, along, other_along = together(
+            (text_part, coeff, other_coeff, along, other_along)
+        )
+        text_part = scatter_sum(text_part, ("xh", "xl")).astype(BF16)
         image_part = jnp.einsum("ti,te->ie", coeff, embed, preferred_element_type=F32)
         image_part = image_part + jnp.einsum(
             "ti,te->ie", other_coeff, other_embed, preferred_element_type=F32
         )
         image_along = jnp.sum(along, axis=0) + jnp.sum(other_along, axis=0)
         image_part = projected(image_part, images, image_norm, image_along[:, None])
-
-    with jax.named_scope("sum_texts"):
-        text_part = kept.astype(F32) + shifted(sent, "c", 1).astype(F32)
-        text_part = text_part.astype(BF16).reshape(2, 2, 2, 4 * share, 2, quarter)
-        text_part = text_part.transpose(1, 4, 0, 2, 3, 5).reshape(4, 16 * share, quarter)
-        text_part = scatter_sum(text_part, ("xh", "xl")).astype(BF16)
         text_part = text_part.reshape(4, 4, share, quarter).swapaxes(0, 1)
-        text_grads = scatter_sum(text_part.reshape(4, 4 * share, quarter), "zh").astype(BF16)
-    with jax.named_scope("sum_images"):
-        image_grads = ring_scatter_sum(ring_scatter_sum(image_part, "y"), "zl").astype(BF16)
-        theirs = shifted(columns(image_grads, (1 - core) * half, half), "c", 1)
-        image_grads = jnp.stack((columns(image_grads, core * half, half), theirs))
-        theirs = shifted(columns(image_grads, (1 - side) * quarter, quarter), "xl", 1)
-        image_grads = jnp.stack((columns(image_grads, side * quarter, quarter), theirs), axis=1)
+        text_part = text_part.reshape(4, 4 * share, quarter)
+        text_grads = scatter_sum(text_part, "zh").astype(BF16)
+        image_part, _ = together((ring_scatter(image_part, "y"), text_part))
+        image_grads = added(ring_scatter(added(image_part), "zl")).astype(BF16)
+        own = core * half + side * quarter
+        image_grads = jnp.stack(
+            [
+                columns(image_grads, own, quarter),
+                shifted(columns(image_grads, core * half + (1 - side) * quarter, quarter), "xl", 1),
+                shifted(columns(image_grads, (1 - core) * half + side * quarter, quarter), "c", 1),
+                opposite(columns(image_grads, 3 * quarter - own, quarter)),
+            ]
+        )
 
     with jax.named_scope("head_grads"):
         grads = jnp.stack((image_grads.reshape(4 * share, quarter), text_grads))

time: 243 us -> 258 us (1.062)
  blocking collectives: 38.1 us -> 57.4 us
  waiting for transfers between devices: 39.7 us -> 35.5 us
  starting transfers between devices: 128 us -> 124 us
    all_to_all x7 -> x6, waiting for transfers between devices: 22 us -> 1.62 us  [exchange(): return lax.all_to_all(blocks, axes, split_axis=0, concat_axis=0, tiled=True)]
    all_to_all x2 -> x3, blocking collectives: 38.1 us -> 57.4 us  [exchange(): return lax.all_to_all(blocks, axes, split_axis=0, concat_axis=0, tiled=True)]
    all_to_all x7 -> x6, starting transfers between devices: 54.1 us -> 38.9 us  [exchange(): return lax.all_to_all(blocks, axes, split_axis=0, concat_axis=0, tiled=True)]
    ppermute x21, waiting for transfers between devices: 17.7 us -> 30.5 us  [shifted(): return lax.ppermute(value, axis, [(i, (i + by) % n) for i in range(n)])]
    ppermute x21, starting transfers between devices: 74.3 us -> 83.3 us  [shifted(): return lax.ppermute(value, axis, [(i, (i + by) % n) for i in range(n)])]
    ppermute x0 -> x1, waiting for transfers between devices: none -> 3.36 us  [opposite(): return lax.ppermute(value, ('xl', 'c'), pairs)]
  transfers between devices with their start and end apart: 28 -> 28, of which waited for: 10 -> 13; matrix products, arithmetic and copies ran while one was open for 8% -> 6% of each run, Pallas kernels for 0% -> 0%
where the time goes in v4:
time: 258 us; the launch traced here: 257 us
  starting transfers between devices  124 us (48%)
  blocking collectives  57.4 us (22%)
  waiting for transfers between devices  35.5 us (14%)
  matrix products  13.2 us (5%)
  local copies, waits for them, and re-layouts  12.4 us (5%)
  other arithmetic  10.6 us (4%)
  between operations  3.41 us (1%)
    ppermute x21, starting transfers between devices, shifted(): return lax.ppermute(value, axis, [(i, (i + by) % n) for i in range(n)])  83.3 us
    all_to_all x3, blocking collectives, exchange(): return lax.all_to_all(blocks, axes, split_axis=0, concat_axis=0, tiled=True)  57.4 us
    all_to_all x6, starting transfers between devices, exchange(): return lax.all_to_all(blocks, axes, split_axis=0, concat_axis=0, tiled=True)  38.9 us
    ppermute x21, waiting for transfers between devices, shifted(): return lax.ppermute(value, axis, [(i, (i + by) % n) for i in range(n)])  30.5 us
  transfers between devices with their start and end apart: 28, of which 13 were waited for; matrix products, arithmetic and copies ran while one was open for 6% of the time, Pallas kernels for 0%

profile of v4, /device:TPU:1, one launch (start us, length us, event | category | flops | bytes accessed | tf_op | source)
XLA Modules:
  0.0 256.6 jit_solution(4807173381985421806)
XLA Ops:
  0.7 1.0 copy.52
  1.6 0.9 copy.53
  2.6 8.8 %collective-permute-start = (bf16[2,128,192]{2,1,0:T(8,128)(2,1)S(1)}, bf16[2,128,192]{2,1,0:T(8,128)(2,1)S(1)}, u32[]{:S(2)}, u32[]{:S(2)}) collective-permute-start(bf16[2,128,192]{2,1,0:T(8,128)(2,1)S(1)} %get-tuple-element.92), channel_id=1, source_target_pairs={{0,8},{8,0},{1,9},{9,1},{2,10},{10,2},{3,11},{11,3},{4,12},{12,4},... | collective-permute-start | bytes 294920 | tf_op jit(solution)/shard_map/gather_features/ppermute | solution.py:37
  11.4 1.4 convolution_convert_fusion
  13.1 1.0 pad_maximum_fusion
  14.0 3.5 %all-to-all-start = ((bf16[8,16,3072]{2,1,0:T(8,128)(2,1)}), bf16[8,16,3072]{2,1,0:T(8,128)(2,1)S(1)}, u32[]{:S(2)}, u32[]{:S(2)}) async-start(bf16[8,16,3072]{2,1,0:T(8,128)(2,1)} %bitcast.2), calls=%async_computation | async-start | bytes 1572864 | tf_op jit(solution)/shard_map/heads/all_to_all | solution.py:23
  17.6 1.9 collective-permute-start.1
  19.6 12.5 %collective-permute-done.1 = bf16[2,2,128,192]{3,2,1,0:T(8,128)(2,1)S(1)} collective-permute-done((bf16[2,2,128,192]{3,2,1,0:T(8,128)(2,1)S(1)}, bf16[2,2,128,192]{3,2,1,0:T(8,128)(2,1)S(1)}, u32[]{:S(2)}, u32[]{:S(2)}) %collective-permute-start.1) | collective-permute-done | bytes 196640 | tf_op jit(solution)/shard_map/gather_features/ppermute | solution.py:37
  33.2 13.4 %all-to-all-start.1 = ((bf16[4,16,1536]{2,1,0:T(8,128)(2,1)}), bf16[4,16,1536]{2,1,0:T(8,128)(2,1)S(1)}, u32[]{:S(2)}, u32[]{:S(2)}) async-start(bf16[4,16,1536]{2,1,0:T(8,128)(2,1)} %broadcast_in_dim.10), calls=%async_computation.1 | async-start | bytes 393216 | tf_op jit(solution)/shard_map/gather/all_to_all | solution.py:23
  46.6 3.5 %collective-permute-start.2 = (bf16[16,1536]{1,0:T(8,128)(2,1)S(1)}, bf16[16,1536]{1,0:T(8,128)(2,1)S(1)}, u32[]{:S(2)}, u32[]{:S(2)}) collective-permute-start(bf16[16,1536]{1,0:T(8,128)(2,1)S(1)} %get-tuple-element.24), channel_id=1, source_target_pairs={{0,48},{16,0},{32,16},{48,32},{1,49},{17,1},{33,17},{49,33},{2,50}... | collective-permute-start | bytes 147464 | tf_op jit(solution)/shard_map/gather/ppermute | solution.py:37
  50.1 2.2 collective-permute-start.3
  52.3 2.6 %collective-permute-start.4 = (bf16[16,1536]{1,0:T(8,128)(2,1)S(1)}, bf16[16,1536]{1,0:T(8,128)(2,1)S(1)}, u32[]{:S(2)}, u32[]{:S(2)}) collective-permute-start(bf16[16,1536]{1,0:T(8,128)(2,1)S(1)} %get-tuple-element.24), channel_id=1, source_target_pairs={{0,16},{16,32},{32,48},{48,0},{1,17},{17,33},{33,49},{49,1},{2,18}... | collective-permute-start | bytes 147464 | tf_op jit(solution)/shard_map/gather/ppermute | solution.py:37
  55.1 1.6 collective-permute-done.3
  56.8 4.0 %collective-permute-done.4 = bf16[16,1536]{1,0:T(8,128)(2,1)S(1)} collective-permute-done((bf16[16,1536]{1,0:T(8,128)(2,1)S(1)}, bf16[16,1536]{1,0:T(8,128)(2,1)S(1)}, u32[]{:S(2)}, u32[]{:S(2)}) %collective-permute-start.4) | collective-permute-done | bytes 49184 | tf_op jit(solution)/shard_map/gather/ppermute | solution.py:37
  60.8 0.9 broadcast_in_dim.11
  61.7 4.5 %all-to-all-start.2 = ((bf16[4,64,1536]{2,1,0:T(8,128)(2,1)}), bf16[4,64,1536]{2,1,0:T(8,128)(2,1)S(1)}, u32[]{:S(2)}, u32[]{:S(2)}) async-start(bf16[4,64,1536]{2,1,0:T(8,128)(2,1)} %broadcast_in_dim.11), calls=%async_computation.2 | async-start | bytes 1572864 | tf_op jit(solution)/shard_map/gather/all_to_all | solution.py:23
  68.2 4.3 %collective-permute-start.5 = (bf16[64,1536]{1,0:T(8,128)(2,1)S(1)}, bf16[64,1536]{1,0:T(8,128)(2,1)S(1)}, u32[]{:S(2)}, u32[]{:S(2)}) collective-permute-start(bf16[64,1536]{1,0:T(8,128)(2,1)S(1)} %pad_maximum_fusion.7), channel_id=1, source_target_pairs={{0,6},{2,0},{4,2},{6,4},{1,7},{3,1},{5,3},{7,5},{8,14},{10,8},{12,... | collective-permute-start | bytes 589832 | tf_op jit(solution)/shard_map/gather/ppermute | solution.py:37
  72.5 2.5 collective-permute-start.6
  75.0 2.5 collective-permute-start.7
  77.5 2.9 %collective-permute-done.6 = bf16[64,1536]{1,0:T(8,128)(2,1)S(1)} collective-permute-done((bf16[64,1536]{1,0:T(8,128)(2,1)S(1)}, bf16[64,1536]{1,0:T(8,128)(2,1)S(1)}, u32[]{:S(2)}, u32[]{:S(2)}) %collective-permute-start.6) | collective-permute-done | bytes 196640 | tf_op jit(solution)/shard_map/gather/ppermute | solution.py:37
  80.4 2.6 collective-permute-done.7
  83.1 6.6 %collective-permute-start.8 = (bf16[256,1536]{1,0:T(8,128)(2,1)S(1)}, bf16[256,1536]{1,0:T(8,128)(2,1)S(1)}, u32[]{:S(2)}, u32[]{:S(2)}) collective-permute-start(bf16[256,1536]{1,0:T(8,128)(2,1)S(1)} %bitcast.135), channel_id=1, source_target_pairs={{0,8},{8,0},{1,9},{9,1},{2,10},{10,2},{3,11},{11,3},{4,12},{12,4},... | collective-permute-start | bytes 2359304 | tf_op jit(solution)/shard_map/gather/ppermute | solution.py:37
  90.4 1.3 fusion.62
  92.5 1.2 fusion.61
  94.4 0.9 pad_maximum_fusion.2
  95.4 1.9 collective-permute-start.9
  97.3 1.5 fusion.14
  99.1 0.8 collective-permute-done.9
  99.9 2.2 add_convert_fusion
  102.1 2.1 reshape.159
  104.1 1.0 copy.56
  105.2 1.1 reduce_sum.137
  106.2 1.1 reduce_sum.138
  107.3 2.5 fusion.56
  109.8 4.7 %all-to-all-start.3 = ((bf16[4,256,384]{2,1,0:T(8,128)(2,1)}), bf16[4,256,384]{2,1,0:T(8,128)(2,1)S(1)}, u32[]{:S(2)}, u32[]{:S(2)}) async-start(bf16[4,256,384]{2,1,0:T(8,128)(2,1)} %bitcast.22), calls=%async_computation.3 | async-start | bytes 1572864 | tf_op jit(solution)/shard_map/sum/all_to_all | solution.py:23
  114.5 2.0 fusion.2
  116.6 1.9 collective-permute-start.10
  118.5 3.1 %collective-permute-start.11 = (bf16[64,1536]{1,0:T(8,128)(2,1)S(1)}, bf16[64,1536]{1,0:T(8,128)(2,1)S(1)}, u32[]{:S(2)}, u32[]{:S(2)}) collective-permute-start(bf16[64,1536]{1,0:T(8,128)(2,1)S(1)} %get-tuple-element.75), channel_id=1, source_target_pairs={{0,4},{2,6},{4,0},{6,2},{1,5},{3,7},{5,1},{7,3},{8,12},{10,14},{12... | collective-permute-start | bytes 589832 | tf_op jit(solution)/shard_map/sum/ppermute | solution.py:37
  121.6 4.0 %collective-permute-start.12 = (bf16[64,1536]{1,0:T(8,128)(2,1)S(1)}, bf16[64,1536]{1,0:T(8,128)(2,1)S(1)}, u32[]{:S(2)}, u32[]{:S(2)}) collective-permute-start(bf16[64,1536]{1,0:T(8,128)(2,1)S(1)} %get-tuple-element.74), channel_id=1, source_target_pairs={{0,6},{2,0},{4,2},{6,4},{1,7},{3,1},{5,3},{7,5},{8,14},{10,8},{12,... | collective-permute-start | bytes 589832 | tf_op jit(solution)/shard_map/sum/ppermute | solution.py:37
  125.6 0.9 all-to-all-done.3
  127.3 2.6 %collective-permute-done.10 = bf16[64,1536]{1,0:T(8,128)(2,1)S(1)} collective-permute-done((bf16[64,1536]{1,0:T(8,128)(2,1)S(1)}, bf16[64,1536]{1,0:T(8,128)(2,1)S(1)}, u32[]{:S(2)}, u32[]{:S(2)}) %collective-permute-start.10) | collective-permute-done | bytes 196640 | tf_op jit(solution)/shard_map/sum/ppermute | solution.py:37
  130.0 2.2 collective-permute-done.12
  132.3 5.4 %collective-permute-start.13 = (bf16[16,1536]{1,0:T(8,128)(2,1)S(1)}, bf16[16,1536]{1,0:T(8,128)(2,1)S(1)}, u32[]{:S(2)}, u32[]{:S(2)}) collective-permute-start(bf16[16,1536]{1,0:T(8,128)(2,1)S(1)} %get-tuple-element.88), channel_id=1, source_target_pairs={{0,16},{16,32},{32,48},{48,0},{1,17},{17,33},{33,49},{49,1},{2,18}... | collective-permute-start | bytes 147464 | tf_op jit(solution)/shard_map/sum/ppermute | solution.py:37
  137.6 3.0 %collective-permute-start.14 = (bf16[16,1536]{1,0:T(8,128)(2,1)S(1)}, bf16[16,1536]{1,0:T(8,128)(2,1)S(1)}, u32[]{:S(2)}, u32[]{:S(2)}) collective-permute-start(bf16[16,1536]{1,0:T(8,128)(2,1)S(1)} %get-tuple-element.90), channel_id=1, source_target_pairs={{0,32},{16,48},{32,0},{48,16},{1,33},{17,49},{33,1},{49,17},{2,34}... | collective-permute-start | bytes 147464 | tf_op jit(solution)/shard_map/sum/ppermute | solution.py:37
  140.6 4.1 %collective-permute-start.15 = (bf16[16,1536]{1,0:T(8,128)(2,1)S(1)}, bf16[16,1536]{1,0:T(8,128)(2,1)S(1)}, u32[]{:S(2)}, u32[]{:S(2)}) collective-permute-start(bf16[16,1536]{1,0:T(8,128)(2,1)S(1)} %get-tuple-element.89), channel_id=1, source_target_pairs={{0,48},{16,0},{32,16},{48,32},{1,49},{17,1},{33,17},{49,33},{2,50}... | collective-permute-start | bytes 147464 | tf_op jit(solution)/shard_map/sum/ppermute | solution.py:37
  144.7 6.9 %all-to-all-start.4 = ((bf16[4,64,384]{2,1,0:T(8,128)(2,1)}), bf16[4,64,384]{2,1,0:T(8,128)(2,1)S(1)}, u32[]{:S(2)}, u32[]{:S(2)}) async-start(bf16[4,64,384]{2,1,0:T(8,128)(2,1)} %bitcast.25), calls=%async_computation.4 | async-start | bytes 393216 | tf_op jit(solution)/shard_map/sum/all_to_all | solution.py:23
  151.7 3.0 %collective-permute-start.16 = (bf16[16,384]{1,0:T(8,128)(2,1)S(1)}, bf16[16,384]{1,0:T(8,128)(2,1)S(1)}, u32[]{:S(2)}, u32[]{:S(2)}) collective-permute-start(bf16[16,384]{1,0:T(8,128)(2,1)S(1)} %get-tuple-element.98), channel_id=1, source_target_pairs={{0,256},{256,0},{1,257},{257,1},{2,258},{258,2},{3,259},{259,3},{4... | collective-permute-start | bytes 36872 | tf_op jit(solution)/shard_map/sum/ppermute | solution.py:37
  154.8 5.1 %collective-permute-start.17 = (bf16[16,384]{1,0:T(8,128)(2,1)S(1)}, bf16[16,384]{1,0:T(8,128)(2,1)S(1)}, u32[]{:S(2)}, u32[]{:S(2)}) collective-permute-start(bf16[16,384]{1,0:T(8,128)(2,1)S(1)} %get-tuple-element.97), channel_id=1, source_target_pairs={{0,8},{8,0},{1,9},{9,1},{2,10},{10,2},{3,11},{11,3},{4,12},{12,4},... | collective-permute-start | bytes 36872 | tf_op jit(solution)/shard_map/sum/ppermute | solution.py:37
  159.9 1.9 collective-permute-start.18
  161.8 3.4 %collective-permute-done.18 = bf16[16,384]{1,0:T(8,128)(2,1)S(1)} collective-permute-done((bf16[16,384]{1,0:T(8,128)(2,1)S(1)}, bf16[16,384]{1,0:T(8,128)(2,1)S(1)}, u32[]{:S(2)}, u32[]{:S(2)}) %collective-permute-start.18) | collective-permute-done | bytes 12320 | tf_op jit(solution)/shard_map/sum/ppermute | solution.py:42
  165.2 0.8 all-to-all-done.4
  166.1 16.5 %all_to_all.45 = bf16[8,2,64,384]{3,2,1,0:T(8,128)(2,1)S(1)} all-to-all(bf16[8,2,64,384]{3,2,1,0:T(8,128)(2,1)S(1)} %broadcast_in_dim.12), channel_id=1, replica_groups=mesh['xl'=2,'zh'=4,'zl'=4,'c'=2,'y'=4,'xh'=2] {'y','xh'}, dimensions={0} | all-to-all | bytes 1572864 | tf_op jit(solution)/shard_map/head_grads/all_to_all | solution.py:23
  183.3 12.6 %all_to_all.46 = bf16[4,2,48,384]{3,2,1,0:T(8,128)(2,1)S(1)} all-to-all(bf16[4,2,48,384]{3,2,1,0:T(8,128)(2,1)S(1)} %pad_maximum_fusion.5), channel_id=1, replica_groups=mesh['xl'=2,'zh'=4,'zl'=4,'c'=2,'y'=4,'xh'=2] {'zl'}, dimensions={0} | all-to-all | bytes 589824 | tf_op jit(solution)/shard_map/weight_grads/all_to_all | solution.py:23
  196.0 28.3 %all_to_all.47 = bf16[4,2,48,384]{3,2,1,0:T(8,128)(2,1)S(1)} all-to-all(bf16[4,2,48,384]{3,2,1,0:T(8,128)(2,1)S(1)} %broadcast_in_dim.13), channel_id=1, replica_groups=mesh['xl'=2,'zh'=4,'zl'=4,'c'=2,'y'=4,'xh'=2] {'zh'}, dimensions={0} | all-to-all | bytes 589824 | tf_op jit(solution)/shard_map/weight_grads/all_to_all | solution.py:23
  224.4 0.9 broadcast_in_dim.14
  225.3 5.8 %all-to-all-start.8 = ((bf16[8,2,48,384]{3,2,1,0:T(8,128)(2,1)}), bf16[8,2,48,384]{3,2,1,0:T(8,128)(2,1)S(1)}, u32[]{:S(2)}, u32[]{:S(2)}) async-start(bf16[8,2,48,384]{3,2,1,0:T(8,128)(2,1)} %broadcast_in_dim.14), calls=%async_computation.8 | async-start | bytes 1179648 | tf_op jit(solution)/shard_map/weight_grads/all_to_all | solution.py:23
  231.4 1.2 fusion.35
  232.8 6.1 %collective-permute-start.19 = (bf16[2,8,2,16,192]{4,3,2,1,0:T(8,128)(2,1)S(1)}, bf16[2,8,2,16,192]{4,3,2,1,0:T(8,128)(2,1)S(1)}, u32[]{:S(2)}, u32[]{:S(2)}) collective-permute-start(bf16[2,8,2,16,192]{4,3,2,1,0:T(8,128)(2,1)S(1)} %fusion.32), channel_id=1, source_target_pairs={{0,8},{8,0},{1,9},{9,1},{2,10},{10,2},{3,11},{11,3},{4,12},{12,4},... | collective-permute-start | bytes 589832 | tf_op jit(solution)/shard_map/input_grads/ppermute | solution.py:37
  238.8 1.1 collective-permute-done.19
  240.1 3.8 %collective-permute-start.20 = (bf16[2,8,16,192]{3,2,1,0:T(8,128)(2,1)S(1)}, bf16[2,8,16,192]{3,2,1,0:T(8,128)(2,1)S(1)}, u32[]{:S(2)}, u32[]{:S(2)}) collective-permute-start(bf16[2,8,16,192]{3,2,1,0:T(8,128)(2,1)S(1)} %fusion.40), channel_id=1, source_target_pairs={{0,256},{256,0},{1,257},{257,1},{2,258},{258,2},{3,259},{259,3},{4... | collective-permute-start | bytes 294920 | tf_op jit(solution)/shard_map/input_grads/ppermute | solution.py:37
  244.9 7.0 %collective-permute-start.21 = (bf16[2,192,768]{2,1,0:T(8,128)(2,1)S(1)}, bf16[2,192,768]{2,1,0:T(8,128)(2,1)S(1)}, u32[]{:S(2)}, u32[]{:S(2)}) collective-permute-start(bf16[2,192,768]{2,1,0:T(8,128)(2,1)S(1)} %reshape.168), channel_id=1, source_target_pairs={{0,8},{8,0},{1,9},{9,1},{2,10},{10,2},{3,11},{11,3},{4,12},{12,4},... | collective-permute-start | bytes 1769480 | tf_op jit(solution)/shard_map/weight_grads/ppermute | solution.py:37
  252.0 0.7 copy.65
  254.3 1.1 maximum_convert_fusion.1
  255.5 1.1 maximum_convert_fusion
  (95 shorter events, 9.3 us)
Async XLA Ops:
  0.6 12.1 %copy-start = (bf16[192,1536]{1,0:T(8,128)(2,1)S(1)}, bf16[192,1536]{1,0:T(8,128)(2,1)}, u32[]{:S(2)}) copy-start(bf16[192,1536]{1,0:T(8,128)(2,1)} %param.9) | copy-start | bytes 1769476
  0.6 12.1 %copy-start.5 = (bf16[128,192]{0,1:T(8,128)(2,1)S(1)}, bf16[128,192]{0,1:T(8,128)(2,1)}, u32[]{:S(2)}) copy-start(bf16[128,192]{0,1:T(8,128)(2,1)} %param.7) | copy-start | bytes 147460
  2.6 15.0 %collective-permute-start = (bf16[2,128,192]{2,1,0:T(8,128)(2,1)S(1)}, bf16[2,128,192]{2,1,0:T(8,128)(2,1)S(1)}, u32[]{:S(2)}, u32[]{:S(2)}) collective-permute-start(bf16[2,128,192]{2,1,0:T(8,128)(2,1)S(1)} %get-tuple-element.92), channel_id=1, source_target_pairs={{0,8},{8,0},{1,9},{9,1},{2,10},{10,2},{3,11},{11,3},{4,12},{12,4},... | collective-permute-start | bytes 294920 | tf_op jit(solution)/shard_map/gather_features/ppermute | solution.py:37
  14.0 18.3 %all-to-all-start = ((bf16[8,16,3072]{2,1,0:T(8,128)(2,1)}), bf16[8,16,3072]{2,1,0:T(8,128)(2,1)S(1)}, u32[]{:S(2)}, u32[]{:S(2)}) async-start(bf16[8,16,3072]{2,1,0:T(8,128)(2,1)} %bitcast.2), calls=%async_computation | async-start | bytes 1572864 | tf_op jit(solution)/shard_map/heads/all_to_all | solution.py:23
  17.6 14.5 %collective-permute-start.1 = (bf16[2,2,128,192]{3,2,1,0:T(8,128)(2,1)S(1)}, bf16[2,2,128,192]{3,2,1,0:T(8,128)(2,1)S(1)}, u32[]{:S(2)}, u32[]{:S(2)}) collective-permute-start(bf16[2,2,128,192]{3,2,1,0:T(8,128)(2,1)S(1)} %pad_maximum_fusion.4), channel_id=1, source_target_pairs={{0,256},{256,0},{1,257},{257,1},{2,258},{258,2},{3,259},{259,3},{4... | collective-permute-start | bytes 589832 | tf_op jit(solution)/shard_map/gather_features/ppermute | solution.py:37
  33.2 27.6 %all-to-all-start.1 = ((bf16[4,16,1536]{2,1,0:T(8,128)(2,1)}), bf16[4,16,1536]{2,1,0:T(8,128)(2,1)S(1)}, u32[]{:S(2)}, u32[]{:S(2)}) async-start(bf16[4,16,1536]{2,1,0:T(8,128)(2,1)} %broadcast_in_dim.10), calls=%async_computation.1 | async-start | bytes 393216 | tf_op jit(solution)/shard_map/gather/all_to_all | solution.py:23
  46.6 8.6 %collective-permute-start.2 = (bf16[16,1536]{1,0:T(8,128)(2,1)S(1)}, bf16[16,1536]{1,0:T(8,128)(2,1)S(1)}, u32[]{:S(2)}, u32[]{:S(2)}) collective-permute-start(bf16[16,1536]{1,0:T(8,128)(2,1)S(1)} %get-tuple-element.24), channel_id=1, source_target_pairs={{0,48},{16,0},{32,16},{48,32},{1,49},{17,1},{33,17},{49,33},{2,50}... | collective-permute-start | bytes 147464 | tf_op jit(solution)/shard_map/gather/ppermute | solution.py:37
  50.1 6.6 %collective-permute-start.3 = (bf16[16,1536]{1,0:T(8,128)(2,1)S(1)}, bf16[16,1536]{1,0:T(8,128)(2,1)S(1)}, u32[]{:S(2)}, u32[]{:S(2)}) collective-permute-start(bf16[16,1536]{1,0:T(8,128)(2,1)S(1)} %get-tuple-element.24), channel_id=1, source_target_pairs={{0,32},{16,48},{32,0},{48,16},{1,33},{17,49},{33,1},{49,17},{2,34}... | collective-permute-start | bytes 147464 | tf_op jit(solution)/shard_map/gather/ppermute | solution.py:37
  52.3 8.4 %collective-permute-start.4 = (bf16[16,1536]{1,0:T(8,128)(2,1)S(1)}, bf16[16,1536]{1,0:T(8,128)(2,1)S(1)}, u32[]{:S(2)}, u32[]{:S(2)}) collective-permute-start(bf16[16,1536]{1,0:T(8,128)(2,1)S(1)} %get-tuple-element.24), channel_id=1, source_target_pairs={{0,16},{16,32},{32,48},{48,0},{1,17},{17,33},{33,49},{49,1},{2,18}... | collective-permute-start | bytes 147464 | tf_op jit(solution)/shard_map/gather/ppermute | solution.py:37
  61.7 21.3 %all-to-all-start.2 = ((bf16[4,64,1536]{2,1,0:T(8,128)(2,1)}), bf16[4,64,1536]{2,1,0:T(8,128)(2,1)S(1)}, u32[]{:S(2)}, u32[]{:S(2)}) async-start(bf16[4,64,1536]{2,1,0:T(8,128)(2,1)} %broadcast_in_dim.11), calls=%async_computation.2 | async-start | bytes 1572864 | tf_op jit(solution)/shard_map/gather/all_to_all | solution.py:23
  68.2 9.3 %collective-permute-start.5 = (bf16[64,1536]{1,0:T(8,128)(2,1)S(1)}, bf16[64,1536]{1,0:T(8,128)(2,1)S(1)}, u32[]{:S(2)}, u32[]{:S(2)}) collective-permute-start(bf16[64,1536]{1,0:T(8,128)(2,1)S(1)} %pad_maximum_fusion.7), channel_id=1, source_target_pairs={{0,6},{2,0},{4,2},{6,4},{1,7},{3,1},{5,3},{7,5},{8,14},{10,8},{12,... | collective-permute-start | bytes 589832 | tf_op jit(solution)/shard_map/gather/ppermute | solution.py:37
  72.5 7.9 %collective-permute-start.6 = (bf16[64,1536]{1,0:T(8,128)(2,1)S(1)}, bf16[64,1536]{1,0:T(8,128)(2,1)S(1)}, u32[]{:S(2)}, u32[]{:S(2)}) collective-permute-start(bf16[64,1536]{1,0:T(8,128)(2,1)S(1)} %pad_maximum_fusion.7), channel_id=1, source_target_pairs={{0,4},{2,6},{4,0},{6,2},{1,5},{3,7},{5,1},{7,3},{8,12},{10,14},{12... | collective-permute-start | bytes 589832 | tf_op jit(solution)/shard_map/gather/ppermute | solution.py:37
  75.0 8.0 %collective-permute-start.7 = (bf16[64,1536]{1,0:T(8,128)(2,1)S(1)}, bf16[64,1536]{1,0:T(8,128)(2,1)S(1)}, u32[]{:S(2)}, u32[]{:S(2)}) collective-permute-start(bf16[64,1536]{1,0:T(8,128)(2,1)S(1)} %pad_maximum_fusion.7), channel_id=1, source_target_pairs={{0,2},{2,4},{4,6},{6,0},{1,3},{3,5},{5,7},{7,1},{8,10},{10,12},{12... | collective-permute-start | bytes 589832 | tf_op jit(solution)/shard_map/gather/ppermute | solution.py:37
  83.1 9.2 %collective-permute-start.8 = (bf16[256,1536]{1,0:T(8,128)(2,1)S(1)}, bf16[256,1536]{1,0:T(8,128)(2,1)S(1)}, u32[]{:S(2)}, u32[]{:S(2)}) collective-permute-start(bf16[256,1536]{1,0:T(8,128)(2,1)S(1)} %bitcast.135), channel_id=1, source_target_pairs={{0,8},{8,0},{1,9},{9,1},{2,10},{10,2},{3,11},{11,3},{4,12},{12,4},... | collective-permute-start | bytes 2359304 | tf_op jit(solution)/shard_map/gather/ppermute | solution.py:37
  90.4 3.4 %copy-start.3 = (bf16[256,1536]{1,0:T(8,128)(2,1)}, bf16[256,1536]{1,0:T(8,128)(2,1)S(1)}, u32[]{:S(2)}) copy-start(bf16[256,1536]{1,0:T(8,128)(2,1)S(1)} %fusion.8) | copy-start | bytes 2359300
  91.6 0.6 copy-start.6
  92.3 6.5 %copy-start.1 = (bf16[256,1536]{1,0:T(8,128)(2,1)}, bf16[256,1536]{1,0:T(8,128)(2,1)S(1)}, u32[]{:S(2)}) copy-start(bf16[256,1536]{1,0:T(8,128)(2,1)S(1)} %collective-permute-done.8) | copy-start | bytes 2359300
  93.8 0.6 copy-start.7
  95.4 4.5 %collective-permute-start.9 = (bf16[2,256,768]{2,1,0:T(8,128)(2,1)}, bf16[2,256,768]{2,1,0:T(8,128)(2,1)}, u32[]{:S(2)}, u32[]{:S(2)}) collective-permute-start(bf16[2,256,768]{2,1,0:T(8,128)(2,1)} %pad_maximum_fusion.2), channel_id=1, source_target_pairs={{0,8},{8,0},{1,9},{9,1},{2,10},{10,2},{3,11},{11,3},{4,12},{12,4},... | collective-permute-start | bytes 2359304 | tf_op jit(solution)/shard_map/sum/ppermute | solution.py:37
  97.3 1.5 copy-start.4
  97.3 1.5 copy-start.8
  109.8 4.7 %copy-start.2 = (bf16[256,1536]{1,0:T(8,128)(2,1)S(1)}, bf16[256,1536]{1,0:T(8,128)(2,1)}, u32[]{:S(2)}) copy-start(bf16[256,1536]{1,0:T(8,128)(2,1)} %copy-done.1) | copy-start | bytes 2359300
  109.8 16.6 %all-to-all-start.3 = ((bf16[4,256,384]{2,1,0:T(8,128)(2,1)}), bf16[4,256,384]{2,1,0:T(8,128)(2,1)S(1)}, u32[]{:S(2)}, u32[]{:S(2)}) async-start(bf16[4,256,384]{2,1,0:T(8,128)(2,1)} %bitcast.22), calls=%async_computation.3 | async-start | bytes 1572864 | tf_op jit(solution)/shard_map/sum/all_to_all | solution.py:23
  116.6 13.4 %collective-permute-start.10 = (bf16[64,1536]{1,0:T(8,128)(2,1)S(1)}, bf16[64,1536]{1,0:T(8,128)(2,1)S(1)}, u32[]{:S(2)}, u32[]{:S(2)}) collective-permute-start(bf16[64,1536]{1,0:T(8,128)(2,1)S(1)} %get-tuple-element.76), channel_id=1, source_target_pairs={{0,2},{2,4},{4,6},{6,0},{1,3},{3,5},{5,7},{7,1},{8,10},{10,12},{12... | collective-permute-start | bytes 589832 | tf_op jit(solution)/shard_map/sum/ppermute | solution.py:37
  118.5 11.4 %collective-permute-start.11 = (bf16[64,1536]{1,0:T(8,128)(2,1)S(1)}, bf16[64,1536]{1,0:T(8,128)(2,1)S(1)}, u32[]{:S(2)}, u32[]{:S(2)}) collective-permute-start(bf16[64,1536]{1,0:T(8,128)(2,1)S(1)} %get-tuple-element.75), channel_id=1, source_target_pairs={{0,4},{2,6},{4,0},{6,2},{1,5},{3,7},{5,1},{7,3},{8,12},{10,14},{12... | collective-permute-start | bytes 589832 | tf_op jit(solution)/shard_map/sum/ppermute | solution.py:37
  121.6 10.5 %collective-permute-start.12 = (bf16[64,1536]{1,0:T(8,128)(2,1)S(1)}, bf16[64,1536]{1,0:T(8,128)(2,1)S(1)}, u32[]{:S(2)}, u32[]{:S(2)}) collective-permute-start(bf16[64,1536]{1,0:T(8,128)(2,1)S(1)} %get-tuple-element.74), channel_id=1, source_target_pairs={{0,6},{2,0},{4,2},{6,4},{1,7},{3,1},{5,3},{7,5},{8,14},{10,8},{12,... | collective-permute-start | bytes 589832 | tf_op jit(solution)/shard_map/sum/ppermute | solution.py:37
  132.3 19.4 %collective-permute-start.13 = (bf16[16,1536]{1,0:T(8,128)(2,1)S(1)}, bf16[16,1536]{1,0:T(8,128)(2,1)S(1)}, u32[]{:S(2)}, u32[]{:S(2)}) collective-permute-start(bf16[16,1536]{1,0:T(8,128)(2,1)S(1)} %get-tuple-element.88), channel_id=1, source_target_pairs={{0,16},{16,32},{32,48},{48,0},{1,17},{17,33},{33,49},{49,1},{2,18}... | collective-permute-start | bytes 147464 | tf_op jit(solution)/shard_map/sum/ppermute | solution.py:37
  137.6 14.0 %collective-permute-start.14 = (bf16[16,1536]{1,0:T(8,128)(2,1)S(1)}, bf16[16,1536]{1,0:T(8,128)(2,1)S(1)}, u32[]{:S(2)}, u32[]{:S(2)}) collective-permute-start(bf16[16,1536]{1,0:T(8,128)(2,1)S(1)} %get-tuple-element.90), channel_id=1, source_target_pairs={{0,32},{16,48},{32,0},{48,16},{1,33},{17,49},{33,1},{49,17},{2,34}... | collective-permute-start | bytes 147464 | tf_op jit(solution)/shard_map/sum/ppermute | solution.py:37
  140.6 11.0 %collective-permute-start.15 = (bf16[16,1536]{1,0:T(8,128)(2,1)S(1)}, bf16[16,1536]{1,0:T(8,128)(2,1)S(1)}, u32[]{:S(2)}, u32[]{:S(2)}) collective-permute-start(bf16[16,1536]{1,0:T(8,128)(2,1)S(1)} %get-tuple-element.89), channel_id=1, source_target_pairs={{0,48},{16,0},{32,16},{48,32},{1,49},{17,1},{33,17},{49,33},{2,50}... | collective-permute-start | bytes 147464 | tf_op jit(solution)/shard_map/sum/ppermute | solution.py:37
  144.7 21.3 %all-to-all-start.4 = ((bf16[4,64,384]{2,1,0:T(8,128)(2,1)}), bf16[4,64,384]{2,1,0:T(8,128)(2,1)S(1)}, u32[]{:S(2)}, u32[]{:S(2)}) async-start(bf16[4,64,384]{2,1,0:T(8,128)(2,1)} %bitcast.25), calls=%async_computation.4 | async-start | bytes 393216 | tf_op jit(solution)/shard_map/sum/all_to_all | solution.py:23
  151.7 10.1 %collective-permute-start.16 = (bf16[16,384]{1,0:T(8,128)(2,1)S(1)}, bf16[16,384]{1,0:T(8,128)(2,1)S(1)}, u32[]{:S(2)}, u32[]{:S(2)}) collective-permute-start(bf16[16,384]{1,0:T(8,128)(2,1)S(1)} %get-tuple-element.98), channel_id=1, source_target_pairs={{0,256},{256,0},{1,257},{257,1},{2,258},{258,2},{3,259},{259,3},{4... | collective-permute-start | bytes 36872 | tf_op jit(solution)/shard_map/sum/ppermute | solution.py:37
  154.8 7.1 %collective-permute-start.17 = (bf16[16,384]{1,0:T(8,128)(2,1)S(1)}, bf16[16,384]{1,0:T(8,128)(2,1)S(1)}, u32[]{:S(2)}, u32[]{:S(2)}) collective-permute-start(bf16[16,384]{1,0:T(8,128)(2,1)S(1)} %get-tuple-element.97), channel_id=1, source_target_pairs={{0,8},{8,0},{1,9},{9,1},{2,10},{10,2},{3,11},{11,3},{4,12},{12,4},... | collective-permute-start | bytes 36872 | tf_op jit(solution)/shard_map/sum/ppermute | solution.py:37
  159.9 5.3 %collective-permute-start.18 = (bf16[16,384]{1,0:T(8,128)(2,1)S(1)}, bf16[16,384]{1,0:T(8,128)(2,1)S(1)}, u32[]{:S(2)}, u32[]{:S(2)}) collective-permute-start(bf16[16,384]{1,0:T(8,128)(2,1)S(1)} %get-tuple-element.96), channel_id=1, source_target_pairs={{0,264},{8,256},{256,8},{264,0},{1,265},{9,257},{257,9},{265,1},{2... | collective-permute-start | bytes 36872 | tf_op jit(solution)/shard_map/sum/ppermute | solution.py:42
  225.3 18.7 %all-to-all-start.8 = ((bf16[8,2,48,384]{3,2,1,0:T(8,128)(2,1)}), bf16[8,2,48,384]{3,2,1,0:T(8,128)(2,1)S(1)}, u32[]{:S(2)}, u32[]{:S(2)}) async-start(bf16[8,2,48,384]{3,2,1,0:T(8,128)(2,1)} %broadcast_in_dim.14), calls=%async_computation.8 | async-start | bytes 1179648 | tf_op jit(solution)/shard_map/weight_grads/all_to_all | solution.py:23
  232.8 7.2 %collective-permute-start.19 = (bf16[2,8,2,16,192]{4,3,2,1,0:T(8,128)(2,1)S(1)}, bf16[2,8,2,16,192]{4,3,2,1,0:T(8,128)(2,1)S(1)}, u32[]{:S(2)}, u32[]{:S(2)}) collective-permute-start(bf16[2,8,2,16,192]{4,3,2,1,0:T(8,128)(2,1)S(1)} %fusion.32), channel_id=1, source_target_pairs={{0,8},{8,0},{1,9},{9,1},{2,10},{10,2},{3,11},{11,3},{4,12},{12,4},... | collective-permute-start | bytes 589832 | tf_op jit(solution)/shard_map/input_grads/ppermute | solution.py:37
  240.1 11.8 %collective-permute-start.20 = (bf16[2,8,16,192]{3,2,1,0:T(8,128)(2,1)S(1)}, bf16[2,8,16,192]{3,2,1,0:T(8,128)(2,1)S(1)}, u32[]{:S(2)}, u32[]{:S(2)}) collective-permute-start(bf16[2,8,16,192]{3,2,1,0:T(8,128)(2,1)S(1)} %fusion.40), channel_id=1, source_target_pairs={{0,256},{256,0},{1,257},{257,1},{2,258},{258,2},{3,259},{259,3},{4... | collective-permute-start | bytes 294920 | tf_op jit(solution)/shard_map/input_grads/ppermute | solution.py:37
  244.9 9.3 %collective-permute-start.21 = (bf16[2,192,768]{2,1,0:T(8,128)(2,1)S(1)}, bf16[2,192,768]{2,1,0:T(8,128)(2,1)S(1)}, u32[]{:S(2)}, u32[]{:S(2)}) collective-permute-start(bf16[2,192,768]{2,1,0:T(8,128)(2,1)S(1)} %reshape.168), channel_id=1, source_target_pairs={{0,8},{8,0},{1,9},{9,1},{2,10},{10,2},{3,11},{11,3},{4,12},{12,4},... | collective-permute-start | bytes 1769480 | tf_op jit(solution)/shard_map/weight_grads/ppermute | solution.py:37

commit v5 on v2

--- a/solution.py
+++ b/solution.py
@@ -6,8 +6,9 @@
 BF16 = jnp.bfloat16
 F32 = jnp.float32
 
-PARTS = {"xl": 2, "zh": 4, "zl": 4, "c": 2, "y": 4, "xh": 2}
-DP = ("xl", "zh", "zl", "c")
+PARTS = {"xl": 2, "zh": 4, "zm": 2, "z0": 2, "c": 2, "y": 4, "xh": 2}
+DP = ("xl", "zh", "zm", "z0", "c")
+ZL = ("zm", "z0")
 MP = ("y", "xh")
 
 
@@ -33,17 +34,17 @@
 
 
 def shifted(value, axis, by):
-    n = PARTS[axis]
+    n = count(axis)
     return lax.ppermute(value, axis, [(i, (i + by) % n) for i in range(n)])
 
 
 def ring_gather(rows, axis):
-    n = PARTS[axis]
+    n = count(axis)
     return jnp.concatenate([rows] + [shifted(rows, axis, n - k) for k in range(1, n)], axis=0)
 
 
 def ring_scatter_sum(total, axis):
-    n = PARTS[axis]
+    n = count(axis)
     blocks = split_rows(total, n)
     own = blocks[0]
     for k in range(1, n):
@@ -104,7 +105,7 @@
         texts = merge_rows(gather(texts, ("xh", "xl")))
         other_texts = shifted(texts, "c", 1)
     with jax.named_scope("gather_images"):
-        images = ring_gather(ring_gather(image_unit.astype(BF16), "zl"), "y")
+        images = ring_gather(ring_gather(image_unit.astype(BF16), ZL), "y")
 
     def coefficients(block, positive):
         scores = (
@@ -131,7 +132,7 @@
         text_part = scatter_sum(split_rows(text_part, count(("xh", "xl"))), ("xh", "xl"))
         text_grads = scatter_sum(split_rows(text_part, count("zh")), "zh")
     with jax.named_scope("sum_images"):
-        image_grads = ring_scatter_sum(ring_scatter_sum(image_part, "y"), "zl")
+        image_grads = ring_scatter_sum(ring_scatter_sum(image_part, "y"), ZL)
 
     with jax.named_scope("head_grads"):
         grads = jnp.stack(
@@ -167,9 +168,13 @@
 
         other = shifted(half_part(1 - at["c"]).astype(BF16), "c", 1)
         part = half_part(at["c"]) + other.astype(F32)
-        part = scatter_sum(part.reshape(8, half // 4, embed_width), ("xl", "zl"))
-        part = jnp.sum(gather(part.astype(BF16), "zh").astype(F32), axis=0).astype(BF16)
-        part = gather(part, ("xl", "zl")).reshape(2, half, embed_width)
+        quarter = embed_width // 4
+        part = scatter_sum(part.reshape(4, half // 2, embed_width), ("xl", "z0"))
+        part = part.reshape(2, half // 4, 4, quarter).transpose(2, 0, 1, 3)
+        part = scatter_sum(part.reshape(8, half // 4, quarter), ("zh", "zm"))
+        part = gather(part.astype(BF16), ("zh", "zm")).reshape(4, 2, half // 4, quarter)
+        part = part.transpose(1, 2, 0, 3).reshape(half // 2, embed_width)
+        part = gather(part, ("xl", "z0")).reshape(2, half, embed_width)
         other = shifted(part, "c", 1)
         first = at["c"] == 0
         image_weight_grad, text_weight_grad = (

time: 230 us -> 224 us (0.974)
  waiting for transfers between devices: 45.3 us -> 37 us
  blocking collectives: 45.1 us -> 50.5 us
  starting transfers between devices: 114 us -> 111 us
    all_to_all x7, waiting for transfers between devices: 41.4 us -> 33.1 us  [exchange(): return lax.all_to_all(blocks, axes, split_axis=0, concat_axis=0, tiled=True)]
    all_to_all x2 -> x3, blocking collectives: 45.1 us -> 50.5 us  [exchange(): return lax.all_to_all(blocks, axes, split_axis=0, concat_axis=0, tiled=True)]
    all_to_all x7, starting transfers between devices: 52.5 us -> 48.1 us  [exchange(): return lax.all_to_all(blocks, axes, split_axis=0, concat_axis=0, tiled=True)]
where the time goes in v5:
time: 224 us; the launch traced here: 223 us
  starting transfers between devices  111 us (50%)
  blocking collectives  50.5 us (23%)
  waiting for transfers between devices  37 us (17%)
  matrix products  9.45 us (4%)
  other arithmetic  6.31 us (3%)
  local copies, waits for them, and re-layouts  5.73 us (3%)
  between operations  3.09 us (1%)
    ppermute x16, starting transfers between devices, shifted(): return lax.ppermute(value, axis, [(i, (i + by) % n) for i in range(n)])  62.8 us
    all_to_all x3, blocking collectives, exchange(): return lax.all_to_all(blocks, axes, split_axis=0, concat_axis=0, tiled=True)  50.5 us
    all_to_all x7, starting transfers between devices, exchange(): return lax.all_to_all(blocks, axes, split_axis=0, concat_axis=0, tiled=True)  48.1 us
    all_to_all x7, waiting for transfers between devices, exchange(): return lax.all_to_all(blocks, axes, split_axis=0, concat_axis=0, tiled=True)  33.1 us
  transfers between devices with their start and end apart: 23, of which 11 were waited for; matrix products, arithmetic and copies ran while one was open for 4% of the time, Pallas kernels for 0%

profile of v5, /device:TPU:1, one launch (start us, length us, event | category | flops | bytes accessed | tf_op | source)
XLA Modules:
  0.0 223.0 jit_solution(9286645933646842050)
XLA Ops:
  0.6 1.4 convolution_convert_fusion.1
  2.1 1.1 convolution_convert_fusion.2
  3.2 1.0 pad_maximum_fusion
  4.2 7.5 %all-to-all-start = ((bf16[8,16,3072]{2,1,0:T(8,128)(2,1)}), bf16[8,16,3072]{2,1,0:T(8,128)(2,1)S(1)}, u32[]{:S(2)}, u32[]{:S(2)}) async-start(bf16[8,16,3072]{2,1,0:T(8,128)(2,1)} %bitcast.2), calls=%async_computation | async-start | bytes 1572864 | tf_op jit(solution)/shard_map/heads/all_to_all | solution.py:24
  11.6 11.2 %all-to-all-done = bf16[8,16,3072]{2,1,0:T(8,128)(2,1)S(1)} async-done(((bf16[8,16,3072]{2,1,0:T(8,128)(2,1)}), bf16[8,16,3072]{2,1,0:T(8,128)(2,1)S(1)}, u32[]{:S(2)}, u32[]{:S(2)}) %all-to-all-start) | async-done | bytes 786464 | tf_op jit(solution)/shard_map/heads/all_to_all | solution.py:24
  23.0 0.1 fusion.23
  23.2 0.7 broadcast_in_dim.14
  23.9 16.8 %all-to-all-start.1 = ((bf16[4,16,1536]{2,1,0:T(8,128)(2,1)}), bf16[4,16,1536]{2,1,0:T(8,128)(2,1)S(1)}, u32[]{:S(2)}, u32[]{:S(2)}) async-start(bf16[4,16,1536]{2,1,0:T(8,128)(2,1)} %broadcast_in_dim.14), calls=%async_computation.1 | async-start | bytes 393216 | tf_op jit(solution)/shard_map/gather_texts/all_to_all | solution.py:24
  40.8 3.5 %collective-permute-start = (bf16[16,1536]{1,0:T(8,128)(2,1)S(1)}, bf16[16,1536]{1,0:T(8,128)(2,1)S(1)}, u32[]{:S(2)}, u32[]{:S(2)}) collective-permute-start(bf16[16,1536]{1,0:T(8,128)(2,1)S(1)} %get-tuple-element.11), channel_id=1, source_target_pairs={{0,48},{16,0},{32,16},{48,32},{1,49},{17,1},{33,17},{49,33},{2,50}... | collective-permute-start | bytes 147464 | tf_op jit(solution)/shard_map/gather_images/ppermute | solution.py:38
  44.3 2.2 collective-permute-start.1
  46.5 2.7 %collective-permute-start.2 = (bf16[16,1536]{1,0:T(8,128)(2,1)S(1)}, bf16[16,1536]{1,0:T(8,128)(2,1)S(1)}, u32[]{:S(2)}, u32[]{:S(2)}) collective-permute-start(bf16[16,1536]{1,0:T(8,128)(2,1)S(1)} %get-tuple-element.11), channel_id=1, source_target_pairs={{0,16},{16,32},{32,48},{48,0},{1,17},{17,33},{33,49},{49,1},{2,18}... | collective-permute-start | bytes 147464 | tf_op jit(solution)/shard_map/gather_images/ppermute | solution.py:38
  51.1 2.2 %all-to-all-done.1 = bf16[4,16,1536]{2,1,0:T(8,128)(2,1)S(1)} async-done(((bf16[4,16,1536]{2,1,0:T(8,128)(2,1)}), bf16[4,16,1536]{2,1,0:T(8,128)(2,1)S(1)}, u32[]{:S(2)}, u32[]{:S(2)}) %all-to-all-start.1) | async-done | bytes 196640 | tf_op jit(solution)/shard_map/gather_texts/all_to_all | solution.py:24
  53.4 0.9 broadcast_in_dim.16
  54.3 3.5 %all-to-all-start.2 = ((bf16[4,64,1536]{2,1,0:T(8,128)(2,1)}), bf16[4,64,1536]{2,1,0:T(8,128)(2,1)S(1)}, u32[]{:S(2)}, u32[]{:S(2)}) async-start(bf16[4,64,1536]{2,1,0:T(8,128)(2,1)} %broadcast_in_dim.16), calls=%async_computation.2 | async-start | bytes 1572864 | tf_op jit(solution)/shard_map/gather_texts/all_to_all | solution.py:24
  57.9 2.8 %collective-permute-start.3 = (bf16[64,1536]{1,0:T(8,128)(2,1)S(1)}, bf16[64,1536]{1,0:T(8,128)(2,1)S(1)}, u32[]{:S(2)}, u32[]{:S(2)}) collective-permute-start(bf16[64,1536]{1,0:T(8,128)(2,1)S(1)} %pad_maximum_fusion.2), channel_id=1, source_target_pairs={{0,6},{2,0},{4,2},{6,4},{1,7},{3,1},{5,3},{7,5},{8,14},{10,8},{12,... | collective-permute-start | bytes 589832 | tf_op jit(solution)/shard_map/gather_images/ppermute | solution.py:38
  60.7 2.9 %collective-permute-start.4 = (bf16[64,1536]{1,0:T(8,128)(2,1)S(1)}, bf16[64,1536]{1,0:T(8,128)(2,1)S(1)}, u32[]{:S(2)}, u32[]{:S(2)}) collective-permute-start(bf16[64,1536]{1,0:T(8,128)(2,1)S(1)} %pad_maximum_fusion.2), channel_id=1, source_target_pairs={{0,4},{2,6},{4,0},{6,2},{1,5},{3,7},{5,1},{7,3},{8,12},{10,14},{12... | collective-permute-start | bytes 589832 | tf_op jit(solution)/shard_map/gather_images/ppermute | solution.py:38
  63.5 1.9 collective-permute-start.5
  65.5 0.6 all-to-all-done.2
  66.1 10.2 %collective-permute-start.6 = (bf16[256,1536]{1,0:T(8,128)(2,1)S(1)}, bf16[256,1536]{1,0:T(8,128)(2,1)S(1)}, u32[]{:S(2)}, u32[]{:S(2)}) collective-permute-start(bf16[256,1536]{1,0:T(8,128)(2,1)S(1)} %bitcast.86), channel_id=1, source_target_pairs={{0,8},{8,0},{1,9},{9,1},{2,10},{10,2},{3,11},{11,3},{4,12},{12,4},... | collective-permute-start | bytes 2359304 | tf_op jit(solution)/shard_map/gather_texts/ppermute | solution.py:38
  76.5 1.8 collective-permute-done.6
  78.3 0.4 fusion.17
  78.7 0.4 convolution_convert_fusion
  79.1 2.8 %collective-permute-start.13 = (bf16[256,1536]{1,0:T(8,128)(2,1)S(1)}, bf16[256,1536]{1,0:T(8,128)(2,1)S(1)}, u32[]{:S(2)}, u32[]{:S(2)}) collective-permute-start(bf16[256,1536]{1,0:T(8,128)(2,1)S(1)} %convolution_convert_fusion), channel_id=1, source_target_pairs={{0,8},{8,0},{1,9},{9,1},{2,10},{10,2},{3,11},{11,3},{4,12},{12,4},... | collective-permute-start | bytes 2359304 | tf_op jit(solution)/shard_map/sum_texts/ppermute | solution.py:38
  81.9 0.4 fusion.18
  82.3 0.4 fusion.46
  82.7 1.3 fusion.45
  84.0 1.3 fusion
  85.3 4.5 %all-to-all-start.3 = ((bf16[4,64,1536]{2,1,0:T(8,128)(2,1)}), bf16[4,64,1536]{2,1,0:T(8,128)(2,1)S(1)}, u32[]{:S(2)}, u32[]{:S(2)}) async-start(bf16[4,64,1536]{2,1,0:T(8,128)(2,1)} %bitcast.7), calls=%async_computation.3 | async-start | bytes 1572864 | tf_op jit(solution)/shard_map/sum_texts/all_to_all | solution.py:24
  89.7 1.9 fusion.42
  91.7 1.9 collective-permute-start.7
  93.6 4.8 %collective-permute-start.8 = (bf16[64,1536]{1,0:T(8,128)(2,1)}, bf16[64,1536]{1,0:T(8,128)(2,1)S(1)}, u32[]{:S(2)}, u32[]{:S(2)}) collective-permute-start(bf16[64,1536]{1,0:T(8,128)(2,1)} %get-tuple-element.20), channel_id=1, source_target_pairs={{0,4},{2,6},{4,0},{6,2},{1,5},{3,7},{5,1},{7,3},{8,12},{10,14},{12... | collective-permute-start | bytes 589832 | tf_op jit(solution)/shard_map/sum_images/ppermute | solution.py:38
  98.4 2.8 %collective-permute-start.9 = (bf16[64,1536]{1,0:T(8,128)(2,1)}, bf16[64,1536]{1,0:T(8,128)(2,1)}, u32[]{:S(2)}, u32[]{:S(2)}) collective-permute-start(bf16[64,1536]{1,0:T(8,128)(2,1)} %get-tuple-element.19), channel_id=1, source_target_pairs={{0,6},{2,0},{4,2},{6,4},{1,7},{3,1},{5,3},{7,5},{8,14},{10,8},{12,... | collective-permute-start | bytes 589832 | tf_op jit(solution)/shard_map/sum_images/ppermute | solution.py:38
  101.2 0.5 all-to-all-done.3
  101.7 0.8 reduce_sum.97
  102.5 6.4 %all-to-all-start.4 = ((bf16[4,16,1536]{2,1,0:T(8,128)(2,1)}), bf16[4,16,1536]{2,1,0:T(8,128)(2,1)S(1)}, u32[]{:S(2)}, u32[]{:S(2)}) async-start(bf16[4,16,1536]{2,1,0:T(8,128)(2,1)} %bitcast.8), calls=%async_computation.4 | async-start | bytes 393216 | tf_op jit(solution)/shard_map/sum_texts/all_to_all | solution.py:24
  108.9 1.0 fusion.38
  109.9 3.5 %collective-permute-start.10 = (bf16[16,1536]{1,0:T(8,128)(2,1)S(1)}, bf16[16,1536]{1,0:T(8,128)(2,1)S(1)}, u32[]{:S(2)}, u32[]{:S(2)}) collective-permute-start(bf16[16,1536]{1,0:T(8,128)(2,1)S(1)} %get-tuple-element.25), channel_id=1, source_target_pairs={{0,16},{16,32},{32,48},{48,0},{1,17},{17,33},{33,49},{49,1},{2,18}... | collective-permute-start | bytes 147464 | tf_op jit(solution)/shard_map/sum_images/ppermute | solution.py:38
  113.5 3.1 %collective-permute-start.11 = (bf16[16,1536]{1,0:T(8,128)(2,1)S(1)}, bf16[16,1536]{1,0:T(8,128)(2,1)S(1)}, u32[]{:S(2)}, u32[]{:S(2)}) collective-permute-start(bf16[16,1536]{1,0:T(8,128)(2,1)S(1)} %get-tuple-element.27), channel_id=1, source_target_pairs={{0,32},{16,48},{32,0},{48,16},{1,33},{17,49},{33,1},{49,17},{2,34}... | collective-permute-start | bytes 147464 | tf_op jit(solution)/shard_map/sum_images/ppermute | solution.py:38
  116.6 3.3 %collective-permute-start.12 = (bf16[16,1536]{1,0:T(8,128)(2,1)S(1)}, bf16[16,1536]{1,0:T(8,128)(2,1)S(1)}, u32[]{:S(2)}, u32[]{:S(2)}) collective-permute-start(bf16[16,1536]{1,0:T(8,128)(2,1)S(1)} %get-tuple-element.26), channel_id=1, source_target_pairs={{0,48},{16,0},{32,16},{48,32},{1,49},{17,1},{33,17},{49,33},{2,50}... | collective-permute-start | bytes 147464 | tf_op jit(solution)/shard_map/sum_images/ppermute | solution.py:38
  119.8 2.1 all-to-all-done.4
  122.0 0.3 collective-permute-done.12
  122.3 0.2 multiply_reduce_fusion.1
  122.7 1.0 broadcast_in_dim.17
  123.6 5.8 %all-to-all-start.5 = ((bf16[8,2,16,1536]{3,2,1,0:T(8,128)(2,1)}), bf16[8,2,16,1536]{3,2,1,0:T(8,128)(2,1)S(1)}, u32[]{:S(2)}, u32[]{:S(2)}) async-start(bf16[8,2,16,1536]{3,2,1,0:T(8,128)(2,1)} %broadcast_in_dim.17), calls=%async_computation.5 | async-start | bytes 1572864 | tf_op jit(solution)/shard_map/head_grads/all_to_all | solution.py:24
  129.5 10.4 %all-to-all-done.5 = bf16[8,2,16,1536]{3,2,1,0:T(8,128)(2,1)S(1)} async-done(((bf16[8,2,16,1536]{3,2,1,0:T(8,128)(2,1)}), bf16[8,2,16,1536]{3,2,1,0:T(8,128)(2,1)S(1)}, u32[]{:S(2)}, u32[]{:S(2)}) %all-to-all-start.5) | async-done | bytes 786464 | tf_op jit(solution)/shard_map/head_grads/all_to_all | solution.py:24
  140.0 0.2 fusion.1
  140.2 0.2 fusion.2
  140.5 9.1 %collective-permute-start.14 = (bf16[2,96,1536]{2,1,0:T(8,128)(2,1)S(1)}, bf16[2,96,1536]{2,1,0:T(8,128)(2,1)S(1)}, u32[]{:S(2)}, u32[]{:S(2)}) collective-permute-start(bf16[2,96,1536]{2,1,0:T(8,128)(2,1)S(1)} %pad_maximum_fusion.1), channel_id=1, source_target_pairs={{0,8},{8,0},{1,9},{9,1},{2,10},{10,2},{3,11},{11,3},{4,12},{12,4},... | collective-permute-start | bytes 1769480 | tf_op jit(solution)/shard_map/weight_grads/ppermute | solution.py:38
  149.6 0.2 convolution_bitcast_fusion
  149.8 0.2 convolution_bitcast_fusion.1
  150.1 1.2 collective-permute-done.14
  151.3 11.1 %all_to_all.50 = bf16[4,48,1536]{2,1,0:T(8,128)(2,1)S(1)} all-to-all(bf16[4,48,1536]{2,1,0:T(8,128)(2,1)S(1)} %bitcast.90), channel_id=1, replica_groups=mesh['xl'=2,'zh'=4,'zm'=2,'z0'=2,'c'=2,'y'=4,'xh'=2] {'xl','z0'}, dimensions={0} | all-to-all | bytes 1179648 | tf_op jit(solution)/shard_map/weight_grads/all_to_all | solution.py:24
  162.6 21.3 %all_to_all.51 = bf16[8,24,384]{2,1,0:T(8,128)(2,1)S(1)} all-to-all(bf16[8,24,384]{2,1,0:T(8,128)(2,1)S(1)} %bitcast.93), channel_id=1, replica_groups=mesh['xl'=2,'zh'=4,'zm'=2,'z0'=2,'c'=2,'y'=4,'xh'=2] {'zh','zm'}, dimensions={0} | all-to-all | bytes 294912 | tf_op jit(solution)/shard_map/weight_grads/all_to_all | solution.py:24
  184.0 18.0 %all_to_all.52 = bf16[8,24,384]{2,1,0:T(8,128)(2,1)S(1)} all-to-all(bf16[8,24,384]{2,1,0:T(8,128)(2,1)S(1)} %broadcast_in_dim.18), channel_id=1, replica_groups=mesh['xl'=2,'zh'=4,'zm'=2,'z0'=2,'c'=2,'y'=4,'xh'=2] {'zh','zm'}, dimensions={0} | all-to-all | bytes 294912 | tf_op jit(solution)/shard_map/weight_grads/all_to_all | solution.py:24
  202.1 0.9 broadcast_in_dim.20
  203.0 3.7 %all-to-all-start.9 = ((bf16[4,48,1536]{2,1,0:T(8,128)(2,1)}), bf16[4,48,1536]{2,1,0:T(8,128)(2,1)S(1)}, u32[]{:S(2)}, u32[]{:S(2)}) async-start(bf16[4,48,1536]{2,1,0:T(8,128)(2,1)} %broadcast_in_dim.20), calls=%async_computation.9 | async-start | bytes 1179648 | tf_op jit(solution)/shard_map/weight_grads/all_to_all | solution.py:24
  206.7 1.0 fusion.47
  207.6 5.9 %all-to-all-done.9 = bf16[4,48,1536]{2,1,0:T(8,128)(2,1)S(1)} async-done(((bf16[4,48,1536]{2,1,0:T(8,128)(2,1)}), bf16[4,48,1536]{2,1,0:T(8,128)(2,1)S(1)}, u32[]{:S(2)}, u32[]{:S(2)}) %all-to-all-start.9) | async-done | bytes 589856 | tf_op jit(solution)/shard_map/weight_grads/all_to_all | solution.py:24
  213.6 5.4 %collective-permute-start.15 = (bf16[2,96,1536]{2,1,0:T(8,128)(2,1)S(1)}, bf16[2,96,1536]{2,1,0:T(8,128)(2,1)S(1)}, u32[]{:S(2)}, u32[]{:S(2)}) collective-permute-start(bf16[2,96,1536]{2,1,0:T(8,128)(2,1)S(1)} %bitcast.89), channel_id=1, source_target_pairs={{0,8},{8,0},{1,9},{9,1},{2,10},{10,2},{3,11},{11,3},{4,12},{12,4},... | collective-permute-start | bytes 1769480 | tf_op jit(solution)/shard_map/weight_grads/ppermute | solution.py:38
  219.0 1.0 fusion.48
  220.0 0.6 collective-permute-done.15
  220.6 0.1 bitcast_select_fusion.1
  220.7 1.1 maximum_convert_fusion.1
  221.8 1.1 maximum_convert_fusion
  (48 shorter events, 1.1 us)
Async XLA Ops:
  0.6 1.5 copy-start
  4.2 18.7 %all-to-all-start = ((bf16[8,16,3072]{2,1,0:T(8,128)(2,1)}), bf16[8,16,3072]{2,1,0:T(8,128)(2,1)S(1)}, u32[]{:S(2)}, u32[]{:S(2)}) async-start(bf16[8,16,3072]{2,1,0:T(8,128)(2,1)} %bitcast.2), calls=%async_computation | async-start | bytes 1572864 | tf_op jit(solution)/shard_map/heads/all_to_all | solution.py:24
  23.9 29.5 %all-to-all-start.1 = ((bf16[4,16,1536]{2,1,0:T(8,128)(2,1)}), bf16[4,16,1536]{2,1,0:T(8,128)(2,1)S(1)}, u32[]{:S(2)}, u32[]{:S(2)}) async-start(bf16[4,16,1536]{2,1,0:T(8,128)(2,1)} %broadcast_in_dim.14), calls=%async_computation.1 | async-start | bytes 393216 | tf_op jit(solution)/shard_map/gather_texts/all_to_all | solution.py:24
  40.8 17.0 %collective-permute-start = (bf16[16,1536]{1,0:T(8,128)(2,1)S(1)}, bf16[16,1536]{1,0:T(8,128)(2,1)S(1)}, u32[]{:S(2)}, u32[]{:S(2)}) collective-permute-start(bf16[16,1536]{1,0:T(8,128)(2,1)S(1)} %get-tuple-element.11), channel_id=1, source_target_pairs={{0,48},{16,0},{32,16},{48,32},{1,49},{17,1},{33,17},{49,33},{2,50}... | collective-permute-start | bytes 147464 | tf_op jit(solution)/shard_map/gather_images/ppermute | solution.py:38
  44.3 13.5 %collective-permute-start.1 = (bf16[16,1536]{1,0:T(8,128)(2,1)S(1)}, bf16[16,1536]{1,0:T(8,128)(2,1)S(1)}, u32[]{:S(2)}, u32[]{:S(2)}) collective-permute-start(bf16[16,1536]{1,0:T(8,128)(2,1)S(1)} %get-tuple-element.11), channel_id=1, source_target_pairs={{0,32},{16,48},{32,0},{48,16},{1,33},{17,49},{33,1},{49,17},{2,34}... | collective-permute-start | bytes 147464 | tf_op jit(solution)/shard_map/gather_images/ppermute | solution.py:38
  46.5 11.3 %collective-permute-start.2 = (bf16[16,1536]{1,0:T(8,128)(2,1)S(1)}, bf16[16,1536]{1,0:T(8,128)(2,1)S(1)}, u32[]{:S(2)}, u32[]{:S(2)}) collective-permute-start(bf16[16,1536]{1,0:T(8,128)(2,1)S(1)} %get-tuple-element.11), channel_id=1, source_target_pairs={{0,16},{16,32},{32,48},{48,0},{1,17},{17,33},{33,49},{49,1},{2,18}... | collective-permute-start | bytes 147464 | tf_op jit(solution)/shard_map/gather_images/ppermute | solution.py:38
  54.3 11.8 %all-to-all-start.2 = ((bf16[4,64,1536]{2,1,0:T(8,128)(2,1)}), bf16[4,64,1536]{2,1,0:T(8,128)(2,1)S(1)}, u32[]{:S(2)}, u32[]{:S(2)}) async-start(bf16[4,64,1536]{2,1,0:T(8,128)(2,1)} %broadcast_in_dim.16), calls=%async_computation.2 | async-start | bytes 1572864 | tf_op jit(solution)/shard_map/gather_texts/all_to_all | solution.py:24
  57.9 18.5 %collective-permute-start.3 = (bf16[64,1536]{1,0:T(8,128)(2,1)S(1)}, bf16[64,1536]{1,0:T(8,128)(2,1)S(1)}, u32[]{:S(2)}, u32[]{:S(2)}) collective-permute-start(bf16[64,1536]{1,0:T(8,128)(2,1)S(1)} %pad_maximum_fusion.2), channel_id=1, source_target_pairs={{0,6},{2,0},{4,2},{6,4},{1,7},{3,1},{5,3},{7,5},{8,14},{10,8},{12,... | collective-permute-start | bytes 589832 | tf_op jit(solution)/shard_map/gather_images/ppermute | solution.py:38
  60.7 15.8 %collective-permute-start.4 = (bf16[64,1536]{1,0:T(8,128)(2,1)S(1)}, bf16[64,1536]{1,0:T(8,128)(2,1)S(1)}, u32[]{:S(2)}, u32[]{:S(2)}) collective-permute-start(bf16[64,1536]{1,0:T(8,128)(2,1)S(1)} %pad_maximum_fusion.2), channel_id=1, source_target_pairs={{0,4},{2,6},{4,0},{6,2},{1,5},{3,7},{5,1},{7,3},{8,12},{10,14},{12... | collective-permute-start | bytes 589832 | tf_op jit(solution)/shard_map/gather_images/ppermute | solution.py:38
  63.5 12.9 %collective-permute-start.5 = (bf16[64,1536]{1,0:T(8,128)(2,1)S(1)}, bf16[64,1536]{1,0:T(8,128)(2,1)S(1)}, u32[]{:S(2)}, u32[]{:S(2)}) collective-permute-start(bf16[64,1536]{1,0:T(8,128)(2,1)S(1)} %pad_maximum_fusion.2), channel_id=1, source_target_pairs={{0,2},{2,4},{4,6},{6,0},{1,3},{3,5},{5,7},{7,1},{8,10},{10,12},{12... | collective-permute-start | bytes 589832 | tf_op jit(solution)/shard_map/gather_images/ppermute | solution.py:38
  66.1 12.1 %collective-permute-start.6 = (bf16[256,1536]{1,0:T(8,128)(2,1)S(1)}, bf16[256,1536]{1,0:T(8,128)(2,1)S(1)}, u32[]{:S(2)}, u32[]{:S(2)}) collective-permute-start(bf16[256,1536]{1,0:T(8,128)(2,1)S(1)} %bitcast.86), channel_id=1, source_target_pairs={{0,8},{8,0},{1,9},{9,1},{2,10},{10,2},{3,11},{11,3},{4,12},{12,4},... | collective-permute-start | bytes 2359304 | tf_op jit(solution)/shard_map/gather_texts/ppermute | solution.py:38
  79.1 4.9 %collective-permute-start.13 = (bf16[256,1536]{1,0:T(8,128)(2,1)S(1)}, bf16[256,1536]{1,0:T(8,128)(2,1)S(1)}, u32[]{:S(2)}, u32[]{:S(2)}) collective-permute-start(bf16[256,1536]{1,0:T(8,128)(2,1)S(1)} %convolution_convert_fusion), channel_id=1, source_target_pairs={{0,8},{8,0},{1,9},{9,1},{2,10},{10,2},{3,11},{11,3},{4,12},{12,4},... | collective-permute-start | bytes 2359304 | tf_op jit(solution)/shard_map/sum_texts/ppermute | solution.py:38
  85.3 16.4 %all-to-all-start.3 = ((bf16[4,64,1536]{2,1,0:T(8,128)(2,1)}), bf16[4,64,1536]{2,1,0:T(8,128)(2,1)S(1)}, u32[]{:S(2)}, u32[]{:S(2)}) async-start(bf16[4,64,1536]{2,1,0:T(8,128)(2,1)} %bitcast.7), calls=%async_computation.3 | async-start | bytes 1572864 | tf_op jit(solution)/shard_map/sum_texts/all_to_all | solution.py:24
  91.7 17.2 %collective-permute-start.7 = (bf16[64,1536]{1,0:T(8,128)(2,1)}, bf16[64,1536]{1,0:T(8,128)(2,1)S(1)}, u32[]{:S(2)}, u32[]{:S(2)}) collective-permute-start(bf16[64,1536]{1,0:T(8,128)(2,1)} %get-tuple-element.18), channel_id=1, source_target_pairs={{0,2},{2,4},{4,6},{6,0},{1,3},{3,5},{5,7},{7,1},{8,10},{10,12},{12... | collective-permute-start | bytes 589832 | tf_op jit(solution)/shard_map/sum_images/ppermute | solution.py:38
  93.6 15.3 %collective-permute-start.8 = (bf16[64,1536]{1,0:T(8,128)(2,1)}, bf16[64,1536]{1,0:T(8,128)(2,1)S(1)}, u32[]{:S(2)}, u32[]{:S(2)}) collective-permute-start(bf16[64,1536]{1,0:T(8,128)(2,1)} %get-tuple-element.20), channel_id=1, source_target_pairs={{0,4},{2,6},{4,0},{6,2},{1,5},{3,7},{5,1},{7,3},{8,12},{10,14},{12... | collective-permute-start | bytes 589832 | tf_op jit(solution)/shard_map/sum_images/ppermute | solution.py:38
  98.4 10.5 %collective-permute-start.9 = (bf16[64,1536]{1,0:T(8,128)(2,1)}, bf16[64,1536]{1,0:T(8,128)(2,1)}, u32[]{:S(2)}, u32[]{:S(2)}) collective-permute-start(bf16[64,1536]{1,0:T(8,128)(2,1)} %get-tuple-element.19), channel_id=1, source_target_pairs={{0,6},{2,0},{4,2},{6,4},{1,7},{3,1},{5,3},{7,5},{8,14},{10,8},{12,... | collective-permute-start | bytes 589832 | tf_op jit(solution)/shard_map/sum_images/ppermute | solution.py:38
  102.5 19.4 %all-to-all-start.4 = ((bf16[4,16,1536]{2,1,0:T(8,128)(2,1)}), bf16[4,16,1536]{2,1,0:T(8,128)(2,1)S(1)}, u32[]{:S(2)}, u32[]{:S(2)}) async-start(bf16[4,16,1536]{2,1,0:T(8,128)(2,1)} %bitcast.8), calls=%async_computation.4 | async-start | bytes 393216 | tf_op jit(solution)/shard_map/sum_texts/all_to_all | solution.py:24
  109.9 12.0 %collective-permute-start.10 = (bf16[16,1536]{1,0:T(8,128)(2,1)S(1)}, bf16[16,1536]{1,0:T(8,128)(2,1)S(1)}, u32[]{:S(2)}, u32[]{:S(2)}) collective-permute-start(bf16[16,1536]{1,0:T(8,128)(2,1)S(1)} %get-tuple-element.25), channel_id=1, source_target_pairs={{0,16},{16,32},{32,48},{48,0},{1,17},{17,33},{33,49},{49,1},{2,18}... | collective-permute-start | bytes 147464 | tf_op jit(solution)/shard_map/sum_images/ppermute | solution.py:38
  113.5 8.5 %collective-permute-start.11 = (bf16[16,1536]{1,0:T(8,128)(2,1)S(1)}, bf16[16,1536]{1,0:T(8,128)(2,1)S(1)}, u32[]{:S(2)}, u32[]{:S(2)}) collective-permute-start(bf16[16,1536]{1,0:T(8,128)(2,1)S(1)} %get-tuple-element.27), channel_id=1, source_target_pairs={{0,32},{16,48},{32,0},{48,16},{1,33},{17,49},{33,1},{49,17},{2,34}... | collective-permute-start | bytes 147464 | tf_op jit(solution)/shard_map/sum_images/ppermute | solution.py:38
  116.6 5.8 %collective-permute-start.12 = (bf16[16,1536]{1,0:T(8,128)(2,1)S(1)}, bf16[16,1536]{1,0:T(8,128)(2,1)S(1)}, u32[]{:S(2)}, u32[]{:S(2)}) collective-permute-start(bf16[16,1536]{1,0:T(8,128)(2,1)S(1)} %get-tuple-element.26), channel_id=1, source_target_pairs={{0,48},{16,0},{32,16},{48,32},{1,49},{17,1},{33,17},{49,33},{2,50}... | collective-permute-start | bytes 147464 | tf_op jit(solution)/shard_map/sum_images/ppermute | solution.py:38
  123.6 16.3 %all-to-all-start.5 = ((bf16[8,2,16,1536]{3,2,1,0:T(8,128)(2,1)}), bf16[8,2,16,1536]{3,2,1,0:T(8,128)(2,1)S(1)}, u32[]{:S(2)}, u32[]{:S(2)}) async-start(bf16[8,2,16,1536]{3,2,1,0:T(8,128)(2,1)} %broadcast_in_dim.17), calls=%async_computation.5 | async-start | bytes 1572864 | tf_op jit(solution)/shard_map/head_grads/all_to_all | solution.py:24
  129.5 10.5 %copy-start.3 = (bf16[128,192]{0,1:T(8,128)(2,1)S(1)}, bf16[128,192]{0,1:T(8,128)(2,1)}, u32[]{:S(2)}) copy-start(bf16[128,192]{0,1:T(8,128)(2,1)} %param.7) | copy-start | bytes 147460
  129.5 10.8 %copy-start.2 = (bf16[128,192]{0,1:T(8,128)(2,1)S(1)}, bf16[128,192]{0,1:T(8,128)(2,1)}, u32[]{:S(2)}) copy-start(bf16[128,192]{0,1:T(8,128)(2,1)} %param.8) | copy-start | bytes 147460
  140.5 10.7 %collective-permute-start.14 = (bf16[2,96,1536]{2,1,0:T(8,128)(2,1)S(1)}, bf16[2,96,1536]{2,1,0:T(8,128)(2,1)S(1)}, u32[]{:S(2)}, u32[]{:S(2)}) collective-permute-start(bf16[2,96,1536]{2,1,0:T(8,128)(2,1)S(1)} %pad_maximum_fusion.1), channel_id=1, source_target_pairs={{0,8},{8,0},{1,9},{9,1},{2,10},{10,2},{3,11},{11,3},{4,12},{12,4},... | collective-permute-start | bytes 1769480 | tf_op jit(solution)/shard_map/weight_grads/ppermute | solution.py:38
  203.0 16.0 %copy-start.1 = (bf16[192,1536]{1,0:T(8,128)(2,1)S(1)}, bf16[192,1536]{1,0:T(8,128)(2,1)}, u32[]{:S(2)}) copy-start(bf16[192,1536]{1,0:T(8,128)(2,1)} %param.10) | copy-start | bytes 1769476
  203.0 10.6 %all-to-all-start.9 = ((bf16[4,48,1536]{2,1,0:T(8,128)(2,1)}), bf16[4,48,1536]{2,1,0:T(8,128)(2,1)S(1)}, u32[]{:S(2)}, u32[]{:S(2)}) async-start(bf16[4,48,1536]{2,1,0:T(8,128)(2,1)} %broadcast_in_dim.20), calls=%async_computation.9 | async-start | bytes 1179648 | tf_op jit(solution)/shard_map/weight_grads/all_to_all | solution.py:24
  213.6 7.0 %collective-permute-start.15 = (bf16[2,96,1536]{2,1,0:T(8,128)(2,1)S(1)}, bf16[2,96,1536]{2,1,0:T(8,128)(2,1)S(1)}, u32[]{:S(2)}, u32[]{:S(2)}) collective-permute-start(bf16[2,96,1536]{2,1,0:T(8,128)(2,1)S(1)} %bitcast.89), channel_id=1, source_target_pairs={{0,8},{8,0},{1,9},{9,1},{2,10},{10,2},{3,11},{11,3},{4,12},{12,4},... | collective-permute-start | bytes 1769480 | tf_op jit(solution)/shard_map/weight_grads/ppermute | solution.py:38

commit v6 on v5

--- a/solution.py
+++ b/solution.py
@@ -1,6 +1,8 @@
 import jax
 import jax.numpy as jnp
 from jax import lax
+from jax.experimental import pallas as pl
+from jax.experimental.pallas import tpu as pltpu
 from jax.sharding import Mesh, PartitionSpec as P
 
 BF16 = jnp.bfloat16
@@ -58,6 +60,90 @@
 
 def merge_rows(value):
     return value.reshape((-1,) + value.shape[2:])
+
+
+VMEM = pl.BlockSpec(memory_space=pltpu.VMEM)
+SMEM = pl.BlockSpec(memory_space=pltpu.SMEM)
+
+
+def local_kernel(body, operands, outs, flops, in_specs=None):
+    moved = sum(x.size * x.dtype.itemsize for x in tuple(operands) + tuple(outs))
+    return pl.pallas_call(
+        body,
+        out_shape=outs,
+        in_specs=in_specs or [VMEM] * len(operands),
+        out_specs=[VMEM] * len(outs),
+        compiler_params=pltpu.CompilerParams(vmem_limit_bytes=24 * 2**20),
+        cost_estimate=pl.CostEstimate(flops=flops, bytes_accessed=moved, transcendentals=0),
+    )(*operands)
+
+
+def contract(left, right, left_dim, right_dim):
+    dims = (((left_dim,), (right_dim,)), ((), ()))
+    return lax.dot_general(left, right, dims, preferred_element_type=F32)
+
+
+def project_body(image_features, text_features, image_weight, text_weight, heads):
+    width = image_weight.shape[1]
+    heads[:, :width] = contract(image_features[...], image_weight[...], 0, 0).astype(BF16)
+    heads[:, width:] = contract(text_features[...], text_weight[...], 0, 0).astype(BF16)
+
+
+def project(image_features, text_features, image_weight, text_weight):
+    rows, depth = image_features.shape
+    width = image_weight.shape[1]
+    (heads,) = local_kernel(
+        project_body,
+        (image_features.T, text_features.T, image_weight, text_weight),
+        [jax.ShapeDtypeStruct((rows, 2 * width), BF16)],
+        4 * rows * depth * width,
+    )
+    return heads
+
+
+def pairs_body(numbers, places, texts, images, coeff, part):
+    scores = numbers[0] * contract(texts[...], images[...], 1, 1) + numbers[1]
+    text_at = lax.broadcasted_iota(jnp.int32, scores.shape, 0) - places[0]
+    image_at = lax.broadcasted_iota(jnp.int32, scores.shape, 1)
+    positive = (text_at == image_at) & (image_at < places[1])
+    value = numbers[2] * (jax.nn.sigmoid(scores) - positive.astype(F32))
+    coeff[...] = value.astype(BF16)
+    part[...] = contract(coeff[...], images[...], 1, 0).astype(part.dtype)
+
+
+def pair_block(numbers, places, texts, images, dtype):
+    rows, width = texts.shape
+    return local_kernel(
+        pairs_body,
+        (numbers, places, texts, images),
+        [
+            jax.ShapeDtypeStruct((rows, images.shape[0]), BF16),
+            jax.ShapeDtypeStruct((rows, width), dtype),
+        ],
+        4 * rows * images.shape[0] * width,
+        [SMEM, SMEM, VMEM, VMEM],
+    )
+
+
+def images_body(coeff, texts, other_coeff, other_texts, own, *sent):
+    rows = own.shape[0]
+    for k, out in enumerate((own,) + sent):
+        at = slice(k * rows, (k + 1) * rows)
+        total = contract(coeff[:, at], texts[...], 0, 0)
+        total = total + contract(other_coeff[:, at], other_texts[...], 0, 0)
+        out[...] = total.astype(out.dtype)
+
+
+def image_blocks(coeff, texts, other_coeff, other_texts, blocks):
+    width = texts.shape[1]
+    rows = coeff.shape[1] // blocks
+    return local_kernel(
+        images_body,
+        (coeff, texts, other_coeff, other_texts),
+        [jax.ShapeDtypeStruct((rows, width), F32)]
+        + [jax.ShapeDtypeStruct((rows, width), BF16)] * (blocks - 1),
+        4 * coeff.shape[0] * coeff.shape[1] * width,
+    )
 
 
 def unit_rows(heads):
@@ -89,13 +175,7 @@
     share = image_features.shape[0] // members
 
     with jax.named_scope("heads"):
-        partial_heads = jnp.concatenate(
-            (
-                jnp.dot(image_features, image_weight, preferred_element_type=F32).astype(BF16),
-                jnp.dot(text_features, text_weight, preferred_element_type=F32).astype(BF16),
-            ),
-            axis=1,
-        )
+        partial_heads = project(image_features, text_features, image_weight, text_weight)
         both_heads = scatter_sum(split_rows(partial_heads, members), MP).astype(BF16)
         image_unit, image_norm = unit_rows(both_heads[:, :embed_width])
         text_unit, text_norm = unit_rows(both_heads[:, embed_width:])
@@ -107,32 +187,26 @@
     with jax.named_scope("gather_images"):
         images = ring_gather(ring_gather(image_unit.astype(BF16), ZL), "y")
 
-    def coefficients(block, positive):
-        scores = (
-            scale * jnp.einsum("te,ie->ti", block, images, preferred_element_type=F32) + shift_bias
-        )
-        return (factor * (jax.nn.sigmoid(scores) - positive)).astype(BF16)
-
     with jax.named_scope("pairs"):
+        numbers = jnp.stack((scale, shift_bias, factor))
         text_base = ((at["xh"] * 2 + at["xl"]) * 4 + at["zh"]) * share
-        text_at = jnp.arange(texts.shape[0], dtype=jnp.int32)[:, None] - text_base
-        image_at = jnp.arange(images.shape[0], dtype=jnp.int32)[None, :]
-        positive = (text_at == image_at) & (image_at < share)
-        coeff = coefficients(texts, positive.astype(F32))
-        other_coeff = coefficients(other_texts, 0.0)
-        other_part = jnp.dot(other_coeff, images, preferred_element_type=F32)
-        text_part = jnp.dot(coeff, images, preferred_element_type=F32)
-        image_part = jnp.einsum("ti,te->ie", coeff, texts, preferred_element_type=F32)
-        image_part = image_part + jnp.einsum(
-            "ti,te->ie", other_coeff, other_texts, preferred_element_type=F32
-        )
+        places = jnp.stack((text_base, jnp.int32(share)))
+        nowhere = jnp.zeros_like(places)
+        other_coeff, other_part = pair_block(numbers, nowhere, other_texts, images, BF16)
+        coeff, text_part = pair_block(numbers, places, texts, images, F32)
 
     with jax.named_scope("sum_texts"):
-        text_part = text_part + shifted(other_part.astype(BF16), "c", 1).astype(F32)
-        text_part = scatter_sum(split_rows(text_part, count(("xh", "xl"))), ("xh", "xl"))
+        text_part = text_part + shifted(other_part, "c", 1).astype(F32)
+        text_part = split_rows(text_part, count(("xh", "xl"))).astype(BF16)
+        text_part, other_coeff = lax.optimization_barrier((text_part, other_coeff))
+        text_part = scatter_sum(text_part, ("xh", "xl"))
         text_grads = scatter_sum(split_rows(text_part, count("zh")), "zh")
     with jax.named_scope("sum_images"):
-        image_grads = ring_scatter_sum(ring_scatter_sum(image_part, "y"), ZL)
+        blocks = image_blocks(coeff, texts, other_coeff, other_texts, count("y"))
+        image_part = blocks[0]
+        for k in range(1, count("y")):
+            image_part = image_part + shifted(blocks[k], "y", k).astype(F32)
+        image_grads = ring_scatter_sum(image_part, ZL)
 
     with jax.named_scope("head_grads"):
         grads = jnp.stack(
@@ -176,13 +250,14 @@
         part = part.transpose(1, 2, 0, 3).reshape(half // 2, embed_width)
         part = gather(part, ("xl", "z0")).reshape(2, half, embed_width)
         other = shifted(part, "c", 1)
-        first = at["c"] == 0
-        image_weight_grad, text_weight_grad = (
-            jnp.concatenate(
-                (jnp.where(first, mine, theirs), jnp.where(first, theirs, mine)), axis=0
-            ).astype(F32)
-            for mine, theirs in zip(part, other)
-        )
+
+        def halves(mine, theirs):
+            mine, theirs = mine.astype(F32), theirs.astype(F32)
+            both = jnp.concatenate((mine, mine), axis=0)
+            return lax.dynamic_update_slice_in_dim(both, theirs, (1 - at["c"]) * half, 0)
+
+        image_weight_grad = halves(part[0], other[0])
+        text_weight_grad = halves(part[1], other[1])
     return (image_input_grad, text_input_grad, image_weight_grad, text_weight_grad)
 
 

time: 224 us -> 226 us (level)
  blocking collectives: 50.5 us -> 70.9 us
  starting transfers between devices: 111 us -> 101 us
  waiting for transfers between devices: 37 us -> 27.1 us
  matrix products: 9.45 us -> 2.8 us
  Pallas kernels: 0 us -> 4.82 us
  local copies, waits for them, and re-layouts: 5.73 us -> 8.9 us
    all_to_all x3 -> x4, blocking collectives: 50.5 us -> 70.9 us  [exchange(): return lax.all_to_all(blocks, axes, split_axis=0, concat_axis=0, tiled=True)]
    all_to_all x7 -> x6, waiting for transfers between devices: 33.1 us -> 21.9 us  [exchange(): return lax.all_to_all(blocks, axes, split_axis=0, concat_axis=0, tiled=True)]
    all_to_all x7 -> x6, starting transfers between devices: 48.1 us -> 39.4 us  [exchange(): return lax.all_to_all(blocks, axes, split_axis=0, concat_axis=0, tiled=True)]
    dot_general x8 -> x0, matrix products: 6.65 us -> none  [the longest x1 1.44 us: on_device(): jnp.dot(text_features, text_weight, preferred_element_type=F32).astype(BF16)]
    unnamed x14 -> x26, local copies, waits for them, and re-layouts: 0.09 us -> 5.2 us
    pallas_call x0 -> x4, Pallas kernels: none -> 4.82 us  [local_kernel(): pl.pallas_call(body, out_shape=outs, in_specs=in_specs or [VMEM] * len(op...]
  transfers between devices with their start and end apart: 23 -> 22, of which waited for: 11 -> 10; matrix products, arithmetic and copies ran while one was open for 4% -> 3% of each run, Pallas kernels for 0% -> 1%
where the time goes in v6:
time: 226 us; the launch traced here: 225 us
  starting transfers between devices  101 us (45%)
  blocking collectives  70.9 us (31%)
  waiting for transfers between devices  27.1 us (12%)
  local copies, waits for them, and re-layouts  8.9 us (4%)
  other arithmetic  5.9 us (3%)
  Pallas kernels  4.82 us (2%)
  between operations  3.13 us (1%)
  matrix products  2.8 us (1%)
    all_to_all x4, blocking collectives, exchange(): return lax.all_to_all(blocks, axes, split_axis=0, concat_axis=0, tiled=True)  70.9 us
    ppermute x16, starting transfers between devices, shifted(): return lax.ppermute(value, axis, [(i, (i + by) % n) for i in range(n)])  61.6 us
    all_to_all x6, starting transfers between devices, exchange(): return lax.all_to_all(blocks, axes, split_axis=0, concat_axis=0, tiled=True)  39.4 us
    all_to_all x6, waiting for transfers between devices, exchange(): return lax.all_to_all(blocks, axes, split_axis=0, concat_axis=0, tiled=True)  21.9 us
    ppermute x16, waiting for transfers between devices, shifted(): return lax.ppermute(value, axis, [(i, (i + by) % n) for i in range(n)])  5.23 us
    unnamed x26, local copies, waits for them, and re-layouts  5.2 us
    pallas_call x4, Pallas kernels, local_kernel(): pl.pallas_call(body, out_shape=outs, in_specs=in_specs or [VMEM] * len(op...  4.82 us
  transfers between devices with their start and end apart: 22, of which 10 were waited for; matrix products, arithmetic and copies ran while one was open for 3% of the time, Pallas kernels for 1%

profile of v6, /device:TPU:1, one launch (start us, length us, event | category | flops | bytes accessed | tf_op | source)
XLA Modules:
  0.0 224.6 jit_solution(2058678773148199232)
XLA Ops:
  0.6 1.1 copy-done
  1.7 1.1 copy-done.2
  2.8 0.8 copy-done.4
  3.6 0.8 copy-done.6
  4.4 0.4 heads.1
  4.8 19.4 %all_to_all.50 = bf16[8,16,3072]{2,1,0:T(8,128)(2,1)S(1)} all-to-all(bf16[8,16,3072]{2,1,0:T(8,128)(2,1)S(1)} %bitcast.55), channel_id=1, replica_groups=mesh['xl'=2,'zh'=4,'zm'=2,'z0'=2,'c'=2,'y'=4,'xh'=2] {'y','xh'}, dimensions={0} | all-to-all | bytes 1572864 | tf_op jit(solution)/shard_map/heads/all_to_all | solution.py:26
  24.3 0.1 fusion.4
  24.5 0.7 broadcast_in_dim.14
  25.2 16.2 %all-to-all-start.1 = ((bf16[4,16,1536]{2,1,0:T(8,128)(2,1)}), bf16[4,16,1536]{2,1,0:T(8,128)(2,1)S(1)}, u32[]{:S(2)}, u32[]{:S(2)}) async-start(bf16[4,16,1536]{2,1,0:T(8,128)(2,1)} %broadcast_in_dim.14), calls=%async_computation.1 | async-start | bytes 393216 | tf_op jit(solution)/shard_map/gather_texts/all_to_all | solution.py:26
  43.4 2.6 %collective-permute-start.2 = (bf16[16,1536]{1,0:T(8,128)(2,1)S(1)}, bf16[16,1536]{1,0:T(8,128)(2,1)S(1)}, u32[]{:S(2)}, u32[]{:S(2)}) collective-permute-start(bf16[16,1536]{1,0:T(8,128)(2,1)S(1)} %get-tuple-element.31), channel_id=1, source_target_pairs={{0,16},{16,32},{32,48},{48,0},{1,17},{17,33},{33,49},{49,1},{2,18}... | collective-permute-start | bytes 147464 | tf_op jit(solution)/shard_map/gather_images/ppermute | solution.py:40
  46.0 3.1 %collective-permute-start.1 = (bf16[16,1536]{1,0:T(8,128)(2,1)S(1)}, bf16[16,1536]{1,0:T(8,128)(2,1)S(1)}, u32[]{:S(2)}, u32[]{:S(2)}) collective-permute-start(bf16[16,1536]{1,0:T(8,128)(2,1)S(1)} %get-tuple-element.31), channel_id=1, source_target_pairs={{0,32},{16,48},{32,0},{48,16},{1,33},{17,49},{33,1},{49,17},{2,34}... | collective-permute-start | bytes 147464 | tf_op jit(solution)/shard_map/gather_images/ppermute | solution.py:40
  49.2 3.5 %collective-permute-start = (bf16[16,1536]{1,0:T(8,128)(2,1)S(1)}, bf16[16,1536]{1,0:T(8,128)(2,1)S(1)}, u32[]{:S(2)}, u32[]{:S(2)}) collective-permute-start(bf16[16,1536]{1,0:T(8,128)(2,1)S(1)} %get-tuple-element.31), channel_id=1, source_target_pairs={{0,48},{16,0},{32,16},{48,32},{1,49},{17,1},{33,17},{49,33},{2,50}... | collective-permute-start | bytes 147464 | tf_op jit(solution)/shard_map/gather_images/ppermute | solution.py:40
  52.8 1.4 all-to-all-done.1
  54.1 0.9 broadcast_in_dim.16
  55.1 3.5 %all-to-all-start.2 = ((bf16[4,64,1536]{2,1,0:T(8,128)(2,1)}), bf16[4,64,1536]{2,1,0:T(8,128)(2,1)S(1)}, u32[]{:S(2)}, u32[]{:S(2)}) async-start(bf16[4,64,1536]{2,1,0:T(8,128)(2,1)} %broadcast_in_dim.16), calls=%async_computation.2 | async-start | bytes 1572864 | tf_op jit(solution)/shard_map/gather_texts/all_to_all | solution.py:26
  58.6 1.9 collective-permute-start.5
  60.6 3.7 %collective-permute-start.4 = (bf16[64,1536]{1,0:T(8,128)(2,1)S(1)}, bf16[64,1536]{1,0:T(8,128)(2,1)S(1)}, u32[]{:S(2)}, u32[]{:S(2)}) collective-permute-start(bf16[64,1536]{1,0:T(8,128)(2,1)S(1)} %pad_maximum_fusion.1), channel_id=1, source_target_pairs={{0,4},{2,6},{4,0},{6,2},{1,5},{3,7},{5,1},{7,3},{8,12},{10,14},{12... | collective-permute-start | bytes 589832 | tf_op jit(solution)/shard_map/gather_images/ppermute | solution.py:40
  64.2 2.8 %collective-permute-start.3 = (bf16[64,1536]{1,0:T(8,128)(2,1)S(1)}, bf16[64,1536]{1,0:T(8,128)(2,1)S(1)}, u32[]{:S(2)}, u32[]{:S(2)}) collective-permute-start(bf16[64,1536]{1,0:T(8,128)(2,1)S(1)} %pad_maximum_fusion.1), channel_id=1, source_target_pairs={{0,6},{2,0},{4,2},{6,4},{1,7},{3,1},{5,3},{7,5},{8,14},{10,8},{12,... | collective-permute-start | bytes 589832 | tf_op jit(solution)/shard_map/gather_images/ppermute | solution.py:40
  67.1 9.0 %collective-permute-start.6 = (bf16[256,1536]{1,0:T(8,128)(2,1)S(1)}, bf16[256,1536]{1,0:T(8,128)(2,1)S(1)}, u32[]{:S(2)}, u32[]{:S(2)}) collective-permute-start(bf16[256,1536]{1,0:T(8,128)(2,1)S(1)} %bitcast.52), channel_id=1, source_target_pairs={{0,8},{8,0},{1,9},{9,1},{2,10},{10,2},{3,11},{11,3},{4,12},{12,4},... | collective-permute-start | bytes 2359304 | tf_op jit(solution)/shard_map/gather_texts/ppermute | solution.py:40
  76.2 1.8 collective-permute-done.6.texts.other_texts
  78.0 1.6 pairs.3
  79.6 2.5 %collective-permute-start.7 = (bf16[256,1536]{1,0:T(8,128)(2,1)S(1)}, bf16[256,1536]{1,0:T(8,128)(2,1)}, u32[]{:S(2)}, u32[]{:S(2)}) collective-permute-start(bf16[256,1536]{1,0:T(8,128)(2,1)S(1)} %get-tuple-element.16), channel_id=1, source_target_pairs={{0,8},{8,0},{1,9},{9,1},{2,10},{10,2},{3,11},{11,3},{4,12},{12,4},... | collective-permute-start | bytes 2359304 | tf_op jit(solution)/shard_map/sum_texts/ppermute | solution.py:40
  82.2 1.6 pairs.2
  83.8 0.3 collective-permute-done.7
  84.2 2.2 add_convert_fusion
  86.4 4.5 %all-to-all-start.3 = ((bf16[4,64,1536]{2,1,0:T(8,128)(2,1)}), bf16[4,64,1536]{2,1,0:T(8,128)(2,1)}, u32[]{:S(2)}, u32[]{:S(2)}) async-start(bf16[4,64,1536]{2,1,0:T(8,128)(2,1)} %bitcast.6), calls=%async_computation.3 | async-start | bytes 1572864 | tf_op jit(solution)/shard_map/sum_texts/all_to_all | solution.py:26
  90.9 1.2 sum_images.1
  92.1 3.4 %collective-permute-start.8 = (bf16[64,1536]{1,0:T(8,128)(2,1)S(1)}, bf16[64,1536]{1,0:T(8,128)(2,1)S(1)}, u32[]{:S(2)}, u32[]{:S(2)}) collective-permute-start(bf16[64,1536]{1,0:T(8,128)(2,1)S(1)} %get-tuple-element.20), channel_id=1, source_target_pairs={{0,2},{2,4},{4,6},{6,0},{1,3},{3,5},{5,7},{7,1},{8,10},{10,12},{12... | collective-permute-start | bytes 589832 | tf_op jit(solution)/shard_map/sum_images/ppermute | solution.py:40
  95.5 3.9 %collective-permute-start.9 = (bf16[64,1536]{1,0:T(8,128)(2,1)S(1)}, bf16[64,1536]{1,0:T(8,128)(2,1)S(1)}, u32[]{:S(2)}, u32[]{:S(2)}) collective-permute-start(bf16[64,1536]{1,0:T(8,128)(2,1)S(1)} %get-tuple-element.21), channel_id=1, source_target_pairs={{0,4},{2,6},{4,0},{6,2},{1,5},{3,7},{5,1},{7,3},{8,12},{10,14},{12... | collective-permute-start | bytes 589832 | tf_op jit(solution)/shard_map/sum_images/ppermute | solution.py:40
  99.5 2.5 %collective-permute-start.10 = (bf16[64,1536]{1,0:T(8,128)(2,1)S(1)}, bf16[64,1536]{1,0:T(8,128)(2,1)S(1)}, u32[]{:S(2)}, u32[]{:S(2)}) collective-permute-start(bf16[64,1536]{1,0:T(8,128)(2,1)S(1)} %get-tuple-element.22), channel_id=1, source_target_pairs={{0,6},{2,0},{4,2},{6,4},{1,7},{3,1},{5,3},{7,5},{8,14},{10,8},{12,... | collective-permute-start | bytes 589832 | tf_op jit(solution)/shard_map/sum_images/ppermute | solution.py:40
  102.0 0.7 all-to-all-done.3
  102.7 2.0 reduce_sum.97
  104.7 7.2 %all-to-all-start.4 = ((bf16[4,16,1536]{2,1,0:T(8,128)(2,1)}), bf16[4,16,1536]{2,1,0:T(8,128)(2,1)S(1)}, u32[]{:S(2)}, u32[]{:S(2)}) async-start(bf16[4,16,1536]{2,1,0:T(8,128)(2,1)} %bitcast.8), calls=%async_computation.4 | async-start | bytes 393216 | tf_op jit(solution)/shard_map/sum_texts/all_to_all | solution.py:26
  112.0 1.9 collective-permute-start.11
  113.9 5.2 %collective-permute-start.13 = (bf16[16,1536]{1,0:T(8,128)(2,1)S(1)}, bf16[16,1536]{1,0:T(8,128)(2,1)S(1)}, u32[]{:S(2)}, u32[]{:S(2)}) collective-permute-start(bf16[16,1536]{1,0:T(8,128)(2,1)S(1)} %get-tuple-element.39), channel_id=1, source_target_pairs={{0,48},{16,0},{32,16},{48,32},{1,49},{17,1},{33,17},{49,33},{2,50}... | collective-permute-start | bytes 147464 | tf_op jit(solution)/shard_map/sum_images/ppermute | solution.py:40
  119.1 1.9 collective-permute-start.12
  121.0 4.3 %all-to-all-done.4 = bf16[4,16,1536]{2,1,0:T(8,128)(2,1)S(1)} async-done(((bf16[4,16,1536]{2,1,0:T(8,128)(2,1)}), bf16[4,16,1536]{2,1,0:T(8,128)(2,1)S(1)}, u32[]{:S(2)}, u32[]{:S(2)}) %all-to-all-start.4) | async-done | bytes 196640 | tf_op jit(solution)/shard_map/sum_texts/all_to_all | solution.py:26
  125.3 0.6 collective-permute-done.12
  126.0 0.2 multiply_reduce_fusion.1
  126.2 0.1 fusion.7
  126.3 1.0 broadcast_in_dim.17
  127.3 4.4 %all-to-all-start.5 = ((bf16[8,2,16,1536]{3,2,1,0:T(8,128)(2,1)}), bf16[8,2,16,1536]{3,2,1,0:T(8,128)(2,1)S(1)}, u32[]{:S(2)}, u32[]{:S(2)}) async-start(bf16[8,2,16,1536]{3,2,1,0:T(8,128)(2,1)} %broadcast_in_dim.17), calls=%async_computation.5 | async-start | bytes 1572864 | tf_op jit(solution)/shard_map/head_grads/all_to_all | solution.py:26
  131.7 10.5 %all-to-all-done.5 = bf16[8,2,16,1536]{3,2,1,0:T(8,128)(2,1)S(1)} async-done(((bf16[8,2,16,1536]{3,2,1,0:T(8,128)(2,1)}), bf16[8,2,16,1536]{3,2,1,0:T(8,128)(2,1)S(1)}, u32[]{:S(2)}, u32[]{:S(2)}) %all-to-all-start.5) | async-done | bytes 786464 | tf_op jit(solution)/shard_map/head_grads/all_to_all | solution.py:26
  142.3 0.2 fusion
  142.5 0.2 fusion.1
  142.8 8.2 %collective-permute-start.14 = (bf16[2,96,1536]{2,1,0:T(8,128)(2,1)S(1)}, bf16[2,96,1536]{2,1,0:T(8,128)(2,1)S(1)}, u32[]{:S(2)}, u32[]{:S(2)}) collective-permute-start(bf16[2,96,1536]{2,1,0:T(8,128)(2,1)S(1)} %pad_maximum_fusion), channel_id=1, source_target_pairs={{0,8},{8,0},{1,9},{9,1},{2,10},{10,2},{3,11},{11,3},{4,12},{12,4},... | collective-permute-start | bytes 1769480 | tf_op jit(solution)/shard_map/weight_grads/ppermute | solution.py:40
  151.0 0.2 convolution_bitcast_fusion.1
  151.2 0.2 convolution_bitcast_fusion
  151.5 1.2 collective-permute-done.14
  152.7 11.4 %all_to_all.51 = bf16[4,48,1536]{2,1,0:T(8,128)(2,1)S(1)} all-to-all(bf16[4,48,1536]{2,1,0:T(8,128)(2,1)S(1)} %bitcast.65), channel_id=1, replica_groups=mesh['xl'=2,'zh'=4,'zm'=2,'z0'=2,'c'=2,'y'=4,'xh'=2] {'xl','z0'}, dimensions={0} | all-to-all | bytes 1179648 | tf_op jit(solution)/shard_map/weight_grads/all_to_all | solution.py:26
  164.3 22.1 %all_to_all.52 = bf16[8,24,384]{2,1,0:T(8,128)(2,1)S(1)} all-to-all(bf16[8,24,384]{2,1,0:T(8,128)(2,1)S(1)} %bitcast.70), channel_id=1, replica_groups=mesh['xl'=2,'zh'=4,'zm'=2,'z0'=2,'c'=2,'y'=4,'xh'=2] {'zh','zm'}, dimensions={0} | all-to-all | bytes 294912 | tf_op jit(solution)/shard_map/weight_grads/all_to_all | solution.py:26
  186.5 18.0 %all_to_all.53 = bf16[8,24,384]{2,1,0:T(8,128)(2,1)S(1)} all-to-all(bf16[8,24,384]{2,1,0:T(8,128)(2,1)S(1)} %broadcast_in_dim.18), channel_id=1, replica_groups=mesh['xl'=2,'zh'=4,'zm'=2,'z0'=2,'c'=2,'y'=4,'xh'=2] {'zh','zm'}, dimensions={0} | all-to-all | bytes 294912 | tf_op jit(solution)/shard_map/weight_grads/all_to_all | solution.py:26
  204.6 0.9 broadcast_in_dim.20
  205.4 3.7 %all-to-all-start.9 = ((bf16[4,48,1536]{2,1,0:T(8,128)(2,1)}), bf16[4,48,1536]{2,1,0:T(8,128)(2,1)S(1)}, u32[]{:S(2)}, u32[]{:S(2)}) async-start(bf16[4,48,1536]{2,1,0:T(8,128)(2,1)} %broadcast_in_dim.20), calls=%async_computation.9 | async-start | bytes 1179648 | tf_op jit(solution)/shard_map/weight_grads/all_to_all | solution.py:26
  209.2 1.0 fusion.24
  210.1 1.0 fusion.25
  211.1 5.0 %all-to-all-done.9 = bf16[4,48,1536]{2,1,0:T(8,128)(2,1)S(1)} async-done(((bf16[4,48,1536]{2,1,0:T(8,128)(2,1)}), bf16[4,48,1536]{2,1,0:T(8,128)(2,1)S(1)}, u32[]{:S(2)}, u32[]{:S(2)}) %all-to-all-start.9) | async-done | bytes 589856 | tf_op jit(solution)/shard_map/weight_grads/all_to_all | solution.py:26
  216.1 5.4 %collective-permute-start.15 = (bf16[2,96,1536]{2,1,0:T(8,128)(2,1)S(1)}, bf16[2,96,1536]{2,1,0:T(8,128)(2,1)S(1)}, u32[]{:S(2)}, u32[]{:S(2)}) collective-permute-start(bf16[2,96,1536]{2,1,0:T(8,128)(2,1)S(1)} %bitcast.64), channel_id=1, source_target_pairs={{0,8},{8,0},{1,9},{9,1},{2,10},{10,2},{3,11},{11,3},{4,12},{12,4},... | collective-permute-start | bytes 1769480 | tf_op jit(solution)/shard_map/weight_grads/ppermute | solution.py:40
  221.5 0.1 maximum_convert_fusion
  221.6 0.1 maximum_convert_fusion.1
  221.7 1.3 collective-permute-done.15
  223.1 0.1 convert_dynamic-update-slice_fusion
  223.2 1.0 copy-done.8
  224.2 0.4 copy-done.9
  (55 shorter events, 1.3 us)
Async XLA Ops:
  0.6 1.1 copy-start
  1.7 1.1 copy-start.2
  2.8 0.8 copy-start.4
  3.6 0.8 copy-start.6
  25.2 29.0 %all-to-all-start.1 = ((bf16[4,16,1536]{2,1,0:T(8,128)(2,1)}), bf16[4,16,1536]{2,1,0:T(8,128)(2,1)S(1)}, u32[]{:S(2)}, u32[]{:S(2)}) async-start(bf16[4,16,1536]{2,1,0:T(8,128)(2,1)} %broadcast_in_dim.14), calls=%async_computation.1 | async-start | bytes 393216 | tf_op jit(solution)/shard_map/gather_texts/all_to_all | solution.py:26
  43.4 15.2 %collective-permute-start.2 = (bf16[16,1536]{1,0:T(8,128)(2,1)S(1)}, bf16[16,1536]{1,0:T(8,128)(2,1)S(1)}, u32[]{:S(2)}, u32[]{:S(2)}) collective-permute-start(bf16[16,1536]{1,0:T(8,128)(2,1)S(1)} %get-tuple-element.31), channel_id=1, source_target_pairs={{0,16},{16,32},{32,48},{48,0},{1,17},{17,33},{33,49},{49,1},{2,18}... | collective-permute-start | bytes 147464 | tf_op jit(solution)/shard_map/gather_images/ppermute | solution.py:40
  46.0 12.6 %collective-permute-start.1 = (bf16[16,1536]{1,0:T(8,128)(2,1)S(1)}, bf16[16,1536]{1,0:T(8,128)(2,1)S(1)}, u32[]{:S(2)}, u32[]{:S(2)}) collective-permute-start(bf16[16,1536]{1,0:T(8,128)(2,1)S(1)} %get-tuple-element.31), channel_id=1, source_target_pairs={{0,32},{16,48},{32,0},{48,16},{1,33},{17,49},{33,1},{49,17},{2,34}... | collective-permute-start | bytes 147464 | tf_op jit(solution)/shard_map/gather_images/ppermute | solution.py:40
  49.2 9.4 %collective-permute-start = (bf16[16,1536]{1,0:T(8,128)(2,1)S(1)}, bf16[16,1536]{1,0:T(8,128)(2,1)S(1)}, u32[]{:S(2)}, u32[]{:S(2)}) collective-permute-start(bf16[16,1536]{1,0:T(8,128)(2,1)S(1)} %get-tuple-element.31), channel_id=1, source_target_pairs={{0,48},{16,0},{32,16},{48,32},{1,49},{17,1},{33,17},{49,33},{2,50}... | collective-permute-start | bytes 147464 | tf_op jit(solution)/shard_map/gather_images/ppermute | solution.py:40
  55.1 12.0 %all-to-all-start.2 = ((bf16[4,64,1536]{2,1,0:T(8,128)(2,1)}), bf16[4,64,1536]{2,1,0:T(8,128)(2,1)S(1)}, u32[]{:S(2)}, u32[]{:S(2)}) async-start(bf16[4,64,1536]{2,1,0:T(8,128)(2,1)} %broadcast_in_dim.16), calls=%async_computation.2 | async-start | bytes 1572864 | tf_op jit(solution)/shard_map/gather_texts/all_to_all | solution.py:26
  58.6 17.6 %collective-permute-start.5 = (bf16[64,1536]{1,0:T(8,128)(2,1)S(1)}, bf16[64,1536]{1,0:T(8,128)(2,1)S(1)}, u32[]{:S(2)}, u32[]{:S(2)}) collective-permute-start(bf16[64,1536]{1,0:T(8,128)(2,1)S(1)} %pad_maximum_fusion.1), channel_id=1, source_target_pairs={{0,2},{2,4},{4,6},{6,0},{1,3},{3,5},{5,7},{7,1},{8,10},{10,12},{12... | collective-permute-start | bytes 589832 | tf_op jit(solution)/shard_map/gather_images/ppermute | solution.py:40
  60.6 15.6 %collective-permute-start.4 = (bf16[64,1536]{1,0:T(8,128)(2,1)S(1)}, bf16[64,1536]{1,0:T(8,128)(2,1)S(1)}, u32[]{:S(2)}, u32[]{:S(2)}) collective-permute-start(bf16[64,1536]{1,0:T(8,128)(2,1)S(1)} %pad_maximum_fusion.1), channel_id=1, source_target_pairs={{0,4},{2,6},{4,0},{6,2},{1,5},{3,7},{5,1},{7,3},{8,12},{10,14},{12... | collective-permute-start | bytes 589832 | tf_op jit(solution)/shard_map/gather_images/ppermute | solution.py:40
  64.2 11.9 %collective-permute-start.3 = (bf16[64,1536]{1,0:T(8,128)(2,1)S(1)}, bf16[64,1536]{1,0:T(8,128)(2,1)S(1)}, u32[]{:S(2)}, u32[]{:S(2)}) collective-permute-start(bf16[64,1536]{1,0:T(8,128)(2,1)S(1)} %pad_maximum_fusion.1), channel_id=1, source_target_pairs={{0,6},{2,0},{4,2},{6,4},{1,7},{3,1},{5,3},{7,5},{8,14},{10,8},{12,... | collective-permute-start | bytes 589832 | tf_op jit(solution)/shard_map/gather_images/ppermute | solution.py:40
  67.1 10.9 %collective-permute-start.6 = (bf16[256,1536]{1,0:T(8,128)(2,1)S(1)}, bf16[256,1536]{1,0:T(8,128)(2,1)S(1)}, u32[]{:S(2)}, u32[]{:S(2)}) collective-permute-start(bf16[256,1536]{1,0:T(8,128)(2,1)S(1)} %bitcast.52), channel_id=1, source_target_pairs={{0,8},{8,0},{1,9},{9,1},{2,10},{10,2},{3,11},{11,3},{4,12},{12,4},... | collective-permute-start | bytes 2359304 | tf_op jit(solution)/shard_map/gather_texts/ppermute | solution.py:40
  79.6 4.6 %collective-permute-start.7 = (bf16[256,1536]{1,0:T(8,128)(2,1)S(1)}, bf16[256,1536]{1,0:T(8,128)(2,1)}, u32[]{:S(2)}, u32[]{:S(2)}) collective-permute-start(bf16[256,1536]{1,0:T(8,128)(2,1)S(1)} %get-tuple-element.16), channel_id=1, source_target_pairs={{0,8},{8,0},{1,9},{9,1},{2,10},{10,2},{3,11},{11,3},{4,12},{12,4},... | collective-permute-start | bytes 2359304 | tf_op jit(solution)/shard_map/sum_texts/ppermute | solution.py:40
  86.4 16.3 %all-to-all-start.3 = ((bf16[4,64,1536]{2,1,0:T(8,128)(2,1)}), bf16[4,64,1536]{2,1,0:T(8,128)(2,1)}, u32[]{:S(2)}, u32[]{:S(2)}) async-start(bf16[4,64,1536]{2,1,0:T(8,128)(2,1)} %bitcast.6), calls=%async_computation.3 | async-start | bytes 1572864 | tf_op jit(solution)/shard_map/sum_texts/all_to_all | solution.py:26
  92.1 19.8 %collective-permute-start.8 = (bf16[64,1536]{1,0:T(8,128)(2,1)S(1)}, bf16[64,1536]{1,0:T(8,128)(2,1)S(1)}, u32[]{:S(2)}, u32[]{:S(2)}) collective-permute-start(bf16[64,1536]{1,0:T(8,128)(2,1)S(1)} %get-tuple-element.20), channel_id=1, source_target_pairs={{0,2},{2,4},{4,6},{6,0},{1,3},{3,5},{5,7},{7,1},{8,10},{10,12},{12... | collective-permute-start | bytes 589832 | tf_op jit(solution)/shard_map/sum_images/ppermute | solution.py:40
  95.5 16.3 %collective-permute-start.9 = (bf16[64,1536]{1,0:T(8,128)(2,1)S(1)}, bf16[64,1536]{1,0:T(8,128)(2,1)S(1)}, u32[]{:S(2)}, u32[]{:S(2)}) collective-permute-start(bf16[64,1536]{1,0:T(8,128)(2,1)S(1)} %get-tuple-element.21), channel_id=1, source_target_pairs={{0,4},{2,6},{4,0},{6,2},{1,5},{3,7},{5,1},{7,3},{8,12},{10,14},{12... | collective-permute-start | bytes 589832 | tf_op jit(solution)/shard_map/sum_images/ppermute | solution.py:40
  99.5 12.4 %collective-permute-start.10 = (bf16[64,1536]{1,0:T(8,128)(2,1)S(1)}, bf16[64,1536]{1,0:T(8,128)(2,1)S(1)}, u32[]{:S(2)}, u32[]{:S(2)}) collective-permute-start(bf16[64,1536]{1,0:T(8,128)(2,1)S(1)} %get-tuple-element.22), channel_id=1, source_target_pairs={{0,6},{2,0},{4,2},{6,4},{1,7},{3,1},{5,3},{7,5},{8,14},{10,8},{12,... | collective-permute-start | bytes 589832 | tf_op jit(solution)/shard_map/sum_images/ppermute | solution.py:40
  104.7 20.6 %all-to-all-start.4 = ((bf16[4,16,1536]{2,1,0:T(8,128)(2,1)}), bf16[4,16,1536]{2,1,0:T(8,128)(2,1)S(1)}, u32[]{:S(2)}, u32[]{:S(2)}) async-start(bf16[4,16,1536]{2,1,0:T(8,128)(2,1)} %bitcast.8), calls=%async_computation.4 | async-start | bytes 393216 | tf_op jit(solution)/shard_map/sum_texts/all_to_all | solution.py:26
  112.0 13.3 %collective-permute-start.11 = (bf16[16,1536]{1,0:T(8,128)(2,1)S(1)}, bf16[16,1536]{1,0:T(8,128)(2,1)S(1)}, u32[]{:S(2)}, u32[]{:S(2)}) collective-permute-start(bf16[16,1536]{1,0:T(8,128)(2,1)S(1)} %get-tuple-element.38), channel_id=1, source_target_pairs={{0,16},{16,32},{32,48},{48,0},{1,17},{17,33},{33,49},{49,1},{2,18}... | collective-permute-start | bytes 147464 | tf_op jit(solution)/shard_map/sum_images/ppermute | solution.py:40
  113.9 11.4 %collective-permute-start.13 = (bf16[16,1536]{1,0:T(8,128)(2,1)S(1)}, bf16[16,1536]{1,0:T(8,128)(2,1)S(1)}, u32[]{:S(2)}, u32[]{:S(2)}) collective-permute-start(bf16[16,1536]{1,0:T(8,128)(2,1)S(1)} %get-tuple-element.39), channel_id=1, source_target_pairs={{0,48},{16,0},{32,16},{48,32},{1,49},{17,1},{33,17},{49,33},{2,50}... | collective-permute-start | bytes 147464 | tf_op jit(solution)/shard_map/sum_images/ppermute | solution.py:40
  119.1 6.9 %collective-permute-start.12 = (bf16[16,1536]{1,0:T(8,128)(2,1)S(1)}, bf16[16,1536]{1,0:T(8,128)(2,1)S(1)}, u32[]{:S(2)}, u32[]{:S(2)}) collective-permute-start(bf16[16,1536]{1,0:T(8,128)(2,1)S(1)} %get-tuple-element.40), channel_id=1, source_target_pairs={{0,32},{16,48},{32,0},{48,16},{1,33},{17,49},{33,1},{49,17},{2,34}... | collective-permute-start | bytes 147464 | tf_op jit(solution)/shard_map/sum_images/ppermute | solution.py:40
  127.3 14.9 %all-to-all-start.5 = ((bf16[8,2,16,1536]{3,2,1,0:T(8,128)(2,1)}), bf16[8,2,16,1536]{3,2,1,0:T(8,128)(2,1)S(1)}, u32[]{:S(2)}, u32[]{:S(2)}) async-start(bf16[8,2,16,1536]{3,2,1,0:T(8,128)(2,1)} %broadcast_in_dim.17), calls=%async_computation.5 | async-start | bytes 1572864 | tf_op jit(solution)/shard_map/head_grads/all_to_all | solution.py:26
  131.6 10.6 %copy-start.5 = (bf16[128,192]{0,1:T(8,128)(2,1)S(1)}, bf16[128,192]{0,1:T(8,128)(2,1)}, u32[]{:S(2)}) copy-start(bf16[128,192]{0,1:T(8,128)(2,1)} %param.7) | copy-start | bytes 147460
  131.7 10.8 %copy-start.7 = (bf16[128,192]{0,1:T(8,128)(2,1)S(1)}, bf16[128,192]{0,1:T(8,128)(2,1)}, u32[]{:S(2)}) copy-start(bf16[128,192]{0,1:T(8,128)(2,1)} %param.8) | copy-start | bytes 147460
  142.8 9.8 %collective-permute-start.14 = (bf16[2,96,1536]{2,1,0:T(8,128)(2,1)S(1)}, bf16[2,96,1536]{2,1,0:T(8,128)(2,1)S(1)}, u32[]{:S(2)}, u32[]{:S(2)}) collective-permute-start(bf16[2,96,1536]{2,1,0:T(8,128)(2,1)S(1)} %pad_maximum_fusion), channel_id=1, source_target_pairs={{0,8},{8,0},{1,9},{9,1},{2,10},{10,2},{3,11},{11,3},{4,12},{12,4},... | collective-permute-start | bytes 1769480 | tf_op jit(solution)/shard_map/weight_grads/ppermute | solution.py:40
  204.5 4.6 %copy-start.1 = (bf16[192,1536]{1,0:T(8,128)(2,1)S(1)}, bf16[192,1536]{1,0:T(8,128)(2,1)}, u32[]{:S(2)}) copy-start(bf16[192,1536]{1,0:T(8,128)(2,1)} %image_weight.1) | copy-start | bytes 1769476
  205.4 4.7 %copy-start.3 = (bf16[192,1536]{1,0:T(8,128)(2,1)S(1)}, bf16[192,1536]{1,0:T(8,128)(2,1)}, u32[]{:S(2)}) copy-start(bf16[192,1536]{1,0:T(8,128)(2,1)} %text_weight.1) | copy-start | bytes 1769476
  205.4 10.6 %all-to-all-start.9 = ((bf16[4,48,1536]{2,1,0:T(8,128)(2,1)}), bf16[4,48,1536]{2,1,0:T(8,128)(2,1)S(1)}, u32[]{:S(2)}, u32[]{:S(2)}) async-start(bf16[4,48,1536]{2,1,0:T(8,128)(2,1)} %broadcast_in_dim.20), calls=%async_computation.9 | async-start | bytes 1179648 | tf_op jit(solution)/shard_map/weight_grads/all_to_all | solution.py:26
  216.1 7.0 %collective-permute-start.15 = (bf16[2,96,1536]{2,1,0:T(8,128)(2,1)S(1)}, bf16[2,96,1536]{2,1,0:T(8,128)(2,1)S(1)}, u32[]{:S(2)}, u32[]{:S(2)}) collective-permute-start(bf16[2,96,1536]{2,1,0:T(8,128)(2,1)S(1)} %bitcast.64), channel_id=1, source_target_pairs={{0,8},{8,0},{1,9},{9,1},{2,10},{10,2},{3,11},{11,3},{4,12},{12,4},... | collective-permute-start | bytes 1769480 | tf_op jit(solution)/shard_map/weight_grads/ppermute | solution.py:40
  223.2 1.0 copy-start.8
  223.2 1.4 copy-start.9

commit v7 on v6

--- a/solution.py
+++ b/solution.py
@@ -10,6 +10,7 @@
 
 PARTS = {"xl": 2, "zh": 4, "zm": 2, "z0": 2, "c": 2, "y": 4, "xh": 2}
 DP = ("xl", "zh", "zm", "z0", "c")
+Z = ("zh", "zm", "z0")
 ZL = ("zm", "z0")
 MP = ("y", "xh")
 
@@ -63,17 +64,18 @@
 
 
 VMEM = pl.BlockSpec(memory_space=pltpu.VMEM)
-SMEM = pl.BlockSpec(memory_space=pltpu.SMEM)
-
-
-def local_kernel(body, operands, outs, flops, in_specs=None):
+HBM = pl.BlockSpec(memory_space=pltpu.HBM)
+
+
+def local_kernel(body, operands, outs, flops, in_space=VMEM, scratch=(), room=12):
     moved = sum(x.size * x.dtype.itemsize for x in tuple(operands) + tuple(outs))
     return pl.pallas_call(
         body,
         out_shape=outs,
-        in_specs=in_specs or [VMEM] * len(operands),
+        in_specs=[in_space] * len(operands),
         out_specs=[VMEM] * len(outs),
-        compiler_params=pltpu.CompilerParams(vmem_limit_bytes=24 * 2**20),
+        scratch_shapes=scratch,
+        compiler_params=pltpu.CompilerParams(vmem_limit_bytes=room * 2**20),
         cost_estimate=pl.CostEstimate(flops=flops, bytes_accessed=moved, transcendentals=0),
     )(*operands)
 
@@ -83,46 +85,38 @@
     return lax.dot_general(left, right, dims, preferred_element_type=F32)
 
 
-def project_body(image_features, text_features, image_weight, text_weight, heads):
-    width = image_weight.shape[1]
-    heads[:, :width] = contract(image_features[...], image_weight[...], 0, 0).astype(BF16)
-    heads[:, width:] = contract(text_features[...], text_weight[...], 0, 0).astype(BF16)
+def project_body(*refs):
+    sources, (heads, *held, done) = refs[:4], refs[4:]
+    copies = [
+        pltpu.make_async_copy(source, kept, done.at[i])
+        for i, (source, kept) in enumerate(zip(sources, held))
+    ]
+    for copy in copies:
+        copy.start()
+    width = heads.shape[1] // 2
+    for i in range(2):
+        copies[2 * i].wait()
+        copies[2 * i + 1].wait()
+        features, weight = held[2 * i], held[2 * i + 1]
+        heads[:, i * width : (i + 1) * width] = contract(
+            features[...], weight[...], 0, 0
+        ).astype(BF16)
 
 
 def project(image_features, text_features, image_weight, text_weight):
     rows, depth = image_features.shape
     width = image_weight.shape[1]
+    operands = (image_features.T, image_weight, text_features.T, text_weight)
     (heads,) = local_kernel(
         project_body,
-        (image_features.T, text_features.T, image_weight, text_weight),
+        operands,
         [jax.ShapeDtypeStruct((rows, 2 * width), BF16)],
         4 * rows * depth * width,
+        HBM,
+        [pltpu.VMEM(x.shape, x.dtype) for x in operands] + [pltpu.SemaphoreType.DMA((4,))],
+        60,
     )
     return heads
-
-
-def pairs_body(numbers, places, texts, images, coeff, part):
-    scores = numbers[0] * contract(texts[...], images[...], 1, 1) + numbers[1]
-    text_at = lax.broadcasted_iota(jnp.int32, scores.shape, 0) - places[0]
-    image_at = lax.broadcasted_iota(jnp.int32, scores.shape, 1)
-    positive = (text_at == image_at) & (image_at < places[1])
-    value = numbers[2] * (jax.nn.sigmoid(scores) - positive.astype(F32))
-    coeff[...] = value.astype(BF16)
-    part[...] = contract(coeff[...], images[...], 1, 0).astype(part.dtype)
-
-
-def pair_block(numbers, places, texts, images, dtype):
-    rows, width = texts.shape
-    return local_kernel(
-        pairs_body,
-        (numbers, places, texts, images),
-        [
-            jax.ShapeDtypeStruct((rows, images.shape[0]), BF16),
-            jax.ShapeDtypeStruct((rows, width), dtype),
-        ],
-        4 * rows * images.shape[0] * width,
-        [SMEM, SMEM, VMEM, VMEM],
-    )
 
 
 def images_body(coeff, texts, other_coeff, other_texts, own, *sent):
@@ -187,16 +181,24 @@
     with jax.named_scope("gather_images"):
         images = ring_gather(ring_gather(image_unit.astype(BF16), ZL), "y")
 
+    def coefficients(block, positive):
+        scores = (
+            scale * jnp.einsum("te,ie->ti", block, images, preferred_element_type=F32) + shift_bias
+        )
+        return (factor * (jax.nn.sigmoid(scores) - positive)).astype(BF16)
+
     with jax.named_scope("pairs"):
-        numbers = jnp.stack((scale, shift_bias, factor))
         text_base = ((at["xh"] * 2 + at["xl"]) * 4 + at["zh"]) * share
-        places = jnp.stack((text_base, jnp.int32(share)))
-        nowhere = jnp.zeros_like(places)
-        other_coeff, other_part = pair_block(numbers, nowhere, other_texts, images, BF16)
-        coeff, text_part = pair_block(numbers, places, texts, images, F32)
+        text_at = jnp.arange(texts.shape[0], dtype=jnp.int32)[:, None] - text_base
+        image_at = jnp.arange(images.shape[0], dtype=jnp.int32)[None, :]
+        positive = (text_at == image_at) & (image_at < share)
+        coeff = coefficients(texts, positive.astype(F32))
+        other_coeff = coefficients(other_texts, 0.0)
+        other_part = jnp.dot(other_coeff, images, preferred_element_type=F32)
+        text_part = jnp.dot(coeff, images, preferred_element_type=F32)
 
     with jax.named_scope("sum_texts"):
-        text_part = text_part + shifted(other_part, "c", 1).astype(F32)
+        text_part = text_part + shifted(other_part.astype(BF16), "c", 1).astype(F32)
         text_part = split_rows(text_part, count(("xh", "xl"))).astype(BF16)
         text_part, other_coeff = lax.optimization_barrier((text_part, other_coeff))
         text_part = scatter_sum(text_part, ("xh", "xl"))
@@ -243,12 +245,11 @@
         other = shifted(half_part(1 - at["c"]).astype(BF16), "c", 1)
         part = half_part(at["c"]) + other.astype(F32)
         quarter = embed_width // 4
-        part = scatter_sum(part.reshape(4, half // 2, embed_width), ("xl", "z0"))
-        part = part.reshape(2, half // 4, 4, quarter).transpose(2, 0, 1, 3)
-        part = scatter_sum(part.reshape(8, half // 4, quarter), ("zh", "zm"))
-        part = gather(part.astype(BF16), ("zh", "zm")).reshape(4, 2, half // 4, quarter)
-        part = part.transpose(1, 2, 0, 3).reshape(half // 2, embed_width)
-        part = gather(part, ("xl", "z0")).reshape(2, half, embed_width)
+        part = part.reshape(2, 4, half // 4, 4, quarter).transpose(0, 3, 1, 2, 4)
+        part = scatter_sum(part.reshape(32, half // 4, quarter), ("xl",) + Z)
+        part = gather(part.astype(BF16), ("xl",) + Z)
+        part = part.reshape(2, 4, 4, half // 4, quarter).transpose(0, 2, 3, 1, 4)
+        part = lax.optimization_barrier(part.reshape(2, half, embed_width))
         other = shifted(part, "c", 1)
 
         def halves(mine, theirs):

time: 226 us -> 244 us (1.080)
  waiting for transfers between devices: 27.1 us -> 54.9 us
  blocking collectives: 70.9 us -> 61.6 us
  matrix products: 2.8 us -> 7.29 us
  local copies, waits for them, and re-layouts: 8.9 us -> 5.77 us
    all_to_all x6, waiting for transfers between devices: 21.9 us -> 48.3 us  [exchange(): return lax.all_to_all(blocks, axes, split_axis=0, concat_axis=0, tiled=True)]
    all_to_all x4 -> x2, blocking collectives: 70.9 us -> 61.6 us  [exchange(): return lax.all_to_all(blocks, axes, split_axis=0, concat_axis=0, tiled=True)]
    dot_general x0 -> x4, matrix products: none -> 4.49 us  [the longest x1 2.38 us: on_device(): text_part = jnp.dot(coeff, images, preferred_element_type=F32)]
    unnamed x26 -> x17, local copies, waits for them, and re-layouts: 5.2 us -> 1.45 us
where the time goes in v7:
time: 244 us; the launch traced here: 242 us
  starting transfers between devices  102 us (42%)
  blocking collectives  61.6 us (25%)
  waiting for transfers between devices  54.9 us (22%)
  matrix products  7.29 us (3%)
  local copies, waits for them, and re-layouts  5.77 us (2%)
  Pallas kernels  3.82 us (2%)
  other arithmetic  3.49 us (1%)
  between operations  3.13 us (1%)
    all_to_all x2, blocking collectives, exchange(): return lax.all_to_all(blocks, axes, split_axis=0, concat_axis=0, tiled=True)  61.6 us
    ppermute x16, starting transfers between devices, shifted(): return lax.ppermute(value, axis, [(i, (i + by) % n) for i in range(n)])  60.9 us
    all_to_all x6, waiting for transfers between devices, exchange(): return lax.all_to_all(blocks, axes, split_axis=0, concat_axis=0, tiled=True)  48.3 us
    all_to_all x6, starting transfers between devices, exchange(): return lax.all_to_all(blocks, axes, split_axis=0, concat_axis=0, tiled=True)  41.1 us
    ppermute x16, waiting for transfers between devices, shifted(): return lax.ppermute(value, axis, [(i, (i + by) % n) for i in range(n)])  6.62 us
  transfers between devices with their start and end apart: 22, of which 10 were waited for; matrix products, arithmetic and copies ran while one was open for 3% of the time, Pallas kernels for 1%

profile of v7, /device:TPU:1, one launch (start us, length us, event | category | flops | bytes accessed | tf_op | source)
XLA Modules:
  0.0 242.0 jit_solution(11552673495933321378)
XLA Ops:
  0.6 2.6 %heads.1 = bf16[128,3072]{1,0:T(8,128)(2,1)} custom-call(bf16[192,128]{1,0:T(8,128)(2,1)} %bitcast.79, bf16[192,1536]{1,0:T(8,128)(2,1)} %refs_1_.1, bf16[192,128]{1,0:T(8,128)(2,1)} %bitcast.80, bf16[192,1536]{1,0:T(8,128)(2,1)} %refs_3_.1), custom_call_target="tpu_custom_call" | custom-call | flops 150994944 | bytes 2064384 | tf_op jit(solution)/shard_map/heads/pallas_call | solution.py:72
  3.2 19.1 %all_to_all.40 = bf16[8,16,3072]{2,1,0:T(8,128)(2,1)S(1)} all-to-all(bf16[8,16,3072]{2,1,0:T(8,128)(2,1)} %bitcast.75), channel_id=1, replica_groups=mesh['xl'=2,'zh'=4,'zm'=2,'z0'=2,'c'=2,'y'=4,'xh'=2] {'y','xh'}, dimensions={0} | all-to-all | bytes 1572864 | tf_op jit(solution)/shard_map/heads/all_to_all | solution.py:27
  22.3 0.1 reduce_sum.81
  22.4 0.1 fusion.21
  22.6 0.7 broadcast_in_dim.10
  23.3 16.7 %all-to-all-start.1 = ((bf16[4,16,1536]{2,1,0:T(8,128)(2,1)}), bf16[4,16,1536]{2,1,0:T(8,128)(2,1)S(1)}, u32[]{:S(2)}, u32[]{:S(2)}) async-start(bf16[4,16,1536]{2,1,0:T(8,128)(2,1)} %broadcast_in_dim.10), calls=%async_computation.1 | async-start | bytes 393216 | tf_op jit(solution)/shard_map/gather_texts/all_to_all | solution.py:27
  40.1 2.6 %collective-permute-start.2 = (bf16[16,1536]{1,0:T(8,128)(2,1)S(1)}, bf16[16,1536]{1,0:T(8,128)(2,1)S(1)}, u32[]{:S(2)}, u32[]{:S(2)}) collective-permute-start(bf16[16,1536]{1,0:T(8,128)(2,1)S(1)} %get-tuple-element.23), channel_id=1, source_target_pairs={{0,16},{16,32},{32,48},{48,0},{1,17},{17,33},{33,49},{49,1},{2,18}... | collective-permute-start | bytes 147464 | tf_op jit(solution)/shard_map/gather_images/ppermute | solution.py:41
  42.8 3.1 %collective-permute-start.1 = (bf16[16,1536]{1,0:T(8,128)(2,1)S(1)}, bf16[16,1536]{1,0:T(8,128)(2,1)S(1)}, u32[]{:S(2)}, u32[]{:S(2)}) collective-permute-start(bf16[16,1536]{1,0:T(8,128)(2,1)S(1)} %get-tuple-element.23), channel_id=1, source_target_pairs={{0,32},{16,48},{32,0},{48,16},{1,33},{17,49},{33,1},{49,17},{2,34}... | collective-permute-start | bytes 147464 | tf_op jit(solution)/shard_map/gather_images/ppermute | solution.py:41
  45.9 3.5 %collective-permute-start = (bf16[16,1536]{1,0:T(8,128)(2,1)S(1)}, bf16[16,1536]{1,0:T(8,128)(2,1)S(1)}, u32[]{:S(2)}, u32[]{:S(2)}) collective-permute-start(bf16[16,1536]{1,0:T(8,128)(2,1)S(1)} %get-tuple-element.23), channel_id=1, source_target_pairs={{0,48},{16,0},{32,16},{48,32},{1,49},{17,1},{33,17},{49,33},{2,50}... | collective-permute-start | bytes 147464 | tf_op jit(solution)/shard_map/gather_images/ppermute | solution.py:41
  51.4 1.5 all-to-all-done.1
  52.9 0.9 broadcast_in_dim.12
  53.8 3.5 %all-to-all-start.2 = ((bf16[4,64,1536]{2,1,0:T(8,128)(2,1)}), bf16[4,64,1536]{2,1,0:T(8,128)(2,1)S(1)}, u32[]{:S(2)}, u32[]{:S(2)}) async-start(bf16[4,64,1536]{2,1,0:T(8,128)(2,1)} %broadcast_in_dim.12), calls=%async_computation.2 | async-start | bytes 1572864 | tf_op jit(solution)/shard_map/gather_texts/all_to_all | solution.py:27
  57.4 1.9 collective-permute-start.5
  59.3 3.7 %collective-permute-start.4 = (bf16[64,1536]{1,0:T(8,128)(2,1)S(1)}, bf16[64,1536]{1,0:T(8,128)(2,1)S(1)}, u32[]{:S(2)}, u32[]{:S(2)}) collective-permute-start(bf16[64,1536]{1,0:T(8,128)(2,1)S(1)} %pad_maximum_fusion.1), channel_id=1, source_target_pairs={{0,4},{2,6},{4,0},{6,2},{1,5},{3,7},{5,1},{7,3},{8,12},{10,14},{12... | collective-permute-start | bytes 589832 | tf_op jit(solution)/shard_map/gather_images/ppermute | solution.py:41
  63.0 2.8 %collective-permute-start.3 = (bf16[64,1536]{1,0:T(8,128)(2,1)S(1)}, bf16[64,1536]{1,0:T(8,128)(2,1)S(1)}, u32[]{:S(2)}, u32[]{:S(2)}) collective-permute-start(bf16[64,1536]{1,0:T(8,128)(2,1)S(1)} %pad_maximum_fusion.1), channel_id=1, source_target_pairs={{0,6},{2,0},{4,2},{6,4},{1,7},{3,1},{5,3},{7,5},{8,14},{10,8},{12,... | collective-permute-start | bytes 589832 | tf_op jit(solution)/shard_map/gather_images/ppermute | solution.py:41
  65.9 10.2 %collective-permute-start.6 = (bf16[256,1536]{1,0:T(8,128)(2,1)S(1)}, bf16[256,1536]{1,0:T(8,128)(2,1)S(1)}, u32[]{:S(2)}, u32[]{:S(2)}) collective-permute-start(bf16[256,1536]{1,0:T(8,128)(2,1)S(1)} %bitcast.66), channel_id=1, source_target_pairs={{0,8},{8,0},{1,9},{9,1},{2,10},{10,2},{3,11},{11,3},{4,12},{12,4},... | collective-permute-start | bytes 2359304 | tf_op jit(solution)/shard_map/gather_texts/ppermute | solution.py:41
  76.1 1.8 collective-permute-done.6.other_texts
  77.9 0.4 fusion.17.other_coeff
  78.3 1.3 convolution_convert_fusion
  79.6 2.5 %collective-permute-start.7 = (bf16[256,1536]{1,0:T(8,128)(2,1)}, bf16[256,1536]{1,0:T(8,128)(2,1)}, u32[]{:S(2)}, u32[]{:S(2)}) collective-permute-start(bf16[256,1536]{1,0:T(8,128)(2,1)} %convolution_convert_fusion), channel_id=1, source_target_pairs={{0,8},{8,0},{1,9},{9,1},{2,10},{10,2},{3,11},{11,3},{4,12},{12,4},... | collective-permute-start | bytes 2359304 | tf_op jit(solution)/shard_map/sum_texts/ppermute | solution.py:41
  82.2 0.4 fusion.18.coeff
  82.6 1.8 collective-permute-done.7
  84.4 2.4 fusion
  86.7 4.5 %all-to-all-start.3 = ((bf16[4,64,1536]{2,1,0:T(8,128)(2,1)}), bf16[4,64,1536]{2,1,0:T(8,128)(2,1)}, u32[]{:S(2)}, u32[]{:S(2)}) async-start(bf16[4,64,1536]{2,1,0:T(8,128)(2,1)} %bitcast.8), calls=%async_computation.3 | async-start | bytes 1572864 | tf_op jit(solution)/shard_map/sum_texts/all_to_all | solution.py:27
  91.2 1.2 sum_images.1
  92.4 3.4 %collective-permute-start.8 = (bf16[64,1536]{1,0:T(8,128)(2,1)S(1)}, bf16[64,1536]{1,0:T(8,128)(2,1)S(1)}, u32[]{:S(2)}, u32[]{:S(2)}) collective-permute-start(bf16[64,1536]{1,0:T(8,128)(2,1)S(1)} %get-tuple-element.12), channel_id=1, source_target_pairs={{0,2},{2,4},{4,6},{6,0},{1,3},{3,5},{5,7},{7,1},{8,10},{10,12},{12... | collective-permute-start | bytes 589832 | tf_op jit(solution)/shard_map/sum_images/ppermute | solution.py:41
  95.8 3.9 %collective-permute-start.9 = (bf16[64,1536]{1,0:T(8,128)(2,1)S(1)}, bf16[64,1536]{1,0:T(8,128)(2,1)S(1)}, u32[]{:S(2)}, u32[]{:S(2)}) collective-permute-start(bf16[64,1536]{1,0:T(8,128)(2,1)S(1)} %get-tuple-element.13), channel_id=1, source_target_pairs={{0,4},{2,6},{4,0},{6,2},{1,5},{3,7},{5,1},{7,3},{8,12},{10,14},{12... | collective-permute-start | bytes 589832 | tf_op jit(solution)/shard_map/sum_images/ppermute | solution.py:41
  99.8 2.5 %collective-permute-start.10 = (bf16[64,1536]{1,0:T(8,128)(2,1)S(1)}, bf16[64,1536]{1,0:T(8,128)(2,1)S(1)}, u32[]{:S(2)}, u32[]{:S(2)}) collective-permute-start(bf16[64,1536]{1,0:T(8,128)(2,1)S(1)} %get-tuple-element.14), channel_id=1, source_target_pairs={{0,6},{2,0},{4,2},{6,4},{1,7},{3,1},{5,3},{7,5},{8,14},{10,8},{12,... | collective-permute-start | bytes 589832 | tf_op jit(solution)/shard_map/sum_images/ppermute | solution.py:41
  102.3 0.7 all-to-all-done.3
  103.0 2.0 reduce_sum.85
  105.0 5.9 %all-to-all-start.4 = ((bf16[4,16,1536]{2,1,0:T(8,128)(2,1)}), bf16[4,16,1536]{2,1,0:T(8,128)(2,1)S(1)}, u32[]{:S(2)}, u32[]{:S(2)}) async-start(bf16[4,16,1536]{2,1,0:T(8,128)(2,1)} %bitcast.10), calls=%async_computation.4 | async-start | bytes 393216 | tf_op jit(solution)/shard_map/sum_texts/all_to_all | solution.py:27
  111.0 1.9 collective-permute-start.11
  112.9 5.2 %collective-permute-start.13 = (bf16[16,1536]{1,0:T(8,128)(2,1)S(1)}, bf16[16,1536]{1,0:T(8,128)(2,1)S(1)}, u32[]{:S(2)}, u32[]{:S(2)}) collective-permute-start(bf16[16,1536]{1,0:T(8,128)(2,1)S(1)} %get-tuple-element.31), channel_id=1, source_target_pairs={{0,48},{16,0},{32,16},{48,32},{1,49},{17,1},{33,17},{49,33},{2,50}... | collective-permute-start | bytes 147464 | tf_op jit(solution)/shard_map/sum_images/ppermute | solution.py:41
  118.1 1.9 collective-permute-start.12
  120.0 4.4 %all-to-all-done.4 = bf16[4,16,1536]{2,1,0:T(8,128)(2,1)S(1)} async-done(((bf16[4,16,1536]{2,1,0:T(8,128)(2,1)}), bf16[4,16,1536]{2,1,0:T(8,128)(2,1)S(1)}, u32[]{:S(2)}, u32[]{:S(2)}) %all-to-all-start.4) | async-done | bytes 196640 | tf_op jit(solution)/shard_map/sum_texts/all_to_all | solution.py:27
  124.5 0.6 collective-permute-done.12
  125.1 0.2 multiply_reduce_fusion.1
  125.3 0.1 fusion.24
  125.4 1.0 broadcast_in_dim.13
  126.4 4.3 %all-to-all-start.5 = ((bf16[8,2,16,1536]{3,2,1,0:T(8,128)(2,1)}), bf16[8,2,16,1536]{3,2,1,0:T(8,128)(2,1)S(1)}, u32[]{:S(2)}, u32[]{:S(2)}) async-start(bf16[8,2,16,1536]{3,2,1,0:T(8,128)(2,1)} %broadcast_in_dim.13), calls=%async_computation.5 | async-start | bytes 1572864 | tf_op jit(solution)/shard_map/head_grads/all_to_all | solution.py:27
  130.7 10.5 %all-to-all-done.5 = bf16[8,2,16,1536]{3,2,1,0:T(8,128)(2,1)S(1)} async-done(((bf16[8,2,16,1536]{3,2,1,0:T(8,128)(2,1)}), bf16[8,2,16,1536]{3,2,1,0:T(8,128)(2,1)S(1)}, u32[]{:S(2)}, u32[]{:S(2)}) %all-to-all-start.5) | async-done | bytes 786464 | tf_op jit(solution)/shard_map/head_grads/all_to_all | solution.py:27
  141.3 0.2 fusion.1
  141.5 0.2 fusion.2
  141.8 8.2 %collective-permute-start.14 = (bf16[2,96,1536]{2,1,0:T(8,128)(2,1)S(1)}, bf16[2,96,1536]{2,1,0:T(8,128)(2,1)S(1)}, u32[]{:S(2)}, u32[]{:S(2)}) collective-permute-start(bf16[2,96,1536]{2,1,0:T(8,128)(2,1)S(1)} %pad_maximum_fusion), channel_id=1, source_target_pairs={{0,8},{8,0},{1,9},{9,1},{2,10},{10,2},{3,11},{11,3},{4,12},{12,4},... | collective-permute-start | bytes 1769480 | tf_op jit(solution)/shard_map/weight_grads/ppermute | solution.py:41
  150.0 0.2 convolution_bitcast_fusion.1
  150.3 0.2 convolution_bitcast_fusion
  150.5 1.2 collective-permute-done.14
  151.6 0.1 fusion.3
  151.7 0.1 convert_element_type.131
  152.0 42.5 %all_to_all.41 = bf16[32,24,384]{2,1,0:T(8,128)(2,1)S(1)} all-to-all(bf16[32,24,384]{2,1,0:T(8,128)(2,1)S(1)} %bitcast.77), channel_id=1, replica_groups=mesh['xl'=2,'zh'=4,'zm'=2,'z0'=2,'c'=2,'y'=4,'xh'=2] {'xl','zh','zm','z0'}, dimensions={0} | all-to-all | bytes 1179648 | tf_op jit(solution)/shard_map/weight_grads/all_to_all | solution.py:27
  194.6 0.9 broadcast_in_dim.14
  195.5 6.3 %all-to-all-start.7 = ((bf16[32,24,384]{2,1,0:T(8,128)(2,1)}), bf16[32,24,384]{2,1,0:T(8,128)(2,1)S(1)}, u32[]{:S(2)}, u32[]{:S(2)}) async-start(bf16[32,24,384]{2,1,0:T(8,128)(2,1)} %broadcast_in_dim.14), calls=%async_computation.7 | async-start | bytes 1179648 | tf_op jit(solution)/shard_map/weight_grads/all_to_all | solution.py:27
  201.8 1.0 fusion.40
  202.7 1.0 fusion.41
  203.7 31.2 %all-to-all-done.7 = bf16[32,24,384]{2,1,0:T(8,128)(2,1)S(1)} async-done(((bf16[32,24,384]{2,1,0:T(8,128)(2,1)}), bf16[32,24,384]{2,1,0:T(8,128)(2,1)S(1)}, u32[]{:S(2)}, u32[]{:S(2)}) %all-to-all-start.7) | async-done | bytes 589856 | tf_op jit(solution)/shard_map/weight_grads/all_to_all | solution.py:27
  234.9 0.3 copy.15
  235.2 0.2 reshape.77
  235.4 3.5 %collective-permute-start.15 = (bf16[2,96,1536]{2,1,0:T(8,128)(2,1)S(1)}, bf16[2,96,1536]{2,1,0:T(8,128)(2,1)S(1)}, u32[]{:S(2)}, u32[]{:S(2)}) collective-permute-start(bf16[2,96,1536]{2,1,0:T(8,128)(2,1)S(1)} %reshape.77), channel_id=1, source_target_pairs={{0,8},{8,0},{1,9},{9,1},{2,10},{10,2},{3,11},{11,3},{4,12},{12,4},... | collective-permute-start | bytes 1769480 | tf_op jit(solution)/shard_map/weight_grads/ppermute | solution.py:41
  238.9 0.1 maximum_convert_fusion.1
  239.0 0.1 maximum_convert_fusion
  239.2 1.3 collective-permute-done.15
  240.5 0.1 convert_dynamic-update-slice_fusion
  240.6 1.0 copy-done.2
  241.6 0.4 copy-done.3
  (43 shorter events, 0.8 us)
Async XLA Ops:
  23.3 29.6 %all-to-all-start.1 = ((bf16[4,16,1536]{2,1,0:T(8,128)(2,1)}), bf16[4,16,1536]{2,1,0:T(8,128)(2,1)S(1)}, u32[]{:S(2)}, u32[]{:S(2)}) async-start(bf16[4,16,1536]{2,1,0:T(8,128)(2,1)} %broadcast_in_dim.10), calls=%async_computation.1 | async-start | bytes 393216 | tf_op jit(solution)/shard_map/gather_texts/all_to_all | solution.py:27
  40.1 17.2 %collective-permute-start.2 = (bf16[16,1536]{1,0:T(8,128)(2,1)S(1)}, bf16[16,1536]{1,0:T(8,128)(2,1)S(1)}, u32[]{:S(2)}, u32[]{:S(2)}) collective-permute-start(bf16[16,1536]{1,0:T(8,128)(2,1)S(1)} %get-tuple-element.23), channel_id=1, source_target_pairs={{0,16},{16,32},{32,48},{48,0},{1,17},{17,33},{33,49},{49,1},{2,18}... | collective-permute-start | bytes 147464 | tf_op jit(solution)/shard_map/gather_images/ppermute | solution.py:41
  42.8 14.5 %collective-permute-start.1 = (bf16[16,1536]{1,0:T(8,128)(2,1)S(1)}, bf16[16,1536]{1,0:T(8,128)(2,1)S(1)}, u32[]{:S(2)}, u32[]{:S(2)}) collective-permute-start(bf16[16,1536]{1,0:T(8,128)(2,1)S(1)} %get-tuple-element.23), channel_id=1, source_target_pairs={{0,32},{16,48},{32,0},{48,16},{1,33},{17,49},{33,1},{49,17},{2,34}... | collective-permute-start | bytes 147464 | tf_op jit(solution)/shard_map/gather_images/ppermute | solution.py:41
  45.9 11.4 %collective-permute-start = (bf16[16,1536]{1,0:T(8,128)(2,1)S(1)}, bf16[16,1536]{1,0:T(8,128)(2,1)S(1)}, u32[]{:S(2)}, u32[]{:S(2)}) collective-permute-start(bf16[16,1536]{1,0:T(8,128)(2,1)S(1)} %get-tuple-element.23), channel_id=1, source_target_pairs={{0,48},{16,0},{32,16},{48,32},{1,49},{17,1},{33,17},{49,33},{2,50}... | collective-permute-start | bytes 147464 | tf_op jit(solution)/shard_map/gather_images/ppermute | solution.py:41
  53.8 12.0 %all-to-all-start.2 = ((bf16[4,64,1536]{2,1,0:T(8,128)(2,1)}), bf16[4,64,1536]{2,1,0:T(8,128)(2,1)S(1)}, u32[]{:S(2)}, u32[]{:S(2)}) async-start(bf16[4,64,1536]{2,1,0:T(8,128)(2,1)} %broadcast_in_dim.12), calls=%async_computation.2 | async-start | bytes 1572864 | tf_op jit(solution)/shard_map/gather_texts/all_to_all | solution.py:27
  57.4 18.7 %collective-permute-start.5 = (bf16[64,1536]{1,0:T(8,128)(2,1)S(1)}, bf16[64,1536]{1,0:T(8,128)(2,1)S(1)}, u32[]{:S(2)}, u32[]{:S(2)}) collective-permute-start(bf16[64,1536]{1,0:T(8,128)(2,1)S(1)} %pad_maximum_fusion.1), channel_id=1, source_target_pairs={{0,2},{2,4},{4,6},{6,0},{1,3},{3,5},{5,7},{7,1},{8,10},{10,12},{12... | collective-permute-start | bytes 589832 | tf_op jit(solution)/shard_map/gather_images/ppermute | solution.py:41
  59.3 16.8 %collective-permute-start.4 = (bf16[64,1536]{1,0:T(8,128)(2,1)S(1)}, bf16[64,1536]{1,0:T(8,128)(2,1)S(1)}, u32[]{:S(2)}, u32[]{:S(2)}) collective-permute-start(bf16[64,1536]{1,0:T(8,128)(2,1)S(1)} %pad_maximum_fusion.1), channel_id=1, source_target_pairs={{0,4},{2,6},{4,0},{6,2},{1,5},{3,7},{5,1},{7,3},{8,12},{10,14},{12... | collective-permute-start | bytes 589832 | tf_op jit(solution)/shard_map/gather_images/ppermute | solution.py:41
  63.0 13.1 %collective-permute-start.3 = (bf16[64,1536]{1,0:T(8,128)(2,1)S(1)}, bf16[64,1536]{1,0:T(8,128)(2,1)S(1)}, u32[]{:S(2)}, u32[]{:S(2)}) collective-permute-start(bf16[64,1536]{1,0:T(8,128)(2,1)S(1)} %pad_maximum_fusion.1), channel_id=1, source_target_pairs={{0,6},{2,0},{4,2},{6,4},{1,7},{3,1},{5,3},{7,5},{8,14},{10,8},{12,... | collective-permute-start | bytes 589832 | tf_op jit(solution)/shard_map/gather_images/ppermute | solution.py:41
  65.9 12.1 %collective-permute-start.6 = (bf16[256,1536]{1,0:T(8,128)(2,1)S(1)}, bf16[256,1536]{1,0:T(8,128)(2,1)S(1)}, u32[]{:S(2)}, u32[]{:S(2)}) collective-permute-start(bf16[256,1536]{1,0:T(8,128)(2,1)S(1)} %bitcast.66), channel_id=1, source_target_pairs={{0,8},{8,0},{1,9},{9,1},{2,10},{10,2},{3,11},{11,3},{4,12},{12,4},... | collective-permute-start | bytes 2359304 | tf_op jit(solution)/shard_map/gather_texts/ppermute | solution.py:41
  79.6 4.8 %collective-permute-start.7 = (bf16[256,1536]{1,0:T(8,128)(2,1)}, bf16[256,1536]{1,0:T(8,128)(2,1)}, u32[]{:S(2)}, u32[]{:S(2)}) collective-permute-start(bf16[256,1536]{1,0:T(8,128)(2,1)} %convolution_convert_fusion), channel_id=1, source_target_pairs={{0,8},{8,0},{1,9},{9,1},{2,10},{10,2},{3,11},{11,3},{4,12},{12,4},... | collective-permute-start | bytes 2359304 | tf_op jit(solution)/shard_map/sum_texts/ppermute | solution.py:41
  86.7 16.3 %all-to-all-start.3 = ((bf16[4,64,1536]{2,1,0:T(8,128)(2,1)}), bf16[4,64,1536]{2,1,0:T(8,128)(2,1)}, u32[]{:S(2)}, u32[]{:S(2)}) async-start(bf16[4,64,1536]{2,1,0:T(8,128)(2,1)} %bitcast.8), calls=%async_computation.3 | async-start | bytes 1572864 | tf_op jit(solution)/shard_map/sum_texts/all_to_all | solution.py:27
  92.4 18.4 %collective-permute-start.8 = (bf16[64,1536]{1,0:T(8,128)(2,1)S(1)}, bf16[64,1536]{1,0:T(8,128)(2,1)S(1)}, u32[]{:S(2)}, u32[]{:S(2)}) collective-permute-start(bf16[64,1536]{1,0:T(8,128)(2,1)S(1)} %get-tuple-element.12), channel_id=1, source_target_pairs={{0,2},{2,4},{4,6},{6,0},{1,3},{3,5},{5,7},{7,1},{8,10},{10,12},{12... | collective-permute-start | bytes 589832 | tf_op jit(solution)/shard_map/sum_images/ppermute | solution.py:41
  95.8 15.0 %collective-permute-start.9 = (bf16[64,1536]{1,0:T(8,128)(2,1)S(1)}, bf16[64,1536]{1,0:T(8,128)(2,1)S(1)}, u32[]{:S(2)}, u32[]{:S(2)}) collective-permute-start(bf16[64,1536]{1,0:T(8,128)(2,1)S(1)} %get-tuple-element.13), channel_id=1, source_target_pairs={{0,4},{2,6},{4,0},{6,2},{1,5},{3,7},{5,1},{7,3},{8,12},{10,14},{12... | collective-permute-start | bytes 589832 | tf_op jit(solution)/shard_map/sum_images/ppermute | solution.py:41
  99.8 11.1 %collective-permute-start.10 = (bf16[64,1536]{1,0:T(8,128)(2,1)S(1)}, bf16[64,1536]{1,0:T(8,128)(2,1)S(1)}, u32[]{:S(2)}, u32[]{:S(2)}) collective-permute-start(bf16[64,1536]{1,0:T(8,128)(2,1)S(1)} %get-tuple-element.14), channel_id=1, source_target_pairs={{0,6},{2,0},{4,2},{6,4},{1,7},{3,1},{5,3},{7,5},{8,14},{10,8},{12,... | collective-permute-start | bytes 589832 | tf_op jit(solution)/shard_map/sum_images/ppermute | solution.py:41
  105.0 19.4 %all-to-all-start.4 = ((bf16[4,16,1536]{2,1,0:T(8,128)(2,1)}), bf16[4,16,1536]{2,1,0:T(8,128)(2,1)S(1)}, u32[]{:S(2)}, u32[]{:S(2)}) async-start(bf16[4,16,1536]{2,1,0:T(8,128)(2,1)} %bitcast.10), calls=%async_computation.4 | async-start | bytes 393216 | tf_op jit(solution)/shard_map/sum_texts/all_to_all | solution.py:27
  111.0 13.4 %collective-permute-start.11 = (bf16[16,1536]{1,0:T(8,128)(2,1)S(1)}, bf16[16,1536]{1,0:T(8,128)(2,1)S(1)}, u32[]{:S(2)}, u32[]{:S(2)}) collective-permute-start(bf16[16,1536]{1,0:T(8,128)(2,1)S(1)} %get-tuple-element.30), channel_id=1, source_target_pairs={{0,16},{16,32},{32,48},{48,0},{1,17},{17,33},{33,49},{49,1},{2,18}... | collective-permute-start | bytes 147464 | tf_op jit(solution)/shard_map/sum_images/ppermute | solution.py:41
  112.9 11.5 %collective-permute-start.13 = (bf16[16,1536]{1,0:T(8,128)(2,1)S(1)}, bf16[16,1536]{1,0:T(8,128)(2,1)S(1)}, u32[]{:S(2)}, u32[]{:S(2)}) collective-permute-start(bf16[16,1536]{1,0:T(8,128)(2,1)S(1)} %get-tuple-element.31), channel_id=1, source_target_pairs={{0,48},{16,0},{32,16},{48,32},{1,49},{17,1},{33,17},{49,33},{2,50}... | collective-permute-start | bytes 147464 | tf_op jit(solution)/shard_map/sum_images/ppermute | solution.py:41
  118.1 7.0 %collective-permute-start.12 = (bf16[16,1536]{1,0:T(8,128)(2,1)S(1)}, bf16[16,1536]{1,0:T(8,128)(2,1)S(1)}, u32[]{:S(2)}, u32[]{:S(2)}) collective-permute-start(bf16[16,1536]{1,0:T(8,128)(2,1)S(1)} %get-tuple-element.32), channel_id=1, source_target_pairs={{0,32},{16,48},{32,0},{48,16},{1,33},{17,49},{33,1},{49,17},{2,34}... | collective-permute-start | bytes 147464 | tf_op jit(solution)/shard_map/sum_images/ppermute | solution.py:41
  126.4 14.8 %all-to-all-start.5 = ((bf16[8,2,16,1536]{3,2,1,0:T(8,128)(2,1)}), bf16[8,2,16,1536]{3,2,1,0:T(8,128)(2,1)S(1)}, u32[]{:S(2)}, u32[]{:S(2)}) async-start(bf16[8,2,16,1536]{3,2,1,0:T(8,128)(2,1)} %broadcast_in_dim.13), calls=%async_computation.5 | async-start | bytes 1572864 | tf_op jit(solution)/shard_map/head_grads/all_to_all | solution.py:27
  130.7 10.6 %copy-start.4 = (bf16[128,192]{0,1:T(8,128)(2,1)S(1)}, bf16[128,192]{0,1:T(8,128)(2,1)}, u32[]{:S(2)}) copy-start(bf16[128,192]{0,1:T(8,128)(2,1)} %param.7) | copy-start | bytes 147460
  130.7 10.8 %copy-start.5 = (bf16[128,192]{0,1:T(8,128)(2,1)S(1)}, bf16[128,192]{0,1:T(8,128)(2,1)}, u32[]{:S(2)}) copy-start(bf16[128,192]{0,1:T(8,128)(2,1)} %param.8) | copy-start | bytes 147460
  141.8 9.8 %collective-permute-start.14 = (bf16[2,96,1536]{2,1,0:T(8,128)(2,1)S(1)}, bf16[2,96,1536]{2,1,0:T(8,128)(2,1)S(1)}, u32[]{:S(2)}, u32[]{:S(2)}) collective-permute-start(bf16[2,96,1536]{2,1,0:T(8,128)(2,1)S(1)} %pad_maximum_fusion), channel_id=1, source_target_pairs={{0,8},{8,0},{1,9},{9,1},{2,10},{10,2},{3,11},{11,3},{4,12},{12,4},... | collective-permute-start | bytes 1769480 | tf_op jit(solution)/shard_map/weight_grads/ppermute | solution.py:41
  194.5 7.3 %copy-start = (bf16[192,1536]{1,0:T(8,128)(2,1)S(1)}, bf16[192,1536]{1,0:T(8,128)(2,1)}, u32[]{:S(2)}) copy-start(bf16[192,1536]{1,0:T(8,128)(2,1)} %refs_1_.1) | copy-start | bytes 1769476
  195.5 7.3 %copy-start.1 = (bf16[192,1536]{1,0:T(8,128)(2,1)S(1)}, bf16[192,1536]{1,0:T(8,128)(2,1)}, u32[]{:S(2)}) copy-start(bf16[192,1536]{1,0:T(8,128)(2,1)} %refs_3_.1) | copy-start | bytes 1769476
  195.5 39.4 %all-to-all-start.7 = ((bf16[32,24,384]{2,1,0:T(8,128)(2,1)}), bf16[32,24,384]{2,1,0:T(8,128)(2,1)S(1)}, u32[]{:S(2)}, u32[]{:S(2)}) async-start(bf16[32,24,384]{2,1,0:T(8,128)(2,1)} %broadcast_in_dim.14), calls=%async_computation.7 | async-start | bytes 1179648 | tf_op jit(solution)/shard_map/weight_grads/all_to_all | solution.py:27
  235.4 5.1 %collective-permute-start.15 = (bf16[2,96,1536]{2,1,0:T(8,128)(2,1)S(1)}, bf16[2,96,1536]{2,1,0:T(8,128)(2,1)S(1)}, u32[]{:S(2)}, u32[]{:S(2)}) collective-permute-start(bf16[2,96,1536]{2,1,0:T(8,128)(2,1)S(1)} %reshape.77), channel_id=1, source_target_pairs={{0,8},{8,0},{1,9},{9,1},{2,10},{10,2},{3,11},{11,3},{4,12},{12,4},... | collective-permute-start | bytes 1769480 | tf_op jit(solution)/shard_map/weight_grads/ppermute | solution.py:41
  240.6 1.0 copy-start.2
  240.6 1.4 copy-start.3

commit v8 on v7

--- a/solution.py
+++ b/solution.py
@@ -10,7 +10,6 @@
 
 PARTS = {"xl": 2, "zh": 4, "zm": 2, "z0": 2, "c": 2, "y": 4, "xh": 2}
 DP = ("xl", "zh", "zm", "z0", "c")
-Z = ("zh", "zm", "z0")
 ZL = ("zm", "z0")
 MP = ("y", "xh")
 
@@ -41,17 +40,18 @@
     return lax.ppermute(value, axis, [(i, (i + by) % n) for i in range(n)])
 
 
-def ring_gather(rows, axis):
-    n = count(axis)
-    return jnp.concatenate([rows] + [shifted(rows, axis, n - k) for k in range(1, n)], axis=0)
-
-
-def ring_scatter_sum(total, axis):
-    n = count(axis)
-    blocks = split_rows(total, n)
+def swapped(value, axis, by):
+    return lax.ppermute(value, axis, [(i, i ^ by) for i in range(count(axis))])
+
+
+def gather_pairs(rows, axis):
+    return jnp.concatenate([rows] + [swapped(rows, axis, k) for k in range(1, count(axis))], axis=0)
+
+
+def scatter_sum_pairs(blocks, axis):
     own = blocks[0]
-    for k in range(1, n):
-        own = own + shifted(blocks[k].astype(BF16), axis, k).astype(F32)
+    for k in range(1, count(axis)):
+        own = own + swapped(blocks[k].astype(BF16), axis, k).astype(F32)
     return own
 
 
@@ -119,27 +119,6 @@
     return heads
 
 
-def images_body(coeff, texts, other_coeff, other_texts, own, *sent):
-    rows = own.shape[0]
-    for k, out in enumerate((own,) + sent):
-        at = slice(k * rows, (k + 1) * rows)
-        total = contract(coeff[:, at], texts[...], 0, 0)
-        total = total + contract(other_coeff[:, at], other_texts[...], 0, 0)
-        out[...] = total.astype(out.dtype)
-
-
-def image_blocks(coeff, texts, other_coeff, other_texts, blocks):
-    width = texts.shape[1]
-    rows = coeff.shape[1] // blocks
-    return local_kernel(
-        images_body,
-        (coeff, texts, other_coeff, other_texts),
-        [jax.ShapeDtypeStruct((rows, width), F32)]
-        + [jax.ShapeDtypeStruct((rows, width), BF16)] * (blocks - 1),
-        4 * coeff.shape[0] * coeff.shape[1] * width,
-    )
-
-
 def unit_rows(heads):
     values = heads.astype(F32)
     norm = jnp.sqrt(jnp.sum(values * values, axis=1, keepdims=True) + 1e-06)
@@ -179,7 +158,7 @@
         texts = merge_rows(gather(texts, ("xh", "xl")))
         other_texts = shifted(texts, "c", 1)
     with jax.named_scope("gather_images"):
-        images = ring_gather(ring_gather(image_unit.astype(BF16), ZL), "y")
+        images = gather_pairs(gather_pairs(image_unit.astype(BF16), ZL), "y")
 
     def coefficients(block, positive):
         scores = (
@@ -200,15 +179,19 @@
     with jax.named_scope("sum_texts"):
         text_part = text_part + shifted(other_part.astype(BF16), "c", 1).astype(F32)
         text_part = split_rows(text_part, count(("xh", "xl"))).astype(BF16)
-        text_part, other_coeff = lax.optimization_barrier((text_part, other_coeff))
         text_part = scatter_sum(text_part, ("xh", "xl"))
         text_grads = scatter_sum(split_rows(text_part, count("zh")), "zh")
     with jax.named_scope("sum_images"):
-        blocks = image_blocks(coeff, texts, other_coeff, other_texts, count("y"))
-        image_part = blocks[0]
-        for k in range(1, count("y")):
-            image_part = image_part + shifted(blocks[k], "y", k).astype(F32)
-        image_grads = ring_scatter_sum(image_part, ZL)
+        rows = images.shape[0] // count("y")
+
+        def image_block(k):
+            at_rows = slice(k * rows, (k + 1) * rows)
+            return contract(coeff[:, at_rows], texts, 0, 0) + contract(
+                other_coeff[:, at_rows], other_texts, 0, 0
+            )
+
+        image_part = scatter_sum_pairs([image_block(k) for k in range(count("y"))], "y")
+        image_grads = scatter_sum_pairs(split_rows(image_part, count(ZL)), ZL)
 
     with jax.named_scope("head_grads"):
         grads = jnp.stack(
@@ -245,11 +228,12 @@
         other = shifted(half_part(1 - at["c"]).astype(BF16), "c", 1)
         part = half_part(at["c"]) + other.astype(F32)
         quarter = embed_width // 4
-        part = part.reshape(2, 4, half // 4, 4, quarter).transpose(0, 3, 1, 2, 4)
-        part = scatter_sum(part.reshape(32, half // 4, quarter), ("xl",) + Z)
-        part = gather(part.astype(BF16), ("xl",) + Z)
-        part = part.reshape(2, 4, 4, half // 4, quarter).transpose(0, 2, 3, 1, 4)
-        part = lax.optimization_barrier(part.reshape(2, half, embed_width))
+        part = scatter_sum(part.reshape(4, half // 2, embed_width), ("xl", "z0"))
+        part = part.reshape(2, half // 4, 4, quarter).transpose(2, 0, 1, 3)
+        part = scatter_sum(part.reshape(8, half // 4, quarter), ("zh", "zm"))
+        part = gather(part.astype(BF16), ("zh", "zm")).reshape(4, 2, half // 4, quarter)
+        part = part.transpose(1, 2, 0, 3).reshape(half // 2, embed_width)
+        part = gather(part, ("xl", "z0")).reshape(2, half, embed_width)
         other = shifted(part, "c", 1)
 
         def halves(mine, theirs):

time: 244 us -> 233 us (0.955)
  blocking collectives: 61.6 us -> 49.8 us
  matrix products: 7.29 us -> 10.3 us
    ppermute x16 -> x4, starting transfers between devices: 60.9 us -> 19.4 us  [shifted(): return lax.ppermute(value, axis, [(i, (i + by) % n) for i in range(n)])]
    ppermute x0 -> x12, starting transfers between devices: none -> 35.6 us  [swapped(): return lax.ppermute(value, axis, [(i, i ^ by) for i in range(count(axis))])]
    all_to_all x2 -> x3, blocking collectives: 61.6 us -> 49.8 us  [exchange(): return lax.all_to_all(blocks, axes, split_axis=0, concat_axis=0, tiled=True)]
    all_to_all x6 -> x7, starting transfers between devices: 41.1 us -> 48.4 us  [exchange(): return lax.all_to_all(blocks, axes, split_axis=0, concat_axis=0, tiled=True)]
    ppermute x0 -> x12, waiting for transfers between devices: none -> 6.69 us  [swapped(): return lax.ppermute(value, axis, [(i, i ^ by) for i in range(count(axis))])]
    dot_general x0 -> x8, matrix products: none -> 5.04 us  [contract(): return lax.dot_general(left, right, dims, preferred_element_type=F32)]
    all_to_all x6 -> x7, waiting for transfers between devices: 48.3 us -> 44.4 us  [exchange(): return lax.all_to_all(blocks, axes, split_axis=0, concat_axis=0, tiled=True)]
    ppermute x16 -> x4, waiting for transfers between devices: 6.62 us -> 3.79 us  [shifted(): return lax.ppermute(value, axis, [(i, (i + by) % n) for i in range(n)])]
  transfers between devices with their start and end apart: 22 -> 23, of which waited for: 10 -> 12; matrix products, arithmetic and copies ran while one was open for 3% -> 5% of each run, Pallas kernels for 1% -> 0%
where the time goes in v8:
time: 233 us; the launch traced here: 232 us
  starting transfers between devices  103 us (44%)
  waiting for transfers between devices  54.9 us (24%)
  blocking collectives  49.8 us (21%)
  matrix products  10.3 us (4%)
  local copies, waits for them, and re-layouts  5.19 us (2%)
  between operations  3.14 us (1%)
  Pallas kernels  2.59 us (1%)
    all_to_all x3, blocking collectives, exchange(): return lax.all_to_all(blocks, axes, split_axis=0, concat_axis=0, tiled=True)  49.8 us
    all_to_all x7, starting transfers between devices, exchange(): return lax.all_to_all(blocks, axes, split_axis=0, concat_axis=0, tiled=True)  48.4 us
    all_to_all x7, waiting for transfers between devices, exchange(): return lax.all_to_all(blocks, axes, split_axis=0, concat_axis=0, tiled=True)  44.4 us
    ppermute x12, starting transfers between devices, swapped(): return lax.ppermute(value, axis, [(i, i ^ by) for i in range(count(axis))])  35.6 us
    ppermute x4, starting transfers between devices, shifted(): return lax.ppermute(value, axis, [(i, (i + by) % n) for i in range(n)])  19.4 us
    ppermute x12, waiting for transfers between devices, swapped(): return lax.ppermute(value, axis, [(i, i ^ by) for i in range(count(axis))])  6.69 us
    dot_general x8, matrix products, contract(): return lax.dot_general(left, right, dims, preferred_element_type=F32)  5.04 us
  transfers between devices with their start and end apart: 23, of which 12 were waited for; matrix products, arithmetic and copies ran while one was open for 5% of the time, Pallas kernels for 0%

profile of v8, /device:TPU:1, one launch (start us, length us, event | category | flops | bytes accessed | tf_op | source)
XLA Modules:
  0.0 231.7 jit_solution(254598953428302616)
XLA Ops:
  0.6 2.6 %heads.1 = bf16[128,3072]{1,0:T(8,128)(2,1)} custom-call(bf16[192,128]{1,0:T(8,128)(2,1)} %bitcast.99, bf16[192,1536]{1,0:T(8,128)(2,1)} %refs_1_.1, bf16[192,128]{1,0:T(8,128)(2,1)} %bitcast.100, bf16[192,1536]{1,0:T(8,128)(2,1)} %refs_3_.1), custom_call_target="tpu_custom_call" | custom-call | flops 150994944 | bytes 2064384 | tf_op jit(solution)/shard_map/heads/pallas_call | solution.py:72
  3.2 7.5 %all-to-all-start = ((bf16[8,16,3072]{2,1,0:T(8,128)(2,1)}), bf16[8,16,3072]{2,1,0:T(8,128)(2,1)S(1)}, u32[]{:S(2)}, u32[]{:S(2)}) async-start(bf16[8,16,3072]{2,1,0:T(8,128)(2,1)} %bitcast.88), calls=%async_computation | async-start | bytes 1572864 | tf_op jit(solution)/shard_map/heads/all_to_all | solution.py:26
  10.7 11.2 %all-to-all-done = bf16[8,16,3072]{2,1,0:T(8,128)(2,1)S(1)} async-done(((bf16[8,16,3072]{2,1,0:T(8,128)(2,1)}), bf16[8,16,3072]{2,1,0:T(8,128)(2,1)S(1)}, u32[]{:S(2)}, u32[]{:S(2)}) %all-to-all-start) | async-done | bytes 786464 | tf_op jit(solution)/shard_map/heads/all_to_all | solution.py:26
  22.3 0.7 broadcast_in_dim.14
  23.0 16.8 %all-to-all-start.1 = ((bf16[4,16,1536]{2,1,0:T(8,128)(2,1)}), bf16[4,16,1536]{2,1,0:T(8,128)(2,1)S(1)}, u32[]{:S(2)}, u32[]{:S(2)}) async-start(bf16[4,16,1536]{2,1,0:T(8,128)(2,1)} %broadcast_in_dim.14), calls=%async_computation.1 | async-start | bytes 393216 | tf_op jit(solution)/shard_map/gather_texts/all_to_all | solution.py:26
  39.9 3.6 %collective-permute-start.2 = (bf16[16,1536]{1,0:T(8,128)(2,1)S(1)}, bf16[16,1536]{1,0:T(8,128)(2,1)S(1)}, u32[]{:S(2)}, u32[]{:S(2)}) collective-permute-start(bf16[16,1536]{1,0:T(8,128)(2,1)S(1)} %get-tuple-element.9), channel_id=1, source_target_pairs={{0,48},{16,32},{32,16},{48,0},{1,49},{17,33},{33,17},{49,1},{2,50}... | collective-permute-start | bytes 147464 | tf_op jit(solution)/shard_map/gather_images/ppermute | solution.py:44
  43.4 2.2 collective-permute-start.1
  45.6 3.5 %collective-permute-start = (bf16[16,1536]{1,0:T(8,128)(2,1)S(1)}, bf16[16,1536]{1,0:T(8,128)(2,1)S(1)}, u32[]{:S(2)}, u32[]{:S(2)}) collective-permute-start(bf16[16,1536]{1,0:T(8,128)(2,1)S(1)} %get-tuple-element.9), channel_id=1, source_target_pairs={{0,16},{16,0},{32,48},{48,32},{1,17},{17,1},{33,49},{49,33},{2,18}... | collective-permute-start | bytes 147464 | tf_op jit(solution)/shard_map/gather_images/ppermute | solution.py:44
  51.1 3.8 %collective-permute-done.1 = bf16[16,1536]{1,0:T(8,128)(2,1)S(1)} collective-permute-done((bf16[16,1536]{1,0:T(8,128)(2,1)S(1)}, bf16[16,1536]{1,0:T(8,128)(2,1)S(1)}, u32[]{:S(2)}, u32[]{:S(2)}) %collective-permute-start.1) | collective-permute-done | bytes 49184 | tf_op jit(solution)/shard_map/gather_images/ppermute | solution.py:44
  54.9 2.8 %collective-permute-start.5 = (bf16[64,1536]{1,0:T(8,128)(2,1)S(1)}, bf16[64,1536]{1,0:T(8,128)(2,1)S(1)}, u32[]{:S(2)}, u32[]{:S(2)}) collective-permute-start(bf16[64,1536]{1,0:T(8,128)(2,1)S(1)} %pad_maximum_fusion.1), channel_id=1, source_target_pairs={{0,6},{2,4},{4,2},{6,0},{1,7},{3,5},{5,3},{7,1},{8,14},{10,12},{12... | collective-permute-start | bytes 589832 | tf_op jit(solution)/shard_map/gather_images/ppermute | solution.py:44
  57.7 2.2 collective-permute-start.4
  59.9 4.0 %collective-permute-start.3 = (bf16[64,1536]{1,0:T(8,128)(2,1)S(1)}, bf16[64,1536]{1,0:T(8,128)(2,1)S(1)}, u32[]{:S(2)}, u32[]{:S(2)}) collective-permute-start(bf16[64,1536]{1,0:T(8,128)(2,1)S(1)} %pad_maximum_fusion.1), channel_id=1, source_target_pairs={{0,2},{2,0},{4,6},{6,4},{1,3},{3,1},{5,7},{7,5},{8,10},{10,8},{12,... | collective-permute-start | bytes 589832 | tf_op jit(solution)/shard_map/gather_images/ppermute | solution.py:44
  63.9 0.9 broadcast_in_dim.16
  64.8 3.5 %all-to-all-start.2 = ((bf16[4,64,1536]{2,1,0:T(8,128)(2,1)}), bf16[4,64,1536]{2,1,0:T(8,128)(2,1)S(1)}, u32[]{:S(2)}, u32[]{:S(2)}) async-start(bf16[4,64,1536]{2,1,0:T(8,128)(2,1)} %broadcast_in_dim.16), calls=%async_computation.2 | async-start | bytes 1572864 | tf_op jit(solution)/shard_map/gather_texts/all_to_all | solution.py:26
  68.4 10.7 %all-to-all-done.2 = bf16[4,64,1536]{2,1,0:T(8,128)(2,1)S(1)} async-done(((bf16[4,64,1536]{2,1,0:T(8,128)(2,1)}), bf16[4,64,1536]{2,1,0:T(8,128)(2,1)S(1)}, u32[]{:S(2)}, u32[]{:S(2)}) %all-to-all-start.2) | async-done | bytes 786464 | tf_op jit(solution)/shard_map/gather_texts/all_to_all | solution.py:26
  79.1 4.3 %collective-permute-start.6 = (bf16[256,1536]{1,0:T(8,128)(2,1)S(1)}, bf16[256,1536]{1,0:T(8,128)(2,1)S(1)}, u32[]{:S(2)}, u32[]{:S(2)}) collective-permute-start(bf16[256,1536]{1,0:T(8,128)(2,1)S(1)} %bitcast.76), channel_id=1, source_target_pairs={{0,8},{8,0},{1,9},{9,1},{2,10},{10,2},{3,11},{11,3},{4,12},{12,4},... | collective-permute-start | bytes 2359304 | tf_op jit(solution)/shard_map/gather_texts/ppermute | solution.py:40
  83.6 0.4 fusion.24
  84.0 1.4 collective-permute-done.6
  85.3 0.4 fusion.23
  85.8 0.4 convolution_convert_fusion
  86.2 2.3 collective-permute-start.13
  88.5 0.3 fusion.33
  88.7 0.3 fusion.36
  89.0 0.3 fusion.39
  89.2 0.9 fusion.6
  90.2 2.7 %collective-permute-start.9 = (bf16[64,1536]{1,0:T(8,128)(2,1)}, bf16[64,1536]{1,0:T(8,128)(2,1)}, u32[]{:S(2)}, u32[]{:S(2)}) collective-permute-start(bf16[64,1536]{1,0:T(8,128)(2,1)} %fusion.6), channel_id=1, source_target_pairs={{0,6},{2,4},{4,2},{6,0},{1,7},{3,5},{5,3},{7,1},{8,14},{10,12},{12... | collective-permute-start | bytes 589832 | tf_op jit(solution)/shard_map/sum_images/ppermute | solution.py:44
  93.0 1.3 fusion
  94.2 3.5 %all-to-all-start.3 = ((bf16[4,64,1536]{2,1,0:T(8,128)(2,1)}), bf16[4,64,1536]{2,1,0:T(8,128)(2,1)S(1)}, u32[]{:S(2)}, u32[]{:S(2)}) async-start(bf16[4,64,1536]{2,1,0:T(8,128)(2,1)} %bitcast.9), calls=%async_computation.3 | async-start | bytes 1572864 | tf_op jit(solution)/shard_map/sum_texts/all_to_all | solution.py:26
  97.7 0.9 fusion.5
  98.7 2.8 %collective-permute-start.8 = (bf16[64,1536]{1,0:T(8,128)(2,1)}, bf16[64,1536]{1,0:T(8,128)(2,1)S(1)}, u32[]{:S(2)}, u32[]{:S(2)}) collective-permute-start(bf16[64,1536]{1,0:T(8,128)(2,1)} %fusion.5), channel_id=1, source_target_pairs={{0,4},{2,6},{4,0},{6,2},{1,5},{3,7},{5,1},{7,3},{8,12},{10,14},{12... | collective-permute-start | bytes 589832 | tf_op jit(solution)/shard_map/sum_images/ppermute | solution.py:44
  101.5 0.9 fusion.4
  102.4 3.4 %collective-permute-start.7 = (bf16[64,1536]{1,0:T(8,128)(2,1)}, bf16[64,1536]{1,0:T(8,128)(2,1)S(1)}, u32[]{:S(2)}, u32[]{:S(2)}) collective-permute-start(bf16[64,1536]{1,0:T(8,128)(2,1)} %fusion.4), channel_id=1, source_target_pairs={{0,2},{2,0},{4,6},{6,4},{1,3},{3,1},{5,7},{7,5},{8,10},{10,8},{12,... | collective-permute-start | bytes 589832 | tf_op jit(solution)/shard_map/sum_images/ppermute | solution.py:44
  105.8 0.3 fusion.42
  106.1 3.6 %all-to-all-done.3 = bf16[4,64,1536]{2,1,0:T(8,128)(2,1)S(1)} async-done(((bf16[4,64,1536]{2,1,0:T(8,128)(2,1)}), bf16[4,64,1536]{2,1,0:T(8,128)(2,1)S(1)}, u32[]{:S(2)}, u32[]{:S(2)}) %all-to-all-start.3) | async-done | bytes 786464 | tf_op jit(solution)/shard_map/sum_texts/all_to_all | solution.py:26
  109.7 0.8 reduce_sum.97
  110.5 10.0 %all-to-all-start.4 = ((bf16[4,16,1536]{2,1,0:T(8,128)(2,1)}), bf16[4,16,1536]{2,1,0:T(8,128)(2,1)S(1)}, u32[]{:S(2)}, u32[]{:S(2)}) async-start(bf16[4,16,1536]{2,1,0:T(8,128)(2,1)} %bitcast.10), calls=%async_computation.4 | async-start | bytes 393216 | tf_op jit(solution)/shard_map/sum_texts/all_to_all | solution.py:26
  120.5 1.2 fusion.58
  121.7 1.9 collective-permute-start.10
  123.6 3.6 %collective-permute-start.12 = (bf16[16,1536]{1,0:T(8,128)(2,1)S(1)}, bf16[16,1536]{1,0:T(8,128)(2,1)S(1)}, u32[]{:S(2)}, u32[]{:S(2)}) collective-permute-start(bf16[16,1536]{1,0:T(8,128)(2,1)S(1)} %get-tuple-element.17), channel_id=1, source_target_pairs={{0,48},{16,32},{32,16},{48,0},{1,49},{17,33},{33,17},{49,1},{2,50}... | collective-permute-start | bytes 147464 | tf_op jit(solution)/shard_map/sum_images/ppermute | solution.py:44
  127.2 2.9 %collective-permute-start.11 = (bf16[16,1536]{1,0:T(8,128)(2,1)S(1)}, bf16[16,1536]{1,0:T(8,128)(2,1)S(1)}, u32[]{:S(2)}, u32[]{:S(2)}) collective-permute-start(bf16[16,1536]{1,0:T(8,128)(2,1)S(1)} %get-tuple-element.18), channel_id=1, source_target_pairs={{0,32},{16,48},{32,0},{48,16},{1,33},{17,49},{33,1},{49,17},{2,34}... | collective-permute-start | bytes 147464 | tf_op jit(solution)/shard_map/sum_images/ppermute | solution.py:44
  130.1 3.5 %all-to-all-done.4 = bf16[4,16,1536]{2,1,0:T(8,128)(2,1)S(1)} async-done(((bf16[4,16,1536]{2,1,0:T(8,128)(2,1)}), bf16[4,16,1536]{2,1,0:T(8,128)(2,1)S(1)}, u32[]{:S(2)}, u32[]{:S(2)}) %all-to-all-start.4) | async-done | bytes 196640 | tf_op jit(solution)/shard_map/sum_texts/all_to_all | solution.py:26
  133.7 2.8 %collective-permute-done.11 = bf16[16,1536]{1,0:T(8,128)(2,1)S(1)} collective-permute-done((bf16[16,1536]{1,0:T(8,128)(2,1)S(1)}, bf16[16,1536]{1,0:T(8,128)(2,1)S(1)}, u32[]{:S(2)}, u32[]{:S(2)}) %collective-permute-start.11) | collective-permute-done | bytes 49184 | tf_op jit(solution)/shard_map/sum_images/ppermute | solution.py:44
  136.9 1.0 broadcast_in_dim.17
  137.9 3.5 %all-to-all-start.5 = ((bf16[8,2,16,1536]{3,2,1,0:T(8,128)(2,1)}), bf16[8,2,16,1536]{3,2,1,0:T(8,128)(2,1)S(1)}, u32[]{:S(2)}, u32[]{:S(2)}) async-start(bf16[8,2,16,1536]{3,2,1,0:T(8,128)(2,1)} %broadcast_in_dim.17), calls=%async_computation.5 | async-start | bytes 1572864 | tf_op jit(solution)/shard_map/head_grads/all_to_all | solution.py:26
  141.5 11.0 %all-to-all-done.5 = bf16[8,2,16,1536]{3,2,1,0:T(8,128)(2,1)S(1)} async-done(((bf16[8,2,16,1536]{3,2,1,0:T(8,128)(2,1)}), bf16[8,2,16,1536]{3,2,1,0:T(8,128)(2,1)S(1)}, u32[]{:S(2)}, u32[]{:S(2)}) %all-to-all-start.5) | async-done | bytes 786464 | tf_op jit(solution)/shard_map/head_grads/all_to_all | solution.py:26
  152.5 0.2 fusion.7
  152.7 0.2 fusion.8
  153.0 6.2 %collective-permute-start.14 = (bf16[2,96,1536]{2,1,0:T(8,128)(2,1)S(1)}, bf16[2,96,1536]{2,1,0:T(8,128)(2,1)S(1)}, u32[]{:S(2)}, u32[]{:S(2)}) collective-permute-start(bf16[2,96,1536]{2,1,0:T(8,128)(2,1)S(1)} %pad_maximum_fusion), channel_id=1, source_target_pairs={{0,8},{8,0},{1,9},{9,1},{2,10},{10,2},{3,11},{11,3},{4,12},{12,4},... | collective-permute-start | bytes 1769480 | tf_op jit(solution)/shard_map/weight_grads/ppermute | solution.py:40
  159.2 0.2 convolution_bitcast_fusion.1
  159.5 0.2 convolution_bitcast_fusion
  159.7 1.2 collective-permute-done.14
  161.0 11.4 %all_to_all.50 = bf16[4,48,1536]{2,1,0:T(8,128)(2,1)S(1)} all-to-all(bf16[4,48,1536]{2,1,0:T(8,128)(2,1)S(1)} %bitcast.90), channel_id=1, replica_groups=mesh['xl'=2,'zh'=4,'zm'=2,'z0'=2,'c'=2,'y'=4,'xh'=2] {'xl','z0'}, dimensions={0} | all-to-all | bytes 1179648 | tf_op jit(solution)/shard_map/weight_grads/all_to_all | solution.py:26
  172.6 21.7 %all_to_all.51 = bf16[8,24,384]{2,1,0:T(8,128)(2,1)S(1)} all-to-all(bf16[8,24,384]{2,1,0:T(8,128)(2,1)S(1)} %bitcast.95), channel_id=1, replica_groups=mesh['xl'=2,'zh'=4,'zm'=2,'z0'=2,'c'=2,'y'=4,'xh'=2] {'zh','zm'}, dimensions={0} | all-to-all | bytes 294912 | tf_op jit(solution)/shard_map/weight_grads/all_to_all | solution.py:26
  194.3 16.7 %all_to_all.52 = bf16[8,24,384]{2,1,0:T(8,128)(2,1)S(1)} all-to-all(bf16[8,24,384]{2,1,0:T(8,128)(2,1)S(1)} %broadcast_in_dim.18), channel_id=1, replica_groups=mesh['xl'=2,'zh'=4,'zm'=2,'z0'=2,'c'=2,'y'=4,'xh'=2] {'zh','zm'}, dimensions={0} | all-to-all | bytes 294912 | tf_op jit(solution)/shard_map/weight_grads/all_to_all | solution.py:26
  211.1 0.9 broadcast_in_dim.20
  211.9 3.6 %all-to-all-start.9 = ((bf16[4,48,1536]{2,1,0:T(8,128)(2,1)}), bf16[4,48,1536]{2,1,0:T(8,128)(2,1)S(1)}, u32[]{:S(2)}, u32[]{:S(2)}) async-start(bf16[4,48,1536]{2,1,0:T(8,128)(2,1)} %broadcast_in_dim.20), calls=%async_computation.9 | async-start | bytes 1179648 | tf_op jit(solution)/shard_map/weight_grads/all_to_all | solution.py:26
  215.6 1.0 fusion.59
  216.5 1.0 fusion.60
  217.5 4.4 %all-to-all-done.9 = bf16[4,48,1536]{2,1,0:T(8,128)(2,1)S(1)} async-done(((bf16[4,48,1536]{2,1,0:T(8,128)(2,1)}), bf16[4,48,1536]{2,1,0:T(8,128)(2,1)S(1)}, u32[]{:S(2)}, u32[]{:S(2)}) %all-to-all-start.9) | async-done | bytes 589856 | tf_op jit(solution)/shard_map/weight_grads/all_to_all | solution.py:26
  221.9 6.6 %collective-permute-start.15 = (bf16[2,96,1536]{2,1,0:T(8,128)(2,1)S(1)}, bf16[2,96,1536]{2,1,0:T(8,128)(2,1)S(1)}, u32[]{:S(2)}, u32[]{:S(2)}) collective-permute-start(bf16[2,96,1536]{2,1,0:T(8,128)(2,1)S(1)} %bitcast.89), channel_id=1, source_target_pairs={{0,8},{8,0},{1,9},{9,1},{2,10},{10,2},{3,11},{11,3},{4,12},{12,4},... | collective-permute-start | bytes 1769480 | tf_op jit(solution)/shard_map/weight_grads/ppermute | solution.py:40
  228.6 0.3 maximum_convert_fusion
  228.8 1.3 collective-permute-done.15
  230.3 1.0 copy-done.2
  231.3 0.4 copy-done.3
  (54 shorter events, 1.7 us)
Async XLA Ops:
  3.2 18.7 %all-to-all-start = ((bf16[8,16,3072]{2,1,0:T(8,128)(2,1)}), bf16[8,16,3072]{2,1,0:T(8,128)(2,1)S(1)}, u32[]{:S(2)}, u32[]{:S(2)}) async-start(bf16[8,16,3072]{2,1,0:T(8,128)(2,1)} %bitcast.88), calls=%async_computation | async-start | bytes 1572864 | tf_op jit(solution)/shard_map/heads/all_to_all | solution.py:26
  23.0 40.9 %all-to-all-start.1 = ((bf16[4,16,1536]{2,1,0:T(8,128)(2,1)}), bf16[4,16,1536]{2,1,0:T(8,128)(2,1)S(1)}, u32[]{:S(2)}, u32[]{:S(2)}) async-start(bf16[4,16,1536]{2,1,0:T(8,128)(2,1)} %broadcast_in_dim.14), calls=%async_computation.1 | async-start | bytes 393216 | tf_op jit(solution)/shard_map/gather_texts/all_to_all | solution.py:26
  39.9 11.3 %collective-permute-start.2 = (bf16[16,1536]{1,0:T(8,128)(2,1)S(1)}, bf16[16,1536]{1,0:T(8,128)(2,1)S(1)}, u32[]{:S(2)}, u32[]{:S(2)}) collective-permute-start(bf16[16,1536]{1,0:T(8,128)(2,1)S(1)} %get-tuple-element.9), channel_id=1, source_target_pairs={{0,48},{16,32},{32,16},{48,0},{1,49},{17,33},{33,17},{49,1},{2,50}... | collective-permute-start | bytes 147464 | tf_op jit(solution)/shard_map/gather_images/ppermute | solution.py:44
  43.4 11.4 %collective-permute-start.1 = (bf16[16,1536]{1,0:T(8,128)(2,1)S(1)}, bf16[16,1536]{1,0:T(8,128)(2,1)S(1)}, u32[]{:S(2)}, u32[]{:S(2)}) collective-permute-start(bf16[16,1536]{1,0:T(8,128)(2,1)S(1)} %get-tuple-element.9), channel_id=1, source_target_pairs={{0,32},{16,48},{32,0},{48,16},{1,33},{17,49},{33,1},{49,17},{2,34}... | collective-permute-start | bytes 147464 | tf_op jit(solution)/shard_map/gather_images/ppermute | solution.py:44
  45.6 9.3 %collective-permute-start = (bf16[16,1536]{1,0:T(8,128)(2,1)S(1)}, bf16[16,1536]{1,0:T(8,128)(2,1)S(1)}, u32[]{:S(2)}, u32[]{:S(2)}) collective-permute-start(bf16[16,1536]{1,0:T(8,128)(2,1)S(1)} %get-tuple-element.9), channel_id=1, source_target_pairs={{0,16},{16,0},{32,48},{48,32},{1,17},{17,1},{33,49},{49,33},{2,18}... | collective-permute-start | bytes 147464 | tf_op jit(solution)/shard_map/gather_images/ppermute | solution.py:44
  54.9 28.6 %collective-permute-start.5 = (bf16[64,1536]{1,0:T(8,128)(2,1)S(1)}, bf16[64,1536]{1,0:T(8,128)(2,1)S(1)}, u32[]{:S(2)}, u32[]{:S(2)}) collective-permute-start(bf16[64,1536]{1,0:T(8,128)(2,1)S(1)} %pad_maximum_fusion.1), channel_id=1, source_target_pairs={{0,6},{2,4},{4,2},{6,0},{1,7},{3,5},{5,3},{7,1},{8,14},{10,12},{12... | collective-permute-start | bytes 589832 | tf_op jit(solution)/shard_map/gather_images/ppermute | solution.py:44
  57.7 25.8 %collective-permute-start.4 = (bf16[64,1536]{1,0:T(8,128)(2,1)S(1)}, bf16[64,1536]{1,0:T(8,128)(2,1)S(1)}, u32[]{:S(2)}, u32[]{:S(2)}) collective-permute-start(bf16[64,1536]{1,0:T(8,128)(2,1)S(1)} %pad_maximum_fusion.1), channel_id=1, source_target_pairs={{0,4},{2,6},{4,0},{6,2},{1,5},{3,7},{5,1},{7,3},{8,12},{10,14},{12... | collective-permute-start | bytes 589832 | tf_op jit(solution)/shard_map/gather_images/ppermute | solution.py:44
  59.9 23.6 %collective-permute-start.3 = (bf16[64,1536]{1,0:T(8,128)(2,1)S(1)}, bf16[64,1536]{1,0:T(8,128)(2,1)S(1)}, u32[]{:S(2)}, u32[]{:S(2)}) collective-permute-start(bf16[64,1536]{1,0:T(8,128)(2,1)S(1)} %pad_maximum_fusion.1), channel_id=1, source_target_pairs={{0,2},{2,0},{4,6},{6,4},{1,3},{3,1},{5,7},{7,5},{8,10},{10,8},{12,... | collective-permute-start | bytes 589832 | tf_op jit(solution)/shard_map/gather_images/ppermute | solution.py:44
  64.8 14.3 %all-to-all-start.2 = ((bf16[4,64,1536]{2,1,0:T(8,128)(2,1)}), bf16[4,64,1536]{2,1,0:T(8,128)(2,1)S(1)}, u32[]{:S(2)}, u32[]{:S(2)}) async-start(bf16[4,64,1536]{2,1,0:T(8,128)(2,1)} %broadcast_in_dim.16), calls=%async_computation.2 | async-start | bytes 1572864 | tf_op jit(solution)/shard_map/gather_texts/all_to_all | solution.py:26
  79.1 6.2 %collective-permute-start.6 = (bf16[256,1536]{1,0:T(8,128)(2,1)S(1)}, bf16[256,1536]{1,0:T(8,128)(2,1)S(1)}, u32[]{:S(2)}, u32[]{:S(2)}) collective-permute-start(bf16[256,1536]{1,0:T(8,128)(2,1)S(1)} %bitcast.76), channel_id=1, source_target_pairs={{0,8},{8,0},{1,9},{9,1},{2,10},{10,2},{3,11},{11,3},{4,12},{12,4},... | collective-permute-start | bytes 2359304 | tf_op jit(solution)/shard_map/gather_texts/ppermute | solution.py:40
  86.2 6.8 %collective-permute-start.13 = (bf16[256,1536]{1,0:T(8,128)(2,1)S(1)}, bf16[256,1536]{1,0:T(8,128)(2,1)S(1)}, u32[]{:S(2)}, u32[]{:S(2)}) collective-permute-start(bf16[256,1536]{1,0:T(8,128)(2,1)S(1)} %convolution_convert_fusion), channel_id=1, source_target_pairs={{0,8},{8,0},{1,9},{9,1},{2,10},{10,2},{3,11},{11,3},{4,12},{12,4},... | collective-permute-start | bytes 2359304 | tf_op jit(solution)/shard_map/sum_texts/ppermute | solution.py:40
  90.2 30.3 %collective-permute-start.9 = (bf16[64,1536]{1,0:T(8,128)(2,1)}, bf16[64,1536]{1,0:T(8,128)(2,1)}, u32[]{:S(2)}, u32[]{:S(2)}) collective-permute-start(bf16[64,1536]{1,0:T(8,128)(2,1)} %fusion.6), channel_id=1, source_target_pairs={{0,6},{2,4},{4,2},{6,0},{1,7},{3,5},{5,3},{7,1},{8,14},{10,12},{12... | collective-permute-start | bytes 589832 | tf_op jit(solution)/shard_map/sum_images/ppermute | solution.py:44
  94.2 15.4 %all-to-all-start.3 = ((bf16[4,64,1536]{2,1,0:T(8,128)(2,1)}), bf16[4,64,1536]{2,1,0:T(8,128)(2,1)S(1)}, u32[]{:S(2)}, u32[]{:S(2)}) async-start(bf16[4,64,1536]{2,1,0:T(8,128)(2,1)} %bitcast.9), calls=%async_computation.3 | async-start | bytes 1572864 | tf_op jit(solution)/shard_map/sum_texts/all_to_all | solution.py:26
  98.7 21.8 %collective-permute-start.8 = (bf16[64,1536]{1,0:T(8,128)(2,1)}, bf16[64,1536]{1,0:T(8,128)(2,1)S(1)}, u32[]{:S(2)}, u32[]{:S(2)}) collective-permute-start(bf16[64,1536]{1,0:T(8,128)(2,1)} %fusion.5), channel_id=1, source_target_pairs={{0,4},{2,6},{4,0},{6,2},{1,5},{3,7},{5,1},{7,3},{8,12},{10,14},{12... | collective-permute-start | bytes 589832 | tf_op jit(solution)/shard_map/sum_images/ppermute | solution.py:44
  102.4 18.0 %collective-permute-start.7 = (bf16[64,1536]{1,0:T(8,128)(2,1)}, bf16[64,1536]{1,0:T(8,128)(2,1)S(1)}, u32[]{:S(2)}, u32[]{:S(2)}) collective-permute-start(bf16[64,1536]{1,0:T(8,128)(2,1)} %fusion.4), channel_id=1, source_target_pairs={{0,2},{2,0},{4,6},{6,4},{1,3},{3,1},{5,7},{7,5},{8,10},{10,8},{12,... | collective-permute-start | bytes 589832 | tf_op jit(solution)/shard_map/sum_images/ppermute | solution.py:44
  110.5 23.1 %all-to-all-start.4 = ((bf16[4,16,1536]{2,1,0:T(8,128)(2,1)}), bf16[4,16,1536]{2,1,0:T(8,128)(2,1)S(1)}, u32[]{:S(2)}, u32[]{:S(2)}) async-start(bf16[4,16,1536]{2,1,0:T(8,128)(2,1)} %bitcast.10), calls=%async_computation.4 | async-start | bytes 393216 | tf_op jit(solution)/shard_map/sum_texts/all_to_all | solution.py:26
  121.7 11.9 %collective-permute-start.10 = (bf16[16,1536]{1,0:T(8,128)(2,1)S(1)}, bf16[16,1536]{1,0:T(8,128)(2,1)S(1)}, u32[]{:S(2)}, u32[]{:S(2)}) collective-permute-start(bf16[16,1536]{1,0:T(8,128)(2,1)S(1)} %get-tuple-element.16), channel_id=1, source_target_pairs={{0,16},{16,0},{32,48},{48,32},{1,17},{17,1},{33,49},{49,33},{2,18}... | collective-permute-start | bytes 147464 | tf_op jit(solution)/shard_map/sum_images/ppermute | solution.py:44
  123.6 10.1 %collective-permute-start.12 = (bf16[16,1536]{1,0:T(8,128)(2,1)S(1)}, bf16[16,1536]{1,0:T(8,128)(2,1)S(1)}, u32[]{:S(2)}, u32[]{:S(2)}) collective-permute-start(bf16[16,1536]{1,0:T(8,128)(2,1)S(1)} %get-tuple-element.17), channel_id=1, source_target_pairs={{0,48},{16,32},{32,16},{48,0},{1,49},{17,33},{33,17},{49,1},{2,50}... | collective-permute-start | bytes 147464 | tf_op jit(solution)/shard_map/sum_images/ppermute | solution.py:44
  127.2 9.4 %collective-permute-start.11 = (bf16[16,1536]{1,0:T(8,128)(2,1)S(1)}, bf16[16,1536]{1,0:T(8,128)(2,1)S(1)}, u32[]{:S(2)}, u32[]{:S(2)}) collective-permute-start(bf16[16,1536]{1,0:T(8,128)(2,1)S(1)} %get-tuple-element.18), channel_id=1, source_target_pairs={{0,32},{16,48},{32,0},{48,16},{1,33},{17,49},{33,1},{49,17},{2,34}... | collective-permute-start | bytes 147464 | tf_op jit(solution)/shard_map/sum_images/ppermute | solution.py:44
  137.9 14.5 %all-to-all-start.5 = ((bf16[8,2,16,1536]{3,2,1,0:T(8,128)(2,1)}), bf16[8,2,16,1536]{3,2,1,0:T(8,128)(2,1)S(1)}, u32[]{:S(2)}, u32[]{:S(2)}) async-start(bf16[8,2,16,1536]{3,2,1,0:T(8,128)(2,1)} %broadcast_in_dim.17), calls=%async_computation.5 | async-start | bytes 1572864 | tf_op jit(solution)/shard_map/head_grads/all_to_all | solution.py:26
  141.4 11.1 %copy-start.4 = (bf16[128,192]{0,1:T(8,128)(2,1)S(1)}, bf16[128,192]{0,1:T(8,128)(2,1)}, u32[]{:S(2)}) copy-start(bf16[128,192]{0,1:T(8,128)(2,1)} %param.7) | copy-start | bytes 147460
  141.4 11.3 %copy-start.5 = (bf16[128,192]{0,1:T(8,128)(2,1)S(1)}, bf16[128,192]{0,1:T(8,128)(2,1)}, u32[]{:S(2)}) copy-start(bf16[128,192]{0,1:T(8,128)(2,1)} %param.8) | copy-start | bytes 147460
  153.0 7.8 %collective-permute-start.14 = (bf16[2,96,1536]{2,1,0:T(8,128)(2,1)S(1)}, bf16[2,96,1536]{2,1,0:T(8,128)(2,1)S(1)}, u32[]{:S(2)}, u32[]{:S(2)}) collective-permute-start(bf16[2,96,1536]{2,1,0:T(8,128)(2,1)S(1)} %pad_maximum_fusion), channel_id=1, source_target_pairs={{0,8},{8,0},{1,9},{9,1},{2,10},{10,2},{3,11},{11,3},{4,12},{12,4},... | collective-permute-start | bytes 1769480 | tf_op jit(solution)/shard_map/weight_grads/ppermute | solution.py:40
  211.0 4.5 %copy-start = (bf16[192,1536]{1,0:T(8,128)(2,1)S(1)}, bf16[192,1536]{1,0:T(8,128)(2,1)}, u32[]{:S(2)}) copy-start(bf16[192,1536]{1,0:T(8,128)(2,1)} %refs_1_.1) | copy-start | bytes 1769476
  211.9 4.6 %copy-start.1 = (bf16[192,1536]{1,0:T(8,128)(2,1)S(1)}, bf16[192,1536]{1,0:T(8,128)(2,1)}, u32[]{:S(2)}) copy-start(bf16[192,1536]{1,0:T(8,128)(2,1)} %refs_3_.1) | copy-start | bytes 1769476
  211.9 9.9 %all-to-all-start.9 = ((bf16[4,48,1536]{2,1,0:T(8,128)(2,1)}), bf16[4,48,1536]{2,1,0:T(8,128)(2,1)S(1)}, u32[]{:S(2)}, u32[]{:S(2)}) async-start(bf16[4,48,1536]{2,1,0:T(8,128)(2,1)} %broadcast_in_dim.20), calls=%async_computation.9 | async-start | bytes 1179648 | tf_op jit(solution)/shard_map/weight_grads/all_to_all | solution.py:26
  221.9 8.3 %collective-permute-start.15 = (bf16[2,96,1536]{2,1,0:T(8,128)(2,1)S(1)}, bf16[2,96,1536]{2,1,0:T(8,128)(2,1)S(1)}, u32[]{:S(2)}, u32[]{:S(2)}) collective-permute-start(bf16[2,96,1536]{2,1,0:T(8,128)(2,1)S(1)} %bitcast.89), channel_id=1, source_target_pairs={{0,8},{8,0},{1,9},{9,1},{2,10},{10,2},{3,11},{11,3},{4,12},{12,4},... | collective-permute-start | bytes 1769480 | tf_op jit(solution)/shard_map/weight_grads/ppermute | solution.py:40
  230.2 1.0 copy-start.2
  230.3 1.4 copy-start.3

commit v9 on v8

--- a/solution.py
+++ b/solution.py
@@ -44,15 +44,16 @@
     return lax.ppermute(value, axis, [(i, i ^ by) for i in range(count(axis))])
 
 
-def gather_pairs(rows, axis):
-    return jnp.concatenate([rows] + [swapped(rows, axis, k) for k in range(1, count(axis))], axis=0)
-
-
-def scatter_sum_pairs(blocks, axis):
-    own = blocks[0]
-    for k in range(1, count(axis)):
-        own = own + swapped(blocks[k].astype(BF16), axis, k).astype(F32)
-    return own
+def ring_gather(rows, axis):
+    rows = jnp.concatenate((rows, swapped(rows, axis, 1)), axis=0)
+    return jnp.concatenate((rows, swapped(rows, axis, 3)), axis=0)
+
+
+def ring_scatter_sum(total, axis):
+    for by in (3, 1):
+        kept, sent = split_rows(total, 2)
+        total = kept + swapped(sent.astype(BF16), axis, by).astype(F32)
+    return total
 
 
 def split_rows(value, n):
@@ -153,12 +154,14 @@
         image_unit, image_norm = unit_rows(both_heads[:, :embed_width])
         text_unit, text_norm = unit_rows(both_heads[:, embed_width:])
 
+    with jax.named_scope("gather_images"):
+        images = merge_rows(gather(image_unit.astype(BF16), ZL))
+        images = merge_rows(gather(images, "y"))
     with jax.named_scope("gather_texts"):
-        texts = merge_rows(gather(text_unit.astype(BF16), "zh"))
+        texts = ring_gather(text_unit.astype(BF16), "zh")
+        texts, images = lax.optimization_barrier((texts, images))
         texts = merge_rows(gather(texts, ("xh", "xl")))
         other_texts = shifted(texts, "c", 1)
-    with jax.named_scope("gather_images"):
-        images = gather_pairs(gather_pairs(image_unit.astype(BF16), ZL), "y")
 
     def coefficients(block, positive):
         scores = (
@@ -167,10 +170,11 @@
         return (factor * (jax.nn.sigmoid(scores) - positive)).astype(BF16)
 
     with jax.named_scope("pairs"):
-        text_base = ((at["xh"] * 2 + at["xl"]) * 4 + at["zh"]) * share
+        text_base = (at["xh"] * 2 + at["xl"]) * 4 * share
+        image_base = (at["y"] * 4 + at["zm"] * 2 + at["z0"]) * share
         text_at = jnp.arange(texts.shape[0], dtype=jnp.int32)[:, None] - text_base
-        image_at = jnp.arange(images.shape[0], dtype=jnp.int32)[None, :]
-        positive = (text_at == image_at) & (image_at < share)
+        image_at = jnp.arange(images.shape[0], dtype=jnp.int32)[None, :] - image_base
+        positive = (text_at == image_at) & (text_at >= 0) & (text_at < share)
         coeff = coefficients(texts, positive.astype(F32))
         other_coeff = coefficients(other_texts, 0.0)
         other_part = jnp.dot(other_coeff, images, preferred_element_type=F32)
@@ -178,20 +182,14 @@
 
     with jax.named_scope("sum_texts"):
         text_part = text_part + shifted(other_part.astype(BF16), "c", 1).astype(F32)
-        text_part = split_rows(text_part, count(("xh", "xl"))).astype(BF16)
-        text_part = scatter_sum(text_part, ("xh", "xl"))
-        text_grads = scatter_sum(split_rows(text_part, count("zh")), "zh")
+        text_part = scatter_sum(split_rows(text_part, count(("xh", "xl"))), ("xh", "xl"))
+        text_grads = ring_scatter_sum(text_part, "zh")
     with jax.named_scope("sum_images"):
-        rows = images.shape[0] // count("y")
-
-        def image_block(k):
-            at_rows = slice(k * rows, (k + 1) * rows)
-            return contract(coeff[:, at_rows], texts, 0, 0) + contract(
-                other_coeff[:, at_rows], other_texts, 0, 0
-            )
-
-        image_part = scatter_sum_pairs([image_block(k) for k in range(count("y"))], "y")
-        image_grads = scatter_sum_pairs(split_rows(image_part, count(ZL)), ZL)
+        image_part = contract(coeff, texts, 0, 0) + contract(other_coeff, other_texts, 0, 0)
+        image_part = split_rows(image_part, count("y")).astype(BF16)
+        image_part, text_part = lax.optimization_barrier((image_part, text_part))
+        image_part = scatter_sum(image_part, "y")
+        image_grads = scatter_sum(split_rows(image_part, count(ZL)), ZL)
 
     with jax.named_scope("head_grads"):
         grads = jnp.stack(

time: 233 us -> 244 us (1.047)
  blocking collectives: 49.8 us -> 98.6 us
  starting transfers between devices: 103 us -> 78.4 us
  waiting for transfers between devices: 54.9 us -> 45.4 us
  matrix products: 10.3 us -> 6.96 us
    all_to_all x3 -> x6, blocking collectives: 49.8 us -> 98.6 us  [exchange(): return lax.all_to_all(blocks, axes, split_axis=0, concat_axis=0, tiled=True)]
    all_to_all x7 -> x6, waiting for transfers between devices: 44.4 us -> 25.6 us  [exchange(): return lax.all_to_all(blocks, axes, split_axis=0, concat_axis=0, tiled=True)]
    all_to_all x7 -> x6, starting transfers between devices: 48.4 us -> 30.5 us  [exchange(): return lax.all_to_all(blocks, axes, split_axis=0, concat_axis=0, tiled=True)]
    ppermute x12 -> x4, starting transfers between devices: 35.6 us -> 20.9 us  [swapped(): return lax.ppermute(value, axis, [(i, i ^ by) for i in range(count(axis))])]
    ppermute x12 -> x4, waiting for transfers between devices: 6.69 us -> 15.7 us  [swapped(): return lax.ppermute(value, axis, [(i, i ^ by) for i in range(count(axis))])]
    ppermute x4, starting transfers between devices: 19.4 us -> 27 us  [shifted(): return lax.ppermute(value, axis, [(i, (i + by) % n) for i in range(n)])]
    dot_general x8 -> x2, matrix products: 5.04 us -> 0.78 us  [contract(): return lax.dot_general(left, right, dims, preferred_element_type=F32)]
  transfers between devices with their start and end apart: 23 -> 14, of which waited for: 12 -> 9; matrix products, arithmetic and copies ran while one was open for 5% -> 2% of each run, Pallas kernels for 0% -> 0%
where the time goes in v9:
time: 244 us; the launch traced here: 243 us
  blocking collectives  98.6 us (40%)
  starting transfers between devices  78.4 us (32%)
  waiting for transfers between devices  45.4 us (19%)
  matrix products  6.96 us (3%)
  local copies, waits for them, and re-layouts  5.18 us (2%)
  between operations  3.04 us (1%)
  Pallas kernels  2.59 us (1%)
    all_to_all x6, blocking collectives, exchange(): return lax.all_to_all(blocks, axes, split_axis=0, concat_axis=0, tiled=True)  98.6 us
    all_to_all x6, starting transfers between devices, exchange(): return lax.all_to_all(blocks, axes, split_axis=0, concat_axis=0, tiled=True)  30.5 us
    ppermute x4, starting transfers between devices, shifted(): return lax.ppermute(value, axis, [(i, (i + by) % n) for i in range(n)])  27 us
    all_to_all x6, waiting for transfers between devices, exchange(): return lax.all_to_all(blocks, axes, split_axis=0, concat_axis=0, tiled=True)  25.6 us
    ppermute x4, starting transfers between devices, swapped(): return lax.ppermute(value, axis, [(i, i ^ by) for i in range(count(axis))])  20.9 us
    ppermute x4, waiting for transfers between devices, swapped(): return lax.ppermute(value, axis, [(i, i ^ by) for i in range(count(axis))])  15.7 us
  transfers between devices with their start and end apart: 14, of which 9 were waited for; matrix products, arithmetic and copies ran while one was open for 2% of the time, Pallas kernels for 0%

profile of v9, /device:TPU:1, one launch (start us, length us, event | category | flops | bytes accessed | tf_op | source)
XLA Modules:
  0.0 242.6 jit_solution(2388952759149324565)
XLA Ops:
  0.6 2.6 %heads.1 = bf16[128,3072]{1,0:T(8,128)(2,1)} custom-call(bf16[192,128]{1,0:T(8,128)(2,1)} %bitcast.99, bf16[192,1536]{1,0:T(8,128)(2,1)} %refs_1_.1, bf16[192,128]{1,0:T(8,128)(2,1)} %bitcast.100, bf16[192,1536]{1,0:T(8,128)(2,1)} %refs_3_.1), custom_call_target="tpu_custom_call" | custom-call | flops 150994944 | bytes 2064384 | tf_op jit(solution)/shard_map/heads/pallas_call | solution.py:73
  3.2 19.1 %all_to_all.60 = bf16[8,16,3072]{2,1,0:T(8,128)(2,1)S(1)} all-to-all(bf16[8,16,3072]{2,1,0:T(8,128)(2,1)} %bitcast.88), channel_id=1, replica_groups=mesh['xl'=2,'zh'=4,'zm'=2,'z0'=2,'c'=2,'y'=4,'xh'=2] {'y','xh'}, dimensions={0} | all-to-all | bytes 1572864 | tf_op jit(solution)/shard_map/heads/all_to_all | solution.py:26
  22.3 0.1 reduce_sum.102
  22.4 0.1 fusion.20
  22.5 0.1 fusion.34
  22.6 0.7 broadcast_in_dim.16
  23.3 7.5 %all-to-all-start.1 = ((bf16[4,16,1536]{2,1,0:T(8,128)(2,1)}), bf16[4,16,1536]{2,1,0:T(8,128)(2,1)S(1)}, u32[]{:S(2)}, u32[]{:S(2)}) async-start(bf16[4,16,1536]{2,1,0:T(8,128)(2,1)} %broadcast_in_dim.16), calls=%async_computation.1 | async-start | bytes 393216 | tf_op jit(solution)/shard_map/gather_images/all_to_all | solution.py:26
  30.9 8.8 %collective-permute-start = (bf16[16,1536]{1,0:T(8,128)(2,1)S(1)}, bf16[16,1536]{1,0:T(8,128)(2,1)S(1)}, u32[]{:S(2)}, u32[]{:S(2)}) collective-permute-start(bf16[16,1536]{1,0:T(8,128)(2,1)S(1)} %get-tuple-element.23), channel_id=1, source_target_pairs={{0,64},{64,0},{128,192},{192,128},{1,65},{65,1},{129,193},{193,129... | collective-permute-start | bytes 147464 | tf_op jit(solution)/shard_map/gather_texts/ppermute | solution.py:44
  39.7 0.9 broadcast_in_dim.18
  40.6 3.5 %all-to-all-start.2 = ((bf16[4,64,1536]{2,1,0:T(8,128)(2,1)}), bf16[4,64,1536]{2,1,0:T(8,128)(2,1)S(1)}, u32[]{:S(2)}, u32[]{:S(2)}) async-start(bf16[4,64,1536]{2,1,0:T(8,128)(2,1)} %broadcast_in_dim.18), calls=%async_computation.2 | async-start | bytes 1572864 | tf_op jit(solution)/shard_map/gather_images/all_to_all | solution.py:26
  44.2 6.6 %collective-permute-start.1 = (bf16[32,1536]{1,0:T(8,128)(2,1)S(1)}, bf16[32,1536]{1,0:T(8,128)(2,1)S(1)}, u32[]{:S(2)}, u32[]{:S(2)}) collective-permute-start(bf16[32,1536]{1,0:T(8,128)(2,1)S(1)} %pad_maximum_fusion.2), channel_id=1, source_target_pairs={{0,192},{64,128},{128,64},{192,0},{1,193},{65,129},{129,65},{193,1... | collective-permute-start | bytes 294920 | tf_op jit(solution)/shard_map/gather_texts/ppermute | solution.py:44
  50.8 3.0 %collective-permute-done.1 = bf16[32,1536]{1,0:T(8,128)(2,1)S(1)} collective-permute-done((bf16[32,1536]{1,0:T(8,128)(2,1)S(1)}, bf16[32,1536]{1,0:T(8,128)(2,1)S(1)}, u32[]{:S(2)}, u32[]{:S(2)}) %collective-permute-start.1) | collective-permute-done | bytes 98336 | tf_op jit(solution)/shard_map/gather_texts/ppermute | solution.py:44
  53.7 0.1 broadcast_in_dim.19
  53.8 10.7 %all_to_all.61 = bf16[4,64,1536]{2,1,0:T(8,128)(2,1)S(1)} all-to-all(bf16[4,64,1536]{2,1,0:T(8,128)(2,1)S(1)} %broadcast_in_dim.19), channel_id=1, replica_groups=mesh['xl'=2,'zh'=4,'zm'=2,'z0'=2,'c'=2,'y'=4,'xh'=2] {'xh','xl'}, dimensions={0} | all-to-all | bytes 1572864 | tf_op jit(solution)/shard_map/gather_texts/all_to_all | solution.py:26
  64.6 9.8 %collective-permute-start.2 = (bf16[256,1536]{1,0:T(8,128)(2,1)S(1)}, bf16[256,1536]{1,0:T(8,128)(2,1)S(1)}, u32[]{:S(2)}, u32[]{:S(2)}) collective-permute-start(bf16[256,1536]{1,0:T(8,128)(2,1)S(1)} %bitcast.84), channel_id=1, source_target_pairs={{0,8},{8,0},{1,9},{9,1},{2,10},{10,2},{3,11},{11,3},{4,12},{12,4},... | collective-permute-start | bytes 2359304 | tf_op jit(solution)/shard_map/gather_texts/ppermute | solution.py:40
  76.3 0.4 fusion.17
  76.8 1.3 convolution_convert_fusion
  78.0 2.2 collective-permute-start.3
  80.3 0.5 fusion.18
  80.7 1.7 collective-permute-done.3
  82.4 1.3 add_convert_fusion
  83.6 3.5 %all-to-all-start.4 = ((bf16[4,64,1536]{2,1,0:T(8,128)(2,1)}), bf16[4,64,1536]{2,1,0:T(8,128)(2,1)S(1)}, u32[]{:S(2)}, u32[]{:S(2)}) async-start(bf16[4,64,1536]{2,1,0:T(8,128)(2,1)} %bitcast.10), calls=%async_computation.4 | async-start | bytes 1572864 | tf_op jit(solution)/shard_map/sum_texts/all_to_all | solution.py:26
  87.1 0.4 fusion.37
  87.5 0.4 fusion
  87.9 11.3 %all-to-all-done.4 = bf16[4,64,1536]{2,1,0:T(8,128)(2,1)S(1)} async-done(((bf16[4,64,1536]{2,1,0:T(8,128)(2,1)}), bf16[4,64,1536]{2,1,0:T(8,128)(2,1)S(1)}, u32[]{:S(2)}, u32[]{:S(2)}) %all-to-all-start.4) | async-done | bytes 786464 | tf_op jit(solution)/shard_map/sum_texts/all_to_all | solution.py:26
  99.2 0.1 convert_reduce_fusion
  99.3 14.3 %all_to_all.62 = bf16[4,64,1536]{2,1,0:T(8,128)(2,1)S(1)} all-to-all(bf16[4,64,1536]{2,1,0:T(8,128)(2,1)S(1)} %bitcast.87), channel_id=1, replica_groups=mesh['xl'=2,'zh'=4,'zm'=2,'z0'=2,'c'=2,'y'=4,'xh'=2] {'y'}, dimensions={0} | all-to-all | bytes 1572864 | tf_op jit(solution)/shard_map/sum_images/all_to_all | solution.py:26
  113.6 0.8 reduce_sum.106
  114.4 8.8 %all-to-all-start.6 = ((bf16[4,16,1536]{2,1,0:T(8,128)(2,1)}), bf16[4,16,1536]{2,1,0:T(8,128)(2,1)S(1)}, u32[]{:S(2)}, u32[]{:S(2)}) async-start(bf16[4,16,1536]{2,1,0:T(8,128)(2,1)} %bitcast.11), calls=%async_computation.6 | async-start | bytes 393216 | tf_op jit(solution)/shard_map/sum_images/all_to_all | solution.py:26
  123.3 2.5 %collective-permute-start.4 = (bf16[32,1536]{1,0:T(8,128)(2,1)S(1)}, bf16[32,1536]{1,0:T(8,128)(2,1)S(1)}, u32[]{:S(2)}, u32[]{:S(2)}) collective-permute-start(bf16[32,1536]{1,0:T(8,128)(2,1)S(1)} %unstack.34), channel_id=1, source_target_pairs={{0,192},{64,128},{128,64},{192,0},{1,193},{65,129},{129,65},{193,1... | collective-permute-start | bytes 294920 | tf_op jit(solution)/shard_map/sum_texts/ppermute | solution.py:44
  125.8 7.0 %collective-permute-done.4 = bf16[32,1536]{1,0:T(8,128)(2,1)S(1)} collective-permute-done((bf16[32,1536]{1,0:T(8,128)(2,1)S(1)}, bf16[32,1536]{1,0:T(8,128)(2,1)S(1)}, u32[]{:S(2)}, u32[]{:S(2)}) %collective-permute-start.4) | collective-permute-done | bytes 98336 | tf_op jit(solution)/shard_map/sum_texts/ppermute | solution.py:44
  132.9 3.0 %collective-permute-start.5 = (bf16[16,1536]{1,0:T(8,128)(2,1)S(1)}, bf16[16,1536]{1,0:T(8,128)(2,1)S(1)}, u32[]{:S(2)}, u32[]{:S(2)}) collective-permute-start(bf16[16,1536]{1,0:T(8,128)(2,1)S(1)} %unstack.35), channel_id=1, source_target_pairs={{0,64},{64,0},{128,192},{192,128},{1,65},{65,1},{129,193},{193,129... | collective-permute-start | bytes 147464 | tf_op jit(solution)/shard_map/sum_texts/ppermute | solution.py:44
  135.9 5.7 %collective-permute-done.5 = bf16[16,1536]{1,0:T(8,128)(2,1)S(1)} collective-permute-done((bf16[16,1536]{1,0:T(8,128)(2,1)S(1)}, bf16[16,1536]{1,0:T(8,128)(2,1)S(1)}, u32[]{:S(2)}, u32[]{:S(2)}) %collective-permute-start.5) | collective-permute-done | bytes 49184 | tf_op jit(solution)/shard_map/sum_texts/ppermute | solution.py:44
  141.6 0.2 multiply_reduce_fusion.1
  141.8 0.1 fusion.21
  142.0 1.0 broadcast_in_dim.20
  142.9 3.5 %all-to-all-start.7 = ((bf16[8,2,16,1536]{3,2,1,0:T(8,128)(2,1)}), bf16[8,2,16,1536]{3,2,1,0:T(8,128)(2,1)S(1)}, u32[]{:S(2)}, u32[]{:S(2)}) async-start(bf16[8,2,16,1536]{3,2,1,0:T(8,128)(2,1)} %broadcast_in_dim.20), calls=%async_computation.7 | async-start | bytes 1572864 | tf_op jit(solution)/shard_map/head_grads/all_to_all | solution.py:26
  146.5 10.5 %all-to-all-done.7 = bf16[8,2,16,1536]{3,2,1,0:T(8,128)(2,1)S(1)} async-done(((bf16[8,2,16,1536]{3,2,1,0:T(8,128)(2,1)}), bf16[8,2,16,1536]{3,2,1,0:T(8,128)(2,1)S(1)}, u32[]{:S(2)}, u32[]{:S(2)}) %all-to-all-start.7) | async-done | bytes 786464 | tf_op jit(solution)/shard_map/head_grads/all_to_all | solution.py:26
  157.0 0.1 fusion.35
  157.0 0.2 fusion.1
  157.3 0.2 fusion.2
  157.5 0.1 pad_maximum_fusion
  157.6 8.0 %collective-permute-start.6 = (bf16[2,96,1536]{2,1,0:T(8,128)(2,1)S(1)}, bf16[2,96,1536]{2,1,0:T(8,128)(2,1)S(1)}, u32[]{:S(2)}, u32[]{:S(2)}) collective-permute-start(bf16[2,96,1536]{2,1,0:T(8,128)(2,1)S(1)} %pad_maximum_fusion), channel_id=1, source_target_pairs={{0,8},{8,0},{1,9},{9,1},{2,10},{10,2},{3,11},{11,3},{4,12},{12,4},... | collective-permute-start | bytes 1769480 | tf_op jit(solution)/shard_map/weight_grads/ppermute | solution.py:40
  165.6 0.2 convolution_bitcast_fusion.1
  165.8 0.2 convolution_bitcast_fusion
  166.0 1.2 collective-permute-done.6
  167.2 0.1 fusion.3
  167.3 11.8 %all_to_all.63 = bf16[4,48,1536]{2,1,0:T(8,128)(2,1)S(1)} all-to-all(bf16[4,48,1536]{2,1,0:T(8,128)(2,1)S(1)} %bitcast.90), channel_id=1, replica_groups=mesh['xl'=2,'zh'=4,'zm'=2,'z0'=2,'c'=2,'y'=4,'xh'=2] {'xl','z0'}, dimensions={0} | all-to-all | bytes 1179648 | tf_op jit(solution)/shard_map/weight_grads/all_to_all | solution.py:26
  179.1 0.1 reduce_sum.110
  179.2 26.0 %all_to_all.64 = bf16[8,24,384]{2,1,0:T(8,128)(2,1)S(1)} all-to-all(bf16[8,24,384]{2,1,0:T(8,128)(2,1)S(1)} %bitcast.95), channel_id=1, replica_groups=mesh['xl'=2,'zh'=4,'zm'=2,'z0'=2,'c'=2,'y'=4,'xh'=2] {'zh','zm'}, dimensions={0} | all-to-all | bytes 294912 | tf_op jit(solution)/shard_map/weight_grads/all_to_all | solution.py:26
  205.3 16.7 %all_to_all.65 = bf16[8,24,384]{2,1,0:T(8,128)(2,1)S(1)} all-to-all(bf16[8,24,384]{2,1,0:T(8,128)(2,1)S(1)} %broadcast_in_dim.21), channel_id=1, replica_groups=mesh['xl'=2,'zh'=4,'zm'=2,'z0'=2,'c'=2,'y'=4,'xh'=2] {'zh','zm'}, dimensions={0} | all-to-all | bytes 294912 | tf_op jit(solution)/shard_map/weight_grads/all_to_all | solution.py:26
  222.0 0.1 copy.14
  222.1 0.9 broadcast_in_dim.23
  223.0 3.6 %all-to-all-start.11 = ((bf16[4,48,1536]{2,1,0:T(8,128)(2,1)}), bf16[4,48,1536]{2,1,0:T(8,128)(2,1)S(1)}, u32[]{:S(2)}, u32[]{:S(2)}) async-start(bf16[4,48,1536]{2,1,0:T(8,128)(2,1)} %broadcast_in_dim.23), calls=%async_computation.11 | async-start | bytes 1179648 | tf_op jit(solution)/shard_map/weight_grads/all_to_all | solution.py:26
  226.6 1.0 fusion.38
  227.6 1.0 fusion.39
  228.5 3.9 %all-to-all-done.11 = bf16[4,48,1536]{2,1,0:T(8,128)(2,1)S(1)} async-done(((bf16[4,48,1536]{2,1,0:T(8,128)(2,1)}), bf16[4,48,1536]{2,1,0:T(8,128)(2,1)S(1)}, u32[]{:S(2)}, u32[]{:S(2)}) %all-to-all-start.11) | async-done | bytes 589856 | tf_op jit(solution)/shard_map/weight_grads/all_to_all | solution.py:26
  232.4 7.0 %collective-permute-start.7 = (bf16[2,96,1536]{2,1,0:T(8,128)(2,1)S(1)}, bf16[2,96,1536]{2,1,0:T(8,128)(2,1)S(1)}, u32[]{:S(2)}, u32[]{:S(2)}) collective-permute-start(bf16[2,96,1536]{2,1,0:T(8,128)(2,1)S(1)} %bitcast.89), channel_id=1, source_target_pairs={{0,8},{8,0},{1,9},{9,1},{2,10},{10,2},{3,11},{11,3},{4,12},{12,4},... | collective-permute-start | bytes 1769480 | tf_op jit(solution)/shard_map/weight_grads/ppermute | solution.py:40
  239.5 0.1 maximum_convert_fusion
  239.6 0.1 maximum_convert_fusion.1
  239.7 1.3 collective-permute-done.7
  241.1 0.1 convert_dynamic-update-slice_fusion
  241.2 1.0 copy-done.2
  242.2 0.4 copy-done.3
  (31 shorter events, 0.3 us)
Async XLA Ops:
  23.3 16.4 %all-to-all-start.1 = ((bf16[4,16,1536]{2,1,0:T(8,128)(2,1)}), bf16[4,16,1536]{2,1,0:T(8,128)(2,1)S(1)}, u32[]{:S(2)}, u32[]{:S(2)}) async-start(bf16[4,16,1536]{2,1,0:T(8,128)(2,1)} %broadcast_in_dim.16), calls=%async_computation.1 | async-start | bytes 393216 | tf_op jit(solution)/shard_map/gather_images/all_to_all | solution.py:26
  30.9 13.3 %collective-permute-start = (bf16[16,1536]{1,0:T(8,128)(2,1)S(1)}, bf16[16,1536]{1,0:T(8,128)(2,1)S(1)}, u32[]{:S(2)}, u32[]{:S(2)}) collective-permute-start(bf16[16,1536]{1,0:T(8,128)(2,1)S(1)} %get-tuple-element.23), channel_id=1, source_target_pairs={{0,64},{64,0},{128,192},{192,128},{1,65},{65,1},{129,193},{193,129... | collective-permute-start | bytes 147464 | tf_op jit(solution)/shard_map/gather_texts/ppermute | solution.py:44
  40.6 13.1 %all-to-all-start.2 = ((bf16[4,64,1536]{2,1,0:T(8,128)(2,1)}), bf16[4,64,1536]{2,1,0:T(8,128)(2,1)S(1)}, u32[]{:S(2)}, u32[]{:S(2)}) async-start(bf16[4,64,1536]{2,1,0:T(8,128)(2,1)} %broadcast_in_dim.18), calls=%async_computation.2 | async-start | bytes 1572864 | tf_op jit(solution)/shard_map/gather_images/all_to_all | solution.py:26
  44.2 9.5 %collective-permute-start.1 = (bf16[32,1536]{1,0:T(8,128)(2,1)S(1)}, bf16[32,1536]{1,0:T(8,128)(2,1)S(1)}, u32[]{:S(2)}, u32[]{:S(2)}) collective-permute-start(bf16[32,1536]{1,0:T(8,128)(2,1)S(1)} %pad_maximum_fusion.2), channel_id=1, source_target_pairs={{0,192},{64,128},{128,64},{192,0},{1,193},{65,129},{129,65},{193,1... | collective-permute-start | bytes 294920 | tf_op jit(solution)/shard_map/gather_texts/ppermute | solution.py:44
  64.6 11.8 %collective-permute-start.2 = (bf16[256,1536]{1,0:T(8,128)(2,1)S(1)}, bf16[256,1536]{1,0:T(8,128)(2,1)S(1)}, u32[]{:S(2)}, u32[]{:S(2)}) collective-permute-start(bf16[256,1536]{1,0:T(8,128)(2,1)S(1)} %bitcast.84), channel_id=1, source_target_pairs={{0,8},{8,0},{1,9},{9,1},{2,10},{10,2},{3,11},{11,3},{4,12},{12,4},... | collective-permute-start | bytes 2359304 | tf_op jit(solution)/shard_map/gather_texts/ppermute | solution.py:40
  78.0 4.4 %collective-permute-start.3 = (bf16[256,1536]{1,0:T(8,128)(2,1)}, bf16[256,1536]{1,0:T(8,128)(2,1)S(1)}, u32[]{:S(2)}, u32[]{:S(2)}) collective-permute-start(bf16[256,1536]{1,0:T(8,128)(2,1)} %convolution_convert_fusion), channel_id=1, source_target_pairs={{0,8},{8,0},{1,9},{9,1},{2,10},{10,2},{3,11},{11,3},{4,12},{12,4},... | collective-permute-start | bytes 2359304 | tf_op jit(solution)/shard_map/sum_texts/ppermute | solution.py:40
  83.6 15.6 %all-to-all-start.4 = ((bf16[4,64,1536]{2,1,0:T(8,128)(2,1)}), bf16[4,64,1536]{2,1,0:T(8,128)(2,1)S(1)}, u32[]{:S(2)}, u32[]{:S(2)}) async-start(bf16[4,64,1536]{2,1,0:T(8,128)(2,1)} %bitcast.10), calls=%async_computation.4 | async-start | bytes 1572864 | tf_op jit(solution)/shard_map/sum_texts/all_to_all | solution.py:26
  114.4 21.4 %all-to-all-start.6 = ((bf16[4,16,1536]{2,1,0:T(8,128)(2,1)}), bf16[4,16,1536]{2,1,0:T(8,128)(2,1)S(1)}, u32[]{:S(2)}, u32[]{:S(2)}) async-start(bf16[4,16,1536]{2,1,0:T(8,128)(2,1)} %bitcast.11), calls=%async_computation.6 | async-start | bytes 393216 | tf_op jit(solution)/shard_map/sum_images/all_to_all | solution.py:26
  123.3 9.5 %collective-permute-start.4 = (bf16[32,1536]{1,0:T(8,128)(2,1)S(1)}, bf16[32,1536]{1,0:T(8,128)(2,1)S(1)}, u32[]{:S(2)}, u32[]{:S(2)}) collective-permute-start(bf16[32,1536]{1,0:T(8,128)(2,1)S(1)} %unstack.34), channel_id=1, source_target_pairs={{0,192},{64,128},{128,64},{192,0},{1,193},{65,129},{129,65},{193,1... | collective-permute-start | bytes 294920 | tf_op jit(solution)/shard_map/sum_texts/ppermute | solution.py:44
  132.9 8.7 %collective-permute-start.5 = (bf16[16,1536]{1,0:T(8,128)(2,1)S(1)}, bf16[16,1536]{1,0:T(8,128)(2,1)S(1)}, u32[]{:S(2)}, u32[]{:S(2)}) collective-permute-start(bf16[16,1536]{1,0:T(8,128)(2,1)S(1)} %unstack.35), channel_id=1, source_target_pairs={{0,64},{64,0},{128,192},{192,128},{1,65},{65,1},{129,193},{193,129... | collective-permute-start | bytes 147464 | tf_op jit(solution)/shard_map/sum_texts/ppermute | solution.py:44
  142.9 14.0 %all-to-all-start.7 = ((bf16[8,2,16,1536]{3,2,1,0:T(8,128)(2,1)}), bf16[8,2,16,1536]{3,2,1,0:T(8,128)(2,1)S(1)}, u32[]{:S(2)}, u32[]{:S(2)}) async-start(bf16[8,2,16,1536]{3,2,1,0:T(8,128)(2,1)} %broadcast_in_dim.20), calls=%async_computation.7 | async-start | bytes 1572864 | tf_op jit(solution)/shard_map/head_grads/all_to_all | solution.py:26
  146.5 10.5 %copy-start.4 = (bf16[128,192]{0,1:T(8,128)(2,1)S(1)}, bf16[128,192]{0,1:T(8,128)(2,1)}, u32[]{:S(2)}) copy-start(bf16[128,192]{0,1:T(8,128)(2,1)} %param.7) | copy-start | bytes 147460
  146.5 10.8 %copy-start.5 = (bf16[128,192]{0,1:T(8,128)(2,1)S(1)}, bf16[128,192]{0,1:T(8,128)(2,1)}, u32[]{:S(2)}) copy-start(bf16[128,192]{0,1:T(8,128)(2,1)} %param.8) | copy-start | bytes 147460
  157.6 9.6 %collective-permute-start.6 = (bf16[2,96,1536]{2,1,0:T(8,128)(2,1)S(1)}, bf16[2,96,1536]{2,1,0:T(8,128)(2,1)S(1)}, u32[]{:S(2)}, u32[]{:S(2)}) collective-permute-start(bf16[2,96,1536]{2,1,0:T(8,128)(2,1)S(1)} %pad_maximum_fusion), channel_id=1, source_target_pairs={{0,8},{8,0},{1,9},{9,1},{2,10},{10,2},{3,11},{11,3},{4,12},{12,4},... | collective-permute-start | bytes 1769480 | tf_op jit(solution)/shard_map/weight_grads/ppermute | solution.py:40
  222.1 4.5 %copy-start = (bf16[192,1536]{1,0:T(8,128)(2,1)S(1)}, bf16[192,1536]{1,0:T(8,128)(2,1)}, u32[]{:S(2)}) copy-start(bf16[192,1536]{1,0:T(8,128)(2,1)} %refs_1_.1) | copy-start | bytes 1769476
  223.0 4.6 %copy-start.1 = (bf16[192,1536]{1,0:T(8,128)(2,1)S(1)}, bf16[192,1536]{1,0:T(8,128)(2,1)}, u32[]{:S(2)}) copy-start(bf16[192,1536]{1,0:T(8,128)(2,1)} %refs_3_.1) | copy-start | bytes 1769476
  223.0 9.4 %all-to-all-start.11 = ((bf16[4,48,1536]{2,1,0:T(8,128)(2,1)}), bf16[4,48,1536]{2,1,0:T(8,128)(2,1)S(1)}, u32[]{:S(2)}, u32[]{:S(2)}) async-start(bf16[4,48,1536]{2,1,0:T(8,128)(2,1)} %broadcast_in_dim.23), calls=%async_computation.11 | async-start | bytes 1179648 | tf_op jit(solution)/shard_map/weight_grads/all_to_all | solution.py:26
  232.4 8.6 %collective-permute-start.7 = (bf16[2,96,1536]{2,1,0:T(8,128)(2,1)S(1)}, bf16[2,96,1536]{2,1,0:T(8,128)(2,1)S(1)}, u32[]{:S(2)}, u32[]{:S(2)}) collective-permute-start(bf16[2,96,1536]{2,1,0:T(8,128)(2,1)S(1)} %bitcast.89), channel_id=1, source_target_pairs={{0,8},{8,0},{1,9},{9,1},{2,10},{10,2},{3,11},{11,3},{4,12},{12,4},... | collective-permute-start | bytes 1769480 | tf_op jit(solution)/shard_map/weight_grads/ppermute | solution.py:40
  241.2 1.0 copy-start.2
  241.2 1.4 copy-start.3

commit v10 on v8

--- a/solution.py
+++ b/solution.py
@@ -40,18 +40,17 @@
     return lax.ppermute(value, axis, [(i, (i + by) % n) for i in range(n)])
 
 
-def swapped(value, axis, by):
-    return lax.ppermute(value, axis, [(i, i ^ by) for i in range(count(axis))])
-
-
-def gather_pairs(rows, axis):
-    return jnp.concatenate([rows] + [swapped(rows, axis, k) for k in range(1, count(axis))], axis=0)
-
-
-def scatter_sum_pairs(blocks, axis):
+def ring_gather(rows, axis):
+    n = count(axis)
+    return jnp.concatenate([rows] + [shifted(rows, axis, n - k) for k in range(1, n)], axis=0)
+
+
+def ring_scatter_sum(total, axis):
+    n = count(axis)
+    blocks = split_rows(total, n)
     own = blocks[0]
-    for k in range(1, count(axis)):
-        own = own + swapped(blocks[k].astype(BF16), axis, k).astype(F32)
+    for k in range(1, n):
+        own = own + shifted(blocks[k].astype(BF16), axis, k).astype(F32)
     return own
 
 
@@ -158,7 +157,7 @@
         texts = merge_rows(gather(texts, ("xh", "xl")))
         other_texts = shifted(texts, "c", 1)
     with jax.named_scope("gather_images"):
-        images = gather_pairs(gather_pairs(image_unit.astype(BF16), ZL), "y")
+        images = ring_gather(ring_gather(image_unit.astype(BF16), ZL), "y")
 
     def coefficients(block, positive):
         scores = (
@@ -175,23 +174,17 @@
         other_coeff = coefficients(other_texts, 0.0)
         other_part = jnp.dot(other_coeff, images, preferred_element_type=F32)
         text_part = jnp.dot(coeff, images, preferred_element_type=F32)
+        image_part = jnp.einsum("ti,te->ie", coeff, texts, preferred_element_type=F32)
+        image_part = image_part + jnp.einsum(
+            "ti,te->ie", other_coeff, other_texts, preferred_element_type=F32
+        )
 
     with jax.named_scope("sum_texts"):
         text_part = text_part + shifted(other_part.astype(BF16), "c", 1).astype(F32)
-        text_part = split_rows(text_part, count(("xh", "xl"))).astype(BF16)
-        text_part = scatter_sum(text_part, ("xh", "xl"))
+        text_part = scatter_sum(split_rows(text_part, count(("xh", "xl"))), ("xh", "xl"))
         text_grads = scatter_sum(split_rows(text_part, count("zh")), "zh")
     with jax.named_scope("sum_images"):
-        rows = images.shape[0] // count("y")
-
-        def image_block(k):
-            at_rows = slice(k * rows, (k + 1) * rows)
-            return contract(coeff[:, at_rows], texts, 0, 0) + contract(
-                other_coeff[:, at_rows], other_texts, 0, 0
-            )
-
-        image_part = scatter_sum_pairs([image_block(k) for k in range(count("y"))], "y")
-        image_grads = scatter_sum_pairs(split_rows(image_part, count(ZL)), ZL)
+        image_grads = ring_scatter_sum(ring_scatter_sum(image_part, "y"), ZL)
 
     with jax.named_scope("head_grads"):
         grads = jnp.stack(

time: 233 us -> 221 us (0.948)
  waiting for transfers between devices: 54.9 us -> 40 us
  starting transfers between devices: 103 us -> 109 us
  matrix products: 10.3 us -> 6.03 us
    ppermute x4 -> x16, starting transfers between devices: 19.4 us -> 62.4 us  [shifted(): return lax.ppermute(value, axis, [(i, (i + by) % n) for i in range(n)])]
    ppermute x12 -> x0, starting transfers between devices: 35.6 us -> none  [swapped(): return lax.ppermute(value, axis, [(i, i ^ by) for i in range(count(axis))])]
    all_to_all x7, waiting for transfers between devices: 44.4 us -> 34.5 us  [exchange(): return lax.all_to_all(blocks, axes, split_axis=0, concat_axis=0, tiled=True)]
    ppermute x12 -> x0, waiting for transfers between devices: 6.69 us -> none  [swapped(): return lax.ppermute(value, axis, [(i, i ^ by) for i in range(count(axis))])]
    dot_general x8 -> x2, matrix products: 5.04 us -> 0.78 us  [the longest x1 0.39 us: on_device(): jnp.einsum('ti,te->ie', other_coeff, other_texts, preferred_element_type=...]
    ppermute x4 -> x16, waiting for transfers between devices: 3.79 us -> 5.5 us  [shifted(): return lax.ppermute(value, axis, [(i, (i + by) % n) for i in range(n)])]
  transfers between devices with their start and end apart: 23 -> 23, of which waited for: 12 -> 11; matrix products, arithmetic and copies ran while one was open for 5% -> 3% of each run, Pallas kernels for 0% -> 0%
where the time goes in v10:
time: 221 us; the launch traced here: 220 us
  starting transfers between devices  109 us (49%)
  blocking collectives  51.5 us (23%)
  waiting for transfers between devices  40 us (18%)
  matrix products  6.03 us (3%)
  local copies, waits for them, and re-layouts  5.95 us (3%)
  between operations  3.12 us (1%)
  Pallas kernels  2.59 us (1%)
  other arithmetic  2.37 us (1%)
    ppermute x16, starting transfers between devices, shifted(): return lax.ppermute(value, axis, [(i, (i + by) % n) for i in range(n)])  62.4 us
    all_to_all x3, blocking collectives, exchange(): return lax.all_to_all(blocks, axes, split_axis=0, concat_axis=0, tiled=True)  51.5 us
    all_to_all x7, starting transfers between devices, exchange(): return lax.all_to_all(blocks, axes, split_axis=0, concat_axis=0, tiled=True)  46.3 us
    all_to_all x7, waiting for transfers between devices, exchange(): return lax.all_to_all(blocks, axes, split_axis=0, concat_axis=0, tiled=True)  34.5 us
    ppermute x16, waiting for transfers between devices, shifted(): return lax.ppermute(value, axis, [(i, (i + by) % n) for i in range(n)])  5.5 us
  transfers between devices with their start and end apart: 23, of which 11 were waited for; matrix products, arithmetic and copies ran while one was open for 3% of the time, Pallas kernels for 0%

profile of v10, /device:TPU:1, one launch (start us, length us, event | category | flops | bytes accessed | tf_op | source)
XLA Modules:
  0.0 220.3 jit_solution(15085277821835304834)
XLA Ops:
  0.6 2.6 %heads.1 = bf16[128,3072]{1,0:T(8,128)(2,1)} custom-call(bf16[192,128]{1,0:T(8,128)(2,1)} %bitcast.92, bf16[192,1536]{1,0:T(8,128)(2,1)} %refs_1_.1, bf16[192,128]{1,0:T(8,128)(2,1)} %bitcast.93, bf16[192,1536]{1,0:T(8,128)(2,1)} %refs_3_.1), custom_call_target="tpu_custom_call" | custom-call | flops 150994944 | bytes 2064384 | tf_op jit(solution)/shard_map/heads/pallas_call | solution.py:71
  3.2 7.5 %all-to-all-start = ((bf16[8,16,3072]{2,1,0:T(8,128)(2,1)}), bf16[8,16,3072]{2,1,0:T(8,128)(2,1)S(1)}, u32[]{:S(2)}, u32[]{:S(2)}) async-start(bf16[8,16,3072]{2,1,0:T(8,128)(2,1)} %bitcast.81), calls=%async_computation | async-start | bytes 1572864 | tf_op jit(solution)/shard_map/heads/all_to_all | solution.py:26
  10.7 11.2 %all-to-all-done = bf16[8,16,3072]{2,1,0:T(8,128)(2,1)S(1)} async-done(((bf16[8,16,3072]{2,1,0:T(8,128)(2,1)}), bf16[8,16,3072]{2,1,0:T(8,128)(2,1)S(1)}, u32[]{:S(2)}, u32[]{:S(2)}) %all-to-all-start) | async-done | bytes 786464 | tf_op jit(solution)/shard_map/heads/all_to_all | solution.py:26
  22.1 0.1 fusion.23
  22.3 0.7 broadcast_in_dim.14
  23.0 16.8 %all-to-all-start.1 = ((bf16[4,16,1536]{2,1,0:T(8,128)(2,1)}), bf16[4,16,1536]{2,1,0:T(8,128)(2,1)S(1)}, u32[]{:S(2)}, u32[]{:S(2)}) async-start(bf16[4,16,1536]{2,1,0:T(8,128)(2,1)} %broadcast_in_dim.14), calls=%async_computation.1 | async-start | bytes 393216 | tf_op jit(solution)/shard_map/gather_texts/all_to_all | solution.py:26
  39.8 2.6 %collective-permute-start.2 = (bf16[16,1536]{1,0:T(8,128)(2,1)S(1)}, bf16[16,1536]{1,0:T(8,128)(2,1)S(1)}, u32[]{:S(2)}, u32[]{:S(2)}) collective-permute-start(bf16[16,1536]{1,0:T(8,128)(2,1)S(1)} %get-tuple-element.11), channel_id=1, source_target_pairs={{0,16},{16,32},{32,48},{48,0},{1,17},{17,33},{33,49},{49,1},{2,18}... | collective-permute-start | bytes 147464 | tf_op jit(solution)/shard_map/gather_images/ppermute | solution.py:40
  42.5 3.1 %collective-permute-start.1 = (bf16[16,1536]{1,0:T(8,128)(2,1)S(1)}, bf16[16,1536]{1,0:T(8,128)(2,1)S(1)}, u32[]{:S(2)}, u32[]{:S(2)}) collective-permute-start(bf16[16,1536]{1,0:T(8,128)(2,1)S(1)} %get-tuple-element.11), channel_id=1, source_target_pairs={{0,32},{16,48},{32,0},{48,16},{1,33},{17,49},{33,1},{49,17},{2,34}... | collective-permute-start | bytes 147464 | tf_op jit(solution)/shard_map/gather_images/ppermute | solution.py:40
  45.6 3.5 %collective-permute-start = (bf16[16,1536]{1,0:T(8,128)(2,1)S(1)}, bf16[16,1536]{1,0:T(8,128)(2,1)S(1)}, u32[]{:S(2)}, u32[]{:S(2)}) collective-permute-start(bf16[16,1536]{1,0:T(8,128)(2,1)S(1)} %get-tuple-element.11), channel_id=1, source_target_pairs={{0,48},{16,0},{32,16},{48,32},{1,49},{17,1},{33,17},{49,33},{2,50}... | collective-permute-start | bytes 147464 | tf_op jit(solution)/shard_map/gather_images/ppermute | solution.py:40
  51.1 1.5 all-to-all-done.1
  52.6 0.9 broadcast_in_dim.16
  53.5 3.5 %all-to-all-start.2 = ((bf16[4,64,1536]{2,1,0:T(8,128)(2,1)}), bf16[4,64,1536]{2,1,0:T(8,128)(2,1)S(1)}, u32[]{:S(2)}, u32[]{:S(2)}) async-start(bf16[4,64,1536]{2,1,0:T(8,128)(2,1)} %broadcast_in_dim.16), calls=%async_computation.2 | async-start | bytes 1572864 | tf_op jit(solution)/shard_map/gather_texts/all_to_all | solution.py:26
  57.1 1.9 collective-permute-start.5
  59.0 4.0 %collective-permute-start.4 = (bf16[64,1536]{1,0:T(8,128)(2,1)S(1)}, bf16[64,1536]{1,0:T(8,128)(2,1)S(1)}, u32[]{:S(2)}, u32[]{:S(2)}) collective-permute-start(bf16[64,1536]{1,0:T(8,128)(2,1)S(1)} %pad_maximum_fusion.1), channel_id=1, source_target_pairs={{0,4},{2,6},{4,0},{6,2},{1,5},{3,7},{5,1},{7,3},{8,12},{10,14},{12... | collective-permute-start | bytes 589832 | tf_op jit(solution)/shard_map/gather_images/ppermute | solution.py:40
  63.0 2.8 %collective-permute-start.3 = (bf16[64,1536]{1,0:T(8,128)(2,1)S(1)}, bf16[64,1536]{1,0:T(8,128)(2,1)S(1)}, u32[]{:S(2)}, u32[]{:S(2)}) collective-permute-start(bf16[64,1536]{1,0:T(8,128)(2,1)S(1)} %pad_maximum_fusion.1), channel_id=1, source_target_pairs={{0,6},{2,0},{4,2},{6,4},{1,7},{3,1},{5,3},{7,5},{8,14},{10,8},{12,... | collective-permute-start | bytes 589832 | tf_op jit(solution)/shard_map/gather_images/ppermute | solution.py:40
  65.8 10.1 %collective-permute-start.6 = (bf16[256,1536]{1,0:T(8,128)(2,1)S(1)}, bf16[256,1536]{1,0:T(8,128)(2,1)S(1)}, u32[]{:S(2)}, u32[]{:S(2)}) collective-permute-start(bf16[256,1536]{1,0:T(8,128)(2,1)S(1)} %bitcast.78), channel_id=1, source_target_pairs={{0,8},{8,0},{1,9},{9,1},{2,10},{10,2},{3,11},{11,3},{4,12},{12,4},... | collective-permute-start | bytes 2359304 | tf_op jit(solution)/shard_map/gather_texts/ppermute | solution.py:40
  76.0 1.8 collective-permute-done.6
  77.8 0.4 fusion.17
  78.2 0.4 convolution_convert_fusion
  78.6 2.6 %collective-permute-start.13 = (bf16[256,1536]{1,0:T(8,128)(2,1)S(1)}, bf16[256,1536]{1,0:T(8,128)(2,1)S(1)}, u32[]{:S(2)}, u32[]{:S(2)}) collective-permute-start(bf16[256,1536]{1,0:T(8,128)(2,1)S(1)} %convolution_convert_fusion), channel_id=1, source_target_pairs={{0,8},{8,0},{1,9},{9,1},{2,10},{10,2},{3,11},{11,3},{4,12},{12,4},... | collective-permute-start | bytes 2359304 | tf_op jit(solution)/shard_map/sum_texts/ppermute | solution.py:40
  81.3 0.4 fusion.18
  81.7 0.4 fusion.46
  82.1 0.4 fusion.45
  82.5 0.7 collective-permute-done.13
  83.1 1.3 fusion
  84.4 4.5 %all-to-all-start.3 = ((bf16[4,64,1536]{2,1,0:T(8,128)(2,1)}), bf16[4,64,1536]{2,1,0:T(8,128)(2,1)S(1)}, u32[]{:S(2)}, u32[]{:S(2)}) async-start(bf16[4,64,1536]{2,1,0:T(8,128)(2,1)} %bitcast.9), calls=%async_computation.3 | async-start | bytes 1572864 | tf_op jit(solution)/shard_map/sum_texts/all_to_all | solution.py:26
  88.9 0.8 fusion.42
  89.6 3.0 %collective-permute-start.7 = (bf16[64,1536]{1,0:T(8,128)(2,1)}, bf16[64,1536]{1,0:T(8,128)(2,1)S(1)}, u32[]{:S(2)}, u32[]{:S(2)}) collective-permute-start(bf16[64,1536]{1,0:T(8,128)(2,1)} %get-tuple-element.14), channel_id=1, source_target_pairs={{0,2},{2,4},{4,6},{6,0},{1,3},{3,5},{5,7},{7,1},{8,10},{10,12},{12... | collective-permute-start | bytes 589832 | tf_op jit(solution)/shard_map/sum_images/ppermute | solution.py:40
  92.7 3.4 %collective-permute-start.9 = (bf16[64,1536]{1,0:T(8,128)(2,1)}, bf16[64,1536]{1,0:T(8,128)(2,1)S(1)}, u32[]{:S(2)}, u32[]{:S(2)}) collective-permute-start(bf16[64,1536]{1,0:T(8,128)(2,1)} %get-tuple-element.15), channel_id=1, source_target_pairs={{0,6},{2,0},{4,2},{6,4},{1,7},{3,1},{5,3},{7,5},{8,14},{10,8},{12,... | collective-permute-start | bytes 589832 | tf_op jit(solution)/shard_map/sum_images/ppermute | solution.py:40
  96.1 2.5 %collective-permute-start.8 = (bf16[64,1536]{1,0:T(8,128)(2,1)S(1)}, bf16[64,1536]{1,0:T(8,128)(2,1)S(1)}, u32[]{:S(2)}, u32[]{:S(2)}) collective-permute-start(bf16[64,1536]{1,0:T(8,128)(2,1)S(1)} %get-tuple-element.16), channel_id=1, source_target_pairs={{0,4},{2,6},{4,0},{6,2},{1,5},{3,7},{5,1},{7,3},{8,12},{10,14},{12... | collective-permute-start | bytes 589832 | tf_op jit(solution)/shard_map/sum_images/ppermute | solution.py:40
  98.7 1.9 all-to-all-done.3
  100.6 0.8 reduce_sum.97
  101.4 5.9 %all-to-all-start.4 = ((bf16[4,16,1536]{2,1,0:T(8,128)(2,1)}), bf16[4,16,1536]{2,1,0:T(8,128)(2,1)S(1)}, u32[]{:S(2)}, u32[]{:S(2)}) async-start(bf16[4,16,1536]{2,1,0:T(8,128)(2,1)} %bitcast.10), calls=%async_computation.4 | async-start | bytes 393216 | tf_op jit(solution)/shard_map/sum_texts/all_to_all | solution.py:26
  107.4 1.9 collective-permute-start.10
  109.4 5.2 %collective-permute-start.12 = (bf16[16,1536]{1,0:T(8,128)(2,1)S(1)}, bf16[16,1536]{1,0:T(8,128)(2,1)S(1)}, u32[]{:S(2)}, u32[]{:S(2)}) collective-permute-start(bf16[16,1536]{1,0:T(8,128)(2,1)S(1)} %get-tuple-element.22), channel_id=1, source_target_pairs={{0,48},{16,0},{32,16},{48,32},{1,49},{17,1},{33,17},{49,33},{2,50}... | collective-permute-start | bytes 147464 | tf_op jit(solution)/shard_map/sum_images/ppermute | solution.py:40
  114.5 1.9 collective-permute-start.11
  116.5 4.4 %all-to-all-done.4 = bf16[4,16,1536]{2,1,0:T(8,128)(2,1)S(1)} async-done(((bf16[4,16,1536]{2,1,0:T(8,128)(2,1)}), bf16[4,16,1536]{2,1,0:T(8,128)(2,1)S(1)}, u32[]{:S(2)}, u32[]{:S(2)}) %all-to-all-start.4) | async-done | bytes 196640 | tf_op jit(solution)/shard_map/sum_texts/all_to_all | solution.py:26
  120.9 0.6 collective-permute-done.11
  121.5 0.2 multiply_reduce_fusion.1
  121.7 0.1 fusion.26
  121.8 1.0 broadcast_in_dim.17
  122.8 4.4 %all-to-all-start.5 = ((bf16[8,2,16,1536]{3,2,1,0:T(8,128)(2,1)}), bf16[8,2,16,1536]{3,2,1,0:T(8,128)(2,1)S(1)}, u32[]{:S(2)}, u32[]{:S(2)}) async-start(bf16[8,2,16,1536]{3,2,1,0:T(8,128)(2,1)} %broadcast_in_dim.17), calls=%async_computation.5 | async-start | bytes 1572864 | tf_op jit(solution)/shard_map/head_grads/all_to_all | solution.py:26
  127.2 10.5 %all-to-all-done.5 = bf16[8,2,16,1536]{3,2,1,0:T(8,128)(2,1)S(1)} async-done(((bf16[8,2,16,1536]{3,2,1,0:T(8,128)(2,1)}), bf16[8,2,16,1536]{3,2,1,0:T(8,128)(2,1)S(1)}, u32[]{:S(2)}, u32[]{:S(2)}) %all-to-all-start.5) | async-done | bytes 786464 | tf_op jit(solution)/shard_map/head_grads/all_to_all | solution.py:26
  137.8 0.2 fusion.1
  138.1 0.2 fusion.2
  138.3 8.4 %collective-permute-start.14 = (bf16[2,96,1536]{2,1,0:T(8,128)(2,1)S(1)}, bf16[2,96,1536]{2,1,0:T(8,128)(2,1)S(1)}, u32[]{:S(2)}, u32[]{:S(2)}) collective-permute-start(bf16[2,96,1536]{2,1,0:T(8,128)(2,1)S(1)} %pad_maximum_fusion), channel_id=1, source_target_pairs={{0,8},{8,0},{1,9},{9,1},{2,10},{10,2},{3,11},{11,3},{4,12},{12,4},... | collective-permute-start | bytes 1769480 | tf_op jit(solution)/shard_map/weight_grads/ppermute | solution.py:40
  146.7 0.2 convolution_bitcast_fusion.1
  146.9 0.2 convolution_bitcast_fusion
  147.2 1.2 collective-permute-done.14
  148.4 11.4 %all_to_all.50 = bf16[4,48,1536]{2,1,0:T(8,128)(2,1)S(1)} all-to-all(bf16[4,48,1536]{2,1,0:T(8,128)(2,1)S(1)} %bitcast.83), channel_id=1, replica_groups=mesh['xl'=2,'zh'=4,'zm'=2,'z0'=2,'c'=2,'y'=4,'xh'=2] {'xl','z0'}, dimensions={0} | all-to-all | bytes 1179648 | tf_op jit(solution)/shard_map/weight_grads/all_to_all | solution.py:26
  160.0 22.1 %all_to_all.51 = bf16[8,24,384]{2,1,0:T(8,128)(2,1)S(1)} all-to-all(bf16[8,24,384]{2,1,0:T(8,128)(2,1)S(1)} %bitcast.88), channel_id=1, replica_groups=mesh['xl'=2,'zh'=4,'zm'=2,'z0'=2,'c'=2,'y'=4,'xh'=2] {'zh','zm'}, dimensions={0} | all-to-all | bytes 294912 | tf_op jit(solution)/shard_map/weight_grads/all_to_all | solution.py:26
  182.1 18.0 %all_to_all.52 = bf16[8,24,384]{2,1,0:T(8,128)(2,1)S(1)} all-to-all(bf16[8,24,384]{2,1,0:T(8,128)(2,1)S(1)} %broadcast_in_dim.18), channel_id=1, replica_groups=mesh['xl'=2,'zh'=4,'zm'=2,'z0'=2,'c'=2,'y'=4,'xh'=2] {'zh','zm'}, dimensions={0} | all-to-all | bytes 294912 | tf_op jit(solution)/shard_map/weight_grads/all_to_all | solution.py:26
  200.2 0.9 broadcast_in_dim.20
  201.1 3.7 %all-to-all-start.9 = ((bf16[4,48,1536]{2,1,0:T(8,128)(2,1)}), bf16[4,48,1536]{2,1,0:T(8,128)(2,1)S(1)}, u32[]{:S(2)}, u32[]{:S(2)}) async-start(bf16[4,48,1536]{2,1,0:T(8,128)(2,1)} %broadcast_in_dim.20), calls=%async_computation.9 | async-start | bytes 1179648 | tf_op jit(solution)/shard_map/weight_grads/all_to_all | solution.py:26
  204.8 0.9 fusion.47
  205.8 0.9 fusion.48
  206.7 5.0 %all-to-all-done.9 = bf16[4,48,1536]{2,1,0:T(8,128)(2,1)S(1)} async-done(((bf16[4,48,1536]{2,1,0:T(8,128)(2,1)}), bf16[4,48,1536]{2,1,0:T(8,128)(2,1)S(1)}, u32[]{:S(2)}, u32[]{:S(2)}) %all-to-all-start.9) | async-done | bytes 589856 | tf_op jit(solution)/shard_map/weight_grads/all_to_all | solution.py:26
  211.7 5.4 %collective-permute-start.15 = (bf16[2,96,1536]{2,1,0:T(8,128)(2,1)S(1)}, bf16[2,96,1536]{2,1,0:T(8,128)(2,1)S(1)}, u32[]{:S(2)}, u32[]{:S(2)}) collective-permute-start(bf16[2,96,1536]{2,1,0:T(8,128)(2,1)S(1)} %bitcast.82), channel_id=1, source_target_pairs={{0,8},{8,0},{1,9},{9,1},{2,10},{10,2},{3,11},{11,3},{4,12},{12,4},... | collective-permute-start | bytes 1769480 | tf_op jit(solution)/shard_map/weight_grads/ppermute | solution.py:40
  217.2 0.1 maximum_convert_fusion
  217.3 0.1 maximum_convert_fusion.1
  217.4 1.3 collective-permute-done.15
  218.7 0.1 convert_dynamic-update-slice_fusion
  218.9 1.0 copy-done.2
  219.9 0.4 copy-done.3
  (50 shorter events, 1.1 us)
Async XLA Ops:
  3.2 18.7 %all-to-all-start = ((bf16[8,16,3072]{2,1,0:T(8,128)(2,1)}), bf16[8,16,3072]{2,1,0:T(8,128)(2,1)S(1)}, u32[]{:S(2)}, u32[]{:S(2)}) async-start(bf16[8,16,3072]{2,1,0:T(8,128)(2,1)} %bitcast.81), calls=%async_computation | async-start | bytes 1572864 | tf_op jit(solution)/shard_map/heads/all_to_all | solution.py:26
  23.0 29.6 %all-to-all-start.1 = ((bf16[4,16,1536]{2,1,0:T(8,128)(2,1)}), bf16[4,16,1536]{2,1,0:T(8,128)(2,1)S(1)}, u32[]{:S(2)}, u32[]{:S(2)}) async-start(bf16[4,16,1536]{2,1,0:T(8,128)(2,1)} %broadcast_in_dim.14), calls=%async_computation.1 | async-start | bytes 393216 | tf_op jit(solution)/shard_map/gather_texts/all_to_all | solution.py:26
  39.8 17.2 %collective-permute-start.2 = (bf16[16,1536]{1,0:T(8,128)(2,1)S(1)}, bf16[16,1536]{1,0:T(8,128)(2,1)S(1)}, u32[]{:S(2)}, u32[]{:S(2)}) collective-permute-start(bf16[16,1536]{1,0:T(8,128)(2,1)S(1)} %get-tuple-element.11), channel_id=1, source_target_pairs={{0,16},{16,32},{32,48},{48,0},{1,17},{17,33},{33,49},{49,1},{2,18}... | collective-permute-start | bytes 147464 | tf_op jit(solution)/shard_map/gather_images/ppermute | solution.py:40
  42.5 14.5 %collective-permute-start.1 = (bf16[16,1536]{1,0:T(8,128)(2,1)S(1)}, bf16[16,1536]{1,0:T(8,128)(2,1)S(1)}, u32[]{:S(2)}, u32[]{:S(2)}) collective-permute-start(bf16[16,1536]{1,0:T(8,128)(2,1)S(1)} %get-tuple-element.11), channel_id=1, source_target_pairs={{0,32},{16,48},{32,0},{48,16},{1,33},{17,49},{33,1},{49,17},{2,34}... | collective-permute-start | bytes 147464 | tf_op jit(solution)/shard_map/gather_images/ppermute | solution.py:40
  45.6 11.4 %collective-permute-start = (bf16[16,1536]{1,0:T(8,128)(2,1)S(1)}, bf16[16,1536]{1,0:T(8,128)(2,1)S(1)}, u32[]{:S(2)}, u32[]{:S(2)}) collective-permute-start(bf16[16,1536]{1,0:T(8,128)(2,1)S(1)} %get-tuple-element.11), channel_id=1, source_target_pairs={{0,48},{16,0},{32,16},{48,32},{1,49},{17,1},{33,17},{49,33},{2,50}... | collective-permute-start | bytes 147464 | tf_op jit(solution)/shard_map/gather_images/ppermute | solution.py:40
  53.5 12.3 %all-to-all-start.2 = ((bf16[4,64,1536]{2,1,0:T(8,128)(2,1)}), bf16[4,64,1536]{2,1,0:T(8,128)(2,1)S(1)}, u32[]{:S(2)}, u32[]{:S(2)}) async-start(bf16[4,64,1536]{2,1,0:T(8,128)(2,1)} %broadcast_in_dim.16), calls=%async_computation.2 | async-start | bytes 1572864 | tf_op jit(solution)/shard_map/gather_texts/all_to_all | solution.py:26
  57.1 18.9 %collective-permute-start.5 = (bf16[64,1536]{1,0:T(8,128)(2,1)S(1)}, bf16[64,1536]{1,0:T(8,128)(2,1)S(1)}, u32[]{:S(2)}, u32[]{:S(2)}) collective-permute-start(bf16[64,1536]{1,0:T(8,128)(2,1)S(1)} %pad_maximum_fusion.1), channel_id=1, source_target_pairs={{0,2},{2,4},{4,6},{6,0},{1,3},{3,5},{5,7},{7,1},{8,10},{10,12},{12... | collective-permute-start | bytes 589832 | tf_op jit(solution)/shard_map/gather_images/ppermute | solution.py:40
  59.0 17.0 %collective-permute-start.4 = (bf16[64,1536]{1,0:T(8,128)(2,1)S(1)}, bf16[64,1536]{1,0:T(8,128)(2,1)S(1)}, u32[]{:S(2)}, u32[]{:S(2)}) collective-permute-start(bf16[64,1536]{1,0:T(8,128)(2,1)S(1)} %pad_maximum_fusion.1), channel_id=1, source_target_pairs={{0,4},{2,6},{4,0},{6,2},{1,5},{3,7},{5,1},{7,3},{8,12},{10,14},{12... | collective-permute-start | bytes 589832 | tf_op jit(solution)/shard_map/gather_images/ppermute | solution.py:40
  63.0 13.0 %collective-permute-start.3 = (bf16[64,1536]{1,0:T(8,128)(2,1)S(1)}, bf16[64,1536]{1,0:T(8,128)(2,1)S(1)}, u32[]{:S(2)}, u32[]{:S(2)}) collective-permute-start(bf16[64,1536]{1,0:T(8,128)(2,1)S(1)} %pad_maximum_fusion.1), channel_id=1, source_target_pairs={{0,6},{2,0},{4,2},{6,4},{1,7},{3,1},{5,3},{7,5},{8,14},{10,8},{12,... | collective-permute-start | bytes 589832 | tf_op jit(solution)/shard_map/gather_images/ppermute | solution.py:40
  65.8 12.0 %collective-permute-start.6 = (bf16[256,1536]{1,0:T(8,128)(2,1)S(1)}, bf16[256,1536]{1,0:T(8,128)(2,1)S(1)}, u32[]{:S(2)}, u32[]{:S(2)}) collective-permute-start(bf16[256,1536]{1,0:T(8,128)(2,1)S(1)} %bitcast.78), channel_id=1, source_target_pairs={{0,8},{8,0},{1,9},{9,1},{2,10},{10,2},{3,11},{11,3},{4,12},{12,4},... | collective-permute-start | bytes 2359304 | tf_op jit(solution)/shard_map/gather_texts/ppermute | solution.py:40
  78.6 4.5 %collective-permute-start.13 = (bf16[256,1536]{1,0:T(8,128)(2,1)S(1)}, bf16[256,1536]{1,0:T(8,128)(2,1)S(1)}, u32[]{:S(2)}, u32[]{:S(2)}) collective-permute-start(bf16[256,1536]{1,0:T(8,128)(2,1)S(1)} %convolution_convert_fusion), channel_id=1, source_target_pairs={{0,8},{8,0},{1,9},{9,1},{2,10},{10,2},{3,11},{11,3},{4,12},{12,4},... | collective-permute-start | bytes 2359304 | tf_op jit(solution)/shard_map/sum_texts/ppermute | solution.py:40
  84.4 16.2 %all-to-all-start.3 = ((bf16[4,64,1536]{2,1,0:T(8,128)(2,1)}), bf16[4,64,1536]{2,1,0:T(8,128)(2,1)S(1)}, u32[]{:S(2)}, u32[]{:S(2)}) async-start(bf16[4,64,1536]{2,1,0:T(8,128)(2,1)} %bitcast.9), calls=%async_computation.3 | async-start | bytes 1572864 | tf_op jit(solution)/shard_map/sum_texts/all_to_all | solution.py:26
  89.6 17.7 %collective-permute-start.7 = (bf16[64,1536]{1,0:T(8,128)(2,1)}, bf16[64,1536]{1,0:T(8,128)(2,1)S(1)}, u32[]{:S(2)}, u32[]{:S(2)}) collective-permute-start(bf16[64,1536]{1,0:T(8,128)(2,1)} %get-tuple-element.14), channel_id=1, source_target_pairs={{0,2},{2,4},{4,6},{6,0},{1,3},{3,5},{5,7},{7,1},{8,10},{10,12},{12... | collective-permute-start | bytes 589832 | tf_op jit(solution)/shard_map/sum_images/ppermute | solution.py:40
  92.7 14.6 %collective-permute-start.9 = (bf16[64,1536]{1,0:T(8,128)(2,1)}, bf16[64,1536]{1,0:T(8,128)(2,1)S(1)}, u32[]{:S(2)}, u32[]{:S(2)}) collective-permute-start(bf16[64,1536]{1,0:T(8,128)(2,1)} %get-tuple-element.15), channel_id=1, source_target_pairs={{0,6},{2,0},{4,2},{6,4},{1,7},{3,1},{5,3},{7,5},{8,14},{10,8},{12,... | collective-permute-start | bytes 589832 | tf_op jit(solution)/shard_map/sum_images/ppermute | solution.py:40
  96.1 11.2 %collective-permute-start.8 = (bf16[64,1536]{1,0:T(8,128)(2,1)S(1)}, bf16[64,1536]{1,0:T(8,128)(2,1)S(1)}, u32[]{:S(2)}, u32[]{:S(2)}) collective-permute-start(bf16[64,1536]{1,0:T(8,128)(2,1)S(1)} %get-tuple-element.16), channel_id=1, source_target_pairs={{0,4},{2,6},{4,0},{6,2},{1,5},{3,7},{5,1},{7,3},{8,12},{10,14},{12... | collective-permute-start | bytes 589832 | tf_op jit(solution)/shard_map/sum_images/ppermute | solution.py:40
  101.4 19.4 %all-to-all-start.4 = ((bf16[4,16,1536]{2,1,0:T(8,128)(2,1)}), bf16[4,16,1536]{2,1,0:T(8,128)(2,1)S(1)}, u32[]{:S(2)}, u32[]{:S(2)}) async-start(bf16[4,16,1536]{2,1,0:T(8,128)(2,1)} %bitcast.10), calls=%async_computation.4 | async-start | bytes 393216 | tf_op jit(solution)/shard_map/sum_texts/all_to_all | solution.py:26
  107.4 13.4 %collective-permute-start.10 = (bf16[16,1536]{1,0:T(8,128)(2,1)S(1)}, bf16[16,1536]{1,0:T(8,128)(2,1)S(1)}, u32[]{:S(2)}, u32[]{:S(2)}) collective-permute-start(bf16[16,1536]{1,0:T(8,128)(2,1)S(1)} %get-tuple-element.21), channel_id=1, source_target_pairs={{0,16},{16,32},{32,48},{48,0},{1,17},{17,33},{33,49},{49,1},{2,18}... | collective-permute-start | bytes 147464 | tf_op jit(solution)/shard_map/sum_images/ppermute | solution.py:40
  109.4 11.5 %collective-permute-start.12 = (bf16[16,1536]{1,0:T(8,128)(2,1)S(1)}, bf16[16,1536]{1,0:T(8,128)(2,1)S(1)}, u32[]{:S(2)}, u32[]{:S(2)}) collective-permute-start(bf16[16,1536]{1,0:T(8,128)(2,1)S(1)} %get-tuple-element.22), channel_id=1, source_target_pairs={{0,48},{16,0},{32,16},{48,32},{1,49},{17,1},{33,17},{49,33},{2,50}... | collective-permute-start | bytes 147464 | tf_op jit(solution)/shard_map/sum_images/ppermute | solution.py:40
  114.5 6.9 %collective-permute-start.11 = (bf16[16,1536]{1,0:T(8,128)(2,1)S(1)}, bf16[16,1536]{1,0:T(8,128)(2,1)S(1)}, u32[]{:S(2)}, u32[]{:S(2)}) collective-permute-start(bf16[16,1536]{1,0:T(8,128)(2,1)S(1)} %get-tuple-element.23), channel_id=1, source_target_pairs={{0,32},{16,48},{32,0},{48,16},{1,33},{17,49},{33,1},{49,17},{2,34}... | collective-permute-start | bytes 147464 | tf_op jit(solution)/shard_map/sum_images/ppermute | solution.py:40
  122.8 15.0 %all-to-all-start.5 = ((bf16[8,2,16,1536]{3,2,1,0:T(8,128)(2,1)}), bf16[8,2,16,1536]{3,2,1,0:T(8,128)(2,1)S(1)}, u32[]{:S(2)}, u32[]{:S(2)}) async-start(bf16[8,2,16,1536]{3,2,1,0:T(8,128)(2,1)} %broadcast_in_dim.17), calls=%async_computation.5 | async-start | bytes 1572864 | tf_op jit(solution)/shard_map/head_grads/all_to_all | solution.py:26
  127.2 10.6 %copy-start.4 = (bf16[128,192]{0,1:T(8,128)(2,1)S(1)}, bf16[128,192]{0,1:T(8,128)(2,1)}, u32[]{:S(2)}) copy-start(bf16[128,192]{0,1:T(8,128)(2,1)} %param.7) | copy-start | bytes 147460
  127.2 10.8 %copy-start.5 = (bf16[128,192]{0,1:T(8,128)(2,1)S(1)}, bf16[128,192]{0,1:T(8,128)(2,1)}, u32[]{:S(2)}) copy-start(bf16[128,192]{0,1:T(8,128)(2,1)} %param.8) | copy-start | bytes 147460
  138.3 10.0 %collective-permute-start.14 = (bf16[2,96,1536]{2,1,0:T(8,128)(2,1)S(1)}, bf16[2,96,1536]{2,1,0:T(8,128)(2,1)S(1)}, u32[]{:S(2)}, u32[]{:S(2)}) collective-permute-start(bf16[2,96,1536]{2,1,0:T(8,128)(2,1)S(1)} %pad_maximum_fusion), channel_id=1, source_target_pairs={{0,8},{8,0},{1,9},{9,1},{2,10},{10,2},{3,11},{11,3},{4,12},{12,4},... | collective-permute-start | bytes 1769480 | tf_op jit(solution)/shard_map/weight_grads/ppermute | solution.py:40
  200.2 4.6 %copy-start = (bf16[192,1536]{1,0:T(8,128)(2,1)S(1)}, bf16[192,1536]{1,0:T(8,128)(2,1)}, u32[]{:S(2)}) copy-start(bf16[192,1536]{1,0:T(8,128)(2,1)} %refs_1_.1) | copy-start | bytes 1769476
  201.1 4.7 %copy-start.1 = (bf16[192,1536]{1,0:T(8,128)(2,1)S(1)}, bf16[192,1536]{1,0:T(8,128)(2,1)}, u32[]{:S(2)}) copy-start(bf16[192,1536]{1,0:T(8,128)(2,1)} %refs_3_.1) | copy-start | bytes 1769476
  201.1 10.6 %all-to-all-start.9 = ((bf16[4,48,1536]{2,1,0:T(8,128)(2,1)}), bf16[4,48,1536]{2,1,0:T(8,128)(2,1)S(1)}, u32[]{:S(2)}, u32[]{:S(2)}) async-start(bf16[4,48,1536]{2,1,0:T(8,128)(2,1)} %broadcast_in_dim.20), calls=%async_computation.9 | async-start | bytes 1179648 | tf_op jit(solution)/shard_map/weight_grads/all_to_all | solution.py:26
  211.7 7.0 %collective-permute-start.15 = (bf16[2,96,1536]{2,1,0:T(8,128)(2,1)S(1)}, bf16[2,96,1536]{2,1,0:T(8,128)(2,1)S(1)}, u32[]{:S(2)}, u32[]{:S(2)}) collective-permute-start(bf16[2,96,1536]{2,1,0:T(8,128)(2,1)S(1)} %bitcast.82), channel_id=1, source_target_pairs={{0,8},{8,0},{1,9},{9,1},{2,10},{10,2},{3,11},{11,3},{4,12},{12,4},... | collective-permute-start | bytes 1769480 | tf_op jit(solution)/shard_map/weight_grads/ppermute | solution.py:40
  218.9 1.0 copy-start.2
  218.9 1.4 copy-start.3

commit v11 on v10

--- a/solution.py
+++ b/solution.py
@@ -186,6 +186,20 @@
     with jax.named_scope("sum_images"):
         image_grads = ring_scatter_sum(ring_scatter_sum(image_part, "y"), ZL)
 
+    core, side = at["c"], at["xl"]
+    quarter = embed_width // 4
+
+    def in_order(mine, theirs, place):
+        first = place == 0
+        return jnp.stack((jnp.where(first, mine, theirs), jnp.where(first, theirs, mine)))
+
+    with jax.named_scope("gather_features"):
+        features = jnp.stack((image_features, text_features))
+        features = in_order(features, shifted(features, "c", 1), core)
+        features = in_order(features, shifted(features, "xl", 1), side)
+        width = features.shape[-1]
+        image_rows, text_rows = (features[:, :, i].reshape(-1, width) for i in range(2))
+
     with jax.named_scope("head_grads"):
         grads = jnp.stack(
             (
@@ -193,50 +207,55 @@
                 head_back(text_unit, text_norm, text_grads),
             )
         )
-        rows = gather(grads, MP)
-        image_rows = merge_rows(rows[:, 0])
-        text_rows = merge_rows(rows[:, 1])
-
-    with jax.named_scope("input_grads"):
-        image_input_grad = jnp.dot(image_rows, image_weight.T, preferred_element_type=F32)
-        text_input_grad = jnp.dot(text_rows, text_weight.T, preferred_element_type=F32)
+        grads = grads.reshape(2, share, 2, 2, quarter).transpose(3, 2, 0, 1, 4)
+        grads = jnp.broadcast_to(grads[:, :, None], (2, 2, members, 2, share, quarter))
+        grads = exchange(grads.reshape(4 * members, 2, share, quarter), ("xl", "c") + MP)
+        image_grads, text_grads = merge_rows(grads[:, 0]), merge_rows(grads[:, 1])
+
     with jax.named_scope("weight_grads"):
-        half = image_features.shape[1] // 2
-
-        def half_part(core):
-            return jnp.stack(
-                [
-                    jnp.dot(
-                        lax.dynamic_slice_in_dim(features, core * half, half, 1).T,
-                        rows,
-                        preferred_element_type=F32,
-                    )
-                    for features, rows in (
-                        (image_features, image_rows),
-                        (text_features, text_rows),
-                    )
-                ]
-            )
-
-        other = shifted(half_part(1 - at["c"]).astype(BF16), "c", 1)
-        part = half_part(at["c"]) + other.astype(F32)
-        quarter = embed_width // 4
-        part = scatter_sum(part.reshape(4, half // 2, embed_width), ("xl", "z0"))
-        part = part.reshape(2, half // 4, 4, quarter).transpose(2, 0, 1, 3)
-        part = scatter_sum(part.reshape(8, half // 4, quarter), ("zh", "zm"))
-        part = gather(part.astype(BF16), ("zh", "zm")).reshape(4, 2, half // 4, quarter)
-        part = part.transpose(1, 2, 0, 3).reshape(half // 2, embed_width)
-        part = gather(part, ("xl", "z0")).reshape(2, half, embed_width)
+        eighth = width // 8
+        part = jnp.stack(
+            [
+                jnp.dot(rows.T, grads, preferred_element_type=F32)
+                .astype(BF16)
+                .reshape(2, 4, eighth, quarter)
+                for rows, grads in ((image_rows, image_grads), (text_rows, text_grads))
+            ]
+        )
+        part = part.transpose(2, 0, 1, 3, 4).reshape(16, eighth, quarter)
+        part = scatter_sum(part, ("zh", "zm", "z0")).astype(BF16)
+        part = gather(part, ("zh", "zm"))
+        part = gather(part, ("xl", "z0")).reshape(2, 2, 4, 2, eighth, quarter)
+        part = part.transpose(3, 1, 2, 4, 0, 5).reshape(2, width, 2 * quarter)
+        part = lax.optimization_barrier(part)
         other = shifted(part, "c", 1)
 
         def halves(mine, theirs):
             mine, theirs = mine.astype(F32), theirs.astype(F32)
-            both = jnp.concatenate((mine, mine), axis=0)
-            return lax.dynamic_update_slice_in_dim(both, theirs, (1 - at["c"]) * half, 0)
+            both = jnp.concatenate((mine, mine), axis=1)
+            return lax.dynamic_update_slice_in_dim(both, theirs, (1 - core) * 2 * quarter, 1)
 
         image_weight_grad = halves(part[0], other[0])
         text_weight_grad = halves(part[1], other[1])
-    return (image_input_grad, text_input_grad, image_weight_grad, text_weight_grad)
+
+    with jax.named_scope("input_grads"):
+        start = (core * 2 + side) * quarter
+        inputs = jnp.stack(
+            [
+                contract(grads, lax.dynamic_slice_in_dim(weight, start, quarter, 1), 1, 1)
+                for grads, weight in ((image_grads, image_weight), (text_grads, text_weight))
+            ]
+        ).reshape(2, 2, 2, members * share, width)
+
+        def half_sum(value, place, axis, name):
+            kept, sent = (
+                lax.dynamic_index_in_dim(value, i, axis, False) for i in (place, 1 - place)
+            )
+            return kept + shifted(sent.astype(BF16), name, 1).astype(F32)
+
+        inputs = half_sum(inputs, core, 2, "c")
+        inputs = half_sum(inputs, side, 1, "xl")
+    return (inputs[0], inputs[1], image_weight_grad, text_weight_grad)
 
 
 def solution(mesh):

time: 221 us -> 229 us (1.036)
  starting transfers between devices: 109 us -> 123 us
  blocking collectives: 51.5 us -> 45.6 us
  waiting for transfers between devices: 40 us -> 35 us
    all_to_all x7, waiting for transfers between devices: 34.5 us -> 16.7 us  [exchange(): return lax.all_to_all(blocks, axes, split_axis=0, concat_axis=0, tiled=True)]
    ppermute x16 -> x19, waiting for transfers between devices: 5.5 us -> 18.3 us  [shifted(): return lax.ppermute(value, axis, [(i, (i + by) % n) for i in range(n)])]
    all_to_all x7, starting transfers between devices: 46.3 us -> 54.8 us  [exchange(): return lax.all_to_all(blocks, axes, split_axis=0, concat_axis=0, tiled=True)]
    all_to_all x3 -> x2, blocking collectives: 51.5 us -> 45.6 us  [exchange(): return lax.all_to_all(blocks, axes, split_axis=0, concat_axis=0, tiled=True)]
    ppermute x16 -> x19, starting transfers between devices: 62.4 us -> 68 us  [shifted(): return lax.ppermute(value, axis, [(i, (i + by) % n) for i in range(n)])]
  transfers between devices with their start and end apart: 23 -> 26, of which waited for: 11 -> 9; matrix products, arithmetic and copies ran while one was open for 3% -> 5% of each run, Pallas kernels for 0% -> 0%
where the time goes in v11:
time: 229 us; the launch traced here: 228 us
  starting transfers between devices  123 us (54%)
  blocking collectives  45.6 us (20%)
  waiting for transfers between devices  35 us (15%)
  local copies, waits for them, and re-layouts  8.2 us (4%)
  matrix products  6.19 us (3%)
  other arithmetic  3.97 us (2%)
  between operations  3.27 us (1%)
  Pallas kernels  2.59 us (1%)
    ppermute x19, starting transfers between devices, shifted(): return lax.ppermute(value, axis, [(i, (i + by) % n) for i in range(n)])  68 us
    all_to_all x7, starting transfers between devices, exchange(): return lax.all_to_all(blocks, axes, split_axis=0, concat_axis=0, tiled=True)  54.8 us
    all_to_all x2, blocking collectives, exchange(): return lax.all_to_all(blocks, axes, split_axis=0, concat_axis=0, tiled=True)  45.6 us
    ppermute x19, waiting for transfers between devices, shifted(): return lax.ppermute(value, axis, [(i, (i + by) % n) for i in range(n)])  18.3 us
    all_to_all x7, waiting for transfers between devices, exchange(): return lax.all_to_all(blocks, axes, split_axis=0, concat_axis=0, tiled=True)  16.7 us
  transfers between devices with their start and end apart: 26, of which 9 were waited for; matrix products, arithmetic and copies ran while one was open for 5% of the time, Pallas kernels for 0%

profile of v11, /device:TPU:1, one launch (start us, length us, event | category | flops | bytes accessed | tf_op | source)
XLA Modules:
  0.0 227.7 jit_solution(17969490068822657682)
XLA Ops:
  0.6 2.6 %heads.1 = bf16[128,3072]{1,0:T(8,128)(2,1)} custom-call(bf16[192,128]{1,0:T(8,128)(2,1)} %bitcast.118, bf16[192,1536]{1,0:T(8,128)(2,1)} %refs_1_.1, bf16[192,128]{1,0:T(8,128)(2,1)} %bitcast.121, bf16[192,1536]{1,0:T(8,128)(2,1)} %refs_3_.1), custom_call_target="tpu_custom_call" | custom-call | flops 150994944 | bytes 2064384 | tf_op jit(solution)/shard_map/heads/pallas_call | solution.py:71
  3.2 7.5 %all-to-all-start = ((bf16[8,16,3072]{2,1,0:T(8,128)(2,1)}), bf16[8,16,3072]{2,1,0:T(8,128)(2,1)S(1)}, u32[]{:S(2)}, u32[]{:S(2)}) async-start(bf16[8,16,3072]{2,1,0:T(8,128)(2,1)} %bitcast.112), calls=%async_computation | async-start | bytes 1572864 | tf_op jit(solution)/shard_map/heads/all_to_all | solution.py:26
  10.7 11.2 %all-to-all-done = bf16[8,16,3072]{2,1,0:T(8,128)(2,1)S(1)} async-done(((bf16[8,16,3072]{2,1,0:T(8,128)(2,1)}), bf16[8,16,3072]{2,1,0:T(8,128)(2,1)S(1)}, u32[]{:S(2)}, u32[]{:S(2)}) %all-to-all-start) | async-done | bytes 786464 | tf_op jit(solution)/shard_map/heads/all_to_all | solution.py:26
  22.3 0.7 broadcast_in_dim.12
  23.0 16.8 %all-to-all-start.1 = ((bf16[4,16,1536]{2,1,0:T(8,128)(2,1)}), bf16[4,16,1536]{2,1,0:T(8,128)(2,1)S(1)}, u32[]{:S(2)}, u32[]{:S(2)}) async-start(bf16[4,16,1536]{2,1,0:T(8,128)(2,1)} %broadcast_in_dim.12), calls=%async_computation.1 | async-start | bytes 393216 | tf_op jit(solution)/shard_map/gather_texts/all_to_all | solution.py:26
  39.8 2.6 %collective-permute-start.2 = (bf16[16,1536]{1,0:T(8,128)(2,1)S(1)}, bf16[16,1536]{1,0:T(8,128)(2,1)S(1)}, u32[]{:S(2)}, u32[]{:S(2)}) collective-permute-start(bf16[16,1536]{1,0:T(8,128)(2,1)S(1)} %get-tuple-element.11), channel_id=1, source_target_pairs={{0,16},{16,32},{32,48},{48,0},{1,17},{17,33},{33,49},{49,1},{2,18}... | collective-permute-start | bytes 147464 | tf_op jit(solution)/shard_map/gather_images/ppermute | solution.py:40
  42.5 3.1 %collective-permute-start.1 = (bf16[16,1536]{1,0:T(8,128)(2,1)S(1)}, bf16[16,1536]{1,0:T(8,128)(2,1)S(1)}, u32[]{:S(2)}, u32[]{:S(2)}) collective-permute-start(bf16[16,1536]{1,0:T(8,128)(2,1)S(1)} %get-tuple-element.11), channel_id=1, source_target_pairs={{0,32},{16,48},{32,0},{48,16},{1,33},{17,49},{33,1},{49,17},{2,34}... | collective-permute-start | bytes 147464 | tf_op jit(solution)/shard_map/gather_images/ppermute | solution.py:40
  45.6 3.5 %collective-permute-start = (bf16[16,1536]{1,0:T(8,128)(2,1)S(1)}, bf16[16,1536]{1,0:T(8,128)(2,1)S(1)}, u32[]{:S(2)}, u32[]{:S(2)}) collective-permute-start(bf16[16,1536]{1,0:T(8,128)(2,1)S(1)} %get-tuple-element.11), channel_id=1, source_target_pairs={{0,48},{16,0},{32,16},{48,32},{1,49},{17,1},{33,17},{49,33},{2,50}... | collective-permute-start | bytes 147464 | tf_op jit(solution)/shard_map/gather_images/ppermute | solution.py:40
  51.1 1.5 all-to-all-done.1
  52.6 0.9 broadcast_in_dim.14
  53.5 3.5 %all-to-all-start.2 = ((bf16[4,64,1536]{2,1,0:T(8,128)(2,1)}), bf16[4,64,1536]{2,1,0:T(8,128)(2,1)S(1)}, u32[]{:S(2)}, u32[]{:S(2)}) async-start(bf16[4,64,1536]{2,1,0:T(8,128)(2,1)} %broadcast_in_dim.14), calls=%async_computation.2 | async-start | bytes 1572864 | tf_op jit(solution)/shard_map/gather_texts/all_to_all | solution.py:26
  57.1 1.9 collective-permute-start.5
  59.0 4.0 %collective-permute-start.4 = (bf16[64,1536]{1,0:T(8,128)(2,1)S(1)}, bf16[64,1536]{1,0:T(8,128)(2,1)S(1)}, u32[]{:S(2)}, u32[]{:S(2)}) collective-permute-start(bf16[64,1536]{1,0:T(8,128)(2,1)S(1)} %pad_maximum_fusion.2), channel_id=1, source_target_pairs={{0,4},{2,6},{4,0},{6,2},{1,5},{3,7},{5,1},{7,3},{8,12},{10,14},{12... | collective-permute-start | bytes 589832 | tf_op jit(solution)/shard_map/gather_images/ppermute | solution.py:40
  63.0 2.8 %collective-permute-start.3 = (bf16[64,1536]{1,0:T(8,128)(2,1)S(1)}, bf16[64,1536]{1,0:T(8,128)(2,1)S(1)}, u32[]{:S(2)}, u32[]{:S(2)}) collective-permute-start(bf16[64,1536]{1,0:T(8,128)(2,1)S(1)} %pad_maximum_fusion.2), channel_id=1, source_target_pairs={{0,6},{2,0},{4,2},{6,4},{1,7},{3,1},{5,3},{7,5},{8,14},{10,8},{12,... | collective-permute-start | bytes 589832 | tf_op jit(solution)/shard_map/gather_images/ppermute | solution.py:40
  65.8 10.1 %collective-permute-start.6 = (bf16[256,1536]{1,0:T(8,128)(2,1)S(1)}, bf16[256,1536]{1,0:T(8,128)(2,1)S(1)}, u32[]{:S(2)}, u32[]{:S(2)}) collective-permute-start(bf16[256,1536]{1,0:T(8,128)(2,1)S(1)} %bitcast.109), channel_id=1, source_target_pairs={{0,8},{8,0},{1,9},{9,1},{2,10},{10,2},{3,11},{11,3},{4,12},{12,4},... | collective-permute-start | bytes 2359304 | tf_op jit(solution)/shard_map/gather_texts/ppermute | solution.py:40
  76.0 1.8 collective-permute-done.6
  77.8 0.4 fusion.14
  78.2 0.4 convolution_convert_fusion
  78.6 2.6 %collective-permute-start.13 = (bf16[256,1536]{1,0:T(8,128)(2,1)S(1)}, bf16[256,1536]{1,0:T(8,128)(2,1)S(1)}, u32[]{:S(2)}, u32[]{:S(2)}) collective-permute-start(bf16[256,1536]{1,0:T(8,128)(2,1)S(1)} %convolution_convert_fusion), channel_id=1, source_target_pairs={{0,8},{8,0},{1,9},{9,1},{2,10},{10,2},{3,11},{11,3},{4,12},{12,4},... | collective-permute-start | bytes 2359304 | tf_op jit(solution)/shard_map/sum_texts/ppermute | solution.py:40
  81.3 0.4 fusion.15
  81.7 0.4 fusion.46
  82.1 0.4 fusion.45
  82.5 0.7 collective-permute-done.13
  83.1 1.3 fusion
  84.4 4.6 %all-to-all-start.3 = ((bf16[4,64,1536]{2,1,0:T(8,128)(2,1)}), bf16[4,64,1536]{2,1,0:T(8,128)(2,1)S(1)}, u32[]{:S(2)}, u32[]{:S(2)}) async-start(bf16[4,64,1536]{2,1,0:T(8,128)(2,1)} %bitcast.8), calls=%async_computation.3 | async-start | bytes 1572864 | tf_op jit(solution)/shard_map/sum_texts/all_to_all | solution.py:26
  89.0 0.8 fusion.43
  89.8 3.0 %collective-permute-start.7 = (bf16[64,1536]{1,0:T(8,128)(2,1)}, bf16[64,1536]{1,0:T(8,128)(2,1)S(1)}, u32[]{:S(2)}, u32[]{:S(2)}) collective-permute-start(bf16[64,1536]{1,0:T(8,128)(2,1)} %get-tuple-element.14), channel_id=1, source_target_pairs={{0,2},{2,4},{4,6},{6,0},{1,3},{3,5},{5,7},{7,1},{8,10},{10,12},{12... | collective-permute-start | bytes 589832 | tf_op jit(solution)/shard_map/sum_images/ppermute | solution.py:40
  92.8 3.4 %collective-permute-start.9 = (bf16[64,1536]{1,0:T(8,128)(2,1)}, bf16[64,1536]{1,0:T(8,128)(2,1)S(1)}, u32[]{:S(2)}, u32[]{:S(2)}) collective-permute-start(bf16[64,1536]{1,0:T(8,128)(2,1)} %get-tuple-element.15), channel_id=1, source_target_pairs={{0,6},{2,0},{4,2},{6,4},{1,7},{3,1},{5,3},{7,5},{8,14},{10,8},{12,... | collective-permute-start | bytes 589832 | tf_op jit(solution)/shard_map/sum_images/ppermute | solution.py:40
  96.3 2.5 %collective-permute-start.8 = (bf16[64,1536]{1,0:T(8,128)(2,1)S(1)}, bf16[64,1536]{1,0:T(8,128)(2,1)S(1)}, u32[]{:S(2)}, u32[]{:S(2)}) collective-permute-start(bf16[64,1536]{1,0:T(8,128)(2,1)S(1)} %get-tuple-element.16), channel_id=1, source_target_pairs={{0,4},{2,6},{4,0},{6,2},{1,5},{3,7},{5,1},{7,3},{8,12},{10,14},{12... | collective-permute-start | bytes 589832 | tf_op jit(solution)/shard_map/sum_images/ppermute | solution.py:40
  98.8 0.7 pad_maximum_fusion.4
  99.5 3.2 %collective-permute-start.16 = (bf16[2,128,192]{1,2,0:T(8,128)(2,1)}, bf16[2,128,192]{1,2,0:T(8,128)(2,1)}, u32[]{:S(2)}, u32[]{:S(2)}) collective-permute-start(bf16[2,128,192]{1,2,0:T(8,128)(2,1)} %pad_maximum_fusion.4), channel_id=1, source_target_pairs={{0,8},{8,0},{1,9},{9,1},{2,10},{10,2},{3,11},{11,3},{4,12},{12,4},... | collective-permute-start | bytes 294920 | tf_op jit(solution)/shard_map/gather_features/ppermute | solution.py:40
  102.7 0.8 reduce_sum.85
  103.6 6.3 %all-to-all-start.4 = ((bf16[4,16,1536]{2,1,0:T(8,128)(2,1)}), bf16[4,16,1536]{2,1,0:T(8,128)(2,1)S(1)}, u32[]{:S(2)}, u32[]{:S(2)}) async-start(bf16[4,16,1536]{2,1,0:T(8,128)(2,1)} %bitcast.9), calls=%async_computation.4 | async-start | bytes 393216 | tf_op jit(solution)/shard_map/sum_texts/all_to_all | solution.py:26
  110.0 1.9 collective-permute-start.10
  111.9 5.2 %collective-permute-start.12 = (bf16[16,1536]{1,0:T(8,128)(2,1)S(1)}, bf16[16,1536]{1,0:T(8,128)(2,1)S(1)}, u32[]{:S(2)}, u32[]{:S(2)}) collective-permute-start(bf16[16,1536]{1,0:T(8,128)(2,1)S(1)} %get-tuple-element.30), channel_id=1, source_target_pairs={{0,48},{16,0},{32,16},{48,32},{1,49},{17,1},{33,17},{49,33},{2,50}... | collective-permute-start | bytes 147464 | tf_op jit(solution)/shard_map/sum_images/ppermute | solution.py:40
  117.1 1.9 collective-permute-start.11
  119.0 3.9 %all-to-all-done.4 = bf16[4,16,1536]{2,1,0:T(8,128)(2,1)S(1)} async-done(((bf16[4,16,1536]{2,1,0:T(8,128)(2,1)}), bf16[4,16,1536]{2,1,0:T(8,128)(2,1)S(1)}, u32[]{:S(2)}, u32[]{:S(2)}) %all-to-all-start.4) | async-done | bytes 196640 | tf_op jit(solution)/shard_map/sum_texts/all_to_all | solution.py:26
  123.0 0.2 multiply_reduce_fusion.1
  123.5 1.0 broadcast_in_dim.15
  124.5 12.7 %all-to-all-start.5 = ((bf16[32,2,16,384]{3,2,1,0:T(8,128)(2,1)}), bf16[32,2,16,384]{3,2,1,0:T(8,128)(2,1)S(1)}, u32[]{:S(2)}, u32[]{:S(2)}) async-start(bf16[32,2,16,384]{3,2,1,0:T(8,128)(2,1)} %bitcast.11), calls=%async_computation.5 | async-start | bytes 1572864 | tf_op jit(solution)/shard_map/head_grads/all_to_all | solution.py:26
  137.3 0.9 select_bitcast_fusion.3
  138.2 3.3 %collective-permute-start.17 = (bf16[2,2,128,192]{2,3,1,0:T(8,128)(2,1)S(1)}, bf16[2,2,128,192]{2,3,1,0:T(8,128)(2,1)S(1)}, u32[]{:S(2)}, u32[]{:S(2)}) collective-permute-start(bf16[2,2,128,192]{2,3,1,0:T(8,128)(2,1)S(1)} %pad_maximum_fusion.3), channel_id=1, source_target_pairs={{0,256},{256,0},{1,257},{257,1},{2,258},{258,2},{3,259},{259,3},{4... | collective-permute-start | bytes 589832 | tf_op jit(solution)/shard_map/gather_features/ppermute | solution.py:40
  141.5 10.6 %collective-permute-done.17 = bf16[2,2,128,192]{2,3,1,0:T(8,128)(2,1)S(1)} collective-permute-done((bf16[2,2,128,192]{2,3,1,0:T(8,128)(2,1)S(1)}, bf16[2,2,128,192]{2,3,1,0:T(8,128)(2,1)S(1)}, u32[]{:S(2)}, u32[]{:S(2)}) %collective-permute-start.17) | collective-permute-done | bytes 196640 | tf_op jit(solution)/shard_map/gather_features/ppermute | solution.py:40
  152.3 0.2 copy.30
  152.6 0.2 copy.31
  153.0 0.3 convolution_convert_fusion.1
  153.2 0.3 convolution_convert_fusion.2
  153.6 21.1 %all_to_all.45 = bf16[16,24,384]{2,1,0:T(8,128)(2,1)S(1)} all-to-all(bf16[16,24,384]{2,1,0:T(8,128)(2,1)S(1)} %bitcast.114), channel_id=1, replica_groups=mesh['xl'=2,'zh'=4,'zm'=2,'z0'=2,'c'=2,'y'=4,'xh'=2] {'zh','zm','z0'}, dimensions={0} | all-to-all | bytes 589824 | tf_op jit(solution)/shard_map/weight_grads/all_to_all | solution.py:26
  174.7 24.6 %all_to_all.46 = bf16[8,24,384]{2,1,0:T(8,128)(2,1)S(1)} all-to-all(bf16[8,24,384]{2,1,0:T(8,128)(2,1)S(1)} %broadcast_in_dim.16), channel_id=1, replica_groups=mesh['xl'=2,'zh'=4,'zm'=2,'z0'=2,'c'=2,'y'=4,'xh'=2] {'zh','zm'}, dimensions={0} | all-to-all | bytes 294912 | tf_op jit(solution)/shard_map/weight_grads/all_to_all | solution.py:26
  199.3 0.9 broadcast_in_dim.17
  200.1 3.5 %all-to-all-start.8 = ((bf16[4,8,24,384]{3,2,1,0:T(8,128)(2,1)}), bf16[4,8,24,384]{3,2,1,0:T(8,128)(2,1)S(1)}, u32[]{:S(2)}, u32[]{:S(2)}) async-start(bf16[4,8,24,384]{3,2,1,0:T(8,128)(2,1)} %broadcast_in_dim.17), calls=%async_computation.8 | async-start | bytes 1179648 | tf_op jit(solution)/shard_map/weight_grads/all_to_all | solution.py:26
  203.6 1.2 convolution_bitcast_fusion
  204.8 1.2 convolution_bitcast_fusion.1
  206.1 6.3 %collective-permute-start.14 = (bf16[2,2,128,192]{2,3,1,0:T(8,128)(2,1)S(1)}, bf16[2,2,128,192]{2,3,1,0:T(8,128)(2,1)S(1)}, u32[]{:S(2)}, u32[]{:S(2)}) collective-permute-start(bf16[2,2,128,192]{2,3,1,0:T(8,128)(2,1)S(1)} %fusion.25), channel_id=1, source_target_pairs={{0,8},{8,0},{1,9},{9,1},{2,10},{10,2},{3,11},{11,3},{4,12},{12,4},... | collective-permute-start | bytes 589832 | tf_op jit(solution)/shard_map/input_grads/ppermute | solution.py:40
  212.4 1.0 collective-permute-done.14
  213.6 3.6 %collective-permute-start.15 = (bf16[2,128,192]{1,2,0:T(8,128)(2,1)S(1)}, bf16[2,128,192]{1,2,0:T(8,128)(2,1)S(1)}, u32[]{:S(2)}, u32[]{:S(2)}) collective-permute-start(bf16[2,128,192]{1,2,0:T(8,128)(2,1)S(1)} %fusion.32), channel_id=1, source_target_pairs={{0,256},{256,0},{1,257},{257,1},{2,258},{258,2},{3,259},{259,3},{4... | collective-permute-start | bytes 294920 | tf_op jit(solution)/shard_map/input_grads/ppermute | solution.py:40
  217.2 2.8 %collective-permute-done.15 = bf16[2,128,192]{1,2,0:T(8,128)(2,1)S(1)} collective-permute-done((bf16[2,128,192]{1,2,0:T(8,128)(2,1)S(1)}, bf16[2,128,192]{1,2,0:T(8,128)(2,1)S(1)}, u32[]{:S(2)}, u32[]{:S(2)}) %collective-permute-start.15) | collective-permute-done | bytes 98336 | tf_op jit(solution)/shard_map/input_grads/ppermute | solution.py:40
  220.0 0.7 slice_bitcast_fusion.4
  220.7 0.6 copy.34
  221.3 0.4 reshape.127
  221.7 2.8 %collective-permute-start.18 = (bf16[2,192,768]{2,1,0:T(8,128)(2,1)S(1)}, bf16[2,192,768]{2,1,0:T(8,128)(2,1)S(1)}, u32[]{:S(2)}, u32[]{:S(2)}) collective-permute-start(bf16[2,192,768]{2,1,0:T(8,128)(2,1)S(1)} %reshape.127), channel_id=1, source_target_pairs={{0,8},{8,0},{1,9},{9,1},{2,10},{10,2},{3,11},{11,3},{4,12},{12,4},... | collective-permute-start | bytes 1769480 | tf_op jit(solution)/shard_map/weight_grads/ppermute | solution.py:40
  224.8 1.4 collective-permute-done.18
  226.3 1.0 copy-done
  227.3 0.4 copy-done.1
  (63 shorter events, 1.9 us)
Async XLA Ops:
  3.2 18.7 %all-to-all-start = ((bf16[8,16,3072]{2,1,0:T(8,128)(2,1)}), bf16[8,16,3072]{2,1,0:T(8,128)(2,1)S(1)}, u32[]{:S(2)}, u32[]{:S(2)}) async-start(bf16[8,16,3072]{2,1,0:T(8,128)(2,1)} %bitcast.112), calls=%async_computation | async-start | bytes 1572864 | tf_op jit(solution)/shard_map/heads/all_to_all | solution.py:26
  23.0 29.6 %all-to-all-start.1 = ((bf16[4,16,1536]{2,1,0:T(8,128)(2,1)}), bf16[4,16,1536]{2,1,0:T(8,128)(2,1)S(1)}, u32[]{:S(2)}, u32[]{:S(2)}) async-start(bf16[4,16,1536]{2,1,0:T(8,128)(2,1)} %broadcast_in_dim.12), calls=%async_computation.1 | async-start | bytes 393216 | tf_op jit(solution)/shard_map/gather_texts/all_to_all | solution.py:26
  39.8 17.2 %collective-permute-start.2 = (bf16[16,1536]{1,0:T(8,128)(2,1)S(1)}, bf16[16,1536]{1,0:T(8,128)(2,1)S(1)}, u32[]{:S(2)}, u32[]{:S(2)}) collective-permute-start(bf16[16,1536]{1,0:T(8,128)(2,1)S(1)} %get-tuple-element.11), channel_id=1, source_target_pairs={{0,16},{16,32},{32,48},{48,0},{1,17},{17,33},{33,49},{49,1},{2,18}... | collective-permute-start | bytes 147464 | tf_op jit(solution)/shard_map/gather_images/ppermute | solution.py:40
  42.5 14.5 %collective-permute-start.1 = (bf16[16,1536]{1,0:T(8,128)(2,1)S(1)}, bf16[16,1536]{1,0:T(8,128)(2,1)S(1)}, u32[]{:S(2)}, u32[]{:S(2)}) collective-permute-start(bf16[16,1536]{1,0:T(8,128)(2,1)S(1)} %get-tuple-element.11), channel_id=1, source_target_pairs={{0,32},{16,48},{32,0},{48,16},{1,33},{17,49},{33,1},{49,17},{2,34}... | collective-permute-start | bytes 147464 | tf_op jit(solution)/shard_map/gather_images/ppermute | solution.py:40
  45.6 11.4 %collective-permute-start = (bf16[16,1536]{1,0:T(8,128)(2,1)S(1)}, bf16[16,1536]{1,0:T(8,128)(2,1)S(1)}, u32[]{:S(2)}, u32[]{:S(2)}) collective-permute-start(bf16[16,1536]{1,0:T(8,128)(2,1)S(1)} %get-tuple-element.11), channel_id=1, source_target_pairs={{0,48},{16,0},{32,16},{48,32},{1,49},{17,1},{33,17},{49,33},{2,50}... | collective-permute-start | bytes 147464 | tf_op jit(solution)/shard_map/gather_images/ppermute | solution.py:40
  53.5 12.3 %all-to-all-start.2 = ((bf16[4,64,1536]{2,1,0:T(8,128)(2,1)}), bf16[4,64,1536]{2,1,0:T(8,128)(2,1)S(1)}, u32[]{:S(2)}, u32[]{:S(2)}) async-start(bf16[4,64,1536]{2,1,0:T(8,128)(2,1)} %broadcast_in_dim.14), calls=%async_computation.2 | async-start | bytes 1572864 | tf_op jit(solution)/shard_map/gather_texts/all_to_all | solution.py:26
  57.1 18.9 %collective-permute-start.5 = (bf16[64,1536]{1,0:T(8,128)(2,1)S(1)}, bf16[64,1536]{1,0:T(8,128)(2,1)S(1)}, u32[]{:S(2)}, u32[]{:S(2)}) collective-permute-start(bf16[64,1536]{1,0:T(8,128)(2,1)S(1)} %pad_maximum_fusion.2), channel_id=1, source_target_pairs={{0,2},{2,4},{4,6},{6,0},{1,3},{3,5},{5,7},{7,1},{8,10},{10,12},{12... | collective-permute-start | bytes 589832 | tf_op jit(solution)/shard_map/gather_images/ppermute | solution.py:40
  59.0 17.0 %collective-permute-start.4 = (bf16[64,1536]{1,0:T(8,128)(2,1)S(1)}, bf16[64,1536]{1,0:T(8,128)(2,1)S(1)}, u32[]{:S(2)}, u32[]{:S(2)}) collective-permute-start(bf16[64,1536]{1,0:T(8,128)(2,1)S(1)} %pad_maximum_fusion.2), channel_id=1, source_target_pairs={{0,4},{2,6},{4,0},{6,2},{1,5},{3,7},{5,1},{7,3},{8,12},{10,14},{12... | collective-permute-start | bytes 589832 | tf_op jit(solution)/shard_map/gather_images/ppermute | solution.py:40
  63.0 13.0 %collective-permute-start.3 = (bf16[64,1536]{1,0:T(8,128)(2,1)S(1)}, bf16[64,1536]{1,0:T(8,128)(2,1)S(1)}, u32[]{:S(2)}, u32[]{:S(2)}) collective-permute-start(bf16[64,1536]{1,0:T(8,128)(2,1)S(1)} %pad_maximum_fusion.2), channel_id=1, source_target_pairs={{0,6},{2,0},{4,2},{6,4},{1,7},{3,1},{5,3},{7,5},{8,14},{10,8},{12,... | collective-permute-start | bytes 589832 | tf_op jit(solution)/shard_map/gather_images/ppermute | solution.py:40
  65.8 12.0 %collective-permute-start.6 = (bf16[256,1536]{1,0:T(8,128)(2,1)S(1)}, bf16[256,1536]{1,0:T(8,128)(2,1)S(1)}, u32[]{:S(2)}, u32[]{:S(2)}) collective-permute-start(bf16[256,1536]{1,0:T(8,128)(2,1)S(1)} %bitcast.109), channel_id=1, source_target_pairs={{0,8},{8,0},{1,9},{9,1},{2,10},{10,2},{3,11},{11,3},{4,12},{12,4},... | collective-permute-start | bytes 2359304 | tf_op jit(solution)/shard_map/gather_texts/ppermute | solution.py:40
  78.6 4.5 %collective-permute-start.13 = (bf16[256,1536]{1,0:T(8,128)(2,1)S(1)}, bf16[256,1536]{1,0:T(8,128)(2,1)S(1)}, u32[]{:S(2)}, u32[]{:S(2)}) collective-permute-start(bf16[256,1536]{1,0:T(8,128)(2,1)S(1)} %convolution_convert_fusion), channel_id=1, source_target_pairs={{0,8},{8,0},{1,9},{9,1},{2,10},{10,2},{3,11},{11,3},{4,12},{12,4},... | collective-permute-start | bytes 2359304 | tf_op jit(solution)/shard_map/sum_texts/ppermute | solution.py:40
  84.4 14.4 %copy-start.2 = (bf16[128,192]{0,1:T(8,128)(2,1)S(1)}, bf16[128,192]{0,1:T(8,128)(2,1)}, u32[]{:S(2)}) copy-start(bf16[128,192]{0,1:T(8,128)(2,1)} %param.7) | copy-start | bytes 147460
  84.4 14.4 %copy-start.3 = (bf16[128,192]{0,1:T(8,128)(2,1)S(1)}, bf16[128,192]{0,1:T(8,128)(2,1)}, u32[]{:S(2)}) copy-start(bf16[128,192]{0,1:T(8,128)(2,1)} %param.8) | copy-start | bytes 147460
  84.4 18.3 %all-to-all-start.3 = ((bf16[4,64,1536]{2,1,0:T(8,128)(2,1)}), bf16[4,64,1536]{2,1,0:T(8,128)(2,1)S(1)}, u32[]{:S(2)}, u32[]{:S(2)}) async-start(bf16[4,64,1536]{2,1,0:T(8,128)(2,1)} %bitcast.8), calls=%async_computation.3 | async-start | bytes 1572864 | tf_op jit(solution)/shard_map/sum_texts/all_to_all | solution.py:26
  89.8 20.0 %collective-permute-start.7 = (bf16[64,1536]{1,0:T(8,128)(2,1)}, bf16[64,1536]{1,0:T(8,128)(2,1)S(1)}, u32[]{:S(2)}, u32[]{:S(2)}) collective-permute-start(bf16[64,1536]{1,0:T(8,128)(2,1)} %get-tuple-element.14), channel_id=1, source_target_pairs={{0,2},{2,4},{4,6},{6,0},{1,3},{3,5},{5,7},{7,1},{8,10},{10,12},{12... | collective-permute-start | bytes 589832 | tf_op jit(solution)/shard_map/sum_images/ppermute | solution.py:40
  92.8 17.0 %collective-permute-start.9 = (bf16[64,1536]{1,0:T(8,128)(2,1)}, bf16[64,1536]{1,0:T(8,128)(2,1)S(1)}, u32[]{:S(2)}, u32[]{:S(2)}) collective-permute-start(bf16[64,1536]{1,0:T(8,128)(2,1)} %get-tuple-element.15), channel_id=1, source_target_pairs={{0,6},{2,0},{4,2},{6,4},{1,7},{3,1},{5,3},{7,5},{8,14},{10,8},{12,... | collective-permute-start | bytes 589832 | tf_op jit(solution)/shard_map/sum_images/ppermute | solution.py:40
  96.3 13.6 %collective-permute-start.8 = (bf16[64,1536]{1,0:T(8,128)(2,1)S(1)}, bf16[64,1536]{1,0:T(8,128)(2,1)S(1)}, u32[]{:S(2)}, u32[]{:S(2)}) collective-permute-start(bf16[64,1536]{1,0:T(8,128)(2,1)S(1)} %get-tuple-element.16), channel_id=1, source_target_pairs={{0,4},{2,6},{4,0},{6,2},{1,5},{3,7},{5,1},{7,3},{8,12},{10,14},{12... | collective-permute-start | bytes 589832 | tf_op jit(solution)/shard_map/sum_images/ppermute | solution.py:40
  99.5 37.8 %collective-permute-start.16 = (bf16[2,128,192]{1,2,0:T(8,128)(2,1)}, bf16[2,128,192]{1,2,0:T(8,128)(2,1)}, u32[]{:S(2)}, u32[]{:S(2)}) collective-permute-start(bf16[2,128,192]{1,2,0:T(8,128)(2,1)} %pad_maximum_fusion.4), channel_id=1, source_target_pairs={{0,8},{8,0},{1,9},{9,1},{2,10},{10,2},{3,11},{11,3},{4,12},{12,4},... | collective-permute-start | bytes 294920 | tf_op jit(solution)/shard_map/gather_features/ppermute | solution.py:40
  103.6 19.4 %all-to-all-start.4 = ((bf16[4,16,1536]{2,1,0:T(8,128)(2,1)}), bf16[4,16,1536]{2,1,0:T(8,128)(2,1)S(1)}, u32[]{:S(2)}, u32[]{:S(2)}) async-start(bf16[4,16,1536]{2,1,0:T(8,128)(2,1)} %bitcast.9), calls=%async_computation.4 | async-start | bytes 393216 | tf_op jit(solution)/shard_map/sum_texts/all_to_all | solution.py:26
  110.0 13.0 %collective-permute-start.10 = (bf16[16,1536]{1,0:T(8,128)(2,1)S(1)}, bf16[16,1536]{1,0:T(8,128)(2,1)S(1)}, u32[]{:S(2)}, u32[]{:S(2)}) collective-permute-start(bf16[16,1536]{1,0:T(8,128)(2,1)S(1)} %get-tuple-element.29), channel_id=1, source_target_pairs={{0,16},{16,32},{32,48},{48,0},{1,17},{17,33},{33,49},{49,1},{2,18}... | collective-permute-start | bytes 147464 | tf_op jit(solution)/shard_map/sum_images/ppermute | solution.py:40
  111.9 11.1 %collective-permute-start.12 = (bf16[16,1536]{1,0:T(8,128)(2,1)S(1)}, bf16[16,1536]{1,0:T(8,128)(2,1)S(1)}, u32[]{:S(2)}, u32[]{:S(2)}) collective-permute-start(bf16[16,1536]{1,0:T(8,128)(2,1)S(1)} %get-tuple-element.30), channel_id=1, source_target_pairs={{0,48},{16,0},{32,16},{48,32},{1,49},{17,1},{33,17},{49,33},{2,50}... | collective-permute-start | bytes 147464 | tf_op jit(solution)/shard_map/sum_images/ppermute | solution.py:40
  117.1 5.9 %collective-permute-start.11 = (bf16[16,1536]{1,0:T(8,128)(2,1)S(1)}, bf16[16,1536]{1,0:T(8,128)(2,1)S(1)}, u32[]{:S(2)}, u32[]{:S(2)}) collective-permute-start(bf16[16,1536]{1,0:T(8,128)(2,1)S(1)} %get-tuple-element.31), channel_id=1, source_target_pairs={{0,32},{16,48},{32,0},{48,16},{1,33},{17,49},{33,1},{49,17},{2,34}... | collective-permute-start | bytes 147464 | tf_op jit(solution)/shard_map/sum_images/ppermute | solution.py:40
  124.5 28.4 %all-to-all-start.5 = ((bf16[32,2,16,384]{3,2,1,0:T(8,128)(2,1)}), bf16[32,2,16,384]{3,2,1,0:T(8,128)(2,1)S(1)}, u32[]{:S(2)}, u32[]{:S(2)}) async-start(bf16[32,2,16,384]{3,2,1,0:T(8,128)(2,1)} %bitcast.11), calls=%async_computation.5 | async-start | bytes 1572864 | tf_op jit(solution)/shard_map/head_grads/all_to_all | solution.py:26
  138.2 14.0 %collective-permute-start.17 = (bf16[2,2,128,192]{2,3,1,0:T(8,128)(2,1)S(1)}, bf16[2,2,128,192]{2,3,1,0:T(8,128)(2,1)S(1)}, u32[]{:S(2)}, u32[]{:S(2)}) collective-permute-start(bf16[2,2,128,192]{2,3,1,0:T(8,128)(2,1)S(1)} %pad_maximum_fusion.3), channel_id=1, source_target_pairs={{0,256},{256,0},{1,257},{257,1},{2,258},{258,2},{3,259},{259,3},{4... | collective-permute-start | bytes 589832 | tf_op jit(solution)/shard_map/gather_features/ppermute | solution.py:40
  200.1 20.6 %all-to-all-start.8 = ((bf16[4,8,24,384]{3,2,1,0:T(8,128)(2,1)}), bf16[4,8,24,384]{3,2,1,0:T(8,128)(2,1)S(1)}, u32[]{:S(2)}, u32[]{:S(2)}) async-start(bf16[4,8,24,384]{3,2,1,0:T(8,128)(2,1)} %broadcast_in_dim.17), calls=%async_computation.8 | async-start | bytes 1179648 | tf_op jit(solution)/shard_map/weight_grads/all_to_all | solution.py:26
  206.1 7.4 %collective-permute-start.14 = (bf16[2,2,128,192]{2,3,1,0:T(8,128)(2,1)S(1)}, bf16[2,2,128,192]{2,3,1,0:T(8,128)(2,1)S(1)}, u32[]{:S(2)}, u32[]{:S(2)}) collective-permute-start(bf16[2,2,128,192]{2,3,1,0:T(8,128)(2,1)S(1)} %fusion.25), channel_id=1, source_target_pairs={{0,8},{8,0},{1,9},{9,1},{2,10},{10,2},{3,11},{11,3},{4,12},{12,4},... | collective-permute-start | bytes 589832 | tf_op jit(solution)/shard_map/input_grads/ppermute | solution.py:40
  213.6 6.4 %collective-permute-start.15 = (bf16[2,128,192]{1,2,0:T(8,128)(2,1)S(1)}, bf16[2,128,192]{1,2,0:T(8,128)(2,1)S(1)}, u32[]{:S(2)}, u32[]{:S(2)}) collective-permute-start(bf16[2,128,192]{1,2,0:T(8,128)(2,1)S(1)} %fusion.32), channel_id=1, source_target_pairs={{0,256},{256,0},{1,257},{257,1},{2,258},{258,2},{3,259},{259,3},{4... | collective-permute-start | bytes 294920 | tf_op jit(solution)/shard_map/input_grads/ppermute | solution.py:40
  221.7 4.5 %collective-permute-start.18 = (bf16[2,192,768]{2,1,0:T(8,128)(2,1)S(1)}, bf16[2,192,768]{2,1,0:T(8,128)(2,1)S(1)}, u32[]{:S(2)}, u32[]{:S(2)}) collective-permute-start(bf16[2,192,768]{2,1,0:T(8,128)(2,1)S(1)} %reshape.127), channel_id=1, source_target_pairs={{0,8},{8,0},{1,9},{9,1},{2,10},{10,2},{3,11},{11,3},{4,12},{12,4},... | collective-permute-start | bytes 1769480 | tf_op jit(solution)/shard_map/weight_grads/ppermute | solution.py:40
  226.3 1.0 copy-start
  226.3 1.4 copy-start.1

commit v12 on v11

--- a/solution.py
+++ b/solution.py
@@ -52,6 +52,11 @@
     for k in range(1, n):
         own = own + shifted(blocks[k].astype(BF16), axis, k).astype(F32)
     return own
+
+
+def in_order(mine, theirs, place):
+    first = place == 0
+    return jnp.stack((jnp.where(first, mine, theirs), jnp.where(first, theirs, mine)))
 
 
 def split_rows(value, n):
@@ -148,9 +153,31 @@
 
     with jax.named_scope("heads"):
         partial_heads = project(image_features, text_features, image_weight, text_weight)
-        both_heads = scatter_sum(split_rows(partial_heads, members), MP).astype(BF16)
+        together = lax.optimization_barrier
+        features = jnp.stack((image_features.T, text_features.T))
+        partial_heads, features = together((partial_heads, features))
+        received = exchange(split_rows(partial_heads, members), MP)
+        other_core = shifted(features, "c", 1)
+        other_pair = shifted(features, "z0", 1)
+        opposite = lax.ppermute(features, ("z0", "c"), [(i, 3 - i) for i in range(4)])
+        received, other_core, other_pair, opposite = together(
+            (received, other_core, other_pair, opposite)
+        )
+        both_heads = jnp.sum(received.astype(F32), axis=0).astype(BF16)
         image_unit, image_norm = unit_rows(both_heads[:, :embed_width])
         text_unit, text_norm = unit_rows(both_heads[:, embed_width:])
+
+    core, pair = at["c"], at["z0"]
+    quarter = embed_width // 4
+
+    with jax.named_scope("features"):
+        features = in_order(
+            in_order(features, other_core, core), in_order(other_pair, opposite, core), pair
+        )
+        image_columns, text_columns = (
+            jnp.concatenate([features[i, j, head] for i in range(2) for j in range(2)], axis=1)
+            for head in range(2)
+        )
 
     with jax.named_scope("gather_texts"):
         texts = merge_rows(gather(text_unit.astype(BF16), "zh"))
@@ -186,20 +213,6 @@
     with jax.named_scope("sum_images"):
         image_grads = ring_scatter_sum(ring_scatter_sum(image_part, "y"), ZL)
 
-    core, side = at["c"], at["xl"]
-    quarter = embed_width // 4
-
-    def in_order(mine, theirs, place):
-        first = place == 0
-        return jnp.stack((jnp.where(first, mine, theirs), jnp.where(first, theirs, mine)))
-
-    with jax.named_scope("gather_features"):
-        features = jnp.stack((image_features, text_features))
-        features = in_order(features, shifted(features, "c", 1), core)
-        features = in_order(features, shifted(features, "xl", 1), side)
-        width = features.shape[-1]
-        image_rows, text_rows = (features[:, :, i].reshape(-1, width) for i in range(2))
-
     with jax.named_scope("head_grads"):
         grads = jnp.stack(
             (
@@ -209,37 +222,12 @@
         )
         grads = grads.reshape(2, share, 2, 2, quarter).transpose(3, 2, 0, 1, 4)
         grads = jnp.broadcast_to(grads[:, :, None], (2, 2, members, 2, share, quarter))
-        grads = exchange(grads.reshape(4 * members, 2, share, quarter), ("xl", "c") + MP)
+        grads = exchange(grads.reshape(4 * members, 2, share, quarter), ("z0", "c") + MP)
         image_grads, text_grads = merge_rows(grads[:, 0]), merge_rows(grads[:, 1])
 
-    with jax.named_scope("weight_grads"):
-        eighth = width // 8
-        part = jnp.stack(
-            [
-                jnp.dot(rows.T, grads, preferred_element_type=F32)
-                .astype(BF16)
-                .reshape(2, 4, eighth, quarter)
-                for rows, grads in ((image_rows, image_grads), (text_rows, text_grads))
-            ]
-        )
-        part = part.transpose(2, 0, 1, 3, 4).reshape(16, eighth, quarter)
-        part = scatter_sum(part, ("zh", "zm", "z0")).astype(BF16)
-        part = gather(part, ("zh", "zm"))
-        part = gather(part, ("xl", "z0")).reshape(2, 2, 4, 2, eighth, quarter)
-        part = part.transpose(3, 1, 2, 4, 0, 5).reshape(2, width, 2 * quarter)
-        part = lax.optimization_barrier(part)
-        other = shifted(part, "c", 1)
-
-        def halves(mine, theirs):
-            mine, theirs = mine.astype(F32), theirs.astype(F32)
-            both = jnp.concatenate((mine, mine), axis=1)
-            return lax.dynamic_update_slice_in_dim(both, theirs, (1 - core) * 2 * quarter, 1)
-
-        image_weight_grad = halves(part[0], other[0])
-        text_weight_grad = halves(part[1], other[1])
-
     with jax.named_scope("input_grads"):
-        start = (core * 2 + side) * quarter
+        start = (core * 2 + pair) * quarter
+        width = image_weight.shape[0]
         inputs = jnp.stack(
             [
                 contract(grads, lax.dynamic_slice_in_dim(weight, start, quarter, 1), 1, 1)
@@ -253,8 +241,31 @@
             )
             return kept + shifted(sent.astype(BF16), name, 1).astype(F32)
 
-        inputs = half_sum(inputs, core, 2, "c")
-        inputs = half_sum(inputs, side, 1, "xl")
+        inputs = half_sum(half_sum(inputs, core, 2, "c"), pair, 1, "z0")
+
+    with jax.named_scope("weight_grads"):
+        part = jnp.stack(
+            [
+                contract(image_columns, image_grads, 1, 0),
+                contract(text_columns, text_grads, 1, 0),
+            ]
+        )
+        part = half_sum(part, at["xl"], 0, "xl")
+        part = scatter_sum(split_rows(part, 8), ("zh", "zm")).astype(BF16)
+        part, inputs = lax.optimization_barrier((part, inputs))
+        part = merge_rows(gather(part, ("zh", "zm")))
+        part = gather(part, ("xl", "z0")).reshape(2, 2, width, quarter)
+        part = part.transpose(0, 2, 1, 3).reshape(2, width, 2 * quarter)
+        part = lax.optimization_barrier(part)
+        other = shifted(part, "c", 1)
+
+        def halves(mine, theirs):
+            mine, theirs = mine.astype(F32), theirs.astype(F32)
+            both = jnp.concatenate((mine, mine), axis=1)
+            return lax.dynamic_update_slice_in_dim(both, theirs, (1 - core) * 2 * quarter, 1)
+
+        image_weight_grad = halves(part[0], other[0])
+        text_weight_grad = halves(part[1], other[1])
     return (inputs[0], inputs[1], image_weight_grad, text_weight_grad)
 
 

time: 229 us -> 224 us (0.978)
  blocking collectives: 45.6 us -> 19.7 us
  starting transfers between devices: 123 us -> 135 us
  waiting for transfers between devices: 35 us -> 44.6 us
    all_to_all x2 -> x1, blocking collectives: 45.6 us -> 19.7 us  [exchange(): return lax.all_to_all(blocks, axes, split_axis=0, concat_axis=0, tiled=True)]
    all_to_all x7 -> x8, waiting for transfers between devices: 16.7 us -> 32.2 us  [exchange(): return lax.all_to_all(blocks, axes, split_axis=0, concat_axis=0, tiled=True)]
    ppermute x19 -> x20, waiting for transfers between devices: 18.3 us -> 12.4 us  [shifted(): return lax.ppermute(value, axis, [(i, (i + by) % n) for i in range(n)])]
    all_to_all x7 -> x8, starting transfers between devices: 54.8 us -> 60.5 us  [exchange(): return lax.all_to_all(blocks, axes, split_axis=0, concat_axis=0, tiled=True)]
    ppermute x0 -> x1, starting transfers between devices: none -> 4.37 us  [on_device(): lax.ppermute(features, ('z0', 'c'), [(i, 3 - i) for i in range(4)])]
    ppermute x19 -> x20, starting transfers between devices: 68 us -> 70.3 us  [shifted(): return lax.ppermute(value, axis, [(i, (i + by) % n) for i in range(n)])]
  transfers between devices with their start and end apart: 26 -> 29, of which waited for: 9 -> 13; matrix products, arithmetic and copies ran while one was open for 5% -> 4% of each run, Pallas kernels for 0% -> 0%
where the time goes in v12:
time: 224 us; the launch traced here: 222 us
  starting transfers between devices  135 us (60%)
  waiting for transfers between devices  44.6 us (20%)
  blocking collectives  19.7 us (9%)
  local copies, waits for them, and re-layouts  6.71 us (3%)
  matrix products  6.18 us (3%)
  other arithmetic  3.96 us (2%)
  between operations  3.29 us (1%)
  Pallas kernels  2.59 us (1%)
    ppermute x20, starting transfers between devices, shifted(): return lax.ppermute(value, axis, [(i, (i + by) % n) for i in range(n)])  70.3 us
    all_to_all x8, starting transfers between devices, exchange(): return lax.all_to_all(blocks, axes, split_axis=0, concat_axis=0, tiled=True)  60.5 us
    all_to_all x8, waiting for transfers between devices, exchange(): return lax.all_to_all(blocks, axes, split_axis=0, concat_axis=0, tiled=True)  32.2 us
    all_to_all x1, blocking collectives, exchange(): return lax.all_to_all(blocks, axes, split_axis=0, concat_axis=0, tiled=True)  19.7 us
    ppermute x20, waiting for transfers between devices, shifted(): return lax.ppermute(value, axis, [(i, (i + by) % n) for i in range(n)])  12.4 us
  transfers between devices with their start and end apart: 29, of which 13 were waited for; matrix products, arithmetic and copies ran while one was open for 4% of the time, Pallas kernels for 0%

profile of v12, /device:TPU:1, one launch (start us, length us, event | category | flops | bytes accessed | tf_op | source)
XLA Modules:
  0.0 222.2 jit_solution(5824962669722302641)
XLA Ops:
  0.6 0.8 pad_maximum_fusion.3
  1.5 2.6 %heads.1 = bf16[128,3072]{1,0:T(8,128)(2,1)} custom-call(bf16[192,128]{1,0:T(8,128)(2,1)} %bitcast.142, bf16[192,1536]{1,0:T(8,128)(2,1)} %refs_1_.1, bf16[192,128]{1,0:T(8,128)(2,1)} %bitcast.144, bf16[192,1536]{1,0:T(8,128)(2,1)} %refs_3_.1), custom_call_target="tpu_custom_call" | custom-call | flops 150994944 | bytes 2064384 | tf_op jit(solution)/shard_map/heads/pallas_call | solution.py:76
  4.1 7.5 %all-to-all-start = ((bf16[8,16,3072]{2,1,0:T(8,128)(2,1)}), bf16[8,16,3072]{2,1,0:T(8,128)(2,1)S(1)}, u32[]{:S(2)}, u32[]{:S(2)}) async-start(bf16[8,16,3072]{2,1,0:T(8,128)(2,1)} %bitcast.131), calls=%async_computation | async-start | bytes 1572864 | tf_op jit(solution)/shard_map/heads/all_to_all | solution.py:26
  11.6 4.4 %collective-permute-start.2 = (bf16[2,192,128]{2,1,0:T(8,128)(2,1)S(1)}, bf16[2,192,128]{2,1,0:T(8,128)(2,1)S(1)}, u32[]{:S(2)}, u32[]{:S(2)}) collective-permute-start(bf16[2,192,128]{2,1,0:T(8,128)(2,1)S(1)} %pad_maximum_fusion.3), channel_id=1, source_target_pairs={{0,24},{8,16},{16,8},{24,0},{1,25},{9,17},{17,9},{25,1},{2,26},{10... | collective-permute-start | bytes 294920 | tf_op jit(solution)/shard_map/heads/ppermute | solution.py:162
  15.9 3.8 %collective-permute-start.1 = (bf16[2,192,128]{2,1,0:T(8,128)(2,1)S(1)}, bf16[2,192,128]{2,1,0:T(8,128)(2,1)S(1)}, u32[]{:S(2)}, u32[]{:S(2)}) collective-permute-start(bf16[2,192,128]{2,1,0:T(8,128)(2,1)S(1)} %pad_maximum_fusion.3), channel_id=1, source_target_pairs={{0,16},{16,0},{1,17},{17,1},{2,18},{18,2},{3,19},{19,3},{4,20},{20... | collective-permute-start | bytes 294920 | tf_op jit(solution)/shard_map/heads/ppermute | solution.py:40
  19.7 1.9 collective-permute-start
  21.7 0.9 collective-permute-done.1
  22.5 0.4 collective-permute-done
  23.2 0.7 broadcast_in_dim.14
  24.0 16.7 %all-to-all-start.1 = ((bf16[4,16,1536]{2,1,0:T(8,128)(2,1)}), bf16[4,16,1536]{2,1,0:T(8,128)(2,1)S(1)}, u32[]{:S(2)}, u32[]{:S(2)}) async-start(bf16[4,16,1536]{2,1,0:T(8,128)(2,1)} %broadcast_in_dim.14), calls=%async_computation.1 | async-start | bytes 393216 | tf_op jit(solution)/shard_map/gather_texts/all_to_all | solution.py:26
  40.7 2.6 %collective-permute-start.5 = (bf16[16,1536]{1,0:T(8,128)(2,1)S(1)}, bf16[16,1536]{1,0:T(8,128)(2,1)S(1)}, u32[]{:S(2)}, u32[]{:S(2)}) collective-permute-start(bf16[16,1536]{1,0:T(8,128)(2,1)S(1)} %get-tuple-element.27), channel_id=1, source_target_pairs={{0,16},{16,32},{32,48},{48,0},{1,17},{17,33},{33,49},{49,1},{2,18}... | collective-permute-start | bytes 147464 | tf_op jit(solution)/shard_map/gather_images/ppermute | solution.py:40
  43.3 3.1 %collective-permute-start.4 = (bf16[16,1536]{1,0:T(8,128)(2,1)S(1)}, bf16[16,1536]{1,0:T(8,128)(2,1)S(1)}, u32[]{:S(2)}, u32[]{:S(2)}) collective-permute-start(bf16[16,1536]{1,0:T(8,128)(2,1)S(1)} %get-tuple-element.27), channel_id=1, source_target_pairs={{0,32},{16,48},{32,0},{48,16},{1,33},{17,49},{33,1},{49,17},{2,34}... | collective-permute-start | bytes 147464 | tf_op jit(solution)/shard_map/gather_images/ppermute | solution.py:40
  46.4 3.6 %collective-permute-start.3 = (bf16[16,1536]{1,0:T(8,128)(2,1)S(1)}, bf16[16,1536]{1,0:T(8,128)(2,1)S(1)}, u32[]{:S(2)}, u32[]{:S(2)}) collective-permute-start(bf16[16,1536]{1,0:T(8,128)(2,1)S(1)} %get-tuple-element.27), channel_id=1, source_target_pairs={{0,48},{16,0},{32,16},{48,32},{1,49},{17,1},{33,17},{49,33},{2,50}... | collective-permute-start | bytes 147464 | tf_op jit(solution)/shard_map/gather_images/ppermute | solution.py:40
  52.0 1.4 all-to-all-done.1
  53.3 0.9 broadcast_in_dim.16
  54.3 3.5 %all-to-all-start.2 = ((bf16[4,64,1536]{2,1,0:T(8,128)(2,1)}), bf16[4,64,1536]{2,1,0:T(8,128)(2,1)S(1)}, u32[]{:S(2)}, u32[]{:S(2)}) async-start(bf16[4,64,1536]{2,1,0:T(8,128)(2,1)} %broadcast_in_dim.16), calls=%async_computation.2 | async-start | bytes 1572864 | tf_op jit(solution)/shard_map/gather_texts/all_to_all | solution.py:26
  57.8 1.9 collective-permute-start.8
  59.8 4.0 %collective-permute-start.7 = (bf16[64,1536]{1,0:T(8,128)(2,1)S(1)}, bf16[64,1536]{1,0:T(8,128)(2,1)S(1)}, u32[]{:S(2)}, u32[]{:S(2)}) collective-permute-start(bf16[64,1536]{1,0:T(8,128)(2,1)S(1)} %pad_maximum_fusion.2), channel_id=1, source_target_pairs={{0,4},{2,6},{4,0},{6,2},{1,5},{3,7},{5,1},{7,3},{8,12},{10,14},{12... | collective-permute-start | bytes 589832 | tf_op jit(solution)/shard_map/gather_images/ppermute | solution.py:40
  63.7 2.8 %collective-permute-start.6 = (bf16[64,1536]{1,0:T(8,128)(2,1)S(1)}, bf16[64,1536]{1,0:T(8,128)(2,1)S(1)}, u32[]{:S(2)}, u32[]{:S(2)}) collective-permute-start(bf16[64,1536]{1,0:T(8,128)(2,1)S(1)} %pad_maximum_fusion.2), channel_id=1, source_target_pairs={{0,6},{2,0},{4,2},{6,4},{1,7},{3,1},{5,3},{7,5},{8,14},{10,8},{12,... | collective-permute-start | bytes 589832 | tf_op jit(solution)/shard_map/gather_images/ppermute | solution.py:40
  66.6 10.1 %collective-permute-start.9 = (bf16[256,1536]{1,0:T(8,128)(2,1)S(1)}, bf16[256,1536]{1,0:T(8,128)(2,1)S(1)}, u32[]{:S(2)}, u32[]{:S(2)}) collective-permute-start(bf16[256,1536]{1,0:T(8,128)(2,1)S(1)} %bitcast.128), channel_id=1, source_target_pairs={{0,8},{8,0},{1,9},{9,1},{2,10},{10,2},{3,11},{11,3},{4,12},{12,4},... | collective-permute-start | bytes 2359304 | tf_op jit(solution)/shard_map/gather_texts/ppermute | solution.py:40
  76.9 1.8 collective-permute-done.9
  78.6 0.4 fusion.14
  79.1 0.4 convolution_convert_fusion
  79.4 2.6 %collective-permute-start.16 = (bf16[256,1536]{1,0:T(8,128)(2,1)S(1)}, bf16[256,1536]{1,0:T(8,128)(2,1)S(1)}, u32[]{:S(2)}, u32[]{:S(2)}) collective-permute-start(bf16[256,1536]{1,0:T(8,128)(2,1)S(1)} %convolution_convert_fusion), channel_id=1, source_target_pairs={{0,8},{8,0},{1,9},{9,1},{2,10},{10,2},{3,11},{11,3},{4,12},{12,4},... | collective-permute-start | bytes 2359304 | tf_op jit(solution)/shard_map/sum_texts/ppermute | solution.py:40
  82.1 0.4 fusion.15
  82.5 0.4 fusion.68
  82.9 0.4 fusion.67
  83.3 0.7 collective-permute-done.16
  84.0 1.3 fusion
  85.2 4.5 %all-to-all-start.3 = ((bf16[4,64,1536]{2,1,0:T(8,128)(2,1)}), bf16[4,64,1536]{2,1,0:T(8,128)(2,1)S(1)}, u32[]{:S(2)}, u32[]{:S(2)}) async-start(bf16[4,64,1536]{2,1,0:T(8,128)(2,1)} %bitcast.18), calls=%async_computation.3 | async-start | bytes 1572864 | tf_op jit(solution)/shard_map/sum_texts/all_to_all | solution.py:26
  89.7 0.8 fusion.65
  90.5 3.0 %collective-permute-start.10 = (bf16[64,1536]{1,0:T(8,128)(2,1)}, bf16[64,1536]{1,0:T(8,128)(2,1)S(1)}, u32[]{:S(2)}, u32[]{:S(2)}) collective-permute-start(bf16[64,1536]{1,0:T(8,128)(2,1)} %get-tuple-element.30), channel_id=1, source_target_pairs={{0,2},{2,4},{4,6},{6,0},{1,3},{3,5},{5,7},{7,1},{8,10},{10,12},{12... | collective-permute-start | bytes 589832 | tf_op jit(solution)/shard_map/sum_images/ppermute | solution.py:40
  93.5 3.4 %collective-permute-start.12 = (bf16[64,1536]{1,0:T(8,128)(2,1)}, bf16[64,1536]{1,0:T(8,128)(2,1)S(1)}, u32[]{:S(2)}, u32[]{:S(2)}) collective-permute-start(bf16[64,1536]{1,0:T(8,128)(2,1)} %get-tuple-element.31), channel_id=1, source_target_pairs={{0,6},{2,0},{4,2},{6,4},{1,7},{3,1},{5,3},{7,5},{8,14},{10,8},{12,... | collective-permute-start | bytes 589832 | tf_op jit(solution)/shard_map/sum_images/ppermute | solution.py:40
  97.0 2.5 %collective-permute-start.11 = (bf16[64,1536]{1,0:T(8,128)(2,1)S(1)}, bf16[64,1536]{1,0:T(8,128)(2,1)S(1)}, u32[]{:S(2)}, u32[]{:S(2)}) collective-permute-start(bf16[64,1536]{1,0:T(8,128)(2,1)S(1)} %get-tuple-element.32), channel_id=1, source_target_pairs={{0,4},{2,6},{4,0},{6,2},{1,5},{3,7},{5,1},{7,3},{8,12},{10,14},{12... | collective-permute-start | bytes 589832 | tf_op jit(solution)/shard_map/sum_images/ppermute | solution.py:40
  99.5 1.9 all-to-all-done.3
  101.4 0.8 reduce_sum.85
  102.2 5.9 %all-to-all-start.4 = ((bf16[4,16,1536]{2,1,0:T(8,128)(2,1)}), bf16[4,16,1536]{2,1,0:T(8,128)(2,1)S(1)}, u32[]{:S(2)}, u32[]{:S(2)}) async-start(bf16[4,16,1536]{2,1,0:T(8,128)(2,1)} %bitcast.19), calls=%async_computation.4 | async-start | bytes 393216 | tf_op jit(solution)/shard_map/sum_texts/all_to_all | solution.py:26
  108.3 1.9 collective-permute-start.13
  110.2 5.2 %collective-permute-start.15 = (bf16[16,1536]{1,0:T(8,128)(2,1)S(1)}, bf16[16,1536]{1,0:T(8,128)(2,1)S(1)}, u32[]{:S(2)}, u32[]{:S(2)}) collective-permute-start(bf16[16,1536]{1,0:T(8,128)(2,1)S(1)} %get-tuple-element.54), channel_id=1, source_target_pairs={{0,48},{16,0},{32,16},{48,32},{1,49},{17,1},{33,17},{49,33},{2,50}... | collective-permute-start | bytes 147464 | tf_op jit(solution)/shard_map/sum_images/ppermute | solution.py:40
  115.4 1.9 collective-permute-start.14
  117.3 4.4 %all-to-all-done.4 = bf16[4,16,1536]{2,1,0:T(8,128)(2,1)S(1)} async-done(((bf16[4,16,1536]{2,1,0:T(8,128)(2,1)}), bf16[4,16,1536]{2,1,0:T(8,128)(2,1)S(1)}, u32[]{:S(2)}, u32[]{:S(2)}) %all-to-all-start.4) | async-done | bytes 196640 | tf_op jit(solution)/shard_map/sum_texts/all_to_all | solution.py:26
  121.7 0.6 collective-permute-done.14
  122.9 1.0 broadcast_in_dim.17
  123.8 10.0 %all-to-all-start.5 = ((bf16[32,2,16,384]{3,2,1,0:T(8,128)(2,1)}), bf16[32,2,16,384]{3,2,1,0:T(8,128)(2,1)S(1)}, u32[]{:S(2)}, u32[]{:S(2)}) async-start(bf16[32,2,16,384]{3,2,1,0:T(8,128)(2,1)} %bitcast.21), calls=%async_computation.5 | async-start | bytes 1572864 | tf_op jit(solution)/shard_map/head_grads/all_to_all | solution.py:26
  134.0 14.0 %all-to-all-done.5 = bf16[32,2,16,384]{3,2,1,0:T(8,128)(2,1)S(1)} async-done(((bf16[32,2,16,384]{3,2,1,0:T(8,128)(2,1)}), bf16[32,2,16,384]{3,2,1,0:T(8,128)(2,1)S(1)}, u32[]{:S(2)}, u32[]{:S(2)}) %all-to-all-start.5) | async-done | bytes 786464 | tf_op jit(solution)/shard_map/head_grads/all_to_all | solution.py:26
  148.2 0.3 convolution_bitcast_fusion.3
  148.8 3.1 %collective-permute-start.17 = (bf16[192,384]{1,0:T(8,128)(2,1)S(1)}, bf16[192,384]{1,0:T(8,128)(2,1)S(1)}, u32[]{:S(2)}, u32[]{:S(2)}) collective-permute-start(bf16[192,384]{1,0:T(8,128)(2,1)S(1)} %fusion.45), channel_id=1, source_target_pairs={{0,256},{256,0},{1,257},{257,1},{2,258},{258,2},{3,259},{259,3},{4... | collective-permute-start | bytes 442376 | tf_op jit(solution)/shard_map/weight_grads/ppermute | solution.py:40
  151.9 1.2 convolution_bitcast_fusion.1
  153.1 1.2 convolution_bitcast_fusion
  154.4 2.6 %collective-permute-start.18 = (bf16[2,2,128,192]{2,3,1,0:T(8,128)(2,1)S(1)}, bf16[2,2,128,192]{2,3,1,0:T(8,128)(2,1)S(1)}, u32[]{:S(2)}, u32[]{:S(2)}) collective-permute-start(bf16[2,2,128,192]{2,3,1,0:T(8,128)(2,1)S(1)} %fusion.30), channel_id=1, source_target_pairs={{0,8},{8,0},{1,9},{9,1},{2,10},{10,2},{3,11},{11,3},{4,12},{12,4},... | collective-permute-start | bytes 589832 | tf_op jit(solution)/shard_map/input_grads/ppermute | solution.py:40
  157.0 0.7 fusion.28
  157.8 9.0 %all-to-all-start.6 = ((bf16[8,24,384]{2,1,0:T(8,128)(2,1)}), bf16[8,24,384]{2,1,0:T(8,128)(2,1)S(1)}, u32[]{:S(2)}, u32[]{:S(2)}) async-start(bf16[8,24,384]{2,1,0:T(8,128)(2,1)} %bitcast.32), calls=%async_computation.6 | async-start | bytes 294912 | tf_op jit(solution)/shard_map/weight_grads/all_to_all | solution.py:26
  166.9 3.1 %collective-permute-start.19 = (bf16[2,128,192]{1,2,0:T(8,128)(2,1)S(1)}, bf16[2,128,192]{1,2,0:T(8,128)(2,1)S(1)}, u32[]{:S(2)}, u32[]{:S(2)}) collective-permute-start(bf16[2,128,192]{1,2,0:T(8,128)(2,1)S(1)} %fusion.52), channel_id=1, source_target_pairs={{0,16},{16,0},{1,17},{17,1},{2,18},{18,2},{3,19},{19,3},{4,20},{20... | collective-permute-start | bytes 294920 | tf_op jit(solution)/shard_map/input_grads/ppermute | solution.py:40
  170.0 6.7 %collective-permute-done.19 = bf16[2,128,192]{1,2,0:T(8,128)(2,1)S(1)} collective-permute-done((bf16[2,128,192]{1,2,0:T(8,128)(2,1)S(1)}, bf16[2,128,192]{1,2,0:T(8,128)(2,1)S(1)}, u32[]{:S(2)}, u32[]{:S(2)}) %collective-permute-start.19) | collective-permute-done | bytes 98336 | tf_op jit(solution)/shard_map/input_grads/ppermute | solution.py:40
  176.7 5.4 %all-to-all-done.6 = bf16[8,24,384]{2,1,0:T(8,128)(2,1)S(1)} async-done(((bf16[8,24,384]{2,1,0:T(8,128)(2,1)}), bf16[8,24,384]{2,1,0:T(8,128)(2,1)S(1)}, u32[]{:S(2)}, u32[]{:S(2)}) %all-to-all-start.6) | async-done | bytes 147488 | tf_op jit(solution)/shard_map/weight_grads/all_to_all | solution.py:26
  182.1 19.7 %all_to_all.45 = bf16[8,24,384]{2,1,0:T(8,128)(2,1)S(1)} all-to-all(bf16[8,24,384]{2,1,0:T(8,128)(2,1)S(1)} %broadcast_in_dim.18), channel_id=1, replica_groups=mesh['xl'=2,'zh'=4,'zm'=2,'z0'=2,'c'=2,'y'=4,'xh'=2] {'zh','zm'}, dimensions={0} | all-to-all | bytes 294912 | tf_op jit(solution)/shard_map/weight_grads/all_to_all | solution.py:26
  201.8 0.9 broadcast_in_dim.20
  202.7 3.5 %all-to-all-start.8 = ((bf16[4,192,384]{2,1,0:T(8,128)(2,1)}), bf16[4,192,384]{2,1,0:T(8,128)(2,1)S(1)}, u32[]{:S(2)}, u32[]{:S(2)}) async-start(bf16[4,192,384]{2,1,0:T(8,128)(2,1)} %broadcast_in_dim.20), calls=%async_computation.8 | async-start | bytes 1179648 | tf_op jit(solution)/shard_map/weight_grads/all_to_all | solution.py:26
  206.2 0.7 slice_bitcast_fusion.4
  206.9 5.1 %all-to-all-done.8 = bf16[4,192,384]{2,1,0:T(8,128)(2,1)S(1)} async-done(((bf16[4,192,384]{2,1,0:T(8,128)(2,1)}), bf16[4,192,384]{2,1,0:T(8,128)(2,1)S(1)}, u32[]{:S(2)}, u32[]{:S(2)}) %all-to-all-start.8) | async-done | bytes 589856 | tf_op jit(solution)/shard_map/weight_grads/all_to_all | solution.py:26
  212.0 7.0 %collective-permute-start.20 = (bf16[2,192,768]{2,1,0:T(8,128)(2,1)S(1)}, bf16[2,192,768]{2,1,0:T(8,128)(2,1)S(1)}, u32[]{:S(2)}, u32[]{:S(2)}) collective-permute-start(bf16[2,192,768]{2,1,0:T(8,128)(2,1)S(1)} %bitcast.133), channel_id=1, source_target_pairs={{0,8},{8,0},{1,9},{9,1},{2,10},{10,2},{3,11},{11,3},{4,12},{12,4},... | collective-permute-start | bytes 1769480 | tf_op jit(solution)/shard_map/weight_grads/ppermute | solution.py:40
  219.3 1.4 collective-permute-done.20
  220.8 1.0 copy-done
  221.8 0.4 copy-done.1
  (71 shorter events, 2.3 us)
Async XLA Ops:
  4.1 18.8 %all-to-all-start = ((bf16[8,16,3072]{2,1,0:T(8,128)(2,1)}), bf16[8,16,3072]{2,1,0:T(8,128)(2,1)S(1)}, u32[]{:S(2)}, u32[]{:S(2)}) async-start(bf16[8,16,3072]{2,1,0:T(8,128)(2,1)} %bitcast.131), calls=%async_computation | async-start | bytes 1572864 | tf_op jit(solution)/shard_map/heads/all_to_all | solution.py:26
  11.6 10.1 %collective-permute-start.2 = (bf16[2,192,128]{2,1,0:T(8,128)(2,1)S(1)}, bf16[2,192,128]{2,1,0:T(8,128)(2,1)S(1)}, u32[]{:S(2)}, u32[]{:S(2)}) collective-permute-start(bf16[2,192,128]{2,1,0:T(8,128)(2,1)S(1)} %pad_maximum_fusion.3), channel_id=1, source_target_pairs={{0,24},{8,16},{16,8},{24,0},{1,25},{9,17},{17,9},{25,1},{2,26},{10... | collective-permute-start | bytes 294920 | tf_op jit(solution)/shard_map/heads/ppermute | solution.py:162
  15.9 6.6 %collective-permute-start.1 = (bf16[2,192,128]{2,1,0:T(8,128)(2,1)S(1)}, bf16[2,192,128]{2,1,0:T(8,128)(2,1)S(1)}, u32[]{:S(2)}, u32[]{:S(2)}) collective-permute-start(bf16[2,192,128]{2,1,0:T(8,128)(2,1)S(1)} %pad_maximum_fusion.3), channel_id=1, source_target_pairs={{0,16},{16,0},{1,17},{17,1},{2,18},{18,2},{3,19},{19,3},{4,20},{20... | collective-permute-start | bytes 294920 | tf_op jit(solution)/shard_map/heads/ppermute | solution.py:40
  19.7 3.2 %collective-permute-start = (bf16[2,192,128]{2,1,0:T(8,128)(2,1)S(1)}, bf16[2,192,128]{2,1,0:T(8,128)(2,1)S(1)}, u32[]{:S(2)}, u32[]{:S(2)}) collective-permute-start(bf16[2,192,128]{2,1,0:T(8,128)(2,1)S(1)} %pad_maximum_fusion.3), channel_id=1, source_target_pairs={{0,8},{8,0},{1,9},{9,1},{2,10},{10,2},{3,11},{11,3},{4,12},{12,4},... | collective-permute-start | bytes 294920 | tf_op jit(solution)/shard_map/heads/ppermute | solution.py:40
  21.6 2.3 %copy-start.2 = (bf16[2,192,128]{2,1,0:T(8,128)(2,1)}, bf16[2,192,128]{2,1,0:T(8,128)(2,1)S(1)}, u32[]{:S(2)}) copy-start(bf16[2,192,128]{2,1,0:T(8,128)(2,1)S(1)} %collective-permute-done.2) | copy-start | bytes 294916
  22.5 1.4 copy-start.4
  22.9 31.4 %copy-start.6 = (bf16[2,192,128]{2,1,0:T(8,128)(2,1)}, bf16[2,192,128]{2,1,0:T(8,128)(2,1)S(1)}, u32[]{:S(2)}) copy-start(bf16[2,192,128]{2,1,0:T(8,128)(2,1)S(1)} %collective-permute-done) | copy-start | bytes 294916
  24.0 29.4 %all-to-all-start.1 = ((bf16[4,16,1536]{2,1,0:T(8,128)(2,1)}), bf16[4,16,1536]{2,1,0:T(8,128)(2,1)S(1)}, u32[]{:S(2)}, u32[]{:S(2)}) async-start(bf16[4,16,1536]{2,1,0:T(8,128)(2,1)} %broadcast_in_dim.14), calls=%async_computation.1 | async-start | bytes 393216 | tf_op jit(solution)/shard_map/gather_texts/all_to_all | solution.py:26
  40.7 17.1 %collective-permute-start.5 = (bf16[16,1536]{1,0:T(8,128)(2,1)S(1)}, bf16[16,1536]{1,0:T(8,128)(2,1)S(1)}, u32[]{:S(2)}, u32[]{:S(2)}) collective-permute-start(bf16[16,1536]{1,0:T(8,128)(2,1)S(1)} %get-tuple-element.27), channel_id=1, source_target_pairs={{0,16},{16,32},{32,48},{48,0},{1,17},{17,33},{33,49},{49,1},{2,18}... | collective-permute-start | bytes 147464 | tf_op jit(solution)/shard_map/gather_images/ppermute | solution.py:40
  43.3 14.4 %collective-permute-start.4 = (bf16[16,1536]{1,0:T(8,128)(2,1)S(1)}, bf16[16,1536]{1,0:T(8,128)(2,1)S(1)}, u32[]{:S(2)}, u32[]{:S(2)}) collective-permute-start(bf16[16,1536]{1,0:T(8,128)(2,1)S(1)} %get-tuple-element.27), channel_id=1, source_target_pairs={{0,32},{16,48},{32,0},{48,16},{1,33},{17,49},{33,1},{49,17},{2,34}... | collective-permute-start | bytes 147464 | tf_op jit(solution)/shard_map/gather_images/ppermute | solution.py:40
  46.4 11.4 %collective-permute-start.3 = (bf16[16,1536]{1,0:T(8,128)(2,1)S(1)}, bf16[16,1536]{1,0:T(8,128)(2,1)S(1)}, u32[]{:S(2)}, u32[]{:S(2)}) collective-permute-start(bf16[16,1536]{1,0:T(8,128)(2,1)S(1)} %get-tuple-element.27), channel_id=1, source_target_pairs={{0,48},{16,0},{32,16},{48,32},{1,49},{17,1},{33,17},{49,33},{2,50}... | collective-permute-start | bytes 147464 | tf_op jit(solution)/shard_map/gather_images/ppermute | solution.py:40
  54.3 12.3 %all-to-all-start.2 = ((bf16[4,64,1536]{2,1,0:T(8,128)(2,1)}), bf16[4,64,1536]{2,1,0:T(8,128)(2,1)S(1)}, u32[]{:S(2)}, u32[]{:S(2)}) async-start(bf16[4,64,1536]{2,1,0:T(8,128)(2,1)} %broadcast_in_dim.16), calls=%async_computation.2 | async-start | bytes 1572864 | tf_op jit(solution)/shard_map/gather_texts/all_to_all | solution.py:26
  57.8 19.0 %collective-permute-start.8 = (bf16[64,1536]{1,0:T(8,128)(2,1)S(1)}, bf16[64,1536]{1,0:T(8,128)(2,1)S(1)}, u32[]{:S(2)}, u32[]{:S(2)}) collective-permute-start(bf16[64,1536]{1,0:T(8,128)(2,1)S(1)} %pad_maximum_fusion.2), channel_id=1, source_target_pairs={{0,2},{2,4},{4,6},{6,0},{1,3},{3,5},{5,7},{7,1},{8,10},{10,12},{12... | collective-permute-start | bytes 589832 | tf_op jit(solution)/shard_map/gather_images/ppermute | solution.py:40
  59.8 17.0 %collective-permute-start.7 = (bf16[64,1536]{1,0:T(8,128)(2,1)S(1)}, bf16[64,1536]{1,0:T(8,128)(2,1)S(1)}, u32[]{:S(2)}, u32[]{:S(2)}) collective-permute-start(bf16[64,1536]{1,0:T(8,128)(2,1)S(1)} %pad_maximum_fusion.2), channel_id=1, source_target_pairs={{0,4},{2,6},{4,0},{6,2},{1,5},{3,7},{5,1},{7,3},{8,12},{10,14},{12... | collective-permute-start | bytes 589832 | tf_op jit(solution)/shard_map/gather_images/ppermute | solution.py:40
  63.7 13.0 %collective-permute-start.6 = (bf16[64,1536]{1,0:T(8,128)(2,1)S(1)}, bf16[64,1536]{1,0:T(8,128)(2,1)S(1)}, u32[]{:S(2)}, u32[]{:S(2)}) collective-permute-start(bf16[64,1536]{1,0:T(8,128)(2,1)S(1)} %pad_maximum_fusion.2), channel_id=1, source_target_pairs={{0,6},{2,0},{4,2},{6,4},{1,7},{3,1},{5,3},{7,5},{8,14},{10,8},{12,... | collective-permute-start | bytes 589832 | tf_op jit(solution)/shard_map/gather_images/ppermute | solution.py:40
  66.6 12.0 %collective-permute-start.9 = (bf16[256,1536]{1,0:T(8,128)(2,1)S(1)}, bf16[256,1536]{1,0:T(8,128)(2,1)S(1)}, u32[]{:S(2)}, u32[]{:S(2)}) collective-permute-start(bf16[256,1536]{1,0:T(8,128)(2,1)S(1)} %bitcast.128), channel_id=1, source_target_pairs={{0,8},{8,0},{1,9},{9,1},{2,10},{10,2},{3,11},{11,3},{4,12},{12,4},... | collective-permute-start | bytes 2359304 | tf_op jit(solution)/shard_map/gather_texts/ppermute | solution.py:40
  79.4 4.5 %collective-permute-start.16 = (bf16[256,1536]{1,0:T(8,128)(2,1)S(1)}, bf16[256,1536]{1,0:T(8,128)(2,1)S(1)}, u32[]{:S(2)}, u32[]{:S(2)}) collective-permute-start(bf16[256,1536]{1,0:T(8,128)(2,1)S(1)} %convolution_convert_fusion), channel_id=1, source_target_pairs={{0,8},{8,0},{1,9},{9,1},{2,10},{10,2},{3,11},{11,3},{4,12},{12,4},... | collective-permute-start | bytes 2359304 | tf_op jit(solution)/shard_map/sum_texts/ppermute | solution.py:40
  85.2 16.2 %all-to-all-start.3 = ((bf16[4,64,1536]{2,1,0:T(8,128)(2,1)}), bf16[4,64,1536]{2,1,0:T(8,128)(2,1)S(1)}, u32[]{:S(2)}, u32[]{:S(2)}) async-start(bf16[4,64,1536]{2,1,0:T(8,128)(2,1)} %bitcast.18), calls=%async_computation.3 | async-start | bytes 1572864 | tf_op jit(solution)/shard_map/sum_texts/all_to_all | solution.py:26
  90.5 17.7 %collective-permute-start.10 = (bf16[64,1536]{1,0:T(8,128)(2,1)}, bf16[64,1536]{1,0:T(8,128)(2,1)S(1)}, u32[]{:S(2)}, u32[]{:S(2)}) collective-permute-start(bf16[64,1536]{1,0:T(8,128)(2,1)} %get-tuple-element.30), channel_id=1, source_target_pairs={{0,2},{2,4},{4,6},{6,0},{1,3},{3,5},{5,7},{7,1},{8,10},{10,12},{12... | collective-permute-start | bytes 589832 | tf_op jit(solution)/shard_map/sum_images/ppermute | solution.py:40
  93.5 14.7 %collective-permute-start.12 = (bf16[64,1536]{1,0:T(8,128)(2,1)}, bf16[64,1536]{1,0:T(8,128)(2,1)S(1)}, u32[]{:S(2)}, u32[]{:S(2)}) collective-permute-start(bf16[64,1536]{1,0:T(8,128)(2,1)} %get-tuple-element.31), channel_id=1, source_target_pairs={{0,6},{2,0},{4,2},{6,4},{1,7},{3,1},{5,3},{7,5},{8,14},{10,8},{12,... | collective-permute-start | bytes 589832 | tf_op jit(solution)/shard_map/sum_images/ppermute | solution.py:40
  97.0 11.2 %collective-permute-start.11 = (bf16[64,1536]{1,0:T(8,128)(2,1)S(1)}, bf16[64,1536]{1,0:T(8,128)(2,1)S(1)}, u32[]{:S(2)}, u32[]{:S(2)}) collective-permute-start(bf16[64,1536]{1,0:T(8,128)(2,1)S(1)} %get-tuple-element.32), channel_id=1, source_target_pairs={{0,4},{2,6},{4,0},{6,2},{1,5},{3,7},{5,1},{7,3},{8,12},{10,14},{12... | collective-permute-start | bytes 589832 | tf_op jit(solution)/shard_map/sum_images/ppermute | solution.py:40
  102.2 19.4 %all-to-all-start.4 = ((bf16[4,16,1536]{2,1,0:T(8,128)(2,1)}), bf16[4,16,1536]{2,1,0:T(8,128)(2,1)S(1)}, u32[]{:S(2)}, u32[]{:S(2)}) async-start(bf16[4,16,1536]{2,1,0:T(8,128)(2,1)} %bitcast.19), calls=%async_computation.4 | async-start | bytes 393216 | tf_op jit(solution)/shard_map/sum_texts/all_to_all | solution.py:26
  108.3 13.4 %collective-permute-start.13 = (bf16[16,1536]{1,0:T(8,128)(2,1)S(1)}, bf16[16,1536]{1,0:T(8,128)(2,1)S(1)}, u32[]{:S(2)}, u32[]{:S(2)}) collective-permute-start(bf16[16,1536]{1,0:T(8,128)(2,1)S(1)} %get-tuple-element.53), channel_id=1, source_target_pairs={{0,16},{16,32},{32,48},{48,0},{1,17},{17,33},{33,49},{49,1},{2,18}... | collective-permute-start | bytes 147464 | tf_op jit(solution)/shard_map/sum_images/ppermute | solution.py:40
  110.2 11.5 %collective-permute-start.15 = (bf16[16,1536]{1,0:T(8,128)(2,1)S(1)}, bf16[16,1536]{1,0:T(8,128)(2,1)S(1)}, u32[]{:S(2)}, u32[]{:S(2)}) collective-permute-start(bf16[16,1536]{1,0:T(8,128)(2,1)S(1)} %get-tuple-element.54), channel_id=1, source_target_pairs={{0,48},{16,0},{32,16},{48,32},{1,49},{17,1},{33,17},{49,33},{2,50}... | collective-permute-start | bytes 147464 | tf_op jit(solution)/shard_map/sum_images/ppermute | solution.py:40
  115.4 6.9 %collective-permute-start.14 = (bf16[16,1536]{1,0:T(8,128)(2,1)S(1)}, bf16[16,1536]{1,0:T(8,128)(2,1)S(1)}, u32[]{:S(2)}, u32[]{:S(2)}) collective-permute-start(bf16[16,1536]{1,0:T(8,128)(2,1)S(1)} %get-tuple-element.55), channel_id=1, source_target_pairs={{0,32},{16,48},{32,0},{48,16},{1,33},{17,49},{33,1},{49,17},{2,34}... | collective-permute-start | bytes 147464 | tf_op jit(solution)/shard_map/sum_images/ppermute | solution.py:40
  122.9 11.0 %copy-start.3 = (bf16[2,192,128]{2,1,0:T(8,128)(2,1)S(1)}, bf16[2,192,128]{2,1,0:T(8,128)(2,1)}, u32[]{:S(2)}) copy-start(bf16[2,192,128]{2,1,0:T(8,128)(2,1)} %copy-done.2) | copy-start | bytes 294916
  122.9 11.0 %copy-start.5 = (bf16[2,192,128]{2,1,0:T(8,128)(2,1)S(1)}, bf16[2,192,128]{2,1,0:T(8,128)(2,1)}, u32[]{:S(2)}) copy-start(bf16[2,192,128]{2,1,0:T(8,128)(2,1)} %copy-done.4) | copy-start | bytes 294916
  122.9 11.0 %copy-start.7 = (bf16[2,192,128]{2,1,0:T(8,128)(2,1)S(1)}, bf16[2,192,128]{2,1,0:T(8,128)(2,1)}, u32[]{:S(2)}) copy-start(bf16[2,192,128]{2,1,0:T(8,128)(2,1)} %copy-done.6) | copy-start | bytes 294916
  123.8 24.2 %all-to-all-start.5 = ((bf16[32,2,16,384]{3,2,1,0:T(8,128)(2,1)}), bf16[32,2,16,384]{3,2,1,0:T(8,128)(2,1)S(1)}, u32[]{:S(2)}, u32[]{:S(2)}) async-start(bf16[32,2,16,384]{3,2,1,0:T(8,128)(2,1)} %bitcast.21), calls=%async_computation.5 | async-start | bytes 1572864 | tf_op jit(solution)/shard_map/head_grads/all_to_all | solution.py:26
  148.8 8.3 %collective-permute-start.17 = (bf16[192,384]{1,0:T(8,128)(2,1)S(1)}, bf16[192,384]{1,0:T(8,128)(2,1)S(1)}, u32[]{:S(2)}, u32[]{:S(2)}) collective-permute-start(bf16[192,384]{1,0:T(8,128)(2,1)S(1)} %fusion.45), channel_id=1, source_target_pairs={{0,256},{256,0},{1,257},{257,1},{2,258},{258,2},{3,259},{259,3},{4... | collective-permute-start | bytes 442376 | tf_op jit(solution)/shard_map/weight_grads/ppermute | solution.py:40
  154.4 12.4 %collective-permute-start.18 = (bf16[2,2,128,192]{2,3,1,0:T(8,128)(2,1)S(1)}, bf16[2,2,128,192]{2,3,1,0:T(8,128)(2,1)S(1)}, u32[]{:S(2)}, u32[]{:S(2)}) collective-permute-start(bf16[2,2,128,192]{2,3,1,0:T(8,128)(2,1)S(1)} %fusion.30), channel_id=1, source_target_pairs={{0,8},{8,0},{1,9},{9,1},{2,10},{10,2},{3,11},{11,3},{4,12},{12,4},... | collective-permute-start | bytes 589832 | tf_op jit(solution)/shard_map/input_grads/ppermute | solution.py:40
  157.8 24.3 %all-to-all-start.6 = ((bf16[8,24,384]{2,1,0:T(8,128)(2,1)}), bf16[8,24,384]{2,1,0:T(8,128)(2,1)S(1)}, u32[]{:S(2)}, u32[]{:S(2)}) async-start(bf16[8,24,384]{2,1,0:T(8,128)(2,1)} %bitcast.32), calls=%async_computation.6 | async-start | bytes 294912 | tf_op jit(solution)/shard_map/weight_grads/all_to_all | solution.py:26
  166.9 9.8 %collective-permute-start.19 = (bf16[2,128,192]{1,2,0:T(8,128)(2,1)S(1)}, bf16[2,128,192]{1,2,0:T(8,128)(2,1)S(1)}, u32[]{:S(2)}, u32[]{:S(2)}) collective-permute-start(bf16[2,128,192]{1,2,0:T(8,128)(2,1)S(1)} %fusion.52), channel_id=1, source_target_pairs={{0,16},{16,0},{1,17},{17,1},{2,18},{18,2},{3,19},{19,3},{4,20},{20... | collective-permute-start | bytes 294920 | tf_op jit(solution)/shard_map/input_grads/ppermute | solution.py:40
  202.7 9.3 %all-to-all-start.8 = ((bf16[4,192,384]{2,1,0:T(8,128)(2,1)}), bf16[4,192,384]{2,1,0:T(8,128)(2,1)S(1)}, u32[]{:S(2)}, u32[]{:S(2)}) async-start(bf16[4,192,384]{2,1,0:T(8,128)(2,1)} %broadcast_in_dim.20), calls=%async_computation.8 | async-start | bytes 1179648 | tf_op jit(solution)/shard_map/weight_grads/all_to_all | solution.py:26
  212.0 8.6 %collective-permute-start.20 = (bf16[2,192,768]{2,1,0:T(8,128)(2,1)S(1)}, bf16[2,192,768]{2,1,0:T(8,128)(2,1)S(1)}, u32[]{:S(2)}, u32[]{:S(2)}) collective-permute-start(bf16[2,192,768]{2,1,0:T(8,128)(2,1)S(1)} %bitcast.133), channel_id=1, source_target_pairs={{0,8},{8,0},{1,9},{9,1},{2,10},{10,2},{3,11},{11,3},{4,12},{12,4},... | collective-permute-start | bytes 1769480 | tf_op jit(solution)/shard_map/weight_grads/ppermute | solution.py:40
  220.8 1.0 copy-start
  220.8 1.4 copy-start.1

commit v13 on v12

--- a/solution.py
+++ b/solution.py
@@ -153,31 +153,13 @@
 
     with jax.named_scope("heads"):
         partial_heads = project(image_features, text_features, image_weight, text_weight)
-        together = lax.optimization_barrier
-        features = jnp.stack((image_features.T, text_features.T))
-        partial_heads, features = together((partial_heads, features))
+        features = (image_features.T, text_features.T)
         received = exchange(split_rows(partial_heads, members), MP)
-        other_core = shifted(features, "c", 1)
-        other_pair = shifted(features, "z0", 1)
-        opposite = lax.ppermute(features, ("z0", "c"), [(i, 3 - i) for i in range(4)])
-        received, other_core, other_pair, opposite = together(
-            (received, other_core, other_pair, opposite)
-        )
+        other_features = tuple(shifted(value, "c", 1) for value in features)
+        received, other_features = lax.optimization_barrier((received, other_features))
         both_heads = jnp.sum(received.astype(F32), axis=0).astype(BF16)
         image_unit, image_norm = unit_rows(both_heads[:, :embed_width])
         text_unit, text_norm = unit_rows(both_heads[:, embed_width:])
-
-    core, pair = at["c"], at["z0"]
-    quarter = embed_width // 4
-
-    with jax.named_scope("features"):
-        features = in_order(
-            in_order(features, other_core, core), in_order(other_pair, opposite, core), pair
-        )
-        image_columns, text_columns = (
-            jnp.concatenate([features[i, j, head] for i in range(2) for j in range(2)], axis=1)
-            for head in range(2)
-        )
 
     with jax.named_scope("gather_texts"):
         texts = merge_rows(gather(text_unit.astype(BF16), "zh"))
@@ -213,6 +195,8 @@
     with jax.named_scope("sum_images"):
         image_grads = ring_scatter_sum(ring_scatter_sum(image_part, "y"), ZL)
 
+    core = at["c"]
+    half = embed_width // 2
     with jax.named_scope("head_grads"):
         grads = jnp.stack(
             (
@@ -220,49 +204,42 @@
                 head_back(text_unit, text_norm, text_grads),
             )
         )
-        grads = grads.reshape(2, share, 2, 2, quarter).transpose(3, 2, 0, 1, 4)
-        grads = jnp.broadcast_to(grads[:, :, None], (2, 2, members, 2, share, quarter))
-        grads = exchange(grads.reshape(4 * members, 2, share, quarter), ("z0", "c") + MP)
-        image_grads, text_grads = merge_rows(grads[:, 0]), merge_rows(grads[:, 1])
+        grads = grads.reshape(2, share, 2, half).transpose(2, 0, 1, 3)
+        grads = jnp.broadcast_to(grads[:, None], (2, members, 2, share, half))
+        grads = exchange(grads.reshape(2 * members, 2, share, half), ("c",) + MP)
+        grads = (merge_rows(grads[:, 0]), merge_rows(grads[:, 1]))
 
     with jax.named_scope("input_grads"):
-        start = (core * 2 + pair) * quarter
-        width = image_weight.shape[0]
+        width, rows = features[0].shape
         inputs = jnp.stack(
             [
-                contract(grads, lax.dynamic_slice_in_dim(weight, start, quarter, 1), 1, 1)
-                for grads, weight in ((image_grads, image_weight), (text_grads, text_weight))
+                contract(grad, lax.dynamic_slice_in_dim(weight, core * half, half, 1), 1, 1)
+                for grad, weight in zip(grads, (image_weight, text_weight))
             ]
-        ).reshape(2, 2, 2, members * share, width)
-
-        def half_sum(value, place, axis, name):
-            kept, sent = (
-                lax.dynamic_index_in_dim(value, i, axis, False) for i in (place, 1 - place)
-            )
-            return kept + shifted(sent.astype(BF16), name, 1).astype(F32)
-
-        inputs = half_sum(half_sum(inputs, core, 2, "c"), pair, 1, "z0")
+        ).reshape(2, 2, rows, width)
+        kept, sent = (lax.dynamic_index_in_dim(inputs, i, 1, False) for i in (core, 1 - core))
+        inputs = kept + shifted(sent.astype(BF16), "c", 1).astype(F32)
 
     with jax.named_scope("weight_grads"):
         part = jnp.stack(
             [
-                contract(image_columns, image_grads, 1, 0),
-                contract(text_columns, text_grads, 1, 0),
+                contract(jnp.concatenate(tuple(in_order(mine, theirs, core)), axis=1), grad, 1, 0)
+                for mine, theirs, grad in zip(features, other_features, grads)
             ]
         )
-        part = half_sum(part, at["xl"], 0, "xl")
-        part = scatter_sum(split_rows(part, 8), ("zh", "zm")).astype(BF16)
-        part, inputs = lax.optimization_barrier((part, inputs))
-        part = merge_rows(gather(part, ("zh", "zm")))
-        part = gather(part, ("xl", "z0")).reshape(2, 2, width, quarter)
-        part = part.transpose(0, 2, 1, 3).reshape(2, width, 2 * quarter)
-        part = lax.optimization_barrier(part)
+        part = scatter_sum(part.reshape(4, width // 2, half), ("xl", "z0"))
+        part = part.reshape(4, width // 8, 2, half // 2).swapaxes(1, 2)
+        part = scatter_sum(part.reshape(8, width // 8, half // 2), ("zh", "zm"))
+        part, inputs = lax.optimization_barrier((part.astype(BF16), inputs))
+        part = gather(part, ("zh", "zm")).reshape(4, 2, width // 8, half // 2)
+        part = part.swapaxes(1, 2).reshape(width // 2, half)
+        part = gather(part, ("xl", "z0")).reshape(2, width, half)
         other = shifted(part, "c", 1)
 
         def halves(mine, theirs):
             mine, theirs = mine.astype(F32), theirs.astype(F32)
             both = jnp.concatenate((mine, mine), axis=1)
-            return lax.dynamic_update_slice_in_dim(both, theirs, (1 - core) * 2 * quarter, 1)
+            return lax.dynamic_update_slice_in_dim(both, theirs, (1 - core) * half, 1)
 
         image_weight_grad = halves(part[0], other[0])
         text_weight_grad = halves(part[1], other[1])

time: 224 us -> 221 us (0.987)
  waiting for transfers between devices: 44.6 us -> 50.5 us
  starting transfers between devices: 135 us -> 131 us
  blocking collectives: 19.7 us -> 17.4 us
    all_to_all x8 -> x9, waiting for transfers between devices: 32.2 us -> 44 us  [exchange(): return lax.all_to_all(blocks, axes, split_axis=0, concat_axis=0, tiled=True)]
    ppermute x20 -> x18, waiting for transfers between devices: 12.4 us -> 6.5 us  [shifted(): return lax.ppermute(value, axis, [(i, (i + by) % n) for i in range(n)])]
    ppermute x1 -> x0, starting transfers between devices: 4.37 us -> none  [on_device(): lax.ppermute(features, ('z0', 'c'), [(i, 3 - i) for i in range(4)])]
    ppermute x20 -> x18, starting transfers between devices: 70.3 us -> 66.5 us  [shifted(): return lax.ppermute(value, axis, [(i, (i + by) % n) for i in range(n)])]
    all_to_all x8 -> x9, starting transfers between devices: 60.5 us -> 64.2 us  [exchange(): return lax.all_to_all(blocks, axes, split_axis=0, concat_axis=0, tiled=True)]
    all_to_all x1, blocking collectives: 19.7 us -> 17.4 us  [exchange(): return lax.all_to_all(blocks, axes, split_axis=0, concat_axis=0, tiled=True)]
  transfers between devices with their start and end apart: 29 -> 27, of which waited for: 13 -> 14; matrix products, arithmetic and copies ran while one was open for 4% -> 3% of each run, Pallas kernels for 0% -> 0%
where the time goes in v13:
time: 221 us; the launch traced here: 219 us
  starting transfers between devices  131 us (59%)
  waiting for transfers between devices  50.5 us (23%)
  blocking collectives  17.4 us (8%)
  local copies, waits for them, and re-layouts  7.44 us (3%)
  matrix products  4.34 us (2%)
  between operations  3.23 us (1%)
  other arithmetic  3.19 us (1%)
  Pallas kernels  2.59 us (1%)
    ppermute x18, starting transfers between devices, shifted(): return lax.ppermute(value, axis, [(i, (i + by) % n) for i in range(n)])  66.5 us
    all_to_all x9, starting transfers between devices, exchange(): return lax.all_to_all(blocks, axes, split_axis=0, concat_axis=0, tiled=True)  64.2 us
    all_to_all x9, waiting for transfers between devices, exchange(): return lax.all_to_all(blocks, axes, split_axis=0, concat_axis=0, tiled=True)  44 us
    all_to_all x1, blocking collectives, exchange(): return lax.all_to_all(blocks, axes, split_axis=0, concat_axis=0, tiled=True)  17.4 us
    ppermute x18, waiting for transfers between devices, shifted(): return lax.ppermute(value, axis, [(i, (i + by) % n) for i in range(n)])  6.5 us
  transfers between devices with their start and end apart: 27, of which 14 were waited for; matrix products, arithmetic and copies ran while one was open for 3% of the time, Pallas kernels for 0%

profile of v13, /device:TPU:1, one launch (start us, length us, event | category | flops | bytes accessed | tf_op | source)
XLA Modules:
  0.0 219.3 jit_solution(7440325258770693167)
XLA Ops:
  0.6 2.6 %heads.1 = bf16[128,3072]{1,0:T(8,128)(2,1)} custom-call(bf16[192,128]{1,0:T(8,128)(2,1)} %bitcast.105, bf16[192,1536]{1,0:T(8,128)(2,1)} %refs_1_.1, bf16[192,128]{1,0:T(8,128)(2,1)} %bitcast.107, bf16[192,1536]{1,0:T(8,128)(2,1)} %refs_3_.1), custom_call_target="tpu_custom_call" | custom-call | flops 150994944 | bytes 2064384 | tf_op jit(solution)/shard_map/heads/pallas_call | solution.py:76
  3.2 7.6 %all-to-all-start = ((bf16[8,16,3072]{2,1,0:T(8,128)(2,1)}), bf16[8,16,3072]{2,1,0:T(8,128)(2,1)S(1)}, u32[]{:S(2)}, u32[]{:S(2)}) async-start(bf16[8,16,3072]{2,1,0:T(8,128)(2,1)} %bitcast.96), calls=%async_computation | async-start | bytes 1572864 | tf_op jit(solution)/shard_map/heads/all_to_all | solution.py:26
  10.9 4.9 %collective-permute-start = (bf16[192,128]{1,0:T(8,128)(2,1)S(1)}, bf16[192,128]{1,0:T(8,128)(2,1)S(1)}, u32[]{:S(2)}, u32[]{:S(2)}) collective-permute-start(bf16[192,128]{1,0:T(8,128)(2,1)S(1)} %bitcast.106), channel_id=1, source_target_pairs={{0,8},{8,0},{1,9},{9,1},{2,10},{10,2},{3,11},{11,3},{4,12},{12,4},... | collective-permute-start | bytes 147464 | tf_op jit(solution)/shard_map/heads/ppermute | solution.py:40
  15.8 1.9 collective-permute-start.1
  17.7 1.2 collective-permute-done.1
  18.9 3.2 %all-to-all-done = bf16[8,16,3072]{2,1,0:T(8,128)(2,1)S(1)} async-done(((bf16[8,16,3072]{2,1,0:T(8,128)(2,1)}), bf16[8,16,3072]{2,1,0:T(8,128)(2,1)S(1)}, u32[]{:S(2)}, u32[]{:S(2)}) %all-to-all-start) | async-done | bytes 786464 | tf_op jit(solution)/shard_map/heads/all_to_all | solution.py:26
  22.5 0.7 broadcast_in_dim.14
  23.2 16.8 %all-to-all-start.1 = ((bf16[4,16,1536]{2,1,0:T(8,128)(2,1)}), bf16[4,16,1536]{2,1,0:T(8,128)(2,1)S(1)}, u32[]{:S(2)}, u32[]{:S(2)}) async-start(bf16[4,16,1536]{2,1,0:T(8,128)(2,1)} %broadcast_in_dim.14), calls=%async_computation.1 | async-start | bytes 393216 | tf_op jit(solution)/shard_map/gather_texts/all_to_all | solution.py:26
  40.0 2.6 %collective-permute-start.4 = (bf16[16,1536]{1,0:T(8,128)(2,1)S(1)}, bf16[16,1536]{1,0:T(8,128)(2,1)S(1)}, u32[]{:S(2)}, u32[]{:S(2)}) collective-permute-start(bf16[16,1536]{1,0:T(8,128)(2,1)S(1)} %get-tuple-element.21), channel_id=1, source_target_pairs={{0,16},{16,32},{32,48},{48,0},{1,17},{17,33},{33,49},{49,1},{2,18}... | collective-permute-start | bytes 147464 | tf_op jit(solution)/shard_map/gather_images/ppermute | solution.py:40
  42.7 3.1 %collective-permute-start.3 = (bf16[16,1536]{1,0:T(8,128)(2,1)S(1)}, bf16[16,1536]{1,0:T(8,128)(2,1)S(1)}, u32[]{:S(2)}, u32[]{:S(2)}) collective-permute-start(bf16[16,1536]{1,0:T(8,128)(2,1)S(1)} %get-tuple-element.21), channel_id=1, source_target_pairs={{0,32},{16,48},{32,0},{48,16},{1,33},{17,49},{33,1},{49,17},{2,34}... | collective-permute-start | bytes 147464 | tf_op jit(solution)/shard_map/gather_images/ppermute | solution.py:40
  45.8 3.5 %collective-permute-start.2 = (bf16[16,1536]{1,0:T(8,128)(2,1)S(1)}, bf16[16,1536]{1,0:T(8,128)(2,1)S(1)}, u32[]{:S(2)}, u32[]{:S(2)}) collective-permute-start(bf16[16,1536]{1,0:T(8,128)(2,1)S(1)} %get-tuple-element.21), channel_id=1, source_target_pairs={{0,48},{16,0},{32,16},{48,32},{1,49},{17,1},{33,17},{49,33},{2,50}... | collective-permute-start | bytes 147464 | tf_op jit(solution)/shard_map/gather_images/ppermute | solution.py:40
  51.3 1.5 all-to-all-done.1
  52.7 0.9 broadcast_in_dim.16
  53.7 3.5 %all-to-all-start.2 = ((bf16[4,64,1536]{2,1,0:T(8,128)(2,1)}), bf16[4,64,1536]{2,1,0:T(8,128)(2,1)S(1)}, u32[]{:S(2)}, u32[]{:S(2)}) async-start(bf16[4,64,1536]{2,1,0:T(8,128)(2,1)} %broadcast_in_dim.16), calls=%async_computation.2 | async-start | bytes 1572864 | tf_op jit(solution)/shard_map/gather_texts/all_to_all | solution.py:26
  57.2 1.9 collective-permute-start.7
  59.2 4.0 %collective-permute-start.6 = (bf16[64,1536]{1,0:T(8,128)(2,1)S(1)}, bf16[64,1536]{1,0:T(8,128)(2,1)S(1)}, u32[]{:S(2)}, u32[]{:S(2)}) collective-permute-start(bf16[64,1536]{1,0:T(8,128)(2,1)S(1)} %pad_maximum_fusion.1), channel_id=1, source_target_pairs={{0,4},{2,6},{4,0},{6,2},{1,5},{3,7},{5,1},{7,3},{8,12},{10,14},{12... | collective-permute-start | bytes 589832 | tf_op jit(solution)/shard_map/gather_images/ppermute | solution.py:40
  63.1 2.8 %collective-permute-start.5 = (bf16[64,1536]{1,0:T(8,128)(2,1)S(1)}, bf16[64,1536]{1,0:T(8,128)(2,1)S(1)}, u32[]{:S(2)}, u32[]{:S(2)}) collective-permute-start(bf16[64,1536]{1,0:T(8,128)(2,1)S(1)} %pad_maximum_fusion.1), channel_id=1, source_target_pairs={{0,6},{2,0},{4,2},{6,4},{1,7},{3,1},{5,3},{7,5},{8,14},{10,8},{12,... | collective-permute-start | bytes 589832 | tf_op jit(solution)/shard_map/gather_images/ppermute | solution.py:40
  66.0 10.1 %collective-permute-start.8 = (bf16[256,1536]{1,0:T(8,128)(2,1)S(1)}, bf16[256,1536]{1,0:T(8,128)(2,1)S(1)}, u32[]{:S(2)}, u32[]{:S(2)}) collective-permute-start(bf16[256,1536]{1,0:T(8,128)(2,1)S(1)} %bitcast.93), channel_id=1, source_target_pairs={{0,8},{8,0},{1,9},{9,1},{2,10},{10,2},{3,11},{11,3},{4,12},{12,4},... | collective-permute-start | bytes 2359304 | tf_op jit(solution)/shard_map/gather_texts/ppermute | solution.py:40
  76.2 1.8 collective-permute-done.8
  78.0 0.4 fusion.16
  78.4 0.4 convolution_convert_fusion
  78.8 2.6 %collective-permute-start.15 = (bf16[256,1536]{1,0:T(8,128)(2,1)S(1)}, bf16[256,1536]{1,0:T(8,128)(2,1)S(1)}, u32[]{:S(2)}, u32[]{:S(2)}) collective-permute-start(bf16[256,1536]{1,0:T(8,128)(2,1)S(1)} %convolution_convert_fusion), channel_id=1, source_target_pairs={{0,8},{8,0},{1,9},{9,1},{2,10},{10,2},{3,11},{11,3},{4,12},{12,4},... | collective-permute-start | bytes 2359304 | tf_op jit(solution)/shard_map/sum_texts/ppermute | solution.py:40
  81.4 0.4 fusion.17
  81.9 0.4 fusion.55
  82.3 0.4 fusion.54
  82.7 0.6 collective-permute-done.15
  83.3 1.3 fusion
  84.6 4.5 %all-to-all-start.3 = ((bf16[4,64,1536]{2,1,0:T(8,128)(2,1)}), bf16[4,64,1536]{2,1,0:T(8,128)(2,1)S(1)}, u32[]{:S(2)}, u32[]{:S(2)}) async-start(bf16[4,64,1536]{2,1,0:T(8,128)(2,1)} %bitcast.8), calls=%async_computation.3 | async-start | bytes 1572864 | tf_op jit(solution)/shard_map/sum_texts/all_to_all | solution.py:26
  89.0 0.8 fusion.51
  89.8 3.0 %collective-permute-start.9 = (bf16[64,1536]{1,0:T(8,128)(2,1)}, bf16[64,1536]{1,0:T(8,128)(2,1)S(1)}, u32[]{:S(2)}, u32[]{:S(2)}) collective-permute-start(bf16[64,1536]{1,0:T(8,128)(2,1)} %get-tuple-element.24), channel_id=1, source_target_pairs={{0,2},{2,4},{4,6},{6,0},{1,3},{3,5},{5,7},{7,1},{8,10},{10,12},{12... | collective-permute-start | bytes 589832 | tf_op jit(solution)/shard_map/sum_images/ppermute | solution.py:40
  92.8 3.4 %collective-permute-start.11 = (bf16[64,1536]{1,0:T(8,128)(2,1)}, bf16[64,1536]{1,0:T(8,128)(2,1)S(1)}, u32[]{:S(2)}, u32[]{:S(2)}) collective-permute-start(bf16[64,1536]{1,0:T(8,128)(2,1)} %get-tuple-element.25), channel_id=1, source_target_pairs={{0,6},{2,0},{4,2},{6,4},{1,7},{3,1},{5,3},{7,5},{8,14},{10,8},{12,... | collective-permute-start | bytes 589832 | tf_op jit(solution)/shard_map/sum_images/ppermute | solution.py:40
  96.3 2.5 %collective-permute-start.10 = (bf16[64,1536]{1,0:T(8,128)(2,1)S(1)}, bf16[64,1536]{1,0:T(8,128)(2,1)S(1)}, u32[]{:S(2)}, u32[]{:S(2)}) collective-permute-start(bf16[64,1536]{1,0:T(8,128)(2,1)S(1)} %get-tuple-element.26), channel_id=1, source_target_pairs={{0,4},{2,6},{4,0},{6,2},{1,5},{3,7},{5,1},{7,3},{8,12},{10,14},{12... | collective-permute-start | bytes 589832 | tf_op jit(solution)/shard_map/sum_images/ppermute | solution.py:40
  98.8 1.9 all-to-all-done.3
  100.7 0.8 reduce_sum.97
  101.6 5.9 %all-to-all-start.4 = ((bf16[4,16,1536]{2,1,0:T(8,128)(2,1)}), bf16[4,16,1536]{2,1,0:T(8,128)(2,1)S(1)}, u32[]{:S(2)}, u32[]{:S(2)}) async-start(bf16[4,16,1536]{2,1,0:T(8,128)(2,1)} %bitcast.9), calls=%async_computation.4 | async-start | bytes 393216 | tf_op jit(solution)/shard_map/sum_texts/all_to_all | solution.py:26
  107.6 1.9 collective-permute-start.12
  109.5 5.2 %collective-permute-start.14 = (bf16[16,1536]{1,0:T(8,128)(2,1)S(1)}, bf16[16,1536]{1,0:T(8,128)(2,1)S(1)}, u32[]{:S(2)}, u32[]{:S(2)}) collective-permute-start(bf16[16,1536]{1,0:T(8,128)(2,1)S(1)} %get-tuple-element.34), channel_id=1, source_target_pairs={{0,48},{16,0},{32,16},{48,32},{1,49},{17,1},{33,17},{49,33},{2,50}... | collective-permute-start | bytes 147464 | tf_op jit(solution)/shard_map/sum_images/ppermute | solution.py:40
  114.7 1.9 collective-permute-start.13
  116.6 4.4 %all-to-all-done.4 = bf16[4,16,1536]{2,1,0:T(8,128)(2,1)S(1)} async-done(((bf16[4,16,1536]{2,1,0:T(8,128)(2,1)}), bf16[4,16,1536]{2,1,0:T(8,128)(2,1)S(1)}, u32[]{:S(2)}, u32[]{:S(2)}) %all-to-all-start.4) | async-done | bytes 196640 | tf_op jit(solution)/shard_map/sum_texts/all_to_all | solution.py:26
  121.0 0.6 collective-permute-done.13
  122.2 1.0 broadcast_in_dim.17
  123.2 9.8 %all-to-all-start.5 = ((bf16[16,2,16,768]{3,2,1,0:T(8,128)(2,1)}), bf16[16,2,16,768]{3,2,1,0:T(8,128)(2,1)S(1)}, u32[]{:S(2)}, u32[]{:S(2)}) async-start(bf16[16,2,16,768]{3,2,1,0:T(8,128)(2,1)} %bitcast.11), calls=%async_computation.5 | async-start | bytes 1572864 | tf_op jit(solution)/shard_map/head_grads/all_to_all | solution.py:26
  133.0 12.5 %all-to-all-done.5 = bf16[16,2,16,768]{3,2,1,0:T(8,128)(2,1)S(1)} async-done(((bf16[16,2,16,768]{3,2,1,0:T(8,128)(2,1)}), bf16[16,2,16,768]{3,2,1,0:T(8,128)(2,1)S(1)}, u32[]{:S(2)}, u32[]{:S(2)}) %all-to-all-start.5) | async-done | bytes 786464 | tf_op jit(solution)/shard_map/head_grads/all_to_all | solution.py:26
  145.6 0.2 fusion.2
  145.9 0.2 fusion.1
  146.2 0.9 pad_maximum_fusion
  147.0 3.5 %all-to-all-start.6 = ((bf16[4,96,768]{2,1,0:T(8,128)(2,1)}), bf16[4,96,768]{2,1,0:T(8,128)(2,1)S(1)}, u32[]{:S(2)}, u32[]{:S(2)}) async-start(bf16[4,96,768]{2,1,0:T(8,128)(2,1)} %bitcast.16), calls=%async_computation.6 | async-start | bytes 1179648 | tf_op jit(solution)/shard_map/weight_grads/all_to_all | solution.py:26
  150.5 0.3 convolution_bitcast_fusion
  150.8 7.1 %all-to-all-done.6 = bf16[4,96,768]{2,1,0:T(8,128)(2,1)S(1)} async-done(((bf16[4,96,768]{2,1,0:T(8,128)(2,1)}), bf16[4,96,768]{2,1,0:T(8,128)(2,1)S(1)}, u32[]{:S(2)}, u32[]{:S(2)}) %all-to-all-start.6) | async-done | bytes 589856 | tf_op jit(solution)/shard_map/weight_grads/all_to_all | solution.py:26
  158.1 0.7 copy.20
  158.8 9.2 %all-to-all-start.7 = ((bf16[8,24,384]{2,1,0:T(8,128)(2,1)}), bf16[8,24,384]{2,1,0:T(8,128)(2,1)S(1)}, u32[]{:S(2)}, u32[]{:S(2)}) async-start(bf16[8,24,384]{2,1,0:T(8,128)(2,1)} %bitcast.18), calls=%async_computation.7 | async-start | bytes 294912 | tf_op jit(solution)/shard_map/weight_grads/all_to_all | solution.py:26
  167.9 0.3 convolution_bitcast_fusion.1
  168.3 4.4 %collective-permute-start.16 = (bf16[2,128,192]{1,2,0:T(8,128)(2,1)S(1)}, bf16[2,128,192]{1,2,0:T(8,128)(2,1)S(1)}, u32[]{:S(2)}, u32[]{:S(2)}) collective-permute-start(bf16[2,128,192]{1,2,0:T(8,128)(2,1)S(1)} %fusion.32), channel_id=1, source_target_pairs={{0,8},{8,0},{1,9},{9,1},{2,10},{10,2},{3,11},{11,3},{4,12},{12,4},... | collective-permute-start | bytes 294920 | tf_op jit(solution)/shard_map/input_grads/ppermute | solution.py:40
  172.7 0.9 collective-permute-done.16
  173.6 8.2 %all-to-all-done.7 = bf16[8,24,384]{2,1,0:T(8,128)(2,1)S(1)} async-done(((bf16[8,24,384]{2,1,0:T(8,128)(2,1)}), bf16[8,24,384]{2,1,0:T(8,128)(2,1)S(1)}, u32[]{:S(2)}, u32[]{:S(2)}) %all-to-all-start.7) | async-done | bytes 147488 | tf_op jit(solution)/shard_map/weight_grads/all_to_all | solution.py:26
  181.9 17.4 %all_to_all.50 = bf16[8,24,384]{2,1,0:T(8,128)(2,1)S(1)} all-to-all(bf16[8,24,384]{2,1,0:T(8,128)(2,1)S(1)} %broadcast_in_dim.18), channel_id=1, replica_groups=mesh['xl'=2,'zh'=4,'zm'=2,'z0'=2,'c'=2,'y'=4,'xh'=2] {'zh','zm'}, dimensions={0} | all-to-all | bytes 294912 | tf_op jit(solution)/shard_map/weight_grads/all_to_all | solution.py:26
  199.4 0.9 broadcast_in_dim.20
  200.2 3.5 %all-to-all-start.9 = ((bf16[4,96,768]{2,1,0:T(8,128)(2,1)}), bf16[4,96,768]{2,1,0:T(8,128)(2,1)S(1)}, u32[]{:S(2)}, u32[]{:S(2)}) async-start(bf16[4,96,768]{2,1,0:T(8,128)(2,1)} %broadcast_in_dim.20), calls=%async_computation.9 | async-start | bytes 1179648 | tf_op jit(solution)/shard_map/weight_grads/all_to_all | solution.py:26
  203.7 0.7 slice_bitcast_fusion.2
  204.4 5.1 %all-to-all-done.9 = bf16[4,96,768]{2,1,0:T(8,128)(2,1)S(1)} async-done(((bf16[4,96,768]{2,1,0:T(8,128)(2,1)}), bf16[4,96,768]{2,1,0:T(8,128)(2,1)S(1)}, u32[]{:S(2)}, u32[]{:S(2)}) %all-to-all-start.9) | async-done | bytes 589856 | tf_op jit(solution)/shard_map/weight_grads/all_to_all | solution.py:26
  209.5 6.6 %collective-permute-start.17 = (bf16[2,192,768]{2,1,0:T(8,128)(2,1)S(1)}, bf16[2,192,768]{2,1,0:T(8,128)(2,1)S(1)}, u32[]{:S(2)}, u32[]{:S(2)}) collective-permute-start(bf16[2,192,768]{2,1,0:T(8,128)(2,1)S(1)} %bitcast.97), channel_id=1, source_target_pairs={{0,8},{8,0},{1,9},{9,1},{2,10},{10,2},{3,11},{11,3},{4,12},{12,4},... | collective-permute-start | bytes 1769480 | tf_op jit(solution)/shard_map/weight_grads/ppermute | solution.py:40
  216.3 1.4 collective-permute-done.17
  217.9 1.0 copy-done.2
  218.9 0.4 copy-done.3
  (68 shorter events, 2.0 us)
Async XLA Ops:
  3.2 7.7 %copy-start.4 = (bf16[128,192]{0,1:T(8,128)(2,1)S(1)}, bf16[128,192]{0,1:T(8,128)(2,1)}, u32[]{:S(2)}) copy-start(bf16[128,192]{0,1:T(8,128)(2,1)} %param.7) | copy-start | bytes 147460
  3.2 12.5 %copy-start.5 = (bf16[128,192]{0,1:T(8,128)(2,1)S(1)}, bf16[128,192]{0,1:T(8,128)(2,1)}, u32[]{:S(2)}) copy-start(bf16[128,192]{0,1:T(8,128)(2,1)} %param.8) | copy-start | bytes 147460
  3.2 18.9 %all-to-all-start = ((bf16[8,16,3072]{2,1,0:T(8,128)(2,1)}), bf16[8,16,3072]{2,1,0:T(8,128)(2,1)S(1)}, u32[]{:S(2)}, u32[]{:S(2)}) async-start(bf16[8,16,3072]{2,1,0:T(8,128)(2,1)} %bitcast.96), calls=%async_computation | async-start | bytes 1572864 | tf_op jit(solution)/shard_map/heads/all_to_all | solution.py:26
  10.9 6.8 %collective-permute-start = (bf16[192,128]{1,0:T(8,128)(2,1)S(1)}, bf16[192,128]{1,0:T(8,128)(2,1)S(1)}, u32[]{:S(2)}, u32[]{:S(2)}) collective-permute-start(bf16[192,128]{1,0:T(8,128)(2,1)S(1)} %bitcast.106), channel_id=1, source_target_pairs={{0,8},{8,0},{1,9},{9,1},{2,10},{10,2},{3,11},{11,3},{4,12},{12,4},... | collective-permute-start | bytes 147464 | tf_op jit(solution)/shard_map/heads/ppermute | solution.py:40
  15.8 3.1 %collective-permute-start.1 = (bf16[192,128]{1,0:T(8,128)(2,1)S(1)}, bf16[192,128]{1,0:T(8,128)(2,1)S(1)}, u32[]{:S(2)}, u32[]{:S(2)}) collective-permute-start(bf16[192,128]{1,0:T(8,128)(2,1)S(1)} %bitcast.108), channel_id=1, source_target_pairs={{0,8},{8,0},{1,9},{9,1},{2,10},{10,2},{3,11},{11,3},{4,12},{12,4},... | collective-permute-start | bytes 147464 | tf_op jit(solution)/shard_map/heads/ppermute | solution.py:40
  17.7 5.4 %copy-start.6 = (bf16[192,128]{1,0:T(8,128)(2,1)}, bf16[192,128]{1,0:T(8,128)(2,1)S(1)}, u32[]{:S(2)}) copy-start(bf16[192,128]{1,0:T(8,128)(2,1)S(1)} %collective-permute-done) | copy-start | bytes 147460
  18.9 4.3 %copy-start.8 = (bf16[192,128]{1,0:T(8,128)(2,1)}, bf16[192,128]{1,0:T(8,128)(2,1)S(1)}, u32[]{:S(2)}) copy-start(bf16[192,128]{1,0:T(8,128)(2,1)S(1)} %collective-permute-done.1) | copy-start | bytes 147460
  23.2 29.6 %all-to-all-start.1 = ((bf16[4,16,1536]{2,1,0:T(8,128)(2,1)}), bf16[4,16,1536]{2,1,0:T(8,128)(2,1)S(1)}, u32[]{:S(2)}, u32[]{:S(2)}) async-start(bf16[4,16,1536]{2,1,0:T(8,128)(2,1)} %broadcast_in_dim.14), calls=%async_computation.1 | async-start | bytes 393216 | tf_op jit(solution)/shard_map/gather_texts/all_to_all | solution.py:26
  40.0 17.2 %collective-permute-start.4 = (bf16[16,1536]{1,0:T(8,128)(2,1)S(1)}, bf16[16,1536]{1,0:T(8,128)(2,1)S(1)}, u32[]{:S(2)}, u32[]{:S(2)}) collective-permute-start(bf16[16,1536]{1,0:T(8,128)(2,1)S(1)} %get-tuple-element.21), channel_id=1, source_target_pairs={{0,16},{16,32},{32,48},{48,0},{1,17},{17,33},{33,49},{49,1},{2,18}... | collective-permute-start | bytes 147464 | tf_op jit(solution)/shard_map/gather_images/ppermute | solution.py:40
  42.7 14.5 %collective-permute-start.3 = (bf16[16,1536]{1,0:T(8,128)(2,1)S(1)}, bf16[16,1536]{1,0:T(8,128)(2,1)S(1)}, u32[]{:S(2)}, u32[]{:S(2)}) collective-permute-start(bf16[16,1536]{1,0:T(8,128)(2,1)S(1)} %get-tuple-element.21), channel_id=1, source_target_pairs={{0,32},{16,48},{32,0},{48,16},{1,33},{17,49},{33,1},{49,17},{2,34}... | collective-permute-start | bytes 147464 | tf_op jit(solution)/shard_map/gather_images/ppermute | solution.py:40
  45.8 11.4 %collective-permute-start.2 = (bf16[16,1536]{1,0:T(8,128)(2,1)S(1)}, bf16[16,1536]{1,0:T(8,128)(2,1)S(1)}, u32[]{:S(2)}, u32[]{:S(2)}) collective-permute-start(bf16[16,1536]{1,0:T(8,128)(2,1)S(1)} %get-tuple-element.21), channel_id=1, source_target_pairs={{0,48},{16,0},{32,16},{48,32},{1,49},{17,1},{33,17},{49,33},{2,50}... | collective-permute-start | bytes 147464 | tf_op jit(solution)/shard_map/gather_images/ppermute | solution.py:40
  53.7 12.3 %all-to-all-start.2 = ((bf16[4,64,1536]{2,1,0:T(8,128)(2,1)}), bf16[4,64,1536]{2,1,0:T(8,128)(2,1)S(1)}, u32[]{:S(2)}, u32[]{:S(2)}) async-start(bf16[4,64,1536]{2,1,0:T(8,128)(2,1)} %broadcast_in_dim.16), calls=%async_computation.2 | async-start | bytes 1572864 | tf_op jit(solution)/shard_map/gather_texts/all_to_all | solution.py:26
  57.2 18.9 %collective-permute-start.7 = (bf16[64,1536]{1,0:T(8,128)(2,1)S(1)}, bf16[64,1536]{1,0:T(8,128)(2,1)S(1)}, u32[]{:S(2)}, u32[]{:S(2)}) collective-permute-start(bf16[64,1536]{1,0:T(8,128)(2,1)S(1)} %pad_maximum_fusion.1), channel_id=1, source_target_pairs={{0,2},{2,4},{4,6},{6,0},{1,3},{3,5},{5,7},{7,1},{8,10},{10,12},{12... | collective-permute-start | bytes 589832 | tf_op jit(solution)/shard_map/gather_images/ppermute | solution.py:40
  59.2 17.0 %collective-permute-start.6 = (bf16[64,1536]{1,0:T(8,128)(2,1)S(1)}, bf16[64,1536]{1,0:T(8,128)(2,1)S(1)}, u32[]{:S(2)}, u32[]{:S(2)}) collective-permute-start(bf16[64,1536]{1,0:T(8,128)(2,1)S(1)} %pad_maximum_fusion.1), channel_id=1, source_target_pairs={{0,4},{2,6},{4,0},{6,2},{1,5},{3,7},{5,1},{7,3},{8,12},{10,14},{12... | collective-permute-start | bytes 589832 | tf_op jit(solution)/shard_map/gather_images/ppermute | solution.py:40
  63.1 13.0 %collective-permute-start.5 = (bf16[64,1536]{1,0:T(8,128)(2,1)S(1)}, bf16[64,1536]{1,0:T(8,128)(2,1)S(1)}, u32[]{:S(2)}, u32[]{:S(2)}) collective-permute-start(bf16[64,1536]{1,0:T(8,128)(2,1)S(1)} %pad_maximum_fusion.1), channel_id=1, source_target_pairs={{0,6},{2,0},{4,2},{6,4},{1,7},{3,1},{5,3},{7,5},{8,14},{10,8},{12,... | collective-permute-start | bytes 589832 | tf_op jit(solution)/shard_map/gather_images/ppermute | solution.py:40
  66.0 12.0 %collective-permute-start.8 = (bf16[256,1536]{1,0:T(8,128)(2,1)S(1)}, bf16[256,1536]{1,0:T(8,128)(2,1)S(1)}, u32[]{:S(2)}, u32[]{:S(2)}) collective-permute-start(bf16[256,1536]{1,0:T(8,128)(2,1)S(1)} %bitcast.93), channel_id=1, source_target_pairs={{0,8},{8,0},{1,9},{9,1},{2,10},{10,2},{3,11},{11,3},{4,12},{12,4},... | collective-permute-start | bytes 2359304 | tf_op jit(solution)/shard_map/gather_texts/ppermute | solution.py:40
  78.8 4.5 %collective-permute-start.15 = (bf16[256,1536]{1,0:T(8,128)(2,1)S(1)}, bf16[256,1536]{1,0:T(8,128)(2,1)S(1)}, u32[]{:S(2)}, u32[]{:S(2)}) collective-permute-start(bf16[256,1536]{1,0:T(8,128)(2,1)S(1)} %convolution_convert_fusion), channel_id=1, source_target_pairs={{0,8},{8,0},{1,9},{9,1},{2,10},{10,2},{3,11},{11,3},{4,12},{12,4},... | collective-permute-start | bytes 2359304 | tf_op jit(solution)/shard_map/sum_texts/ppermute | solution.py:40
  84.6 16.2 %all-to-all-start.3 = ((bf16[4,64,1536]{2,1,0:T(8,128)(2,1)}), bf16[4,64,1536]{2,1,0:T(8,128)(2,1)S(1)}, u32[]{:S(2)}, u32[]{:S(2)}) async-start(bf16[4,64,1536]{2,1,0:T(8,128)(2,1)} %bitcast.8), calls=%async_computation.3 | async-start | bytes 1572864 | tf_op jit(solution)/shard_map/sum_texts/all_to_all | solution.py:26
  89.8 17.7 %collective-permute-start.9 = (bf16[64,1536]{1,0:T(8,128)(2,1)}, bf16[64,1536]{1,0:T(8,128)(2,1)S(1)}, u32[]{:S(2)}, u32[]{:S(2)}) collective-permute-start(bf16[64,1536]{1,0:T(8,128)(2,1)} %get-tuple-element.24), channel_id=1, source_target_pairs={{0,2},{2,4},{4,6},{6,0},{1,3},{3,5},{5,7},{7,1},{8,10},{10,12},{12... | collective-permute-start | bytes 589832 | tf_op jit(solution)/shard_map/sum_images/ppermute | solution.py:40
  92.8 14.6 %collective-permute-start.11 = (bf16[64,1536]{1,0:T(8,128)(2,1)}, bf16[64,1536]{1,0:T(8,128)(2,1)S(1)}, u32[]{:S(2)}, u32[]{:S(2)}) collective-permute-start(bf16[64,1536]{1,0:T(8,128)(2,1)} %get-tuple-element.25), channel_id=1, source_target_pairs={{0,6},{2,0},{4,2},{6,4},{1,7},{3,1},{5,3},{7,5},{8,14},{10,8},{12,... | collective-permute-start | bytes 589832 | tf_op jit(solution)/shard_map/sum_images/ppermute | solution.py:40
  96.3 11.2 %collective-permute-start.10 = (bf16[64,1536]{1,0:T(8,128)(2,1)S(1)}, bf16[64,1536]{1,0:T(8,128)(2,1)S(1)}, u32[]{:S(2)}, u32[]{:S(2)}) collective-permute-start(bf16[64,1536]{1,0:T(8,128)(2,1)S(1)} %get-tuple-element.26), channel_id=1, source_target_pairs={{0,4},{2,6},{4,0},{6,2},{1,5},{3,7},{5,1},{7,3},{8,12},{10,14},{12... | collective-permute-start | bytes 589832 | tf_op jit(solution)/shard_map/sum_images/ppermute | solution.py:40
  101.6 19.4 %all-to-all-start.4 = ((bf16[4,16,1536]{2,1,0:T(8,128)(2,1)}), bf16[4,16,1536]{2,1,0:T(8,128)(2,1)S(1)}, u32[]{:S(2)}, u32[]{:S(2)}) async-start(bf16[4,16,1536]{2,1,0:T(8,128)(2,1)} %bitcast.9), calls=%async_computation.4 | async-start | bytes 393216 | tf_op jit(solution)/shard_map/sum_texts/all_to_all | solution.py:26
  107.6 13.4 %collective-permute-start.12 = (bf16[16,1536]{1,0:T(8,128)(2,1)S(1)}, bf16[16,1536]{1,0:T(8,128)(2,1)S(1)}, u32[]{:S(2)}, u32[]{:S(2)}) collective-permute-start(bf16[16,1536]{1,0:T(8,128)(2,1)S(1)} %get-tuple-element.33), channel_id=1, source_target_pairs={{0,16},{16,32},{32,48},{48,0},{1,17},{17,33},{33,49},{49,1},{2,18}... | collective-permute-start | bytes 147464 | tf_op jit(solution)/shard_map/sum_images/ppermute | solution.py:40
  109.5 11.5 %collective-permute-start.14 = (bf16[16,1536]{1,0:T(8,128)(2,1)S(1)}, bf16[16,1536]{1,0:T(8,128)(2,1)S(1)}, u32[]{:S(2)}, u32[]{:S(2)}) collective-permute-start(bf16[16,1536]{1,0:T(8,128)(2,1)S(1)} %get-tuple-element.34), channel_id=1, source_target_pairs={{0,48},{16,0},{32,16},{48,32},{1,49},{17,1},{33,17},{49,33},{2,50}... | collective-permute-start | bytes 147464 | tf_op jit(solution)/shard_map/sum_images/ppermute | solution.py:40
  114.7 6.9 %collective-permute-start.13 = (bf16[16,1536]{1,0:T(8,128)(2,1)S(1)}, bf16[16,1536]{1,0:T(8,128)(2,1)S(1)}, u32[]{:S(2)}, u32[]{:S(2)}) collective-permute-start(bf16[16,1536]{1,0:T(8,128)(2,1)S(1)} %get-tuple-element.35), channel_id=1, source_target_pairs={{0,32},{16,48},{32,0},{48,16},{1,33},{17,49},{33,1},{49,17},{2,34}... | collective-permute-start | bytes 147464 | tf_op jit(solution)/shard_map/sum_images/ppermute | solution.py:40
  122.2 10.8 %copy-start.7 = (bf16[192,128]{1,0:T(8,128)(2,1)S(1)}, bf16[192,128]{1,0:T(8,128)(2,1)}, u32[]{:S(2)}) copy-start(bf16[192,128]{1,0:T(8,128)(2,1)} %copy-done.6) | copy-start | bytes 147460
  122.2 10.8 %copy-start.9 = (bf16[192,128]{1,0:T(8,128)(2,1)S(1)}, bf16[192,128]{1,0:T(8,128)(2,1)}, u32[]{:S(2)}) copy-start(bf16[192,128]{1,0:T(8,128)(2,1)} %copy-done.8) | copy-start | bytes 147460
  123.2 22.4 %all-to-all-start.5 = ((bf16[16,2,16,768]{3,2,1,0:T(8,128)(2,1)}), bf16[16,2,16,768]{3,2,1,0:T(8,128)(2,1)S(1)}, u32[]{:S(2)}, u32[]{:S(2)}) async-start(bf16[16,2,16,768]{3,2,1,0:T(8,128)(2,1)} %bitcast.11), calls=%async_computation.5 | async-start | bytes 1572864 | tf_op jit(solution)/shard_map/head_grads/all_to_all | solution.py:26
  146.1 4.4 %copy-start = (bf16[192,1536]{1,0:T(8,128)(2,1)S(1)}, bf16[192,1536]{1,0:T(8,128)(2,1)}, u32[]{:S(2)}) copy-start(bf16[192,1536]{1,0:T(8,128)(2,1)} %refs_3_.1) | copy-start | bytes 1769476
  147.0 10.9 %all-to-all-start.6 = ((bf16[4,96,768]{2,1,0:T(8,128)(2,1)}), bf16[4,96,768]{2,1,0:T(8,128)(2,1)S(1)}, u32[]{:S(2)}, u32[]{:S(2)}) async-start(bf16[4,96,768]{2,1,0:T(8,128)(2,1)} %bitcast.16), calls=%async_computation.6 | async-start | bytes 1179648 | tf_op jit(solution)/shard_map/weight_grads/all_to_all | solution.py:26
  150.5 17.4 %copy-start.1 = (bf16[192,1536]{1,0:T(8,128)(2,1)S(1)}, bf16[192,1536]{1,0:T(8,128)(2,1)}, u32[]{:S(2)}) copy-start(bf16[192,1536]{1,0:T(8,128)(2,1)} %refs_1_.1) | copy-start | bytes 1769476
  158.8 23.0 %all-to-all-start.7 = ((bf16[8,24,384]{2,1,0:T(8,128)(2,1)}), bf16[8,24,384]{2,1,0:T(8,128)(2,1)S(1)}, u32[]{:S(2)}, u32[]{:S(2)}) async-start(bf16[8,24,384]{2,1,0:T(8,128)(2,1)} %bitcast.18), calls=%async_computation.7 | async-start | bytes 294912 | tf_op jit(solution)/shard_map/weight_grads/all_to_all | solution.py:26
  168.3 5.3 %collective-permute-start.16 = (bf16[2,128,192]{1,2,0:T(8,128)(2,1)S(1)}, bf16[2,128,192]{1,2,0:T(8,128)(2,1)S(1)}, u32[]{:S(2)}, u32[]{:S(2)}) collective-permute-start(bf16[2,128,192]{1,2,0:T(8,128)(2,1)S(1)} %fusion.32), channel_id=1, source_target_pairs={{0,8},{8,0},{1,9},{9,1},{2,10},{10,2},{3,11},{11,3},{4,12},{12,4},... | collective-permute-start | bytes 294920 | tf_op jit(solution)/shard_map/input_grads/ppermute | solution.py:40
  200.2 9.3 %all-to-all-start.9 = ((bf16[4,96,768]{2,1,0:T(8,128)(2,1)}), bf16[4,96,768]{2,1,0:T(8,128)(2,1)S(1)}, u32[]{:S(2)}, u32[]{:S(2)}) async-start(bf16[4,96,768]{2,1,0:T(8,128)(2,1)} %broadcast_in_dim.20), calls=%async_computation.9 | async-start | bytes 1179648 | tf_op jit(solution)/shard_map/weight_grads/all_to_all | solution.py:26
  209.5 8.2 %collective-permute-start.17 = (bf16[2,192,768]{2,1,0:T(8,128)(2,1)S(1)}, bf16[2,192,768]{2,1,0:T(8,128)(2,1)S(1)}, u32[]{:S(2)}, u32[]{:S(2)}) collective-permute-start(bf16[2,192,768]{2,1,0:T(8,128)(2,1)S(1)} %bitcast.97), channel_id=1, source_target_pairs={{0,8},{8,0},{1,9},{9,1},{2,10},{10,2},{3,11},{11,3},{4,12},{12,4},... | collective-permute-start | bytes 1769480 | tf_op jit(solution)/shard_map/weight_grads/ppermute | solution.py:40
  217.9 1.0 copy-start.2
  217.9 1.4 copy-start.3

commit v14 on v12

--- a/solution.py
+++ b/solution.py
@@ -154,8 +154,8 @@
     with jax.named_scope("heads"):
         partial_heads = project(image_features, text_features, image_weight, text_weight)
         together = lax.optimization_barrier
-        features = jnp.stack((image_features.T, text_features.T))
-        partial_heads, features = together((partial_heads, features))
+        partial_heads, *features = together((partial_heads, image_features.T, text_features.T))
+        features = jnp.stack(features)
         received = exchange(split_rows(partial_heads, members), MP)
         other_core = shifted(features, "c", 1)
         other_pair = shifted(features, "z0", 1)
@@ -250,12 +250,11 @@
                 contract(text_columns, text_grads, 1, 0),
             ]
         )
-        part = half_sum(part, at["xl"], 0, "xl")
-        part = scatter_sum(split_rows(part, 8), ("zh", "zm")).astype(BF16)
+        part = scatter_sum(part.reshape(4, width // 2, quarter), ("xl", "zm"))
+        part = jnp.sum(gather(part.astype(BF16), "zh").astype(F32), axis=0).astype(BF16)
         part, inputs = lax.optimization_barrier((part, inputs))
-        part = merge_rows(gather(part, ("zh", "zm")))
-        part = gather(part, ("xl", "z0")).reshape(2, 2, width, quarter)
-        part = part.transpose(0, 2, 1, 3).reshape(2, width, 2 * quarter)
+        part = gather(part, ("xl", "zm", "z0")).reshape(2, 2, 2, width // 2, quarter)
+        part = part.transpose(0, 1, 3, 2, 4).reshape(2, width, 2 * quarter)
         part = lax.optimization_barrier(part)
         other = shifted(part, "c", 1)
 

time: 224 us -> 219 us (0.978)
  blocking collectives: 19.7 us -> 0 us
  waiting for transfers between devices: 44.6 us -> 54.2 us
  starting transfers between devices: 135 us -> 140 us
    all_to_all x1 -> x0, blocking collectives: 19.7 us -> none  [exchange(): return lax.all_to_all(blocks, axes, split_axis=0, concat_axis=0, tiled=True)]
    all_to_all x8 -> x9, waiting for transfers between devices: 32.2 us -> 38.2 us  [exchange(): return lax.all_to_all(blocks, axes, split_axis=0, concat_axis=0, tiled=True)]
    all_to_all x8 -> x9, starting transfers between devices: 60.5 us -> 66.3 us  [exchange(): return lax.all_to_all(blocks, axes, split_axis=0, concat_axis=0, tiled=True)]
    ppermute x20 -> x19, waiting for transfers between devices: 12.4 us -> 16 us  [shifted(): return lax.ppermute(value, axis, [(i, (i + by) % n) for i in range(n)])]
    ppermute x20 -> x19, starting transfers between devices: 70.3 us -> 69.3 us  [shifted(): return lax.ppermute(value, axis, [(i, (i + by) % n) for i in range(n)])]
  transfers between devices with their start and end apart: 29 -> 29, of which waited for: 13 -> 14; matrix products, arithmetic and copies ran while one was open for 4% -> 3% of each run, Pallas kernels for 0% -> 0%
where the time goes in v14:
time: 219 us; the launch traced here: 218 us
  starting transfers between devices  140 us (64%)
  waiting for transfers between devices  54.2 us (25%)
  local copies, waits for them, and re-layouts  8.22 us (4%)
  matrix products  6.18 us (3%)
  between operations  3.31 us (2%)
  other arithmetic  3.15 us (1%)
  Pallas kernels  2.59 us (1%)
    ppermute x19, starting transfers between devices, shifted(): return lax.ppermute(value, axis, [(i, (i + by) % n) for i in range(n)])  69.3 us
    all_to_all x9, starting transfers between devices, exchange(): return lax.all_to_all(blocks, axes, split_axis=0, concat_axis=0, tiled=True)  66.3 us
    all_to_all x9, waiting for transfers between devices, exchange(): return lax.all_to_all(blocks, axes, split_axis=0, concat_axis=0, tiled=True)  38.2 us
    ppermute x19, waiting for transfers between devices, shifted(): return lax.ppermute(value, axis, [(i, (i + by) % n) for i in range(n)])  16 us
    ppermute x1, starting transfers between devices, on_device(): lax.ppermute(features, ('z0', 'c'), [(i, 3 - i) for i in range(4)])  4.39 us
  transfers between devices with their start and end apart: 29, of which 14 were waited for; matrix products, arithmetic and copies ran while one was open for 3% of the time, Pallas kernels for 0%

profile of v14, /device:TPU:1, one launch (start us, length us, event | category | flops | bytes accessed | tf_op | source)
XLA Modules:
  0.0 217.5 jit_solution(221931153552385924)
XLA Ops:
  0.6 2.6 %heads.1 = bf16[128,3072]{1,0:T(8,128)(2,1)} custom-call(bf16[192,128]{1,0:T(8,128)(2,1)} %bitcast.125, bf16[192,1536]{1,0:T(8,128)(2,1)} %refs_1_.1, bf16[192,128]{1,0:T(8,128)(2,1)} %bitcast.128, bf16[192,1536]{1,0:T(8,128)(2,1)} %refs_3_.1), custom_call_target="tpu_custom_call" | custom-call | flops 150994944 | bytes 2064384 | tf_op jit(solution)/shard_map/heads/pallas_call | solution.py:76
  3.2 7.6 %all-to-all-start = ((bf16[8,16,3072]{2,1,0:T(8,128)(2,1)}), bf16[8,16,3072]{2,1,0:T(8,128)(2,1)S(1)}, u32[]{:S(2)}, u32[]{:S(2)}) async-start(bf16[8,16,3072]{2,1,0:T(8,128)(2,1)} %bitcast.118), calls=%async_computation | async-start | bytes 1572864 | tf_op jit(solution)/shard_map/heads/all_to_all | solution.py:26
  10.9 4.4 %collective-permute-start.2 = (bf16[2,192,128]{2,1,0:T(8,128)(2,1)S(1)}, bf16[2,192,128]{2,1,0:T(8,128)(2,1)S(1)}, u32[]{:S(2)}, u32[]{:S(2)}) collective-permute-start(bf16[2,192,128]{2,1,0:T(8,128)(2,1)S(1)} %pad_maximum_fusion.4), channel_id=1, source_target_pairs={{0,24},{8,16},{16,8},{24,0},{1,25},{9,17},{17,9},{25,1},{2,26},{10... | collective-permute-start | bytes 294920 | tf_op jit(solution)/shard_map/heads/ppermute | solution.py:162
  15.3 3.7 %collective-permute-start.1 = (bf16[2,192,128]{2,1,0:T(8,128)(2,1)S(1)}, bf16[2,192,128]{2,1,0:T(8,128)(2,1)S(1)}, u32[]{:S(2)}, u32[]{:S(2)}) collective-permute-start(bf16[2,192,128]{2,1,0:T(8,128)(2,1)S(1)} %pad_maximum_fusion.4), channel_id=1, source_target_pairs={{0,16},{16,0},{1,17},{17,1},{2,18},{18,2},{3,19},{19,3},{4,20},{20... | collective-permute-start | bytes 294920 | tf_op jit(solution)/shard_map/heads/ppermute | solution.py:40
  19.1 1.9 collective-permute-start
  21.0 0.9 collective-permute-done.1
  21.9 0.4 collective-permute-done
  22.6 0.7 broadcast_in_dim.12
  23.3 16.6 %all-to-all-start.1 = ((bf16[4,16,1536]{2,1,0:T(8,128)(2,1)}), bf16[4,16,1536]{2,1,0:T(8,128)(2,1)S(1)}, u32[]{:S(2)}, u32[]{:S(2)}) async-start(bf16[4,16,1536]{2,1,0:T(8,128)(2,1)} %broadcast_in_dim.12), calls=%async_computation.1 | async-start | bytes 393216 | tf_op jit(solution)/shard_map/gather_texts/all_to_all | solution.py:26
  40.0 2.6 %collective-permute-start.5 = (bf16[16,1536]{1,0:T(8,128)(2,1)S(1)}, bf16[16,1536]{1,0:T(8,128)(2,1)S(1)}, u32[]{:S(2)}, u32[]{:S(2)}) collective-permute-start(bf16[16,1536]{1,0:T(8,128)(2,1)S(1)} %get-tuple-element.29), channel_id=1, source_target_pairs={{0,16},{16,32},{32,48},{48,0},{1,17},{17,33},{33,49},{49,1},{2,18}... | collective-permute-start | bytes 147464 | tf_op jit(solution)/shard_map/gather_images/ppermute | solution.py:40
  42.7 3.1 %collective-permute-start.4 = (bf16[16,1536]{1,0:T(8,128)(2,1)S(1)}, bf16[16,1536]{1,0:T(8,128)(2,1)S(1)}, u32[]{:S(2)}, u32[]{:S(2)}) collective-permute-start(bf16[16,1536]{1,0:T(8,128)(2,1)S(1)} %get-tuple-element.29), channel_id=1, source_target_pairs={{0,32},{16,48},{32,0},{48,16},{1,33},{17,49},{33,1},{49,17},{2,34}... | collective-permute-start | bytes 147464 | tf_op jit(solution)/shard_map/gather_images/ppermute | solution.py:40
  45.8 3.5 %collective-permute-start.3 = (bf16[16,1536]{1,0:T(8,128)(2,1)S(1)}, bf16[16,1536]{1,0:T(8,128)(2,1)S(1)}, u32[]{:S(2)}, u32[]{:S(2)}) collective-permute-start(bf16[16,1536]{1,0:T(8,128)(2,1)S(1)} %get-tuple-element.29), channel_id=1, source_target_pairs={{0,48},{16,0},{32,16},{48,32},{1,49},{17,1},{33,17},{49,33},{2,50}... | collective-permute-start | bytes 147464 | tf_op jit(solution)/shard_map/gather_images/ppermute | solution.py:40
  51.3 1.5 all-to-all-done.1
  52.7 0.9 broadcast_in_dim.14
  53.7 3.5 %all-to-all-start.2 = ((bf16[4,64,1536]{2,1,0:T(8,128)(2,1)}), bf16[4,64,1536]{2,1,0:T(8,128)(2,1)S(1)}, u32[]{:S(2)}, u32[]{:S(2)}) async-start(bf16[4,64,1536]{2,1,0:T(8,128)(2,1)} %broadcast_in_dim.14), calls=%async_computation.2 | async-start | bytes 1572864 | tf_op jit(solution)/shard_map/gather_texts/all_to_all | solution.py:26
  57.2 1.9 collective-permute-start.8
  59.2 4.0 %collective-permute-start.7 = (bf16[64,1536]{1,0:T(8,128)(2,1)S(1)}, bf16[64,1536]{1,0:T(8,128)(2,1)S(1)}, u32[]{:S(2)}, u32[]{:S(2)}) collective-permute-start(bf16[64,1536]{1,0:T(8,128)(2,1)S(1)} %pad_maximum_fusion.3), channel_id=1, source_target_pairs={{0,4},{2,6},{4,0},{6,2},{1,5},{3,7},{5,1},{7,3},{8,12},{10,14},{12... | collective-permute-start | bytes 589832 | tf_op jit(solution)/shard_map/gather_images/ppermute | solution.py:40
  63.1 2.8 %collective-permute-start.6 = (bf16[64,1536]{1,0:T(8,128)(2,1)S(1)}, bf16[64,1536]{1,0:T(8,128)(2,1)S(1)}, u32[]{:S(2)}, u32[]{:S(2)}) collective-permute-start(bf16[64,1536]{1,0:T(8,128)(2,1)S(1)} %pad_maximum_fusion.3), channel_id=1, source_target_pairs={{0,6},{2,0},{4,2},{6,4},{1,7},{3,1},{5,3},{7,5},{8,14},{10,8},{12,... | collective-permute-start | bytes 589832 | tf_op jit(solution)/shard_map/gather_images/ppermute | solution.py:40
  66.0 10.1 %collective-permute-start.9 = (bf16[256,1536]{1,0:T(8,128)(2,1)S(1)}, bf16[256,1536]{1,0:T(8,128)(2,1)S(1)}, u32[]{:S(2)}, u32[]{:S(2)}) collective-permute-start(bf16[256,1536]{1,0:T(8,128)(2,1)S(1)} %bitcast.115), channel_id=1, source_target_pairs={{0,8},{8,0},{1,9},{9,1},{2,10},{10,2},{3,11},{11,3},{4,12},{12,4},... | collective-permute-start | bytes 2359304 | tf_op jit(solution)/shard_map/gather_texts/ppermute | solution.py:40
  76.2 1.8 collective-permute-done.9
  78.0 0.4 fusion.14
  78.8 2.6 %collective-permute-start.16 = (bf16[256,1536]{1,0:T(8,128)(2,1)S(1)}, bf16[256,1536]{1,0:T(8,128)(2,1)S(1)}, u32[]{:S(2)}, u32[]{:S(2)}) collective-permute-start(bf16[256,1536]{1,0:T(8,128)(2,1)S(1)} %convolution_convert_fusion), channel_id=1, source_target_pairs={{0,8},{8,0},{1,9},{9,1},{2,10},{10,2},{3,11},{11,3},{4,12},{12,4},... | collective-permute-start | bytes 2359304 | tf_op jit(solution)/shard_map/sum_texts/ppermute | solution.py:40
  81.4 0.4 fusion.15
  81.9 0.4 fusion.63
  82.3 0.4 fusion.62
  82.7 0.7 collective-permute-done.16
  83.3 1.3 fusion
  84.6 4.5 %all-to-all-start.3 = ((bf16[4,64,1536]{2,1,0:T(8,128)(2,1)}), bf16[4,64,1536]{2,1,0:T(8,128)(2,1)S(1)}, u32[]{:S(2)}, u32[]{:S(2)}) async-start(bf16[4,64,1536]{2,1,0:T(8,128)(2,1)} %bitcast.18), calls=%async_computation.3 | async-start | bytes 1572864 | tf_op jit(solution)/shard_map/sum_texts/all_to_all | solution.py:26
  89.0 0.8 fusion.60
  89.8 3.0 %collective-permute-start.10 = (bf16[64,1536]{1,0:T(8,128)(2,1)}, bf16[64,1536]{1,0:T(8,128)(2,1)S(1)}, u32[]{:S(2)}, u32[]{:S(2)}) collective-permute-start(bf16[64,1536]{1,0:T(8,128)(2,1)} %get-tuple-element.32), channel_id=1, source_target_pairs={{0,2},{2,4},{4,6},{6,0},{1,3},{3,5},{5,7},{7,1},{8,10},{10,12},{12... | collective-permute-start | bytes 589832 | tf_op jit(solution)/shard_map/sum_images/ppermute | solution.py:40
  92.8 3.5 %collective-permute-start.12 = (bf16[64,1536]{1,0:T(8,128)(2,1)}, bf16[64,1536]{1,0:T(8,128)(2,1)S(1)}, u32[]{:S(2)}, u32[]{:S(2)}) collective-permute-start(bf16[64,1536]{1,0:T(8,128)(2,1)} %get-tuple-element.33), channel_id=1, source_target_pairs={{0,6},{2,0},{4,2},{6,4},{1,7},{3,1},{5,3},{7,5},{8,14},{10,8},{12,... | collective-permute-start | bytes 589832 | tf_op jit(solution)/shard_map/sum_images/ppermute | solution.py:40
  96.3 2.5 %collective-permute-start.11 = (bf16[64,1536]{1,0:T(8,128)(2,1)S(1)}, bf16[64,1536]{1,0:T(8,128)(2,1)S(1)}, u32[]{:S(2)}, u32[]{:S(2)}) collective-permute-start(bf16[64,1536]{1,0:T(8,128)(2,1)S(1)} %get-tuple-element.34), channel_id=1, source_target_pairs={{0,4},{2,6},{4,0},{6,2},{1,5},{3,7},{5,1},{7,3},{8,12},{10,14},{12... | collective-permute-start | bytes 589832 | tf_op jit(solution)/shard_map/sum_images/ppermute | solution.py:40
  98.8 1.9 all-to-all-done.3
  100.7 0.8 reduce_sum.97
  101.6 5.9 %all-to-all-start.4 = ((bf16[4,16,1536]{2,1,0:T(8,128)(2,1)}), bf16[4,16,1536]{2,1,0:T(8,128)(2,1)S(1)}, u32[]{:S(2)}, u32[]{:S(2)}) async-start(bf16[4,16,1536]{2,1,0:T(8,128)(2,1)} %bitcast.19), calls=%async_computation.4 | async-start | bytes 393216 | tf_op jit(solution)/shard_map/sum_texts/all_to_all | solution.py:26
  107.6 1.9 collective-permute-start.13
  109.5 5.2 %collective-permute-start.15 = (bf16[16,1536]{1,0:T(8,128)(2,1)S(1)}, bf16[16,1536]{1,0:T(8,128)(2,1)S(1)}, u32[]{:S(2)}, u32[]{:S(2)}) collective-permute-start(bf16[16,1536]{1,0:T(8,128)(2,1)S(1)} %get-tuple-element.56), channel_id=1, source_target_pairs={{0,48},{16,0},{32,16},{48,32},{1,49},{17,1},{33,17},{49,33},{2,50}... | collective-permute-start | bytes 147464 | tf_op jit(solution)/shard_map/sum_images/ppermute | solution.py:40
  114.7 1.9 collective-permute-start.14
  116.6 4.4 %all-to-all-done.4 = bf16[4,16,1536]{2,1,0:T(8,128)(2,1)S(1)} async-done(((bf16[4,16,1536]{2,1,0:T(8,128)(2,1)}), bf16[4,16,1536]{2,1,0:T(8,128)(2,1)S(1)}, u32[]{:S(2)}, u32[]{:S(2)}) %all-to-all-start.4) | async-done | bytes 196640 | tf_op jit(solution)/shard_map/sum_texts/all_to_all | solution.py:26
  121.0 0.6 collective-permute-done.14
  122.2 1.0 broadcast_in_dim.15
  123.2 10.0 %all-to-all-start.5 = ((bf16[32,2,16,384]{3,2,1,0:T(8,128)(2,1)}), bf16[32,2,16,384]{3,2,1,0:T(8,128)(2,1)S(1)}, u32[]{:S(2)}, u32[]{:S(2)}) async-start(bf16[32,2,16,384]{3,2,1,0:T(8,128)(2,1)} %bitcast.21), calls=%async_computation.5 | async-start | bytes 1572864 | tf_op jit(solution)/shard_map/head_grads/all_to_all | solution.py:26
  133.3 14.0 %all-to-all-done.5 = bf16[32,2,16,384]{3,2,1,0:T(8,128)(2,1)S(1)} async-done(((bf16[32,2,16,384]{3,2,1,0:T(8,128)(2,1)}), bf16[32,2,16,384]{3,2,1,0:T(8,128)(2,1)S(1)}, u32[]{:S(2)}, u32[]{:S(2)}) %all-to-all-start.5) | async-done | bytes 786464 | tf_op jit(solution)/shard_map/head_grads/all_to_all | solution.py:26
  148.0 0.8 pad_maximum_fusion
  148.7 3.5 %all-to-all-start.6 = ((bf16[4,96,384]{2,1,0:T(8,128)(2,1)}), bf16[4,96,384]{2,1,0:T(8,128)(2,1)S(1)}, u32[]{:S(2)}, u32[]{:S(2)}) async-start(bf16[4,96,384]{2,1,0:T(8,128)(2,1)} %bitcast.30), calls=%async_computation.6 | async-start | bytes 589824 | tf_op jit(solution)/shard_map/weight_grads/all_to_all | solution.py:26
  152.2 1.2 convolution_bitcast_fusion
  153.4 1.2 convolution_bitcast_fusion.1
  154.6 5.8 %all-to-all-done.6 = bf16[4,96,384]{2,1,0:T(8,128)(2,1)S(1)} async-done(((bf16[4,96,384]{2,1,0:T(8,128)(2,1)}), bf16[4,96,384]{2,1,0:T(8,128)(2,1)S(1)}, u32[]{:S(2)}, u32[]{:S(2)}) %all-to-all-start.6) | async-done | bytes 294944 | tf_op jit(solution)/shard_map/weight_grads/all_to_all | solution.py:26
  160.5 0.7 broadcast_in_dim.16
  161.2 9.2 %all-to-all-start.7 = ((bf16[4,96,384]{2,1,0:T(8,128)(2,1)}), bf16[4,96,384]{2,1,0:T(8,128)(2,1)S(1)}, u32[]{:S(2)}, u32[]{:S(2)}) async-start(bf16[4,96,384]{2,1,0:T(8,128)(2,1)} %broadcast_in_dim.16), calls=%async_computation.7 | async-start | bytes 589824 | tf_op jit(solution)/shard_map/weight_grads/all_to_all | solution.py:26
  170.4 4.6 %collective-permute-start.17 = (bf16[2,2,128,192]{2,3,1,0:T(8,128)(2,1)S(1)}, bf16[2,2,128,192]{2,3,1,0:T(8,128)(2,1)S(1)}, u32[]{:S(2)}, u32[]{:S(2)}) collective-permute-start(bf16[2,2,128,192]{2,3,1,0:T(8,128)(2,1)S(1)} %fusion.26), channel_id=1, source_target_pairs={{0,8},{8,0},{1,9},{9,1},{2,10},{10,2},{3,11},{11,3},{4,12},{12,4},... | collective-permute-start | bytes 589832 | tf_op jit(solution)/shard_map/input_grads/ppermute | solution.py:40
  175.0 1.0 collective-permute-done.17
  176.1 1.9 collective-permute-start.18
  178.0 9.3 %collective-permute-done.18 = bf16[2,128,192]{1,2,0:T(8,128)(2,1)S(1)} collective-permute-done((bf16[2,128,192]{1,2,0:T(8,128)(2,1)S(1)}, bf16[2,128,192]{1,2,0:T(8,128)(2,1)S(1)}, u32[]{:S(2)}, u32[]{:S(2)}) %collective-permute-start.18) | collective-permute-done | bytes 98336 | tf_op jit(solution)/shard_map/input_grads/ppermute | solution.py:40
  187.4 0.9 broadcast_in_dim.17
  188.3 5.6 %all-to-all-start.8 = ((bf16[8,96,384]{2,1,0:T(8,128)(2,1)}), bf16[8,96,384]{2,1,0:T(8,128)(2,1)S(1)}, u32[]{:S(2)}, u32[]{:S(2)}) async-start(bf16[8,96,384]{2,1,0:T(8,128)(2,1)} %broadcast_in_dim.17), calls=%async_computation.8 | async-start | bytes 1179648 | tf_op jit(solution)/shard_map/weight_grads/all_to_all | solution.py:26
  193.9 0.7 slice_bitcast_fusion.4
  194.6 10.6 %all-to-all-done.8 = bf16[8,96,384]{2,1,0:T(8,128)(2,1)S(1)} async-done(((bf16[8,96,384]{2,1,0:T(8,128)(2,1)}), bf16[8,96,384]{2,1,0:T(8,128)(2,1)S(1)}, u32[]{:S(2)}, u32[]{:S(2)}) %all-to-all-start.8) | async-done | bytes 589856 | tf_op jit(solution)/shard_map/weight_grads/all_to_all | solution.py:26
  205.1 0.5 copy.18
  205.6 0.4 reshape.235
  206.0 8.4 %collective-permute-start.19 = (bf16[2,192,768]{2,1,0:T(8,128)(2,1)S(1)}, bf16[2,192,768]{2,1,0:T(8,128)(2,1)S(1)}, u32[]{:S(2)}, u32[]{:S(2)}) collective-permute-start(bf16[2,192,768]{2,1,0:T(8,128)(2,1)S(1)} %reshape.235), channel_id=1, source_target_pairs={{0,8},{8,0},{1,9},{9,1},{2,10},{10,2},{3,11},{11,3},{4,12},{12,4},... | collective-permute-start | bytes 1769480 | tf_op jit(solution)/shard_map/weight_grads/ppermute | solution.py:40
  214.6 1.4 collective-permute-done.19
  216.2 1.0 copy-done
  217.2 0.4 copy-done.1
  (75 shorter events, 2.9 us)
Async XLA Ops:
  3.2 7.7 %copy-start.2 = (bf16[128,192]{0,1:T(8,128)(2,1)S(1)}, bf16[128,192]{0,1:T(8,128)(2,1)}, u32[]{:S(2)}) copy-start(bf16[128,192]{0,1:T(8,128)(2,1)} %param.7) | copy-start | bytes 147460
  3.2 7.6 %copy-start.3 = (bf16[128,192]{0,1:T(8,128)(2,1)S(1)}, bf16[128,192]{0,1:T(8,128)(2,1)}, u32[]{:S(2)}) copy-start(bf16[128,192]{0,1:T(8,128)(2,1)} %param.8) | copy-start | bytes 147460
  3.2 19.0 %all-to-all-start = ((bf16[8,16,3072]{2,1,0:T(8,128)(2,1)}), bf16[8,16,3072]{2,1,0:T(8,128)(2,1)S(1)}, u32[]{:S(2)}, u32[]{:S(2)}) async-start(bf16[8,16,3072]{2,1,0:T(8,128)(2,1)} %bitcast.118), calls=%async_computation | async-start | bytes 1572864 | tf_op jit(solution)/shard_map/heads/all_to_all | solution.py:26
  10.9 10.1 %collective-permute-start.2 = (bf16[2,192,128]{2,1,0:T(8,128)(2,1)S(1)}, bf16[2,192,128]{2,1,0:T(8,128)(2,1)S(1)}, u32[]{:S(2)}, u32[]{:S(2)}) collective-permute-start(bf16[2,192,128]{2,1,0:T(8,128)(2,1)S(1)} %pad_maximum_fusion.4), channel_id=1, source_target_pairs={{0,24},{8,16},{16,8},{24,0},{1,25},{9,17},{17,9},{25,1},{2,26},{10... | collective-permute-start | bytes 294920 | tf_op jit(solution)/shard_map/heads/ppermute | solution.py:162
  15.3 6.6 %collective-permute-start.1 = (bf16[2,192,128]{2,1,0:T(8,128)(2,1)S(1)}, bf16[2,192,128]{2,1,0:T(8,128)(2,1)S(1)}, u32[]{:S(2)}, u32[]{:S(2)}) collective-permute-start(bf16[2,192,128]{2,1,0:T(8,128)(2,1)S(1)} %pad_maximum_fusion.4), channel_id=1, source_target_pairs={{0,16},{16,0},{1,17},{17,1},{2,18},{18,2},{3,19},{19,3},{4,20},{20... | collective-permute-start | bytes 294920 | tf_op jit(solution)/shard_map/heads/ppermute | solution.py:40
  19.1 3.2 %collective-permute-start = (bf16[2,192,128]{2,1,0:T(8,128)(2,1)S(1)}, bf16[2,192,128]{2,1,0:T(8,128)(2,1)S(1)}, u32[]{:S(2)}, u32[]{:S(2)}) collective-permute-start(bf16[2,192,128]{2,1,0:T(8,128)(2,1)S(1)} %pad_maximum_fusion.4), channel_id=1, source_target_pairs={{0,8},{8,0},{1,9},{9,1},{2,10},{10,2},{3,11},{11,3},{4,12},{12,4},... | collective-permute-start | bytes 294920 | tf_op jit(solution)/shard_map/heads/ppermute | solution.py:40
  21.0 2.3 %copy-start.4 = (bf16[2,192,128]{2,1,0:T(8,128)(2,1)}, bf16[2,192,128]{2,1,0:T(8,128)(2,1)S(1)}, u32[]{:S(2)}) copy-start(bf16[2,192,128]{2,1,0:T(8,128)(2,1)S(1)} %collective-permute-done.2) | copy-start | bytes 294916
  21.9 31.8 %copy-start.6 = (bf16[2,192,128]{2,1,0:T(8,128)(2,1)}, bf16[2,192,128]{2,1,0:T(8,128)(2,1)S(1)}, u32[]{:S(2)}) copy-start(bf16[2,192,128]{2,1,0:T(8,128)(2,1)S(1)} %collective-permute-done.1) | copy-start | bytes 294916
  22.2 31.4 %copy-start.8 = (bf16[2,192,128]{2,1,0:T(8,128)(2,1)}, bf16[2,192,128]{2,1,0:T(8,128)(2,1)S(1)}, u32[]{:S(2)}) copy-start(bf16[2,192,128]{2,1,0:T(8,128)(2,1)S(1)} %collective-permute-done) | copy-start | bytes 294916
  23.3 29.4 %all-to-all-start.1 = ((bf16[4,16,1536]{2,1,0:T(8,128)(2,1)}), bf16[4,16,1536]{2,1,0:T(8,128)(2,1)S(1)}, u32[]{:S(2)}, u32[]{:S(2)}) async-start(bf16[4,16,1536]{2,1,0:T(8,128)(2,1)} %broadcast_in_dim.12), calls=%async_computation.1 | async-start | bytes 393216 | tf_op jit(solution)/shard_map/gather_texts/all_to_all | solution.py:26
  40.0 17.2 %collective-permute-start.5 = (bf16[16,1536]{1,0:T(8,128)(2,1)S(1)}, bf16[16,1536]{1,0:T(8,128)(2,1)S(1)}, u32[]{:S(2)}, u32[]{:S(2)}) collective-permute-start(bf16[16,1536]{1,0:T(8,128)(2,1)S(1)} %get-tuple-element.29), channel_id=1, source_target_pairs={{0,16},{16,32},{32,48},{48,0},{1,17},{17,33},{33,49},{49,1},{2,18}... | collective-permute-start | bytes 147464 | tf_op jit(solution)/shard_map/gather_images/ppermute | solution.py:40
  42.7 14.5 %collective-permute-start.4 = (bf16[16,1536]{1,0:T(8,128)(2,1)S(1)}, bf16[16,1536]{1,0:T(8,128)(2,1)S(1)}, u32[]{:S(2)}, u32[]{:S(2)}) collective-permute-start(bf16[16,1536]{1,0:T(8,128)(2,1)S(1)} %get-tuple-element.29), channel_id=1, source_target_pairs={{0,32},{16,48},{32,0},{48,16},{1,33},{17,49},{33,1},{49,17},{2,34}... | collective-permute-start | bytes 147464 | tf_op jit(solution)/shard_map/gather_images/ppermute | solution.py:40
  45.8 11.4 %collective-permute-start.3 = (bf16[16,1536]{1,0:T(8,128)(2,1)S(1)}, bf16[16,1536]{1,0:T(8,128)(2,1)S(1)}, u32[]{:S(2)}, u32[]{:S(2)}) collective-permute-start(bf16[16,1536]{1,0:T(8,128)(2,1)S(1)} %get-tuple-element.29), channel_id=1, source_target_pairs={{0,48},{16,0},{32,16},{48,32},{1,49},{17,1},{33,17},{49,33},{2,50}... | collective-permute-start | bytes 147464 | tf_op jit(solution)/shard_map/gather_images/ppermute | solution.py:40
  53.7 12.3 %all-to-all-start.2 = ((bf16[4,64,1536]{2,1,0:T(8,128)(2,1)}), bf16[4,64,1536]{2,1,0:T(8,128)(2,1)S(1)}, u32[]{:S(2)}, u32[]{:S(2)}) async-start(bf16[4,64,1536]{2,1,0:T(8,128)(2,1)} %broadcast_in_dim.14), calls=%async_computation.2 | async-start | bytes 1572864 | tf_op jit(solution)/shard_map/gather_texts/all_to_all | solution.py:26
  57.2 18.9 %collective-permute-start.8 = (bf16[64,1536]{1,0:T(8,128)(2,1)S(1)}, bf16[64,1536]{1,0:T(8,128)(2,1)S(1)}, u32[]{:S(2)}, u32[]{:S(2)}) collective-permute-start(bf16[64,1536]{1,0:T(8,128)(2,1)S(1)} %pad_maximum_fusion.3), channel_id=1, source_target_pairs={{0,2},{2,4},{4,6},{6,0},{1,3},{3,5},{5,7},{7,1},{8,10},{10,12},{12... | collective-permute-start | bytes 589832 | tf_op jit(solution)/shard_map/gather_images/ppermute | solution.py:40
  59.2 17.0 %collective-permute-start.7 = (bf16[64,1536]{1,0:T(8,128)(2,1)S(1)}, bf16[64,1536]{1,0:T(8,128)(2,1)S(1)}, u32[]{:S(2)}, u32[]{:S(2)}) collective-permute-start(bf16[64,1536]{1,0:T(8,128)(2,1)S(1)} %pad_maximum_fusion.3), channel_id=1, source_target_pairs={{0,4},{2,6},{4,0},{6,2},{1,5},{3,7},{5,1},{7,3},{8,12},{10,14},{12... | collective-permute-start | bytes 589832 | tf_op jit(solution)/shard_map/gather_images/ppermute | solution.py:40
  63.1 13.0 %collective-permute-start.6 = (bf16[64,1536]{1,0:T(8,128)(2,1)S(1)}, bf16[64,1536]{1,0:T(8,128)(2,1)S(1)}, u32[]{:S(2)}, u32[]{:S(2)}) collective-permute-start(bf16[64,1536]{1,0:T(8,128)(2,1)S(1)} %pad_maximum_fusion.3), channel_id=1, source_target_pairs={{0,6},{2,0},{4,2},{6,4},{1,7},{3,1},{5,3},{7,5},{8,14},{10,8},{12,... | collective-permute-start | bytes 589832 | tf_op jit(solution)/shard_map/gather_images/ppermute | solution.py:40
  66.0 12.0 %collective-permute-start.9 = (bf16[256,1536]{1,0:T(8,128)(2,1)S(1)}, bf16[256,1536]{1,0:T(8,128)(2,1)S(1)}, u32[]{:S(2)}, u32[]{:S(2)}) collective-permute-start(bf16[256,1536]{1,0:T(8,128)(2,1)S(1)} %bitcast.115), channel_id=1, source_target_pairs={{0,8},{8,0},{1,9},{9,1},{2,10},{10,2},{3,11},{11,3},{4,12},{12,4},... | collective-permute-start | bytes 2359304 | tf_op jit(solution)/shard_map/gather_texts/ppermute | solution.py:40
  78.8 4.5 %collective-permute-start.16 = (bf16[256,1536]{1,0:T(8,128)(2,1)S(1)}, bf16[256,1536]{1,0:T(8,128)(2,1)S(1)}, u32[]{:S(2)}, u32[]{:S(2)}) collective-permute-start(bf16[256,1536]{1,0:T(8,128)(2,1)S(1)} %convolution_convert_fusion), channel_id=1, source_target_pairs={{0,8},{8,0},{1,9},{9,1},{2,10},{10,2},{3,11},{11,3},{4,12},{12,4},... | collective-permute-start | bytes 2359304 | tf_op jit(solution)/shard_map/sum_texts/ppermute | solution.py:40
  84.6 16.2 %all-to-all-start.3 = ((bf16[4,64,1536]{2,1,0:T(8,128)(2,1)}), bf16[4,64,1536]{2,1,0:T(8,128)(2,1)S(1)}, u32[]{:S(2)}, u32[]{:S(2)}) async-start(bf16[4,64,1536]{2,1,0:T(8,128)(2,1)} %bitcast.18), calls=%async_computation.3 | async-start | bytes 1572864 | tf_op jit(solution)/shard_map/sum_texts/all_to_all | solution.py:26
  89.8 17.7 %collective-permute-start.10 = (bf16[64,1536]{1,0:T(8,128)(2,1)}, bf16[64,1536]{1,0:T(8,128)(2,1)S(1)}, u32[]{:S(2)}, u32[]{:S(2)}) collective-permute-start(bf16[64,1536]{1,0:T(8,128)(2,1)} %get-tuple-element.32), channel_id=1, source_target_pairs={{0,2},{2,4},{4,6},{6,0},{1,3},{3,5},{5,7},{7,1},{8,10},{10,12},{12... | collective-permute-start | bytes 589832 | tf_op jit(solution)/shard_map/sum_images/ppermute | solution.py:40
  92.8 14.6 %collective-permute-start.12 = (bf16[64,1536]{1,0:T(8,128)(2,1)}, bf16[64,1536]{1,0:T(8,128)(2,1)S(1)}, u32[]{:S(2)}, u32[]{:S(2)}) collective-permute-start(bf16[64,1536]{1,0:T(8,128)(2,1)} %get-tuple-element.33), channel_id=1, source_target_pairs={{0,6},{2,0},{4,2},{6,4},{1,7},{3,1},{5,3},{7,5},{8,14},{10,8},{12,... | collective-permute-start | bytes 589832 | tf_op jit(solution)/shard_map/sum_images/ppermute | solution.py:40
  96.3 11.2 %collective-permute-start.11 = (bf16[64,1536]{1,0:T(8,128)(2,1)S(1)}, bf16[64,1536]{1,0:T(8,128)(2,1)S(1)}, u32[]{:S(2)}, u32[]{:S(2)}) collective-permute-start(bf16[64,1536]{1,0:T(8,128)(2,1)S(1)} %get-tuple-element.34), channel_id=1, source_target_pairs={{0,4},{2,6},{4,0},{6,2},{1,5},{3,7},{5,1},{7,3},{8,12},{10,14},{12... | collective-permute-start | bytes 589832 | tf_op jit(solution)/shard_map/sum_images/ppermute | solution.py:40
  101.6 19.4 %all-to-all-start.4 = ((bf16[4,16,1536]{2,1,0:T(8,128)(2,1)}), bf16[4,16,1536]{2,1,0:T(8,128)(2,1)S(1)}, u32[]{:S(2)}, u32[]{:S(2)}) async-start(bf16[4,16,1536]{2,1,0:T(8,128)(2,1)} %bitcast.19), calls=%async_computation.4 | async-start | bytes 393216 | tf_op jit(solution)/shard_map/sum_texts/all_to_all | solution.py:26
  107.6 13.4 %collective-permute-start.13 = (bf16[16,1536]{1,0:T(8,128)(2,1)S(1)}, bf16[16,1536]{1,0:T(8,128)(2,1)S(1)}, u32[]{:S(2)}, u32[]{:S(2)}) collective-permute-start(bf16[16,1536]{1,0:T(8,128)(2,1)S(1)} %get-tuple-element.55), channel_id=1, source_target_pairs={{0,16},{16,32},{32,48},{48,0},{1,17},{17,33},{33,49},{49,1},{2,18}... | collective-permute-start | bytes 147464 | tf_op jit(solution)/shard_map/sum_images/ppermute | solution.py:40
  109.5 11.5 %collective-permute-start.15 = (bf16[16,1536]{1,0:T(8,128)(2,1)S(1)}, bf16[16,1536]{1,0:T(8,128)(2,1)S(1)}, u32[]{:S(2)}, u32[]{:S(2)}) collective-permute-start(bf16[16,1536]{1,0:T(8,128)(2,1)S(1)} %get-tuple-element.56), channel_id=1, source_target_pairs={{0,48},{16,0},{32,16},{48,32},{1,49},{17,1},{33,17},{49,33},{2,50}... | collective-permute-start | bytes 147464 | tf_op jit(solution)/shard_map/sum_images/ppermute | solution.py:40
  114.7 6.9 %collective-permute-start.14 = (bf16[16,1536]{1,0:T(8,128)(2,1)S(1)}, bf16[16,1536]{1,0:T(8,128)(2,1)S(1)}, u32[]{:S(2)}, u32[]{:S(2)}) collective-permute-start(bf16[16,1536]{1,0:T(8,128)(2,1)S(1)} %get-tuple-element.57), channel_id=1, source_target_pairs={{0,32},{16,48},{32,0},{48,16},{1,33},{17,49},{33,1},{49,17},{2,34}... | collective-permute-start | bytes 147464 | tf_op jit(solution)/shard_map/sum_images/ppermute | solution.py:40
  122.2 11.0 %copy-start.5 = (bf16[2,192,128]{2,1,0:T(8,128)(2,1)S(1)}, bf16[2,192,128]{2,1,0:T(8,128)(2,1)}, u32[]{:S(2)}) copy-start(bf16[2,192,128]{2,1,0:T(8,128)(2,1)} %copy-done.4) | copy-start | bytes 294916
  122.2 11.0 %copy-start.7 = (bf16[2,192,128]{2,1,0:T(8,128)(2,1)S(1)}, bf16[2,192,128]{2,1,0:T(8,128)(2,1)}, u32[]{:S(2)}) copy-start(bf16[2,192,128]{2,1,0:T(8,128)(2,1)} %copy-done.6) | copy-start | bytes 294916
  122.2 11.0 %copy-start.9 = (bf16[2,192,128]{2,1,0:T(8,128)(2,1)S(1)}, bf16[2,192,128]{2,1,0:T(8,128)(2,1)}, u32[]{:S(2)}) copy-start(bf16[2,192,128]{2,1,0:T(8,128)(2,1)} %copy-done.8) | copy-start | bytes 294916
  123.2 24.2 %all-to-all-start.5 = ((bf16[32,2,16,384]{3,2,1,0:T(8,128)(2,1)}), bf16[32,2,16,384]{3,2,1,0:T(8,128)(2,1)S(1)}, u32[]{:S(2)}, u32[]{:S(2)}) async-start(bf16[32,2,16,384]{3,2,1,0:T(8,128)(2,1)} %bitcast.21), calls=%async_computation.5 | async-start | bytes 1572864 | tf_op jit(solution)/shard_map/head_grads/all_to_all | solution.py:26
  148.7 11.7 %all-to-all-start.6 = ((bf16[4,96,384]{2,1,0:T(8,128)(2,1)}), bf16[4,96,384]{2,1,0:T(8,128)(2,1)S(1)}, u32[]{:S(2)}, u32[]{:S(2)}) async-start(bf16[4,96,384]{2,1,0:T(8,128)(2,1)} %bitcast.30), calls=%async_computation.6 | async-start | bytes 589824 | tf_op jit(solution)/shard_map/weight_grads/all_to_all | solution.py:26
  161.2 26.1 %all-to-all-start.7 = ((bf16[4,96,384]{2,1,0:T(8,128)(2,1)}), bf16[4,96,384]{2,1,0:T(8,128)(2,1)S(1)}, u32[]{:S(2)}, u32[]{:S(2)}) async-start(bf16[4,96,384]{2,1,0:T(8,128)(2,1)} %broadcast_in_dim.16), calls=%async_computation.7 | async-start | bytes 589824 | tf_op jit(solution)/shard_map/weight_grads/all_to_all | solution.py:26
  170.4 5.6 %collective-permute-start.17 = (bf16[2,2,128,192]{2,3,1,0:T(8,128)(2,1)S(1)}, bf16[2,2,128,192]{2,3,1,0:T(8,128)(2,1)S(1)}, u32[]{:S(2)}, u32[]{:S(2)}) collective-permute-start(bf16[2,2,128,192]{2,3,1,0:T(8,128)(2,1)S(1)} %fusion.26), channel_id=1, source_target_pairs={{0,8},{8,0},{1,9},{9,1},{2,10},{10,2},{3,11},{11,3},{4,12},{12,4},... | collective-permute-start | bytes 589832 | tf_op jit(solution)/shard_map/input_grads/ppermute | solution.py:40
  176.1 11.2 %collective-permute-start.18 = (bf16[2,128,192]{1,2,0:T(8,128)(2,1)S(1)}, bf16[2,128,192]{1,2,0:T(8,128)(2,1)S(1)}, u32[]{:S(2)}, u32[]{:S(2)}) collective-permute-start(bf16[2,128,192]{1,2,0:T(8,128)(2,1)S(1)} %fusion.47), channel_id=1, source_target_pairs={{0,16},{16,0},{1,17},{17,1},{2,18},{18,2},{3,19},{19,3},{4,20},{20... | collective-permute-start | bytes 294920 | tf_op jit(solution)/shard_map/input_grads/ppermute | solution.py:40
  188.3 16.9 %all-to-all-start.8 = ((bf16[8,96,384]{2,1,0:T(8,128)(2,1)}), bf16[8,96,384]{2,1,0:T(8,128)(2,1)S(1)}, u32[]{:S(2)}, u32[]{:S(2)}) async-start(bf16[8,96,384]{2,1,0:T(8,128)(2,1)} %broadcast_in_dim.17), calls=%async_computation.8 | async-start | bytes 1179648 | tf_op jit(solution)/shard_map/weight_grads/all_to_all | solution.py:26
  206.0 10.0 %collective-permute-start.19 = (bf16[2,192,768]{2,1,0:T(8,128)(2,1)S(1)}, bf16[2,192,768]{2,1,0:T(8,128)(2,1)S(1)}, u32[]{:S(2)}, u32[]{:S(2)}) collective-permute-start(bf16[2,192,768]{2,1,0:T(8,128)(2,1)S(1)} %reshape.235), channel_id=1, source_target_pairs={{0,8},{8,0},{1,9},{9,1},{2,10},{10,2},{3,11},{11,3},{4,12},{12,4},... | collective-permute-start | bytes 1769480 | tf_op jit(solution)/shard_map/weight_grads/ppermute | solution.py:40
  216.1 1.0 copy-start
  216.2 1.4 copy-start.1

commit v15 on v14

--- a/solution.py
+++ b/solution.py
@@ -241,7 +241,7 @@
             )
             return kept + shifted(sent.astype(BF16), name, 1).astype(F32)
 
-        inputs = half_sum(half_sum(inputs, core, 2, "c"), pair, 1, "z0")
+        inputs = half_sum(inputs, core, 2, "c")
 
     with jax.named_scope("weight_grads"):
         part = jnp.stack(
@@ -253,6 +253,7 @@
         part = scatter_sum(part.reshape(4, width // 2, quarter), ("xl", "zm"))
         part = jnp.sum(gather(part.astype(BF16), "zh").astype(F32), axis=0).astype(BF16)
         part, inputs = lax.optimization_barrier((part, inputs))
+        inputs = half_sum(inputs, pair, 1, "z0")
         part = gather(part, ("xl", "zm", "z0")).reshape(2, 2, 2, width // 2, quarter)
         part = part.transpose(0, 1, 3, 2, 4).reshape(2, width, 2 * quarter)
         part = lax.optimization_barrier(part)

time: 219 us -> 218 us (level)
  waiting for transfers between devices: 54.2 us -> 41.9 us
  blocking collectives: 0 us -> 11.9 us
    all_to_all x0 -> x1, blocking collectives: none -> 11.9 us  [exchange(): return lax.all_to_all(blocks, axes, split_axis=0, concat_axis=0, tiled=True)]
    all_to_all x9 -> x8, waiting for transfers between devices: 38.2 us -> 29.7 us  [exchange(): return lax.all_to_all(blocks, axes, split_axis=0, concat_axis=0, tiled=True)]
    ppermute x19, waiting for transfers between devices: 16 us -> 12.2 us  [shifted(): return lax.ppermute(value, axis, [(i, (i + by) % n) for i in range(n)])]
    all_to_all x9 -> x8, starting transfers between devices: 66.3 us -> 63.3 us  [exchange(): return lax.all_to_all(blocks, axes, split_axis=0, concat_axis=0, tiled=True)]
  transfers between devices with their start and end apart: 29 -> 28, of which waited for: 14 -> 14; matrix products, arithmetic and copies ran while one was open for 3% -> 4% of each run, Pallas kernels for 0% -> 0%
where the time goes in v15:
time: 218 us; the launch traced here: 216 us
  starting transfers between devices  139 us (64%)
  waiting for transfers between devices  41.9 us (19%)
  blocking collectives  11.9 us (5%)
  local copies, waits for them, and re-layouts  8.22 us (4%)
  matrix products  6.18 us (3%)
  between operations  3.29 us (2%)
  Pallas kernels  2.59 us (1%)
  other arithmetic  2.44 us (1%)
    ppermute x19, starting transfers between devices, shifted(): return lax.ppermute(value, axis, [(i, (i + by) % n) for i in range(n)])  71.4 us
    all_to_all x8, starting transfers between devices, exchange(): return lax.all_to_all(blocks, axes, split_axis=0, concat_axis=0, tiled=True)  63.3 us
    all_to_all x8, waiting for transfers between devices, exchange(): return lax.all_to_all(blocks, axes, split_axis=0, concat_axis=0, tiled=True)  29.7 us
    ppermute x19, waiting for transfers between devices, shifted(): return lax.ppermute(value, axis, [(i, (i + by) % n) for i in range(n)])  12.2 us
    all_to_all x1, blocking collectives, exchange(): return lax.all_to_all(blocks, axes, split_axis=0, concat_axis=0, tiled=True)  11.9 us
    ppermute x1, starting transfers between devices, on_device(): lax.ppermute(features, ('z0', 'c'), [(i, 3 - i) for i in range(4)])  4.39 us
  transfers between devices with their start and end apart: 28, of which 14 were waited for; matrix products, arithmetic and copies ran while one was open for 4% of the time, Pallas kernels for 0%

profile of v15, /device:TPU:1, one launch (start us, length us, event | category | flops | bytes accessed | tf_op | source)
XLA Modules:
  0.0 215.6 jit_solution(15356715328051845967)
XLA Ops:
  0.6 2.6 %heads.1 = bf16[128,3072]{1,0:T(8,128)(2,1)} custom-call(bf16[192,128]{1,0:T(8,128)(2,1)} %bitcast.126, bf16[192,1536]{1,0:T(8,128)(2,1)} %refs_1_.1, bf16[192,128]{1,0:T(8,128)(2,1)} %bitcast.129, bf16[192,1536]{1,0:T(8,128)(2,1)} %refs_3_.1), custom_call_target="tpu_custom_call" | custom-call | flops 150994944 | bytes 2064384 | tf_op jit(solution)/shard_map/heads/pallas_call | solution.py:76
  3.2 7.6 %all-to-all-start = ((bf16[8,16,3072]{2,1,0:T(8,128)(2,1)}), bf16[8,16,3072]{2,1,0:T(8,128)(2,1)S(1)}, u32[]{:S(2)}, u32[]{:S(2)}) async-start(bf16[8,16,3072]{2,1,0:T(8,128)(2,1)} %bitcast.118), calls=%async_computation | async-start | bytes 1572864 | tf_op jit(solution)/shard_map/heads/all_to_all | solution.py:26
  10.9 4.4 %collective-permute-start.2 = (bf16[2,192,128]{2,1,0:T(8,128)(2,1)S(1)}, bf16[2,192,128]{2,1,0:T(8,128)(2,1)S(1)}, u32[]{:S(2)}, u32[]{:S(2)}) collective-permute-start(bf16[2,192,128]{2,1,0:T(8,128)(2,1)S(1)} %pad_maximum_fusion.4), channel_id=1, source_target_pairs={{0,24},{8,16},{16,8},{24,0},{1,25},{9,17},{17,9},{25,1},{2,26},{10... | collective-permute-start | bytes 294920 | tf_op jit(solution)/shard_map/heads/ppermute | solution.py:162
  15.3 3.7 %collective-permute-start.1 = (bf16[2,192,128]{2,1,0:T(8,128)(2,1)S(1)}, bf16[2,192,128]{2,1,0:T(8,128)(2,1)S(1)}, u32[]{:S(2)}, u32[]{:S(2)}) collective-permute-start(bf16[2,192,128]{2,1,0:T(8,128)(2,1)S(1)} %pad_maximum_fusion.4), channel_id=1, source_target_pairs={{0,16},{16,0},{1,17},{17,1},{2,18},{18,2},{3,19},{19,3},{4,20},{20... | collective-permute-start | bytes 294920 | tf_op jit(solution)/shard_map/heads/ppermute | solution.py:40
  19.1 1.9 collective-permute-start
  21.0 0.9 collective-permute-done.1
  21.9 0.4 collective-permute-done
  22.6 0.7 broadcast_in_dim.12
  23.3 16.6 %all-to-all-start.1 = ((bf16[4,16,1536]{2,1,0:T(8,128)(2,1)}), bf16[4,16,1536]{2,1,0:T(8,128)(2,1)S(1)}, u32[]{:S(2)}, u32[]{:S(2)}) async-start(bf16[4,16,1536]{2,1,0:T(8,128)(2,1)} %broadcast_in_dim.12), calls=%async_computation.1 | async-start | bytes 393216 | tf_op jit(solution)/shard_map/gather_texts/all_to_all | solution.py:26
  40.0 2.6 %collective-permute-start.5 = (bf16[16,1536]{1,0:T(8,128)(2,1)S(1)}, bf16[16,1536]{1,0:T(8,128)(2,1)S(1)}, u32[]{:S(2)}, u32[]{:S(2)}) collective-permute-start(bf16[16,1536]{1,0:T(8,128)(2,1)S(1)} %get-tuple-element.29), channel_id=1, source_target_pairs={{0,16},{16,32},{32,48},{48,0},{1,17},{17,33},{33,49},{49,1},{2,18}... | collective-permute-start | bytes 147464 | tf_op jit(solution)/shard_map/gather_images/ppermute | solution.py:40
  42.7 3.1 %collective-permute-start.4 = (bf16[16,1536]{1,0:T(8,128)(2,1)S(1)}, bf16[16,1536]{1,0:T(8,128)(2,1)S(1)}, u32[]{:S(2)}, u32[]{:S(2)}) collective-permute-start(bf16[16,1536]{1,0:T(8,128)(2,1)S(1)} %get-tuple-element.29), channel_id=1, source_target_pairs={{0,32},{16,48},{32,0},{48,16},{1,33},{17,49},{33,1},{49,17},{2,34}... | collective-permute-start | bytes 147464 | tf_op jit(solution)/shard_map/gather_images/ppermute | solution.py:40
  45.8 3.5 %collective-permute-start.3 = (bf16[16,1536]{1,0:T(8,128)(2,1)S(1)}, bf16[16,1536]{1,0:T(8,128)(2,1)S(1)}, u32[]{:S(2)}, u32[]{:S(2)}) collective-permute-start(bf16[16,1536]{1,0:T(8,128)(2,1)S(1)} %get-tuple-element.29), channel_id=1, source_target_pairs={{0,48},{16,0},{32,16},{48,32},{1,49},{17,1},{33,17},{49,33},{2,50}... | collective-permute-start | bytes 147464 | tf_op jit(solution)/shard_map/gather_images/ppermute | solution.py:40
  51.3 1.5 all-to-all-done.1
  52.7 0.9 broadcast_in_dim.14
  53.7 3.5 %all-to-all-start.2 = ((bf16[4,64,1536]{2,1,0:T(8,128)(2,1)}), bf16[4,64,1536]{2,1,0:T(8,128)(2,1)S(1)}, u32[]{:S(2)}, u32[]{:S(2)}) async-start(bf16[4,64,1536]{2,1,0:T(8,128)(2,1)} %broadcast_in_dim.14), calls=%async_computation.2 | async-start | bytes 1572864 | tf_op jit(solution)/shard_map/gather_texts/all_to_all | solution.py:26
  57.2 1.9 collective-permute-start.8
  59.2 4.0 %collective-permute-start.7 = (bf16[64,1536]{1,0:T(8,128)(2,1)S(1)}, bf16[64,1536]{1,0:T(8,128)(2,1)S(1)}, u32[]{:S(2)}, u32[]{:S(2)}) collective-permute-start(bf16[64,1536]{1,0:T(8,128)(2,1)S(1)} %pad_maximum_fusion.3), channel_id=1, source_target_pairs={{0,4},{2,6},{4,0},{6,2},{1,5},{3,7},{5,1},{7,3},{8,12},{10,14},{12... | collective-permute-start | bytes 589832 | tf_op jit(solution)/shard_map/gather_images/ppermute | solution.py:40
  63.1 2.8 %collective-permute-start.6 = (bf16[64,1536]{1,0:T(8,128)(2,1)S(1)}, bf16[64,1536]{1,0:T(8,128)(2,1)S(1)}, u32[]{:S(2)}, u32[]{:S(2)}) collective-permute-start(bf16[64,1536]{1,0:T(8,128)(2,1)S(1)} %pad_maximum_fusion.3), channel_id=1, source_target_pairs={{0,6},{2,0},{4,2},{6,4},{1,7},{3,1},{5,3},{7,5},{8,14},{10,8},{12,... | collective-permute-start | bytes 589832 | tf_op jit(solution)/shard_map/gather_images/ppermute | solution.py:40
  66.0 10.1 %collective-permute-start.9 = (bf16[256,1536]{1,0:T(8,128)(2,1)S(1)}, bf16[256,1536]{1,0:T(8,128)(2,1)S(1)}, u32[]{:S(2)}, u32[]{:S(2)}) collective-permute-start(bf16[256,1536]{1,0:T(8,128)(2,1)S(1)} %bitcast.115), channel_id=1, source_target_pairs={{0,8},{8,0},{1,9},{9,1},{2,10},{10,2},{3,11},{11,3},{4,12},{12,4},... | collective-permute-start | bytes 2359304 | tf_op jit(solution)/shard_map/gather_texts/ppermute | solution.py:40
  76.2 1.8 collective-permute-done.9
  78.0 0.4 fusion.14
  78.4 0.4 convolution_convert_fusion
  78.8 2.6 %collective-permute-start.16 = (bf16[256,1536]{1,0:T(8,128)(2,1)S(1)}, bf16[256,1536]{1,0:T(8,128)(2,1)S(1)}, u32[]{:S(2)}, u32[]{:S(2)}) collective-permute-start(bf16[256,1536]{1,0:T(8,128)(2,1)S(1)} %convolution_convert_fusion), channel_id=1, source_target_pairs={{0,8},{8,0},{1,9},{9,1},{2,10},{10,2},{3,11},{11,3},{4,12},{12,4},... | collective-permute-start | bytes 2359304 | tf_op jit(solution)/shard_map/sum_texts/ppermute | solution.py:40
  81.4 0.4 fusion.15
  81.9 0.4 fusion.63
  82.3 0.4 fusion.62
  82.7 0.7 collective-permute-done.16
  83.3 1.3 fusion
  84.6 4.5 %all-to-all-start.3 = ((bf16[4,64,1536]{2,1,0:T(8,128)(2,1)}), bf16[4,64,1536]{2,1,0:T(8,128)(2,1)S(1)}, u32[]{:S(2)}, u32[]{:S(2)}) async-start(bf16[4,64,1536]{2,1,0:T(8,128)(2,1)} %bitcast.18), calls=%async_computation.3 | async-start | bytes 1572864 | tf_op jit(solution)/shard_map/sum_texts/all_to_all | solution.py:26
  89.0 0.8 fusion.60
  89.8 3.0 %collective-permute-start.10 = (bf16[64,1536]{1,0:T(8,128)(2,1)}, bf16[64,1536]{1,0:T(8,128)(2,1)S(1)}, u32[]{:S(2)}, u32[]{:S(2)}) collective-permute-start(bf16[64,1536]{1,0:T(8,128)(2,1)} %get-tuple-element.32), channel_id=1, source_target_pairs={{0,2},{2,4},{4,6},{6,0},{1,3},{3,5},{5,7},{7,1},{8,10},{10,12},{12... | collective-permute-start | bytes 589832 | tf_op jit(solution)/shard_map/sum_images/ppermute | solution.py:40
  92.8 3.5 %collective-permute-start.12 = (bf16[64,1536]{1,0:T(8,128)(2,1)}, bf16[64,1536]{1,0:T(8,128)(2,1)S(1)}, u32[]{:S(2)}, u32[]{:S(2)}) collective-permute-start(bf16[64,1536]{1,0:T(8,128)(2,1)} %get-tuple-element.33), channel_id=1, source_target_pairs={{0,6},{2,0},{4,2},{6,4},{1,7},{3,1},{5,3},{7,5},{8,14},{10,8},{12,... | collective-permute-start | bytes 589832 | tf_op jit(solution)/shard_map/sum_images/ppermute | solution.py:40
  96.3 2.5 %collective-permute-start.11 = (bf16[64,1536]{1,0:T(8,128)(2,1)S(1)}, bf16[64,1536]{1,0:T(8,128)(2,1)S(1)}, u32[]{:S(2)}, u32[]{:S(2)}) collective-permute-start(bf16[64,1536]{1,0:T(8,128)(2,1)S(1)} %get-tuple-element.34), channel_id=1, source_target_pairs={{0,4},{2,6},{4,0},{6,2},{1,5},{3,7},{5,1},{7,3},{8,12},{10,14},{12... | collective-permute-start | bytes 589832 | tf_op jit(solution)/shard_map/sum_images/ppermute | solution.py:40
  98.8 1.9 all-to-all-done.3
  100.7 0.8 reduce_sum.97
  101.6 5.9 %all-to-all-start.4 = ((bf16[4,16,1536]{2,1,0:T(8,128)(2,1)}), bf16[4,16,1536]{2,1,0:T(8,128)(2,1)S(1)}, u32[]{:S(2)}, u32[]{:S(2)}) async-start(bf16[4,16,1536]{2,1,0:T(8,128)(2,1)} %bitcast.19), calls=%async_computation.4 | async-start | bytes 393216 | tf_op jit(solution)/shard_map/sum_texts/all_to_all | solution.py:26
  107.6 1.9 collective-permute-start.13
  109.5 5.2 %collective-permute-start.15 = (bf16[16,1536]{1,0:T(8,128)(2,1)S(1)}, bf16[16,1536]{1,0:T(8,128)(2,1)S(1)}, u32[]{:S(2)}, u32[]{:S(2)}) collective-permute-start(bf16[16,1536]{1,0:T(8,128)(2,1)S(1)} %get-tuple-element.56), channel_id=1, source_target_pairs={{0,48},{16,0},{32,16},{48,32},{1,49},{17,1},{33,17},{49,33},{2,50}... | collective-permute-start | bytes 147464 | tf_op jit(solution)/shard_map/sum_images/ppermute | solution.py:40
  114.7 1.9 collective-permute-start.14
  116.6 4.4 %all-to-all-done.4 = bf16[4,16,1536]{2,1,0:T(8,128)(2,1)S(1)} async-done(((bf16[4,16,1536]{2,1,0:T(8,128)(2,1)}), bf16[4,16,1536]{2,1,0:T(8,128)(2,1)S(1)}, u32[]{:S(2)}, u32[]{:S(2)}) %all-to-all-start.4) | async-done | bytes 196640 | tf_op jit(solution)/shard_map/sum_texts/all_to_all | solution.py:26
  121.0 0.6 collective-permute-done.14
  122.2 1.0 broadcast_in_dim.15
  123.2 10.0 %all-to-all-start.5 = ((bf16[32,2,16,384]{3,2,1,0:T(8,128)(2,1)}), bf16[32,2,16,384]{3,2,1,0:T(8,128)(2,1)S(1)}, u32[]{:S(2)}, u32[]{:S(2)}) async-start(bf16[32,2,16,384]{3,2,1,0:T(8,128)(2,1)} %bitcast.21), calls=%async_computation.5 | async-start | bytes 1572864 | tf_op jit(solution)/shard_map/head_grads/all_to_all | solution.py:26
  133.3 14.0 %all-to-all-done.5 = bf16[32,2,16,384]{3,2,1,0:T(8,128)(2,1)S(1)} async-done(((bf16[32,2,16,384]{3,2,1,0:T(8,128)(2,1)}), bf16[32,2,16,384]{3,2,1,0:T(8,128)(2,1)S(1)}, u32[]{:S(2)}, u32[]{:S(2)}) %all-to-all-start.5) | async-done | bytes 786464 | tf_op jit(solution)/shard_map/head_grads/all_to_all | solution.py:26
  148.0 11.9 %all_to_all.45 = bf16[4,96,384]{2,1,0:T(8,128)(2,1)S(1)} all-to-all(bf16[4,96,384]{2,1,0:T(8,128)(2,1)S(1)} %bitcast.124), channel_id=1, replica_groups=mesh['xl'=2,'zh'=4,'zm'=2,'z0'=2,'c'=2,'y'=4,'xh'=2] {'xl','zm'}, dimensions={0} | all-to-all | bytes 589824 | tf_op jit(solution)/shard_map/weight_grads/all_to_all | solution.py:26
  160.0 0.7 broadcast_in_dim.16
  160.7 7.8 %all-to-all-start.7 = ((bf16[4,96,384]{2,1,0:T(8,128)(2,1)}), bf16[4,96,384]{2,1,0:T(8,128)(2,1)S(1)}, u32[]{:S(2)}, u32[]{:S(2)}) async-start(bf16[4,96,384]{2,1,0:T(8,128)(2,1)} %broadcast_in_dim.16), calls=%async_computation.7 | async-start | bytes 589824 | tf_op jit(solution)/shard_map/weight_grads/all_to_all | solution.py:26
  168.6 1.2 convolution_bitcast_fusion
  169.8 1.2 convolution_bitcast_fusion.1
  171.0 5.3 %collective-permute-start.17 = (bf16[2,2,128,192]{2,3,1,0:T(8,128)(2,1)S(1)}, bf16[2,2,128,192]{2,3,1,0:T(8,128)(2,1)S(1)}, u32[]{:S(2)}, u32[]{:S(2)}) collective-permute-start(bf16[2,2,128,192]{2,3,1,0:T(8,128)(2,1)S(1)} %fusion.26), channel_id=1, source_target_pairs={{0,8},{8,0},{1,9},{9,1},{2,10},{10,2},{3,11},{11,3},{4,12},{12,4},... | collective-permute-start | bytes 589832 | tf_op jit(solution)/shard_map/input_grads/ppermute | solution.py:40
  176.3 1.0 collective-permute-done.17
  177.4 6.2 %all-to-all-done.7 = bf16[4,96,384]{2,1,0:T(8,128)(2,1)S(1)} async-done(((bf16[4,96,384]{2,1,0:T(8,128)(2,1)}), bf16[4,96,384]{2,1,0:T(8,128)(2,1)S(1)}, u32[]{:S(2)}, u32[]{:S(2)}) %all-to-all-start.7) | async-done | bytes 294944 | tf_op jit(solution)/shard_map/weight_grads/all_to_all | solution.py:26
  183.7 0.9 broadcast_in_dim.17
  184.6 7.4 %all-to-all-start.8 = ((bf16[8,96,384]{2,1,0:T(8,128)(2,1)}), bf16[8,96,384]{2,1,0:T(8,128)(2,1)S(1)}, u32[]{:S(2)}, u32[]{:S(2)}) async-start(bf16[8,96,384]{2,1,0:T(8,128)(2,1)} %broadcast_in_dim.17), calls=%async_computation.8 | async-start | bytes 1179648 | tf_op jit(solution)/shard_map/weight_grads/all_to_all | solution.py:26
  192.0 3.4 %collective-permute-start.18 = (bf16[2,128,192]{1,2,0:T(8,128)(2,1)S(1)}, bf16[2,128,192]{1,2,0:T(8,128)(2,1)S(1)}, u32[]{:S(2)}, u32[]{:S(2)}) collective-permute-start(bf16[2,128,192]{1,2,0:T(8,128)(2,1)S(1)} %fusion.47), channel_id=1, source_target_pairs={{0,16},{16,0},{1,17},{17,1},{2,18},{18,2},{3,19},{19,3},{4,20},{20... | collective-permute-start | bytes 294920 | tf_op jit(solution)/shard_map/weight_grads/ppermute | solution.py:40
  195.3 5.5 %collective-permute-done.18 = bf16[2,128,192]{1,2,0:T(8,128)(2,1)S(1)} collective-permute-done((bf16[2,128,192]{1,2,0:T(8,128)(2,1)S(1)}, bf16[2,128,192]{1,2,0:T(8,128)(2,1)S(1)}, u32[]{:S(2)}, u32[]{:S(2)}) %collective-permute-start.18) | collective-permute-done | bytes 98336 | tf_op jit(solution)/shard_map/weight_grads/ppermute | solution.py:40
  200.8 0.7 slice_bitcast_fusion.4
  201.5 1.7 all-to-all-done.8
  203.2 0.5 copy.18
  203.7 0.4 reshape.235
  204.0 8.4 %collective-permute-start.19 = (bf16[2,192,768]{2,1,0:T(8,128)(2,1)S(1)}, bf16[2,192,768]{2,1,0:T(8,128)(2,1)S(1)}, u32[]{:S(2)}, u32[]{:S(2)}) collective-permute-start(bf16[2,192,768]{2,1,0:T(8,128)(2,1)S(1)} %reshape.235), channel_id=1, source_target_pairs={{0,8},{8,0},{1,9},{9,1},{2,10},{10,2},{3,11},{11,3},{4,12},{12,4},... | collective-permute-start | bytes 1769480 | tf_op jit(solution)/shard_map/weight_grads/ppermute | solution.py:40
  212.7 1.4 collective-permute-done.19
  214.2 1.0 copy-done
  215.2 0.4 copy-done.1
  (74 shorter events, 2.5 us)
Async XLA Ops:
  3.2 7.7 %copy-start.2 = (bf16[128,192]{0,1:T(8,128)(2,1)S(1)}, bf16[128,192]{0,1:T(8,128)(2,1)}, u32[]{:S(2)}) copy-start(bf16[128,192]{0,1:T(8,128)(2,1)} %param.7) | copy-start | bytes 147460
  3.2 7.6 %copy-start.3 = (bf16[128,192]{0,1:T(8,128)(2,1)S(1)}, bf16[128,192]{0,1:T(8,128)(2,1)}, u32[]{:S(2)}) copy-start(bf16[128,192]{0,1:T(8,128)(2,1)} %param.8) | copy-start | bytes 147460
  3.2 19.0 %all-to-all-start = ((bf16[8,16,3072]{2,1,0:T(8,128)(2,1)}), bf16[8,16,3072]{2,1,0:T(8,128)(2,1)S(1)}, u32[]{:S(2)}, u32[]{:S(2)}) async-start(bf16[8,16,3072]{2,1,0:T(8,128)(2,1)} %bitcast.118), calls=%async_computation | async-start | bytes 1572864 | tf_op jit(solution)/shard_map/heads/all_to_all | solution.py:26
  10.9 10.1 %collective-permute-start.2 = (bf16[2,192,128]{2,1,0:T(8,128)(2,1)S(1)}, bf16[2,192,128]{2,1,0:T(8,128)(2,1)S(1)}, u32[]{:S(2)}, u32[]{:S(2)}) collective-permute-start(bf16[2,192,128]{2,1,0:T(8,128)(2,1)S(1)} %pad_maximum_fusion.4), channel_id=1, source_target_pairs={{0,24},{8,16},{16,8},{24,0},{1,25},{9,17},{17,9},{25,1},{2,26},{10... | collective-permute-start | bytes 294920 | tf_op jit(solution)/shard_map/heads/ppermute | solution.py:162
  15.3 6.6 %collective-permute-start.1 = (bf16[2,192,128]{2,1,0:T(8,128)(2,1)S(1)}, bf16[2,192,128]{2,1,0:T(8,128)(2,1)S(1)}, u32[]{:S(2)}, u32[]{:S(2)}) collective-permute-start(bf16[2,192,128]{2,1,0:T(8,128)(2,1)S(1)} %pad_maximum_fusion.4), channel_id=1, source_target_pairs={{0,16},{16,0},{1,17},{17,1},{2,18},{18,2},{3,19},{19,3},{4,20},{20... | collective-permute-start | bytes 294920 | tf_op jit(solution)/shard_map/heads/ppermute | solution.py:40
  19.1 3.2 %collective-permute-start = (bf16[2,192,128]{2,1,0:T(8,128)(2,1)S(1)}, bf16[2,192,128]{2,1,0:T(8,128)(2,1)S(1)}, u32[]{:S(2)}, u32[]{:S(2)}) collective-permute-start(bf16[2,192,128]{2,1,0:T(8,128)(2,1)S(1)} %pad_maximum_fusion.4), channel_id=1, source_target_pairs={{0,8},{8,0},{1,9},{9,1},{2,10},{10,2},{3,11},{11,3},{4,12},{12,4},... | collective-permute-start | bytes 294920 | tf_op jit(solution)/shard_map/heads/ppermute | solution.py:40
  21.0 2.3 %copy-start.4 = (bf16[2,192,128]{2,1,0:T(8,128)(2,1)}, bf16[2,192,128]{2,1,0:T(8,128)(2,1)S(1)}, u32[]{:S(2)}) copy-start(bf16[2,192,128]{2,1,0:T(8,128)(2,1)S(1)} %collective-permute-done.2) | copy-start | bytes 294916
  21.9 31.8 %copy-start.6 = (bf16[2,192,128]{2,1,0:T(8,128)(2,1)}, bf16[2,192,128]{2,1,0:T(8,128)(2,1)S(1)}, u32[]{:S(2)}) copy-start(bf16[2,192,128]{2,1,0:T(8,128)(2,1)S(1)} %collective-permute-done.1) | copy-start | bytes 294916
  22.2 31.4 %copy-start.8 = (bf16[2,192,128]{2,1,0:T(8,128)(2,1)}, bf16[2,192,128]{2,1,0:T(8,128)(2,1)S(1)}, u32[]{:S(2)}) copy-start(bf16[2,192,128]{2,1,0:T(8,128)(2,1)S(1)} %collective-permute-done) | copy-start | bytes 294916
  23.3 29.4 %all-to-all-start.1 = ((bf16[4,16,1536]{2,1,0:T(8,128)(2,1)}), bf16[4,16,1536]{2,1,0:T(8,128)(2,1)S(1)}, u32[]{:S(2)}, u32[]{:S(2)}) async-start(bf16[4,16,1536]{2,1,0:T(8,128)(2,1)} %broadcast_in_dim.12), calls=%async_computation.1 | async-start | bytes 393216 | tf_op jit(solution)/shard_map/gather_texts/all_to_all | solution.py:26
  40.0 17.2 %collective-permute-start.5 = (bf16[16,1536]{1,0:T(8,128)(2,1)S(1)}, bf16[16,1536]{1,0:T(8,128)(2,1)S(1)}, u32[]{:S(2)}, u32[]{:S(2)}) collective-permute-start(bf16[16,1536]{1,0:T(8,128)(2,1)S(1)} %get-tuple-element.29), channel_id=1, source_target_pairs={{0,16},{16,32},{32,48},{48,0},{1,17},{17,33},{33,49},{49,1},{2,18}... | collective-permute-start | bytes 147464 | tf_op jit(solution)/shard_map/gather_images/ppermute | solution.py:40
  42.7 14.5 %collective-permute-start.4 = (bf16[16,1536]{1,0:T(8,128)(2,1)S(1)}, bf16[16,1536]{1,0:T(8,128)(2,1)S(1)}, u32[]{:S(2)}, u32[]{:S(2)}) collective-permute-start(bf16[16,1536]{1,0:T(8,128)(2,1)S(1)} %get-tuple-element.29), channel_id=1, source_target_pairs={{0,32},{16,48},{32,0},{48,16},{1,33},{17,49},{33,1},{49,17},{2,34}... | collective-permute-start | bytes 147464 | tf_op jit(solution)/shard_map/gather_images/ppermute | solution.py:40
  45.8 11.4 %collective-permute-start.3 = (bf16[16,1536]{1,0:T(8,128)(2,1)S(1)}, bf16[16,1536]{1,0:T(8,128)(2,1)S(1)}, u32[]{:S(2)}, u32[]{:S(2)}) collective-permute-start(bf16[16,1536]{1,0:T(8,128)(2,1)S(1)} %get-tuple-element.29), channel_id=1, source_target_pairs={{0,48},{16,0},{32,16},{48,32},{1,49},{17,1},{33,17},{49,33},{2,50}... | collective-permute-start | bytes 147464 | tf_op jit(solution)/shard_map/gather_images/ppermute | solution.py:40
  53.7 12.3 %all-to-all-start.2 = ((bf16[4,64,1536]{2,1,0:T(8,128)(2,1)}), bf16[4,64,1536]{2,1,0:T(8,128)(2,1)S(1)}, u32[]{:S(2)}, u32[]{:S(2)}) async-start(bf16[4,64,1536]{2,1,0:T(8,128)(2,1)} %broadcast_in_dim.14), calls=%async_computation.2 | async-start | bytes 1572864 | tf_op jit(solution)/shard_map/gather_texts/all_to_all | solution.py:26
  57.2 18.9 %collective-permute-start.8 = (bf16[64,1536]{1,0:T(8,128)(2,1)S(1)}, bf16[64,1536]{1,0:T(8,128)(2,1)S(1)}, u32[]{:S(2)}, u32[]{:S(2)}) collective-permute-start(bf16[64,1536]{1,0:T(8,128)(2,1)S(1)} %pad_maximum_fusion.3), channel_id=1, source_target_pairs={{0,2},{2,4},{4,6},{6,0},{1,3},{3,5},{5,7},{7,1},{8,10},{10,12},{12... | collective-permute-start | bytes 589832 | tf_op jit(solution)/shard_map/gather_images/ppermute | solution.py:40
  59.2 17.0 %collective-permute-start.7 = (bf16[64,1536]{1,0:T(8,128)(2,1)S(1)}, bf16[64,1536]{1,0:T(8,128)(2,1)S(1)}, u32[]{:S(2)}, u32[]{:S(2)}) collective-permute-start(bf16[64,1536]{1,0:T(8,128)(2,1)S(1)} %pad_maximum_fusion.3), channel_id=1, source_target_pairs={{0,4},{2,6},{4,0},{6,2},{1,5},{3,7},{5,1},{7,3},{8,12},{10,14},{12... | collective-permute-start | bytes 589832 | tf_op jit(solution)/shard_map/gather_images/ppermute | solution.py:40
  63.1 13.0 %collective-permute-start.6 = (bf16[64,1536]{1,0:T(8,128)(2,1)S(1)}, bf16[64,1536]{1,0:T(8,128)(2,1)S(1)}, u32[]{:S(2)}, u32[]{:S(2)}) collective-permute-start(bf16[64,1536]{1,0:T(8,128)(2,1)S(1)} %pad_maximum_fusion.3), channel_id=1, source_target_pairs={{0,6},{2,0},{4,2},{6,4},{1,7},{3,1},{5,3},{7,5},{8,14},{10,8},{12,... | collective-permute-start | bytes 589832 | tf_op jit(solution)/shard_map/gather_images/ppermute | solution.py:40
  66.0 12.0 %collective-permute-start.9 = (bf16[256,1536]{1,0:T(8,128)(2,1)S(1)}, bf16[256,1536]{1,0:T(8,128)(2,1)S(1)}, u32[]{:S(2)}, u32[]{:S(2)}) collective-permute-start(bf16[256,1536]{1,0:T(8,128)(2,1)S(1)} %bitcast.115), channel_id=1, source_target_pairs={{0,8},{8,0},{1,9},{9,1},{2,10},{10,2},{3,11},{11,3},{4,12},{12,4},... | collective-permute-start | bytes 2359304 | tf_op jit(solution)/shard_map/gather_texts/ppermute | solution.py:40
  78.8 4.5 %collective-permute-start.16 = (bf16[256,1536]{1,0:T(8,128)(2,1)S(1)}, bf16[256,1536]{1,0:T(8,128)(2,1)S(1)}, u32[]{:S(2)}, u32[]{:S(2)}) collective-permute-start(bf16[256,1536]{1,0:T(8,128)(2,1)S(1)} %convolution_convert_fusion), channel_id=1, source_target_pairs={{0,8},{8,0},{1,9},{9,1},{2,10},{10,2},{3,11},{11,3},{4,12},{12,4},... | collective-permute-start | bytes 2359304 | tf_op jit(solution)/shard_map/sum_texts/ppermute | solution.py:40
  84.6 16.2 %all-to-all-start.3 = ((bf16[4,64,1536]{2,1,0:T(8,128)(2,1)}), bf16[4,64,1536]{2,1,0:T(8,128)(2,1)S(1)}, u32[]{:S(2)}, u32[]{:S(2)}) async-start(bf16[4,64,1536]{2,1,0:T(8,128)(2,1)} %bitcast.18), calls=%async_computation.3 | async-start | bytes 1572864 | tf_op jit(solution)/shard_map/sum_texts/all_to_all | solution.py:26
  89.8 17.7 %collective-permute-start.10 = (bf16[64,1536]{1,0:T(8,128)(2,1)}, bf16[64,1536]{1,0:T(8,128)(2,1)S(1)}, u32[]{:S(2)}, u32[]{:S(2)}) collective-permute-start(bf16[64,1536]{1,0:T(8,128)(2,1)} %get-tuple-element.32), channel_id=1, source_target_pairs={{0,2},{2,4},{4,6},{6,0},{1,3},{3,5},{5,7},{7,1},{8,10},{10,12},{12... | collective-permute-start | bytes 589832 | tf_op jit(solution)/shard_map/sum_images/ppermute | solution.py:40
  92.8 14.6 %collective-permute-start.12 = (bf16[64,1536]{1,0:T(8,128)(2,1)}, bf16[64,1536]{1,0:T(8,128)(2,1)S(1)}, u32[]{:S(2)}, u32[]{:S(2)}) collective-permute-start(bf16[64,1536]{1,0:T(8,128)(2,1)} %get-tuple-element.33), channel_id=1, source_target_pairs={{0,6},{2,0},{4,2},{6,4},{1,7},{3,1},{5,3},{7,5},{8,14},{10,8},{12,... | collective-permute-start | bytes 589832 | tf_op jit(solution)/shard_map/sum_images/ppermute | solution.py:40
  96.3 11.2 %collective-permute-start.11 = (bf16[64,1536]{1,0:T(8,128)(2,1)S(1)}, bf16[64,1536]{1,0:T(8,128)(2,1)S(1)}, u32[]{:S(2)}, u32[]{:S(2)}) collective-permute-start(bf16[64,1536]{1,0:T(8,128)(2,1)S(1)} %get-tuple-element.34), channel_id=1, source_target_pairs={{0,4},{2,6},{4,0},{6,2},{1,5},{3,7},{5,1},{7,3},{8,12},{10,14},{12... | collective-permute-start | bytes 589832 | tf_op jit(solution)/shard_map/sum_images/ppermute | solution.py:40
  101.6 19.4 %all-to-all-start.4 = ((bf16[4,16,1536]{2,1,0:T(8,128)(2,1)}), bf16[4,16,1536]{2,1,0:T(8,128)(2,1)S(1)}, u32[]{:S(2)}, u32[]{:S(2)}) async-start(bf16[4,16,1536]{2,1,0:T(8,128)(2,1)} %bitcast.19), calls=%async_computation.4 | async-start | bytes 393216 | tf_op jit(solution)/shard_map/sum_texts/all_to_all | solution.py:26
  107.6 13.4 %collective-permute-start.13 = (bf16[16,1536]{1,0:T(8,128)(2,1)S(1)}, bf16[16,1536]{1,0:T(8,128)(2,1)S(1)}, u32[]{:S(2)}, u32[]{:S(2)}) collective-permute-start(bf16[16,1536]{1,0:T(8,128)(2,1)S(1)} %get-tuple-element.55), channel_id=1, source_target_pairs={{0,16},{16,32},{32,48},{48,0},{1,17},{17,33},{33,49},{49,1},{2,18}... | collective-permute-start | bytes 147464 | tf_op jit(solution)/shard_map/sum_images/ppermute | solution.py:40
  109.5 11.5 %collective-permute-start.15 = (bf16[16,1536]{1,0:T(8,128)(2,1)S(1)}, bf16[16,1536]{1,0:T(8,128)(2,1)S(1)}, u32[]{:S(2)}, u32[]{:S(2)}) collective-permute-start(bf16[16,1536]{1,0:T(8,128)(2,1)S(1)} %get-tuple-element.56), channel_id=1, source_target_pairs={{0,48},{16,0},{32,16},{48,32},{1,49},{17,1},{33,17},{49,33},{2,50}... | collective-permute-start | bytes 147464 | tf_op jit(solution)/shard_map/sum_images/ppermute | solution.py:40
  114.7 6.9 %collective-permute-start.14 = (bf16[16,1536]{1,0:T(8,128)(2,1)S(1)}, bf16[16,1536]{1,0:T(8,128)(2,1)S(1)}, u32[]{:S(2)}, u32[]{:S(2)}) collective-permute-start(bf16[16,1536]{1,0:T(8,128)(2,1)S(1)} %get-tuple-element.57), channel_id=1, source_target_pairs={{0,32},{16,48},{32,0},{48,16},{1,33},{17,49},{33,1},{49,17},{2,34}... | collective-permute-start | bytes 147464 | tf_op jit(solution)/shard_map/sum_images/ppermute | solution.py:40
  122.2 11.0 %copy-start.5 = (bf16[2,192,128]{2,1,0:T(8,128)(2,1)S(1)}, bf16[2,192,128]{2,1,0:T(8,128)(2,1)}, u32[]{:S(2)}) copy-start(bf16[2,192,128]{2,1,0:T(8,128)(2,1)} %copy-done.4) | copy-start | bytes 294916
  122.2 11.0 %copy-start.7 = (bf16[2,192,128]{2,1,0:T(8,128)(2,1)S(1)}, bf16[2,192,128]{2,1,0:T(8,128)(2,1)}, u32[]{:S(2)}) copy-start(bf16[2,192,128]{2,1,0:T(8,128)(2,1)} %copy-done.6) | copy-start | bytes 294916
  122.2 11.0 %copy-start.9 = (bf16[2,192,128]{2,1,0:T(8,128)(2,1)S(1)}, bf16[2,192,128]{2,1,0:T(8,128)(2,1)}, u32[]{:S(2)}) copy-start(bf16[2,192,128]{2,1,0:T(8,128)(2,1)} %copy-done.8) | copy-start | bytes 294916
  123.2 24.2 %all-to-all-start.5 = ((bf16[32,2,16,384]{3,2,1,0:T(8,128)(2,1)}), bf16[32,2,16,384]{3,2,1,0:T(8,128)(2,1)S(1)}, u32[]{:S(2)}, u32[]{:S(2)}) async-start(bf16[32,2,16,384]{3,2,1,0:T(8,128)(2,1)} %bitcast.21), calls=%async_computation.5 | async-start | bytes 1572864 | tf_op jit(solution)/shard_map/head_grads/all_to_all | solution.py:26
  160.7 22.9 %all-to-all-start.7 = ((bf16[4,96,384]{2,1,0:T(8,128)(2,1)}), bf16[4,96,384]{2,1,0:T(8,128)(2,1)S(1)}, u32[]{:S(2)}, u32[]{:S(2)}) async-start(bf16[4,96,384]{2,1,0:T(8,128)(2,1)} %broadcast_in_dim.16), calls=%async_computation.7 | async-start | bytes 589824 | tf_op jit(solution)/shard_map/weight_grads/all_to_all | solution.py:26
  171.0 6.3 %collective-permute-start.17 = (bf16[2,2,128,192]{2,3,1,0:T(8,128)(2,1)S(1)}, bf16[2,2,128,192]{2,3,1,0:T(8,128)(2,1)S(1)}, u32[]{:S(2)}, u32[]{:S(2)}) collective-permute-start(bf16[2,2,128,192]{2,3,1,0:T(8,128)(2,1)S(1)} %fusion.26), channel_id=1, source_target_pairs={{0,8},{8,0},{1,9},{9,1},{2,10},{10,2},{3,11},{11,3},{4,12},{12,4},... | collective-permute-start | bytes 589832 | tf_op jit(solution)/shard_map/input_grads/ppermute | solution.py:40
  184.6 18.6 %all-to-all-start.8 = ((bf16[8,96,384]{2,1,0:T(8,128)(2,1)}), bf16[8,96,384]{2,1,0:T(8,128)(2,1)S(1)}, u32[]{:S(2)}, u32[]{:S(2)}) async-start(bf16[8,96,384]{2,1,0:T(8,128)(2,1)} %broadcast_in_dim.17), calls=%async_computation.8 | async-start | bytes 1179648 | tf_op jit(solution)/shard_map/weight_grads/all_to_all | solution.py:26
  192.0 8.9 %collective-permute-start.18 = (bf16[2,128,192]{1,2,0:T(8,128)(2,1)S(1)}, bf16[2,128,192]{1,2,0:T(8,128)(2,1)S(1)}, u32[]{:S(2)}, u32[]{:S(2)}) collective-permute-start(bf16[2,128,192]{1,2,0:T(8,128)(2,1)S(1)} %fusion.47), channel_id=1, source_target_pairs={{0,16},{16,0},{1,17},{17,1},{2,18},{18,2},{3,19},{19,3},{4,20},{20... | collective-permute-start | bytes 294920 | tf_op jit(solution)/shard_map/weight_grads/ppermute | solution.py:40
  204.0 10.0 %collective-permute-start.19 = (bf16[2,192,768]{2,1,0:T(8,128)(2,1)S(1)}, bf16[2,192,768]{2,1,0:T(8,128)(2,1)S(1)}, u32[]{:S(2)}, u32[]{:S(2)}) collective-permute-start(bf16[2,192,768]{2,1,0:T(8,128)(2,1)S(1)} %reshape.235), channel_id=1, source_target_pairs={{0,8},{8,0},{1,9},{9,1},{2,10},{10,2},{3,11},{11,3},{4,12},{12,4},... | collective-permute-start | bytes 1769480 | tf_op jit(solution)/shard_map/weight_grads/ppermute | solution.py:40
  214.2 1.0 copy-start
  214.2 1.4 copy-start.1

commit v16 on v15

--- a/solution.py
+++ b/solution.py
@@ -251,9 +251,10 @@
             ]
         )
         part = scatter_sum(part.reshape(4, width // 2, quarter), ("xl", "zm"))
-        part = jnp.sum(gather(part.astype(BF16), "zh").astype(F32), axis=0).astype(BF16)
+        part, inputs = lax.optimization_barrier((part.astype(BF16), inputs))
+        part = jnp.sum(gather(part, "zh").astype(F32), axis=0).astype(BF16)
+        inputs = half_sum(inputs, pair, 1, "z0")
         part, inputs = lax.optimization_barrier((part, inputs))
-        inputs = half_sum(inputs, pair, 1, "z0")
         part = gather(part, ("xl", "zm", "z0")).reshape(2, 2, 2, width // 2, quarter)
         part = part.transpose(0, 1, 3, 2, 4).reshape(2, width, 2 * quarter)
         part = lax.optimization_barrier(part)

time: 218 us -> 219 us (level)
  blocking collectives: 11.9 us -> 0 us
  waiting for transfers between devices: 41.9 us -> 52.5 us
  starting transfers between devices: 139 us -> 142 us
    all_to_all x1 -> x0, blocking collectives: 11.9 us -> none  [exchange(): return lax.all_to_all(blocks, axes, split_axis=0, concat_axis=0, tiled=True)]
    all_to_all x8 -> x9, waiting for transfers between devices: 29.7 us -> 38.3 us  [exchange(): return lax.all_to_all(blocks, axes, split_axis=0, concat_axis=0, tiled=True)]
    all_to_all x8 -> x9, starting transfers between devices: 63.3 us -> 68.5 us  [exchange(): return lax.all_to_all(blocks, axes, split_axis=0, concat_axis=0, tiled=True)]
    ppermute x19, starting transfers between devices: 71.4 us -> 68.7 us  [shifted(): return lax.ppermute(value, axis, [(i, (i + by) % n) for i in range(n)])]
  transfers between devices with their start and end apart: 28 -> 29, of which waited for: 14 -> 15; matrix products, arithmetic and copies ran while one was open for 4% -> 3% of each run, Pallas kernels for 0% -> 0%
where the time goes in v16:
time: 219 us; the launch traced here: 218 us
  starting transfers between devices  142 us (65%)
  waiting for transfers between devices  52.5 us (24%)
  local copies, waits for them, and re-layouts  8.21 us (4%)
  matrix products  6.18 us (3%)
  between operations  3.3 us (2%)
  other arithmetic  3.16 us (1%)
  Pallas kernels  2.59 us (1%)
    ppermute x19, starting transfers between devices, shifted(): return lax.ppermute(value, axis, [(i, (i + by) % n) for i in range(n)])  68.7 us
    all_to_all x9, starting transfers between devices, exchange(): return lax.all_to_all(blocks, axes, split_axis=0, concat_axis=0, tiled=True)  68.5 us
    all_to_all x9, waiting for transfers between devices, exchange(): return lax.all_to_all(blocks, axes, split_axis=0, concat_axis=0, tiled=True)  38.3 us
    ppermute x19, waiting for transfers between devices, shifted(): return lax.ppermute(value, axis, [(i, (i + by) % n) for i in range(n)])  14.2 us
    ppermute x1, starting transfers between devices, on_device(): lax.ppermute(features, ('z0', 'c'), [(i, 3 - i) for i in range(4)])  4.39 us
  transfers between devices with their start and end apart: 29, of which 15 were waited for; matrix products, arithmetic and copies ran while one was open for 3% of the time, Pallas kernels for 0%

profile of v16, /device:TPU:1, one launch (start us, length us, event | category | flops | bytes accessed | tf_op | source)
XLA Modules:
  0.0 217.5 jit_solution(10134993820164907960)
XLA Ops:
  0.6 2.6 %heads.1 = bf16[128,3072]{1,0:T(8,128)(2,1)} custom-call(bf16[192,128]{1,0:T(8,128)(2,1)} %bitcast.125, bf16[192,1536]{1,0:T(8,128)(2,1)} %refs_1_.1, bf16[192,128]{1,0:T(8,128)(2,1)} %bitcast.128, bf16[192,1536]{1,0:T(8,128)(2,1)} %refs_3_.1), custom_call_target="tpu_custom_call" | custom-call | flops 150994944 | bytes 2064384 | tf_op jit(solution)/shard_map/heads/pallas_call | solution.py:76
  3.2 7.6 %all-to-all-start = ((bf16[8,16,3072]{2,1,0:T(8,128)(2,1)}), bf16[8,16,3072]{2,1,0:T(8,128)(2,1)S(1)}, u32[]{:S(2)}, u32[]{:S(2)}) async-start(bf16[8,16,3072]{2,1,0:T(8,128)(2,1)} %bitcast.118), calls=%async_computation | async-start | bytes 1572864 | tf_op jit(solution)/shard_map/heads/all_to_all | solution.py:26
  10.9 4.4 %collective-permute-start.2 = (bf16[2,192,128]{2,1,0:T(8,128)(2,1)S(1)}, bf16[2,192,128]{2,1,0:T(8,128)(2,1)S(1)}, u32[]{:S(2)}, u32[]{:S(2)}) collective-permute-start(bf16[2,192,128]{2,1,0:T(8,128)(2,1)S(1)} %pad_maximum_fusion.4), channel_id=1, source_target_pairs={{0,24},{8,16},{16,8},{24,0},{1,25},{9,17},{17,9},{25,1},{2,26},{10... | collective-permute-start | bytes 294920 | tf_op jit(solution)/shard_map/heads/ppermute | solution.py:162
  15.3 3.7 %collective-permute-start.1 = (bf16[2,192,128]{2,1,0:T(8,128)(2,1)S(1)}, bf16[2,192,128]{2,1,0:T(8,128)(2,1)S(1)}, u32[]{:S(2)}, u32[]{:S(2)}) collective-permute-start(bf16[2,192,128]{2,1,0:T(8,128)(2,1)S(1)} %pad_maximum_fusion.4), channel_id=1, source_target_pairs={{0,16},{16,0},{1,17},{17,1},{2,18},{18,2},{3,19},{19,3},{4,20},{20... | collective-permute-start | bytes 294920 | tf_op jit(solution)/shard_map/heads/ppermute | solution.py:40
  19.1 1.9 collective-permute-start
  21.0 0.9 collective-permute-done.1
  22.6 0.7 broadcast_in_dim.12
  23.3 16.6 %all-to-all-start.1 = ((bf16[4,16,1536]{2,1,0:T(8,128)(2,1)}), bf16[4,16,1536]{2,1,0:T(8,128)(2,1)S(1)}, u32[]{:S(2)}, u32[]{:S(2)}) async-start(bf16[4,16,1536]{2,1,0:T(8,128)(2,1)} %broadcast_in_dim.12), calls=%async_computation.1 | async-start | bytes 393216 | tf_op jit(solution)/shard_map/gather_texts/all_to_all | solution.py:26
  40.0 2.6 %collective-permute-start.5 = (bf16[16,1536]{1,0:T(8,128)(2,1)S(1)}, bf16[16,1536]{1,0:T(8,128)(2,1)S(1)}, u32[]{:S(2)}, u32[]{:S(2)}) collective-permute-start(bf16[16,1536]{1,0:T(8,128)(2,1)S(1)} %get-tuple-element.33), channel_id=1, source_target_pairs={{0,16},{16,32},{32,48},{48,0},{1,17},{17,33},{33,49},{49,1},{2,18}... | collective-permute-start | bytes 147464 | tf_op jit(solution)/shard_map/gather_images/ppermute | solution.py:40
  42.7 3.1 %collective-permute-start.4 = (bf16[16,1536]{1,0:T(8,128)(2,1)S(1)}, bf16[16,1536]{1,0:T(8,128)(2,1)S(1)}, u32[]{:S(2)}, u32[]{:S(2)}) collective-permute-start(bf16[16,1536]{1,0:T(8,128)(2,1)S(1)} %get-tuple-element.33), channel_id=1, source_target_pairs={{0,32},{16,48},{32,0},{48,16},{1,33},{17,49},{33,1},{49,17},{2,34}... | collective-permute-start | bytes 147464 | tf_op jit(solution)/shard_map/gather_images/ppermute | solution.py:40
  45.8 3.5 %collective-permute-start.3 = (bf16[16,1536]{1,0:T(8,128)(2,1)S(1)}, bf16[16,1536]{1,0:T(8,128)(2,1)S(1)}, u32[]{:S(2)}, u32[]{:S(2)}) collective-permute-start(bf16[16,1536]{1,0:T(8,128)(2,1)S(1)} %get-tuple-element.33), channel_id=1, source_target_pairs={{0,48},{16,0},{32,16},{48,32},{1,49},{17,1},{33,17},{49,33},{2,50}... | collective-permute-start | bytes 147464 | tf_op jit(solution)/shard_map/gather_images/ppermute | solution.py:40
  51.3 1.5 all-to-all-done.1
  52.7 0.9 broadcast_in_dim.14
  53.7 3.5 %all-to-all-start.2 = ((bf16[4,64,1536]{2,1,0:T(8,128)(2,1)}), bf16[4,64,1536]{2,1,0:T(8,128)(2,1)S(1)}, u32[]{:S(2)}, u32[]{:S(2)}) async-start(bf16[4,64,1536]{2,1,0:T(8,128)(2,1)} %broadcast_in_dim.14), calls=%async_computation.2 | async-start | bytes 1572864 | tf_op jit(solution)/shard_map/gather_texts/all_to_all | solution.py:26
  57.2 1.9 collective-permute-start.8
  59.2 4.0 %collective-permute-start.7 = (bf16[64,1536]{1,0:T(8,128)(2,1)S(1)}, bf16[64,1536]{1,0:T(8,128)(2,1)S(1)}, u32[]{:S(2)}, u32[]{:S(2)}) collective-permute-start(bf16[64,1536]{1,0:T(8,128)(2,1)S(1)} %pad_maximum_fusion.3), channel_id=1, source_target_pairs={{0,4},{2,6},{4,0},{6,2},{1,5},{3,7},{5,1},{7,3},{8,12},{10,14},{12... | collective-permute-start | bytes 589832 | tf_op jit(solution)/shard_map/gather_images/ppermute | solution.py:40
  63.1 2.8 %collective-permute-start.6 = (bf16[64,1536]{1,0:T(8,128)(2,1)S(1)}, bf16[64,1536]{1,0:T(8,128)(2,1)S(1)}, u32[]{:S(2)}, u32[]{:S(2)}) collective-permute-start(bf16[64,1536]{1,0:T(8,128)(2,1)S(1)} %pad_maximum_fusion.3), channel_id=1, source_target_pairs={{0,6},{2,0},{4,2},{6,4},{1,7},{3,1},{5,3},{7,5},{8,14},{10,8},{12,... | collective-permute-start | bytes 589832 | tf_op jit(solution)/shard_map/gather_images/ppermute | solution.py:40
  66.0 10.1 %collective-permute-start.9 = (bf16[256,1536]{1,0:T(8,128)(2,1)S(1)}, bf16[256,1536]{1,0:T(8,128)(2,1)S(1)}, u32[]{:S(2)}, u32[]{:S(2)}) collective-permute-start(bf16[256,1536]{1,0:T(8,128)(2,1)S(1)} %bitcast.115), channel_id=1, source_target_pairs={{0,8},{8,0},{1,9},{9,1},{2,10},{10,2},{3,11},{11,3},{4,12},{12,4},... | collective-permute-start | bytes 2359304 | tf_op jit(solution)/shard_map/gather_texts/ppermute | solution.py:40
  76.2 1.8 collective-permute-done.9
  78.0 0.4 fusion.14
  78.8 2.6 %collective-permute-start.16 = (bf16[256,1536]{1,0:T(8,128)(2,1)S(1)}, bf16[256,1536]{1,0:T(8,128)(2,1)S(1)}, u32[]{:S(2)}, u32[]{:S(2)}) collective-permute-start(bf16[256,1536]{1,0:T(8,128)(2,1)S(1)} %convolution_convert_fusion), channel_id=1, source_target_pairs={{0,8},{8,0},{1,9},{9,1},{2,10},{10,2},{3,11},{11,3},{4,12},{12,4},... | collective-permute-start | bytes 2359304 | tf_op jit(solution)/shard_map/sum_texts/ppermute | solution.py:40
  81.4 0.4 fusion.15
  81.9 0.4 fusion.63
  82.3 0.4 fusion.62
  82.7 0.7 collective-permute-done.16
  83.3 1.3 fusion
  84.6 4.5 %all-to-all-start.3 = ((bf16[4,64,1536]{2,1,0:T(8,128)(2,1)}), bf16[4,64,1536]{2,1,0:T(8,128)(2,1)S(1)}, u32[]{:S(2)}, u32[]{:S(2)}) async-start(bf16[4,64,1536]{2,1,0:T(8,128)(2,1)} %bitcast.18), calls=%async_computation.3 | async-start | bytes 1572864 | tf_op jit(solution)/shard_map/sum_texts/all_to_all | solution.py:26
  89.0 0.8 fusion.60
  89.8 3.0 %collective-permute-start.10 = (bf16[64,1536]{1,0:T(8,128)(2,1)}, bf16[64,1536]{1,0:T(8,128)(2,1)S(1)}, u32[]{:S(2)}, u32[]{:S(2)}) collective-permute-start(bf16[64,1536]{1,0:T(8,128)(2,1)} %get-tuple-element.36), channel_id=1, source_target_pairs={{0,2},{2,4},{4,6},{6,0},{1,3},{3,5},{5,7},{7,1},{8,10},{10,12},{12... | collective-permute-start | bytes 589832 | tf_op jit(solution)/shard_map/sum_images/ppermute | solution.py:40
  92.8 3.5 %collective-permute-start.12 = (bf16[64,1536]{1,0:T(8,128)(2,1)}, bf16[64,1536]{1,0:T(8,128)(2,1)S(1)}, u32[]{:S(2)}, u32[]{:S(2)}) collective-permute-start(bf16[64,1536]{1,0:T(8,128)(2,1)} %get-tuple-element.37), channel_id=1, source_target_pairs={{0,6},{2,0},{4,2},{6,4},{1,7},{3,1},{5,3},{7,5},{8,14},{10,8},{12,... | collective-permute-start | bytes 589832 | tf_op jit(solution)/shard_map/sum_images/ppermute | solution.py:40
  96.3 2.5 %collective-permute-start.11 = (bf16[64,1536]{1,0:T(8,128)(2,1)S(1)}, bf16[64,1536]{1,0:T(8,128)(2,1)S(1)}, u32[]{:S(2)}, u32[]{:S(2)}) collective-permute-start(bf16[64,1536]{1,0:T(8,128)(2,1)S(1)} %get-tuple-element.38), channel_id=1, source_target_pairs={{0,4},{2,6},{4,0},{6,2},{1,5},{3,7},{5,1},{7,3},{8,12},{10,14},{12... | collective-permute-start | bytes 589832 | tf_op jit(solution)/shard_map/sum_images/ppermute | solution.py:40
  98.8 1.9 all-to-all-done.3
  100.7 0.8 reduce_sum.97
  101.6 5.9 %all-to-all-start.4 = ((bf16[4,16,1536]{2,1,0:T(8,128)(2,1)}), bf16[4,16,1536]{2,1,0:T(8,128)(2,1)S(1)}, u32[]{:S(2)}, u32[]{:S(2)}) async-start(bf16[4,16,1536]{2,1,0:T(8,128)(2,1)} %bitcast.19), calls=%async_computation.4 | async-start | bytes 393216 | tf_op jit(solution)/shard_map/sum_texts/all_to_all | solution.py:26
  107.6 1.9 collective-permute-start.13
  109.5 5.2 %collective-permute-start.15 = (bf16[16,1536]{1,0:T(8,128)(2,1)S(1)}, bf16[16,1536]{1,0:T(8,128)(2,1)S(1)}, u32[]{:S(2)}, u32[]{:S(2)}) collective-permute-start(bf16[16,1536]{1,0:T(8,128)(2,1)S(1)} %get-tuple-element.60), channel_id=1, source_target_pairs={{0,48},{16,0},{32,16},{48,32},{1,49},{17,1},{33,17},{49,33},{2,50}... | collective-permute-start | bytes 147464 | tf_op jit(solution)/shard_map/sum_images/ppermute | solution.py:40
  114.7 1.9 collective-permute-start.14
  116.6 4.4 %all-to-all-done.4 = bf16[4,16,1536]{2,1,0:T(8,128)(2,1)S(1)} async-done(((bf16[4,16,1536]{2,1,0:T(8,128)(2,1)}), bf16[4,16,1536]{2,1,0:T(8,128)(2,1)S(1)}, u32[]{:S(2)}, u32[]{:S(2)}) %all-to-all-start.4) | async-done | bytes 196640 | tf_op jit(solution)/shard_map/sum_texts/all_to_all | solution.py:26
  121.0 0.6 collective-permute-done.14
  122.2 1.0 broadcast_in_dim.15
  123.2 10.0 %all-to-all-start.5 = ((bf16[32,2,16,384]{3,2,1,0:T(8,128)(2,1)}), bf16[32,2,16,384]{3,2,1,0:T(8,128)(2,1)S(1)}, u32[]{:S(2)}, u32[]{:S(2)}) async-start(bf16[32,2,16,384]{3,2,1,0:T(8,128)(2,1)} %bitcast.21), calls=%async_computation.5 | async-start | bytes 1572864 | tf_op jit(solution)/shard_map/head_grads/all_to_all | solution.py:26
  133.3 14.0 %all-to-all-done.5 = bf16[32,2,16,384]{3,2,1,0:T(8,128)(2,1)S(1)} async-done(((bf16[32,2,16,384]{3,2,1,0:T(8,128)(2,1)}), bf16[32,2,16,384]{3,2,1,0:T(8,128)(2,1)S(1)}, u32[]{:S(2)}, u32[]{:S(2)}) %all-to-all-start.5) | async-done | bytes 786464 | tf_op jit(solution)/shard_map/head_grads/all_to_all | solution.py:26
  148.0 0.8 pad_maximum_fusion
  148.7 3.5 %all-to-all-start.6 = ((bf16[4,96,384]{2,1,0:T(8,128)(2,1)}), bf16[4,96,384]{2,1,0:T(8,128)(2,1)S(1)}, u32[]{:S(2)}, u32[]{:S(2)}) async-start(bf16[4,96,384]{2,1,0:T(8,128)(2,1)} %bitcast.30), calls=%async_computation.6 | async-start | bytes 589824 | tf_op jit(solution)/shard_map/weight_grads/all_to_all | solution.py:26
  152.2 1.2 convolution_bitcast_fusion
  153.4 1.2 convolution_bitcast_fusion.1
  154.7 3.1 %collective-permute-start.17 = (bf16[2,2,128,192]{2,3,1,0:T(8,128)(2,1)S(1)}, bf16[2,2,128,192]{2,3,1,0:T(8,128)(2,1)S(1)}, u32[]{:S(2)}, u32[]{:S(2)}) collective-permute-start(bf16[2,2,128,192]{2,3,1,0:T(8,128)(2,1)S(1)} %fusion.26), channel_id=1, source_target_pairs={{0,8},{8,0},{1,9},{9,1},{2,10},{10,2},{3,11},{11,3},{4,12},{12,4},... | collective-permute-start | bytes 589832 | tf_op jit(solution)/shard_map/input_grads/ppermute | solution.py:40
  157.8 1.0 collective-permute-done.17
  158.9 1.5 all-to-all-done.6
  160.5 0.7 broadcast_in_dim.16
  161.2 9.2 %all-to-all-start.7 = ((bf16[4,96,384]{2,1,0:T(8,128)(2,1)}), bf16[4,96,384]{2,1,0:T(8,128)(2,1)S(1)}, u32[]{:S(2)}, u32[]{:S(2)}) async-start(bf16[4,96,384]{2,1,0:T(8,128)(2,1)} %broadcast_in_dim.16), calls=%async_computation.7 | async-start | bytes 589824 | tf_op jit(solution)/shard_map/weight_grads/all_to_all | solution.py:26
  170.4 2.2 %collective-permute-start.18 = (bf16[2,128,192]{1,2,0:T(8,128)(2,1)S(1)}, bf16[2,128,192]{1,2,0:T(8,128)(2,1)S(1)}, u32[]{:S(2)}, u32[]{:S(2)}) collective-permute-start(bf16[2,128,192]{1,2,0:T(8,128)(2,1)S(1)} %fusion.47), channel_id=1, source_target_pairs={{0,16},{16,0},{1,17},{17,1},{2,18},{18,2},{3,19},{19,3},{4,20},{20... | collective-permute-start | bytes 294920 | tf_op jit(solution)/shard_map/weight_grads/ppermute | solution.py:40
  172.6 7.5 %collective-permute-done.18 = bf16[2,128,192]{1,2,0:T(8,128)(2,1)S(1)} collective-permute-done((bf16[2,128,192]{1,2,0:T(8,128)(2,1)S(1)}, bf16[2,128,192]{1,2,0:T(8,128)(2,1)S(1)}, u32[]{:S(2)}, u32[]{:S(2)}) %collective-permute-start.18) | collective-permute-done | bytes 98336 | tf_op jit(solution)/shard_map/weight_grads/ppermute | solution.py:40
  180.1 4.8 %all-to-all-done.7 = bf16[4,96,384]{2,1,0:T(8,128)(2,1)S(1)} async-done(((bf16[4,96,384]{2,1,0:T(8,128)(2,1)}), bf16[4,96,384]{2,1,0:T(8,128)(2,1)S(1)}, u32[]{:S(2)}, u32[]{:S(2)}) %all-to-all-start.7) | async-done | bytes 294944 | tf_op jit(solution)/shard_map/weight_grads/all_to_all | solution.py:26
  185.0 0.9 broadcast_in_dim.17
  185.8 7.9 %all-to-all-start.8 = ((bf16[8,96,384]{2,1,0:T(8,128)(2,1)}), bf16[8,96,384]{2,1,0:T(8,128)(2,1)S(1)}, u32[]{:S(2)}, u32[]{:S(2)}) async-start(bf16[8,96,384]{2,1,0:T(8,128)(2,1)} %broadcast_in_dim.17), calls=%async_computation.8 | async-start | bytes 1179648 | tf_op jit(solution)/shard_map/weight_grads/all_to_all | solution.py:26
  193.7 0.7 slice_bitcast_fusion.4
  194.4 10.2 %all-to-all-done.8 = bf16[8,96,384]{2,1,0:T(8,128)(2,1)S(1)} async-done(((bf16[8,96,384]{2,1,0:T(8,128)(2,1)}), bf16[8,96,384]{2,1,0:T(8,128)(2,1)S(1)}, u32[]{:S(2)}, u32[]{:S(2)}) %all-to-all-start.8) | async-done | bytes 589856 | tf_op jit(solution)/shard_map/weight_grads/all_to_all | solution.py:26
  204.6 0.5 copy.18
  205.0 0.4 reshape.235
  205.4 9.0 %collective-permute-start.19 = (bf16[2,192,768]{2,1,0:T(8,128)(2,1)S(1)}, bf16[2,192,768]{2,1,0:T(8,128)(2,1)S(1)}, u32[]{:S(2)}, u32[]{:S(2)}) collective-permute-start(bf16[2,192,768]{2,1,0:T(8,128)(2,1)S(1)} %reshape.235), channel_id=1, source_target_pairs={{0,8},{8,0},{1,9},{9,1},{2,10},{10,2},{3,11},{11,3},{4,12},{12,4},... | collective-permute-start | bytes 1769480 | tf_op jit(solution)/shard_map/weight_grads/ppermute | solution.py:40
  214.6 1.4 collective-permute-done.19
  216.2 1.0 copy-done
  217.2 0.4 copy-done.1
  (75 shorter events, 3.2 us)
Async XLA Ops:
  3.2 7.7 %copy-start.2 = (bf16[128,192]{0,1:T(8,128)(2,1)S(1)}, bf16[128,192]{0,1:T(8,128)(2,1)}, u32[]{:S(2)}) copy-start(bf16[128,192]{0,1:T(8,128)(2,1)} %param.7) | copy-start | bytes 147460
  3.2 7.6 %copy-start.3 = (bf16[128,192]{0,1:T(8,128)(2,1)S(1)}, bf16[128,192]{0,1:T(8,128)(2,1)}, u32[]{:S(2)}) copy-start(bf16[128,192]{0,1:T(8,128)(2,1)} %param.8) | copy-start | bytes 147460
  3.2 19.0 %all-to-all-start = ((bf16[8,16,3072]{2,1,0:T(8,128)(2,1)}), bf16[8,16,3072]{2,1,0:T(8,128)(2,1)S(1)}, u32[]{:S(2)}, u32[]{:S(2)}) async-start(bf16[8,16,3072]{2,1,0:T(8,128)(2,1)} %bitcast.118), calls=%async_computation | async-start | bytes 1572864 | tf_op jit(solution)/shard_map/heads/all_to_all | solution.py:26
  10.9 10.1 %collective-permute-start.2 = (bf16[2,192,128]{2,1,0:T(8,128)(2,1)S(1)}, bf16[2,192,128]{2,1,0:T(8,128)(2,1)S(1)}, u32[]{:S(2)}, u32[]{:S(2)}) collective-permute-start(bf16[2,192,128]{2,1,0:T(8,128)(2,1)S(1)} %pad_maximum_fusion.4), channel_id=1, source_target_pairs={{0,24},{8,16},{16,8},{24,0},{1,25},{9,17},{17,9},{25,1},{2,26},{10... | collective-permute-start | bytes 294920 | tf_op jit(solution)/shard_map/heads/ppermute | solution.py:162
  15.3 6.6 %collective-permute-start.1 = (bf16[2,192,128]{2,1,0:T(8,128)(2,1)S(1)}, bf16[2,192,128]{2,1,0:T(8,128)(2,1)S(1)}, u32[]{:S(2)}, u32[]{:S(2)}) collective-permute-start(bf16[2,192,128]{2,1,0:T(8,128)(2,1)S(1)} %pad_maximum_fusion.4), channel_id=1, source_target_pairs={{0,16},{16,0},{1,17},{17,1},{2,18},{18,2},{3,19},{19,3},{4,20},{20... | collective-permute-start | bytes 294920 | tf_op jit(solution)/shard_map/heads/ppermute | solution.py:40
  19.1 3.2 %collective-permute-start = (bf16[2,192,128]{2,1,0:T(8,128)(2,1)S(1)}, bf16[2,192,128]{2,1,0:T(8,128)(2,1)S(1)}, u32[]{:S(2)}, u32[]{:S(2)}) collective-permute-start(bf16[2,192,128]{2,1,0:T(8,128)(2,1)S(1)} %pad_maximum_fusion.4), channel_id=1, source_target_pairs={{0,8},{8,0},{1,9},{9,1},{2,10},{10,2},{3,11},{11,3},{4,12},{12,4},... | collective-permute-start | bytes 294920 | tf_op jit(solution)/shard_map/heads/ppermute | solution.py:40
  21.0 2.3 %copy-start.4 = (bf16[2,192,128]{2,1,0:T(8,128)(2,1)}, bf16[2,192,128]{2,1,0:T(8,128)(2,1)S(1)}, u32[]{:S(2)}) copy-start(bf16[2,192,128]{2,1,0:T(8,128)(2,1)S(1)} %collective-permute-done.2) | copy-start | bytes 294916
  21.9 31.8 %copy-start.6 = (bf16[2,192,128]{2,1,0:T(8,128)(2,1)}, bf16[2,192,128]{2,1,0:T(8,128)(2,1)S(1)}, u32[]{:S(2)}) copy-start(bf16[2,192,128]{2,1,0:T(8,128)(2,1)S(1)} %collective-permute-done.1) | copy-start | bytes 294916
  22.2 31.4 %copy-start.8 = (bf16[2,192,128]{2,1,0:T(8,128)(2,1)}, bf16[2,192,128]{2,1,0:T(8,128)(2,1)S(1)}, u32[]{:S(2)}) copy-start(bf16[2,192,128]{2,1,0:T(8,128)(2,1)S(1)} %collective-permute-done) | copy-start | bytes 294916
  23.3 29.4 %all-to-all-start.1 = ((bf16[4,16,1536]{2,1,0:T(8,128)(2,1)}), bf16[4,16,1536]{2,1,0:T(8,128)(2,1)S(1)}, u32[]{:S(2)}, u32[]{:S(2)}) async-start(bf16[4,16,1536]{2,1,0:T(8,128)(2,1)} %broadcast_in_dim.12), calls=%async_computation.1 | async-start | bytes 393216 | tf_op jit(solution)/shard_map/gather_texts/all_to_all | solution.py:26
  40.0 17.2 %collective-permute-start.5 = (bf16[16,1536]{1,0:T(8,128)(2,1)S(1)}, bf16[16,1536]{1,0:T(8,128)(2,1)S(1)}, u32[]{:S(2)}, u32[]{:S(2)}) collective-permute-start(bf16[16,1536]{1,0:T(8,128)(2,1)S(1)} %get-tuple-element.33), channel_id=1, source_target_pairs={{0,16},{16,32},{32,48},{48,0},{1,17},{17,33},{33,49},{49,1},{2,18}... | collective-permute-start | bytes 147464 | tf_op jit(solution)/shard_map/gather_images/ppermute | solution.py:40
  42.7 14.5 %collective-permute-start.4 = (bf16[16,1536]{1,0:T(8,128)(2,1)S(1)}, bf16[16,1536]{1,0:T(8,128)(2,1)S(1)}, u32[]{:S(2)}, u32[]{:S(2)}) collective-permute-start(bf16[16,1536]{1,0:T(8,128)(2,1)S(1)} %get-tuple-element.33), channel_id=1, source_target_pairs={{0,32},{16,48},{32,0},{48,16},{1,33},{17,49},{33,1},{49,17},{2,34}... | collective-permute-start | bytes 147464 | tf_op jit(solution)/shard_map/gather_images/ppermute | solution.py:40
  45.8 11.4 %collective-permute-start.3 = (bf16[16,1536]{1,0:T(8,128)(2,1)S(1)}, bf16[16,1536]{1,0:T(8,128)(2,1)S(1)}, u32[]{:S(2)}, u32[]{:S(2)}) collective-permute-start(bf16[16,1536]{1,0:T(8,128)(2,1)S(1)} %get-tuple-element.33), channel_id=1, source_target_pairs={{0,48},{16,0},{32,16},{48,32},{1,49},{17,1},{33,17},{49,33},{2,50}... | collective-permute-start | bytes 147464 | tf_op jit(solution)/shard_map/gather_images/ppermute | solution.py:40
  53.7 12.3 %all-to-all-start.2 = ((bf16[4,64,1536]{2,1,0:T(8,128)(2,1)}), bf16[4,64,1536]{2,1,0:T(8,128)(2,1)S(1)}, u32[]{:S(2)}, u32[]{:S(2)}) async-start(bf16[4,64,1536]{2,1,0:T(8,128)(2,1)} %broadcast_in_dim.14), calls=%async_computation.2 | async-start | bytes 1572864 | tf_op jit(solution)/shard_map/gather_texts/all_to_all | solution.py:26
  57.2 18.9 %collective-permute-start.8 = (bf16[64,1536]{1,0:T(8,128)(2,1)S(1)}, bf16[64,1536]{1,0:T(8,128)(2,1)S(1)}, u32[]{:S(2)}, u32[]{:S(2)}) collective-permute-start(bf16[64,1536]{1,0:T(8,128)(2,1)S(1)} %pad_maximum_fusion.3), channel_id=1, source_target_pairs={{0,2},{2,4},{4,6},{6,0},{1,3},{3,5},{5,7},{7,1},{8,10},{10,12},{12... | collective-permute-start | bytes 589832 | tf_op jit(solution)/shard_map/gather_images/ppermute | solution.py:40
  59.2 17.0 %collective-permute-start.7 = (bf16[64,1536]{1,0:T(8,128)(2,1)S(1)}, bf16[64,1536]{1,0:T(8,128)(2,1)S(1)}, u32[]{:S(2)}, u32[]{:S(2)}) collective-permute-start(bf16[64,1536]{1,0:T(8,128)(2,1)S(1)} %pad_maximum_fusion.3), channel_id=1, source_target_pairs={{0,4},{2,6},{4,0},{6,2},{1,5},{3,7},{5,1},{7,3},{8,12},{10,14},{12... | collective-permute-start | bytes 589832 | tf_op jit(solution)/shard_map/gather_images/ppermute | solution.py:40
  63.1 13.0 %collective-permute-start.6 = (bf16[64,1536]{1,0:T(8,128)(2,1)S(1)}, bf16[64,1536]{1,0:T(8,128)(2,1)S(1)}, u32[]{:S(2)}, u32[]{:S(2)}) collective-permute-start(bf16[64,1536]{1,0:T(8,128)(2,1)S(1)} %pad_maximum_fusion.3), channel_id=1, source_target_pairs={{0,6},{2,0},{4,2},{6,4},{1,7},{3,1},{5,3},{7,5},{8,14},{10,8},{12,... | collective-permute-start | bytes 589832 | tf_op jit(solution)/shard_map/gather_images/ppermute | solution.py:40
  66.0 12.0 %collective-permute-start.9 = (bf16[256,1536]{1,0:T(8,128)(2,1)S(1)}, bf16[256,1536]{1,0:T(8,128)(2,1)S(1)}, u32[]{:S(2)}, u32[]{:S(2)}) collective-permute-start(bf16[256,1536]{1,0:T(8,128)(2,1)S(1)} %bitcast.115), channel_id=1, source_target_pairs={{0,8},{8,0},{1,9},{9,1},{2,10},{10,2},{3,11},{11,3},{4,12},{12,4},... | collective-permute-start | bytes 2359304 | tf_op jit(solution)/shard_map/gather_texts/ppermute | solution.py:40
  78.8 4.5 %collective-permute-start.16 = (bf16[256,1536]{1,0:T(8,128)(2,1)S(1)}, bf16[256,1536]{1,0:T(8,128)(2,1)S(1)}, u32[]{:S(2)}, u32[]{:S(2)}) collective-permute-start(bf16[256,1536]{1,0:T(8,128)(2,1)S(1)} %convolution_convert_fusion), channel_id=1, source_target_pairs={{0,8},{8,0},{1,9},{9,1},{2,10},{10,2},{3,11},{11,3},{4,12},{12,4},... | collective-permute-start | bytes 2359304 | tf_op jit(solution)/shard_map/sum_texts/ppermute | solution.py:40
  84.6 16.2 %all-to-all-start.3 = ((bf16[4,64,1536]{2,1,0:T(8,128)(2,1)}), bf16[4,64,1536]{2,1,0:T(8,128)(2,1)S(1)}, u32[]{:S(2)}, u32[]{:S(2)}) async-start(bf16[4,64,1536]{2,1,0:T(8,128)(2,1)} %bitcast.18), calls=%async_computation.3 | async-start | bytes 1572864 | tf_op jit(solution)/shard_map/sum_texts/all_to_all | solution.py:26
  89.8 17.7 %collective-permute-start.10 = (bf16[64,1536]{1,0:T(8,128)(2,1)}, bf16[64,1536]{1,0:T(8,128)(2,1)S(1)}, u32[]{:S(2)}, u32[]{:S(2)}) collective-permute-start(bf16[64,1536]{1,0:T(8,128)(2,1)} %get-tuple-element.36), channel_id=1, source_target_pairs={{0,2},{2,4},{4,6},{6,0},{1,3},{3,5},{5,7},{7,1},{8,10},{10,12},{12... | collective-permute-start | bytes 589832 | tf_op jit(solution)/shard_map/sum_images/ppermute | solution.py:40
  92.8 14.6 %collective-permute-start.12 = (bf16[64,1536]{1,0:T(8,128)(2,1)}, bf16[64,1536]{1,0:T(8,128)(2,1)S(1)}, u32[]{:S(2)}, u32[]{:S(2)}) collective-permute-start(bf16[64,1536]{1,0:T(8,128)(2,1)} %get-tuple-element.37), channel_id=1, source_target_pairs={{0,6},{2,0},{4,2},{6,4},{1,7},{3,1},{5,3},{7,5},{8,14},{10,8},{12,... | collective-permute-start | bytes 589832 | tf_op jit(solution)/shard_map/sum_images/ppermute | solution.py:40
  96.3 11.2 %collective-permute-start.11 = (bf16[64,1536]{1,0:T(8,128)(2,1)S(1)}, bf16[64,1536]{1,0:T(8,128)(2,1)S(1)}, u32[]{:S(2)}, u32[]{:S(2)}) collective-permute-start(bf16[64,1536]{1,0:T(8,128)(2,1)S(1)} %get-tuple-element.38), channel_id=1, source_target_pairs={{0,4},{2,6},{4,0},{6,2},{1,5},{3,7},{5,1},{7,3},{8,12},{10,14},{12... | collective-permute-start | bytes 589832 | tf_op jit(solution)/shard_map/sum_images/ppermute | solution.py:40
  101.6 19.4 %all-to-all-start.4 = ((bf16[4,16,1536]{2,1,0:T(8,128)(2,1)}), bf16[4,16,1536]{2,1,0:T(8,128)(2,1)S(1)}, u32[]{:S(2)}, u32[]{:S(2)}) async-start(bf16[4,16,1536]{2,1,0:T(8,128)(2,1)} %bitcast.19), calls=%async_computation.4 | async-start | bytes 393216 | tf_op jit(solution)/shard_map/sum_texts/all_to_all | solution.py:26
  107.6 13.4 %collective-permute-start.13 = (bf16[16,1536]{1,0:T(8,128)(2,1)S(1)}, bf16[16,1536]{1,0:T(8,128)(2,1)S(1)}, u32[]{:S(2)}, u32[]{:S(2)}) collective-permute-start(bf16[16,1536]{1,0:T(8,128)(2,1)S(1)} %get-tuple-element.59), channel_id=1, source_target_pairs={{0,16},{16,32},{32,48},{48,0},{1,17},{17,33},{33,49},{49,1},{2,18}... | collective-permute-start | bytes 147464 | tf_op jit(solution)/shard_map/sum_images/ppermute | solution.py:40
  109.5 11.5 %collective-permute-start.15 = (bf16[16,1536]{1,0:T(8,128)(2,1)S(1)}, bf16[16,1536]{1,0:T(8,128)(2,1)S(1)}, u32[]{:S(2)}, u32[]{:S(2)}) collective-permute-start(bf16[16,1536]{1,0:T(8,128)(2,1)S(1)} %get-tuple-element.60), channel_id=1, source_target_pairs={{0,48},{16,0},{32,16},{48,32},{1,49},{17,1},{33,17},{49,33},{2,50}... | collective-permute-start | bytes 147464 | tf_op jit(solution)/shard_map/sum_images/ppermute | solution.py:40
  114.7 6.9 %collective-permute-start.14 = (bf16[16,1536]{1,0:T(8,128)(2,1)S(1)}, bf16[16,1536]{1,0:T(8,128)(2,1)S(1)}, u32[]{:S(2)}, u32[]{:S(2)}) collective-permute-start(bf16[16,1536]{1,0:T(8,128)(2,1)S(1)} %get-tuple-element.61), channel_id=1, source_target_pairs={{0,32},{16,48},{32,0},{48,16},{1,33},{17,49},{33,1},{49,17},{2,34}... | collective-permute-start | bytes 147464 | tf_op jit(solution)/shard_map/sum_images/ppermute | solution.py:40
  122.2 11.0 %copy-start.5 = (bf16[2,192,128]{2,1,0:T(8,128)(2,1)S(1)}, bf16[2,192,128]{2,1,0:T(8,128)(2,1)}, u32[]{:S(2)}) copy-start(bf16[2,192,128]{2,1,0:T(8,128)(2,1)} %copy-done.4) | copy-start | bytes 294916
  122.2 11.0 %copy-start.7 = (bf16[2,192,128]{2,1,0:T(8,128)(2,1)S(1)}, bf16[2,192,128]{2,1,0:T(8,128)(2,1)}, u32[]{:S(2)}) copy-start(bf16[2,192,128]{2,1,0:T(8,128)(2,1)} %copy-done.6) | copy-start | bytes 294916
  122.2 11.0 %copy-start.9 = (bf16[2,192,128]{2,1,0:T(8,128)(2,1)S(1)}, bf16[2,192,128]{2,1,0:T(8,128)(2,1)}, u32[]{:S(2)}) copy-start(bf16[2,192,128]{2,1,0:T(8,128)(2,1)} %copy-done.8) | copy-start | bytes 294916
  123.2 24.2 %all-to-all-start.5 = ((bf16[32,2,16,384]{3,2,1,0:T(8,128)(2,1)}), bf16[32,2,16,384]{3,2,1,0:T(8,128)(2,1)S(1)}, u32[]{:S(2)}, u32[]{:S(2)}) async-start(bf16[32,2,16,384]{3,2,1,0:T(8,128)(2,1)} %bitcast.21), calls=%async_computation.5 | async-start | bytes 1572864 | tf_op jit(solution)/shard_map/head_grads/all_to_all | solution.py:26
  148.7 11.7 %all-to-all-start.6 = ((bf16[4,96,384]{2,1,0:T(8,128)(2,1)}), bf16[4,96,384]{2,1,0:T(8,128)(2,1)S(1)}, u32[]{:S(2)}, u32[]{:S(2)}) async-start(bf16[4,96,384]{2,1,0:T(8,128)(2,1)} %bitcast.30), calls=%async_computation.6 | async-start | bytes 589824 | tf_op jit(solution)/shard_map/weight_grads/all_to_all | solution.py:26
  154.7 4.2 %collective-permute-start.17 = (bf16[2,2,128,192]{2,3,1,0:T(8,128)(2,1)S(1)}, bf16[2,2,128,192]{2,3,1,0:T(8,128)(2,1)S(1)}, u32[]{:S(2)}, u32[]{:S(2)}) collective-permute-start(bf16[2,2,128,192]{2,3,1,0:T(8,128)(2,1)S(1)} %fusion.26), channel_id=1, source_target_pairs={{0,8},{8,0},{1,9},{9,1},{2,10},{10,2},{3,11},{11,3},{4,12},{12,4},... | collective-permute-start | bytes 589832 | tf_op jit(solution)/shard_map/input_grads/ppermute | solution.py:40
  161.2 23.7 %all-to-all-start.7 = ((bf16[4,96,384]{2,1,0:T(8,128)(2,1)}), bf16[4,96,384]{2,1,0:T(8,128)(2,1)S(1)}, u32[]{:S(2)}, u32[]{:S(2)}) async-start(bf16[4,96,384]{2,1,0:T(8,128)(2,1)} %broadcast_in_dim.16), calls=%async_computation.7 | async-start | bytes 589824 | tf_op jit(solution)/shard_map/weight_grads/all_to_all | solution.py:26
  170.4 9.8 %collective-permute-start.18 = (bf16[2,128,192]{1,2,0:T(8,128)(2,1)S(1)}, bf16[2,128,192]{1,2,0:T(8,128)(2,1)S(1)}, u32[]{:S(2)}, u32[]{:S(2)}) collective-permute-start(bf16[2,128,192]{1,2,0:T(8,128)(2,1)S(1)} %fusion.47), channel_id=1, source_target_pairs={{0,16},{16,0},{1,17},{17,1},{2,18},{18,2},{3,19},{19,3},{4,20},{20... | collective-permute-start | bytes 294920 | tf_op jit(solution)/shard_map/weight_grads/ppermute | solution.py:40
  185.8 18.8 %all-to-all-start.8 = ((bf16[8,96,384]{2,1,0:T(8,128)(2,1)}), bf16[8,96,384]{2,1,0:T(8,128)(2,1)S(1)}, u32[]{:S(2)}, u32[]{:S(2)}) async-start(bf16[8,96,384]{2,1,0:T(8,128)(2,1)} %broadcast_in_dim.17), calls=%async_computation.8 | async-start | bytes 1179648 | tf_op jit(solution)/shard_map/weight_grads/all_to_all | solution.py:26
  205.4 10.6 %collective-permute-start.19 = (bf16[2,192,768]{2,1,0:T(8,128)(2,1)S(1)}, bf16[2,192,768]{2,1,0:T(8,128)(2,1)S(1)}, u32[]{:S(2)}, u32[]{:S(2)}) collective-permute-start(bf16[2,192,768]{2,1,0:T(8,128)(2,1)S(1)} %reshape.235), channel_id=1, source_target_pairs={{0,8},{8,0},{1,9},{9,1},{2,10},{10,2},{3,11},{11,3},{4,12},{12,4},... | collective-permute-start | bytes 1769480 | tf_op jit(solution)/shard_map/weight_grads/ppermute | solution.py:40
  216.1 1.0 copy-start
  216.1 1.4 copy-start.1

commit v17 on v15

--- a/solution.py
+++ b/solution.py
@@ -179,12 +179,16 @@
             for head in range(2)
         )
 
-    with jax.named_scope("gather_texts"):
-        texts = merge_rows(gather(text_unit.astype(BF16), "zh"))
+    with jax.named_scope("gather"):
+        own = image_unit.astype(BF16)
+        texts, ahead = together(
+            (merge_rows(gather(text_unit.astype(BF16), ZL)), shifted(own, "zh", 3))
+        )
         texts = merge_rows(gather(texts, ("xh", "xl")))
+        images = [own, ahead, shifted(own, "zh", 2), shifted(own, "zh", 1)]
+        texts, images = together((texts, jnp.concatenate(images, axis=0)))
+        images = merge_rows(gather(images, "y"))
         other_texts = shifted(texts, "c", 1)
-    with jax.named_scope("gather_images"):
-        images = ring_gather(ring_gather(image_unit.astype(BF16), ZL), "y")
 
     def coefficients(block, positive):
         scores = (
@@ -193,10 +197,11 @@
         return (factor * (jax.nn.sigmoid(scores) - positive)).astype(BF16)
 
     with jax.named_scope("pairs"):
-        text_base = ((at["xh"] * 2 + at["xl"]) * 4 + at["zh"]) * share
+        text_base = ((at["xh"] * 2 + at["xl"]) * 4 + at["zm"] * 2 + at["z0"]) * share
+        image_base = at["y"] * 4 * share
         text_at = jnp.arange(texts.shape[0], dtype=jnp.int32)[:, None] - text_base
-        image_at = jnp.arange(images.shape[0], dtype=jnp.int32)[None, :]
-        positive = (text_at == image_at) & (image_at < share)
+        image_at = jnp.arange(images.shape[0], dtype=jnp.int32)[None, :] - image_base
+        positive = (text_at == image_at) & (text_at >= 0) & (text_at < share)
         coeff = coefficients(texts, positive.astype(F32))
         other_coeff = coefficients(other_texts, 0.0)
         other_part = jnp.dot(other_coeff, images, preferred_element_type=F32)
@@ -206,12 +211,19 @@
             "ti,te->ie", other_coeff, other_texts, preferred_element_type=F32
         )
 
-    with jax.named_scope("sum_texts"):
+    with jax.named_scope("sum"):
         text_part = text_part + shifted(other_part.astype(BF16), "c", 1).astype(F32)
-        text_part = scatter_sum(split_rows(text_part, count(("xh", "xl"))), ("xh", "xl"))
-        text_grads = scatter_sum(split_rows(text_part, count("zh")), "zh")
-    with jax.named_scope("sum_images"):
-        image_grads = ring_scatter_sum(ring_scatter_sum(image_part, "y"), ZL)
+        text_part = split_rows(text_part, count(("xh", "xl"))).astype(BF16)
+        image_part = scatter_sum(split_rows(image_part, count("y")), "y")
+        text_part, image_part = together((text_part, image_part))
+        blocks = split_rows(image_part, 4)
+        text_part, first = together(
+            (scatter_sum(text_part, ("xh", "xl")), shifted(blocks[1].astype(BF16), "zh", 1))
+        )
+        text_grads = scatter_sum(split_rows(text_part, count(ZL)), ZL)
+        image_grads = blocks[0] + first.astype(F32)
+        for k in (2, 3):
+            image_grads = image_grads + shifted(blocks[k].astype(BF16), "zh", k).astype(F32)
 
     with jax.named_scope("head_grads"):
         grads = jnp.stack(

time: 218 us -> 240 us (1.10)
  blocking collectives: 11.9 us -> 27.9 us
  waiting for transfers between devices: 41.9 us -> 47.7 us
    all_to_all x1 -> x2, blocking collectives: 11.9 us -> 27.9 us  [exchange(): return lax.all_to_all(blocks, axes, split_axis=0, concat_axis=0, tiled=True)]
    ppermute x19 -> x13, waiting for transfers between devices: 12.2 us -> 20.7 us  [shifted(): return lax.ppermute(value, axis, [(i, (i + by) % n) for i in range(n)])]
    ppermute x19 -> x13, starting transfers between devices: 71.4 us -> 79.8 us  [shifted(): return lax.ppermute(value, axis, [(i, (i + by) % n) for i in range(n)])]
    all_to_all x8 -> x9, starting transfers between devices: 63.3 us -> 56.5 us  [exchange(): return lax.all_to_all(blocks, axes, split_axis=0, concat_axis=0, tiled=True)]
    all_to_all x8 -> x9, waiting for transfers between devices: 29.7 us -> 26.9 us  [exchange(): return lax.all_to_all(blocks, axes, split_axis=0, concat_axis=0, tiled=True)]
  transfers between devices with their start and end apart: 28 -> 23, of which waited for: 14 -> 13; matrix products, arithmetic and copies ran while one was open for 4% -> 2% of each run, Pallas kernels for 0% -> 0%
where the time goes in v17:
time: 240 us; the launch traced here: 239 us
  starting transfers between devices  141 us (59%)
  waiting for transfers between devices  47.7 us (20%)
  blocking collectives  27.9 us (12%)
  local copies, waits for them, and re-layouts  8.28 us (3%)
  matrix products  6.19 us (3%)
  between operations  3.12 us (1%)
  Pallas kernels  2.59 us (1%)
    ppermute x13, starting transfers between devices, shifted(): return lax.ppermute(value, axis, [(i, (i + by) % n) for i in range(n)])  79.8 us
    all_to_all x9, starting transfers between devices, exchange(): return lax.all_to_all(blocks, axes, split_axis=0, concat_axis=0, tiled=True)  56.5 us
    all_to_all x2, blocking collectives, exchange(): return lax.all_to_all(blocks, axes, split_axis=0, concat_axis=0, tiled=True)  27.9 us
    all_to_all x9, waiting for transfers between devices, exchange(): return lax.all_to_all(blocks, axes, split_axis=0, concat_axis=0, tiled=True)  26.9 us
    ppermute x13, waiting for transfers between devices, shifted(): return lax.ppermute(value, axis, [(i, (i + by) % n) for i in range(n)])  20.7 us
  transfers between devices with their start and end apart: 23, of which 13 were waited for; matrix products, arithmetic and copies ran while one was open for 2% of the time, Pallas kernels for 0%

profile of v17, /device:TPU:1, one launch (start us, length us, event | category | flops | bytes accessed | tf_op | source)
XLA Modules:
  0.0 238.8 jit_solution(1546690246742594151)
XLA Ops:
  0.6 2.6 %heads.1 = bf16[128,3072]{1,0:T(8,128)(2,1)} custom-call(bf16[192,128]{1,0:T(8,128)(2,1)} %bitcast.133, bf16[192,1536]{1,0:T(8,128)(2,1)} %refs_1_.1, bf16[192,128]{1,0:T(8,128)(2,1)} %bitcast.136, bf16[192,1536]{1,0:T(8,128)(2,1)} %refs_3_.1), custom_call_target="tpu_custom_call" | custom-call | flops 150994944 | bytes 2064384 | tf_op jit(solution)/shard_map/heads/pallas_call | solution.py:76
  3.2 7.6 %all-to-all-start = ((bf16[8,16,3072]{2,1,0:T(8,128)(2,1)}), bf16[8,16,3072]{2,1,0:T(8,128)(2,1)S(1)}, u32[]{:S(2)}, u32[]{:S(2)}) async-start(bf16[8,16,3072]{2,1,0:T(8,128)(2,1)} %bitcast.124), calls=%async_computation | async-start | bytes 1572864 | tf_op jit(solution)/shard_map/heads/all_to_all | solution.py:26
  10.9 4.4 %collective-permute-start.2 = (bf16[2,192,128]{2,1,0:T(8,128)(2,1)S(1)}, bf16[2,192,128]{2,1,0:T(8,128)(2,1)S(1)}, u32[]{:S(2)}, u32[]{:S(2)}) collective-permute-start(bf16[2,192,128]{2,1,0:T(8,128)(2,1)S(1)} %pad_maximum_fusion.4), channel_id=1, source_target_pairs={{0,24},{8,16},{16,8},{24,0},{1,25},{9,17},{17,9},{25,1},{2,26},{10... | collective-permute-start | bytes 294920 | tf_op jit(solution)/shard_map/heads/ppermute | solution.py:162
  15.3 3.7 %collective-permute-start.1 = (bf16[2,192,128]{2,1,0:T(8,128)(2,1)S(1)}, bf16[2,192,128]{2,1,0:T(8,128)(2,1)S(1)}, u32[]{:S(2)}, u32[]{:S(2)}) collective-permute-start(bf16[2,192,128]{2,1,0:T(8,128)(2,1)S(1)} %pad_maximum_fusion.4), channel_id=1, source_target_pairs={{0,16},{16,0},{1,17},{17,1},{2,18},{18,2},{3,19},{19,3},{4,20},{20... | collective-permute-start | bytes 294920 | tf_op jit(solution)/shard_map/heads/ppermute | solution.py:40
  19.1 1.9 collective-permute-start
  21.0 0.9 collective-permute-done.1
  21.9 0.4 collective-permute-done
  22.4 0.1 fusion.43
  22.6 0.7 broadcast_in_dim.12
  23.3 7.4 %all-to-all-start.1 = ((bf16[4,16,1536]{2,1,0:T(8,128)(2,1)}), bf16[4,16,1536]{2,1,0:T(8,128)(2,1)S(1)}, u32[]{:S(2)}, u32[]{:S(2)}) async-start(bf16[4,16,1536]{2,1,0:T(8,128)(2,1)} %broadcast_in_dim.12), calls=%async_computation.1 | async-start | bytes 393216 | tf_op jit(solution)/shard_map/gather/all_to_all | solution.py:26
  30.7 10.2 %collective-permute-start.3 = (bf16[16,1536]{1,0:T(8,128)(2,1)S(1)}, bf16[16,1536]{1,0:T(8,128)(2,1)S(1)}, u32[]{:S(2)}, u32[]{:S(2)}) collective-permute-start(bf16[16,1536]{1,0:T(8,128)(2,1)S(1)} %get-tuple-element.69), channel_id=1, source_target_pairs={{0,192},{64,0},{128,64},{192,128},{1,193},{65,1},{129,65},{193,129... | collective-permute-start | bytes 147464 | tf_op jit(solution)/shard_map/gather/ppermute | solution.py:40
  41.0 1.2 collective-permute-done.3
  42.1 0.9 broadcast_in_dim.13
  43.1 3.5 %all-to-all-start.2 = ((bf16[4,64,1536]{2,1,0:T(8,128)(2,1)}), bf16[4,64,1536]{2,1,0:T(8,128)(2,1)S(1)}, u32[]{:S(2)}, u32[]{:S(2)}) async-start(bf16[4,64,1536]{2,1,0:T(8,128)(2,1)} %broadcast_in_dim.13), calls=%async_computation.2 | async-start | bytes 1572864 | tf_op jit(solution)/shard_map/gather/all_to_all | solution.py:26
  46.6 6.3 %collective-permute-start.5 = (bf16[16,1536]{1,0:T(8,128)(2,1)S(1)}, bf16[16,1536]{1,0:T(8,128)(2,1)S(1)}, u32[]{:S(2)}, u32[]{:S(2)}) collective-permute-start(bf16[16,1536]{1,0:T(8,128)(2,1)S(1)} %get-tuple-element.69), channel_id=1, source_target_pairs={{0,64},{64,128},{128,192},{192,0},{1,65},{65,129},{129,193},{193,1... | collective-permute-start | bytes 147464 | tf_op jit(solution)/shard_map/gather/ppermute | solution.py:40
  52.9 8.4 %collective-permute-start.4 = (bf16[16,1536]{1,0:T(8,128)(2,1)S(1)}, bf16[16,1536]{1,0:T(8,128)(2,1)S(1)}, u32[]{:S(2)}, u32[]{:S(2)}) collective-permute-start(bf16[16,1536]{1,0:T(8,128)(2,1)S(1)} %get-tuple-element.69), channel_id=1, source_target_pairs={{0,128},{64,192},{128,0},{192,64},{1,129},{65,193},{129,1},{193,65... | collective-permute-start | bytes 147464 | tf_op jit(solution)/shard_map/gather/ppermute | solution.py:40
  61.3 5.4 %collective-permute-done.4 = bf16[16,1536]{1,0:T(8,128)(2,1)S(1)} collective-permute-done((bf16[16,1536]{1,0:T(8,128)(2,1)S(1)}, bf16[16,1536]{1,0:T(8,128)(2,1)S(1)}, u32[]{:S(2)}, u32[]{:S(2)}) %collective-permute-start.4) | collective-permute-done | bytes 49184 | tf_op jit(solution)/shard_map/gather/ppermute | solution.py:40
  66.7 0.9 broadcast_in_dim.14
  67.6 3.9 %all-to-all-start.3 = ((bf16[4,64,1536]{2,1,0:T(8,128)(2,1)}), bf16[4,64,1536]{2,1,0:T(8,128)(2,1)S(1)}, u32[]{:S(2)}, u32[]{:S(2)}) async-start(bf16[4,64,1536]{2,1,0:T(8,128)(2,1)} %broadcast_in_dim.14), calls=%async_computation.3 | async-start | bytes 1572864 | tf_op jit(solution)/shard_map/gather/all_to_all | solution.py:26
  71.5 6.8 %collective-permute-start.6 = (bf16[256,1536]{1,0:T(8,128)(2,1)S(1)}, bf16[256,1536]{1,0:T(8,128)(2,1)S(1)}, u32[]{:S(2)}, u32[]{:S(2)}) collective-permute-start(bf16[256,1536]{1,0:T(8,128)(2,1)S(1)} %bitcast.121), channel_id=1, source_target_pairs={{0,8},{8,0},{1,9},{9,1},{2,10},{10,2},{3,11},{11,3},{4,12},{12,4},... | collective-permute-start | bytes 2359304 | tf_op jit(solution)/shard_map/gather/ppermute | solution.py:40
  80.3 0.5 fusion.15
  80.8 0.4 fusion.55
  81.2 0.4 fusion.14
  81.6 0.4 convolution_convert_fusion
  82.0 7.4 %collective-permute-start.7 = (bf16[256,1536]{1,0:T(8,128)(2,1)S(1)}, bf16[256,1536]{1,0:T(8,128)(2,1)S(1)}, u32[]{:S(2)}, u32[]{:S(2)}) collective-permute-start(bf16[256,1536]{1,0:T(8,128)(2,1)S(1)} %convolution_convert_fusion), channel_id=1, source_target_pairs={{0,8},{8,0},{1,9},{9,1},{2,10},{10,2},{3,11},{11,3},{4,12},{12,4},... | collective-permute-start | bytes 2359304 | tf_op jit(solution)/shard_map/sum/ppermute | solution.py:40
  89.4 0.4 fusion
  89.8 14.6 %all_to_all.55 = bf16[4,64,1536]{2,1,0:T(8,128)(2,1)S(1)} all-to-all(bf16[4,64,1536]{2,1,0:T(8,128)(2,1)S(1)} %bitcast.125), channel_id=1, replica_groups=mesh['xl'=2,'zh'=4,'zm'=2,'z0'=2,'c'=2,'y'=4,'xh'=2] {'y'}, dimensions={0} | all-to-all | bytes 1572864 | tf_op jit(solution)/shard_map/sum/all_to_all | solution.py:26
  104.5 1.3 add_convert_fusion
  105.8 4.5 %all-to-all-start.5 = ((bf16[4,64,1536]{2,1,0:T(8,128)(2,1)}), bf16[4,64,1536]{2,1,0:T(8,128)(2,1)S(1)}, u32[]{:S(2)}, u32[]{:S(2)}) async-start(bf16[4,64,1536]{2,1,0:T(8,128)(2,1)} %bitcast.19), calls=%async_computation.5 | async-start | bytes 1572864 | tf_op jit(solution)/shard_map/sum/all_to_all | solution.py:26
  110.3 6.4 %collective-permute-start.8 = (bf16[16,1536]{1,0:T(8,128)(2,1)S(1)}, bf16[16,1536]{1,0:T(8,128)(2,1)S(1)}, u32[]{:S(2)}, u32[]{:S(2)}) collective-permute-start(bf16[16,1536]{1,0:T(8,128)(2,1)S(1)} %get-tuple-element.66), channel_id=1, source_target_pairs={{0,64},{64,128},{128,192},{192,0},{1,65},{65,129},{129,193},{193,1... | collective-permute-start | bytes 147464 | tf_op jit(solution)/shard_map/sum/ppermute | solution.py:40
  116.7 4.5 %all-to-all-done.5 = bf16[4,64,1536]{2,1,0:T(8,128)(2,1)S(1)} async-done(((bf16[4,64,1536]{2,1,0:T(8,128)(2,1)}), bf16[4,64,1536]{2,1,0:T(8,128)(2,1)S(1)}, u32[]{:S(2)}, u32[]{:S(2)}) %all-to-all-start.5) | async-done | bytes 786464 | tf_op jit(solution)/shard_map/sum/all_to_all | solution.py:26
  121.2 0.8 convert_reduce_fusion
  122.0 5.8 %all-to-all-start.6 = ((bf16[4,16,1536]{2,1,0:T(8,128)(2,1)}), bf16[4,16,1536]{2,1,0:T(8,128)(2,1)S(1)}, u32[]{:S(2)}, u32[]{:S(2)}) async-start(bf16[4,16,1536]{2,1,0:T(8,128)(2,1)} %bitcast.21), calls=%async_computation.6 | async-start | bytes 393216 | tf_op jit(solution)/shard_map/sum/all_to_all | solution.py:26
  127.8 7.6 %collective-permute-start.9 = (bf16[16,1536]{1,0:T(8,128)(2,1)S(1)}, bf16[16,1536]{1,0:T(8,128)(2,1)S(1)}, u32[]{:S(2)}, u32[]{:S(2)}) collective-permute-start(bf16[16,1536]{1,0:T(8,128)(2,1)S(1)} %get-tuple-element.64), channel_id=1, source_target_pairs={{0,128},{64,192},{128,0},{192,64},{1,129},{65,193},{129,1},{193,65... | collective-permute-start | bytes 147464 | tf_op jit(solution)/shard_map/sum/ppermute | solution.py:40
  135.4 5.9 %collective-permute-start.10 = (bf16[16,1536]{1,0:T(8,128)(2,1)S(1)}, bf16[16,1536]{1,0:T(8,128)(2,1)S(1)}, u32[]{:S(2)}, u32[]{:S(2)}) collective-permute-start(bf16[16,1536]{1,0:T(8,128)(2,1)S(1)} %get-tuple-element.65), channel_id=1, source_target_pairs={{0,192},{64,0},{128,64},{192,128},{1,193},{65,1},{129,65},{193,129... | collective-permute-start | bytes 147464 | tf_op jit(solution)/shard_map/sum/ppermute | solution.py:40
  141.3 0.3 collective-permute-done.9
  141.5 3.3 %collective-permute-done.10 = bf16[16,1536]{1,0:T(8,128)(2,1)S(1)} collective-permute-done((bf16[16,1536]{1,0:T(8,128)(2,1)S(1)}, bf16[16,1536]{1,0:T(8,128)(2,1)S(1)}, u32[]{:S(2)}, u32[]{:S(2)}) %collective-permute-start.10) | collective-permute-done | bytes 49184 | tf_op jit(solution)/shard_map/sum/ppermute | solution.py:40
  144.8 0.2 multiply_reduce_fusion.1
  145.2 0.1 maximum_bitcast_fusion
  145.4 1.0 broadcast_in_dim.15
  146.3 9.4 %all-to-all-start.7 = ((bf16[32,2,16,384]{3,2,1,0:T(8,128)(2,1)}), bf16[32,2,16,384]{3,2,1,0:T(8,128)(2,1)S(1)}, u32[]{:S(2)}, u32[]{:S(2)}) async-start(bf16[32,2,16,384]{3,2,1,0:T(8,128)(2,1)} %bitcast.23), calls=%async_computation.7 | async-start | bytes 1572864 | tf_op jit(solution)/shard_map/head_grads/all_to_all | solution.py:26
  155.9 14.1 %all-to-all-done.7 = bf16[32,2,16,384]{3,2,1,0:T(8,128)(2,1)S(1)} async-done(((bf16[32,2,16,384]{3,2,1,0:T(8,128)(2,1)}), bf16[32,2,16,384]{3,2,1,0:T(8,128)(2,1)S(1)}, u32[]{:S(2)}, u32[]{:S(2)}) %all-to-all-start.7) | async-done | bytes 786464 | tf_op jit(solution)/shard_map/head_grads/all_to_all | solution.py:26
  170.0 0.3 fusion.16
  170.3 0.3 fusion.17
  170.6 13.4 %all_to_all.56 = bf16[4,96,384]{2,1,0:T(8,128)(2,1)S(1)} all-to-all(bf16[4,96,384]{2,1,0:T(8,128)(2,1)S(1)} %bitcast.131), channel_id=1, replica_groups=mesh['xl'=2,'zh'=4,'zm'=2,'z0'=2,'c'=2,'y'=4,'xh'=2] {'xl','zm'}, dimensions={0} | all-to-all | bytes 589824 | tf_op jit(solution)/shard_map/weight_grads/all_to_all | solution.py:26
  184.0 0.7 broadcast_in_dim.16
  184.8 5.2 %all-to-all-start.9 = ((bf16[4,96,384]{2,1,0:T(8,128)(2,1)}), bf16[4,96,384]{2,1,0:T(8,128)(2,1)S(1)}, u32[]{:S(2)}, u32[]{:S(2)}) async-start(bf16[4,96,384]{2,1,0:T(8,128)(2,1)} %broadcast_in_dim.16), calls=%async_computation.9 | async-start | bytes 589824 | tf_op jit(solution)/shard_map/weight_grads/all_to_all | solution.py:26
  190.0 1.2 convolution_bitcast_fusion
  191.2 1.2 convolution_bitcast_fusion.1
  192.5 4.5 %collective-permute-start.11 = (bf16[2,2,128,192]{2,3,1,0:T(8,128)(2,1)S(1)}, bf16[2,2,128,192]{2,3,1,0:T(8,128)(2,1)S(1)}, u32[]{:S(2)}, u32[]{:S(2)}) collective-permute-start(bf16[2,2,128,192]{2,3,1,0:T(8,128)(2,1)S(1)} %fusion.23), channel_id=1, source_target_pairs={{0,8},{8,0},{1,9},{9,1},{2,10},{10,2},{3,11},{11,3},{4,12},{12,4},... | collective-permute-start | bytes 589832 | tf_op jit(solution)/shard_map/input_grads/ppermute | solution.py:40
  196.9 1.0 collective-permute-done.11
  198.0 7.0 %all-to-all-done.9 = bf16[4,96,384]{2,1,0:T(8,128)(2,1)S(1)} async-done(((bf16[4,96,384]{2,1,0:T(8,128)(2,1)}), bf16[4,96,384]{2,1,0:T(8,128)(2,1)S(1)}, u32[]{:S(2)}, u32[]{:S(2)}) %all-to-all-start.9) | async-done | bytes 294944 | tf_op jit(solution)/shard_map/weight_grads/all_to_all | solution.py:26
  205.0 0.9 broadcast_in_dim.17
  205.9 9.1 %all-to-all-start.10 = ((bf16[8,96,384]{2,1,0:T(8,128)(2,1)}), bf16[8,96,384]{2,1,0:T(8,128)(2,1)S(1)}, u32[]{:S(2)}, u32[]{:S(2)}) async-start(bf16[8,96,384]{2,1,0:T(8,128)(2,1)} %broadcast_in_dim.17), calls=%async_computation.10 | async-start | bytes 1179648 | tf_op jit(solution)/shard_map/weight_grads/all_to_all | solution.py:26
  215.0 3.4 %collective-permute-start.12 = (bf16[2,128,192]{1,2,0:T(8,128)(2,1)S(1)}, bf16[2,128,192]{1,2,0:T(8,128)(2,1)S(1)}, u32[]{:S(2)}, u32[]{:S(2)}) collective-permute-start(bf16[2,128,192]{1,2,0:T(8,128)(2,1)S(1)} %fusion.44), channel_id=1, source_target_pairs={{0,16},{16,0},{1,17},{17,1},{2,18},{18,2},{3,19},{19,3},{4,20},{20... | collective-permute-start | bytes 294920 | tf_op jit(solution)/shard_map/weight_grads/ppermute | solution.py:40
  218.4 7.0 %collective-permute-done.12 = bf16[2,128,192]{1,2,0:T(8,128)(2,1)S(1)} collective-permute-done((bf16[2,128,192]{1,2,0:T(8,128)(2,1)S(1)}, bf16[2,128,192]{1,2,0:T(8,128)(2,1)S(1)}, u32[]{:S(2)}, u32[]{:S(2)}) %collective-permute-start.12) | collective-permute-done | bytes 98336 | tf_op jit(solution)/shard_map/weight_grads/ppermute | solution.py:40
  225.4 0.7 slice_bitcast_fusion.4
  226.1 1.4 all-to-all-done.10
  227.6 0.5 copy.17
  228.0 0.4 reshape.242
  228.4 7.2 %collective-permute-start.13 = (bf16[2,192,768]{2,1,0:T(8,128)(2,1)S(1)}, bf16[2,192,768]{2,1,0:T(8,128)(2,1)S(1)}, u32[]{:S(2)}, u32[]{:S(2)}) collective-permute-start(bf16[2,192,768]{2,1,0:T(8,128)(2,1)S(1)} %reshape.242), channel_id=1, source_target_pairs={{0,8},{8,0},{1,9},{9,1},{2,10},{10,2},{3,11},{11,3},{4,12},{12,4},... | collective-permute-start | bytes 1769480 | tf_op jit(solution)/shard_map/weight_grads/ppermute | solution.py:40
  235.9 1.4 collective-permute-done.13
  237.4 1.0 copy-done
  238.4 0.4 copy-done.1
  (47 shorter events, 1.4 us)
Async XLA Ops:
  3.2 7.7 %copy-start.2 = (bf16[128,192]{0,1:T(8,128)(2,1)S(1)}, bf16[128,192]{0,1:T(8,128)(2,1)}, u32[]{:S(2)}) copy-start(bf16[128,192]{0,1:T(8,128)(2,1)} %param.7) | copy-start | bytes 147460
  3.2 7.6 %copy-start.3 = (bf16[128,192]{0,1:T(8,128)(2,1)S(1)}, bf16[128,192]{0,1:T(8,128)(2,1)}, u32[]{:S(2)}) copy-start(bf16[128,192]{0,1:T(8,128)(2,1)} %param.8) | copy-start | bytes 147460
  3.2 19.0 %all-to-all-start = ((bf16[8,16,3072]{2,1,0:T(8,128)(2,1)}), bf16[8,16,3072]{2,1,0:T(8,128)(2,1)S(1)}, u32[]{:S(2)}, u32[]{:S(2)}) async-start(bf16[8,16,3072]{2,1,0:T(8,128)(2,1)} %bitcast.124), calls=%async_computation | async-start | bytes 1572864 | tf_op jit(solution)/shard_map/heads/all_to_all | solution.py:26
  10.9 10.1 %collective-permute-start.2 = (bf16[2,192,128]{2,1,0:T(8,128)(2,1)S(1)}, bf16[2,192,128]{2,1,0:T(8,128)(2,1)S(1)}, u32[]{:S(2)}, u32[]{:S(2)}) collective-permute-start(bf16[2,192,128]{2,1,0:T(8,128)(2,1)S(1)} %pad_maximum_fusion.4), channel_id=1, source_target_pairs={{0,24},{8,16},{16,8},{24,0},{1,25},{9,17},{17,9},{25,1},{2,26},{10... | collective-permute-start | bytes 294920 | tf_op jit(solution)/shard_map/heads/ppermute | solution.py:162
  15.3 6.6 %collective-permute-start.1 = (bf16[2,192,128]{2,1,0:T(8,128)(2,1)S(1)}, bf16[2,192,128]{2,1,0:T(8,128)(2,1)S(1)}, u32[]{:S(2)}, u32[]{:S(2)}) collective-permute-start(bf16[2,192,128]{2,1,0:T(8,128)(2,1)S(1)} %pad_maximum_fusion.4), channel_id=1, source_target_pairs={{0,16},{16,0},{1,17},{17,1},{2,18},{18,2},{3,19},{19,3},{4,20},{20... | collective-permute-start | bytes 294920 | tf_op jit(solution)/shard_map/heads/ppermute | solution.py:40
  19.1 3.2 %collective-permute-start = (bf16[2,192,128]{2,1,0:T(8,128)(2,1)S(1)}, bf16[2,192,128]{2,1,0:T(8,128)(2,1)S(1)}, u32[]{:S(2)}, u32[]{:S(2)}) collective-permute-start(bf16[2,192,128]{2,1,0:T(8,128)(2,1)S(1)} %pad_maximum_fusion.4), channel_id=1, source_target_pairs={{0,8},{8,0},{1,9},{9,1},{2,10},{10,2},{3,11},{11,3},{4,12},{12,4},... | collective-permute-start | bytes 294920 | tf_op jit(solution)/shard_map/heads/ppermute | solution.py:40
  23.3 18.8 %all-to-all-start.1 = ((bf16[4,16,1536]{2,1,0:T(8,128)(2,1)}), bf16[4,16,1536]{2,1,0:T(8,128)(2,1)S(1)}, u32[]{:S(2)}, u32[]{:S(2)}) async-start(bf16[4,16,1536]{2,1,0:T(8,128)(2,1)} %broadcast_in_dim.12), calls=%async_computation.1 | async-start | bytes 393216 | tf_op jit(solution)/shard_map/gather/all_to_all | solution.py:26
  30.7 11.4 %collective-permute-start.3 = (bf16[16,1536]{1,0:T(8,128)(2,1)S(1)}, bf16[16,1536]{1,0:T(8,128)(2,1)S(1)}, u32[]{:S(2)}, u32[]{:S(2)}) collective-permute-start(bf16[16,1536]{1,0:T(8,128)(2,1)S(1)} %get-tuple-element.69), channel_id=1, source_target_pairs={{0,192},{64,0},{128,64},{192,128},{1,193},{65,1},{129,65},{193,129... | collective-permute-start | bytes 147464 | tf_op jit(solution)/shard_map/gather/ppermute | solution.py:40
  43.1 23.6 %all-to-all-start.2 = ((bf16[4,64,1536]{2,1,0:T(8,128)(2,1)}), bf16[4,64,1536]{2,1,0:T(8,128)(2,1)S(1)}, u32[]{:S(2)}, u32[]{:S(2)}) async-start(bf16[4,64,1536]{2,1,0:T(8,128)(2,1)} %broadcast_in_dim.13), calls=%async_computation.2 | async-start | bytes 1572864 | tf_op jit(solution)/shard_map/gather/all_to_all | solution.py:26
  46.6 14.7 %collective-permute-start.5 = (bf16[16,1536]{1,0:T(8,128)(2,1)S(1)}, bf16[16,1536]{1,0:T(8,128)(2,1)S(1)}, u32[]{:S(2)}, u32[]{:S(2)}) collective-permute-start(bf16[16,1536]{1,0:T(8,128)(2,1)S(1)} %get-tuple-element.69), channel_id=1, source_target_pairs={{0,64},{64,128},{128,192},{192,0},{1,65},{65,129},{129,193},{193,1... | collective-permute-start | bytes 147464 | tf_op jit(solution)/shard_map/gather/ppermute | solution.py:40
  52.9 13.8 %collective-permute-start.4 = (bf16[16,1536]{1,0:T(8,128)(2,1)S(1)}, bf16[16,1536]{1,0:T(8,128)(2,1)S(1)}, u32[]{:S(2)}, u32[]{:S(2)}) collective-permute-start(bf16[16,1536]{1,0:T(8,128)(2,1)S(1)} %get-tuple-element.69), channel_id=1, source_target_pairs={{0,128},{64,192},{128,0},{192,64},{1,129},{65,193},{129,1},{193,65... | collective-permute-start | bytes 147464 | tf_op jit(solution)/shard_map/gather/ppermute | solution.py:40
  67.6 12.7 %all-to-all-start.3 = ((bf16[4,64,1536]{2,1,0:T(8,128)(2,1)}), bf16[4,64,1536]{2,1,0:T(8,128)(2,1)S(1)}, u32[]{:S(2)}, u32[]{:S(2)}) async-start(bf16[4,64,1536]{2,1,0:T(8,128)(2,1)} %broadcast_in_dim.14), calls=%async_computation.3 | async-start | bytes 1572864 | tf_op jit(solution)/shard_map/gather/all_to_all | solution.py:26
  71.5 9.7 %collective-permute-start.6 = (bf16[256,1536]{1,0:T(8,128)(2,1)S(1)}, bf16[256,1536]{1,0:T(8,128)(2,1)S(1)}, u32[]{:S(2)}, u32[]{:S(2)}) collective-permute-start(bf16[256,1536]{1,0:T(8,128)(2,1)S(1)} %bitcast.121), channel_id=1, source_target_pairs={{0,8},{8,0},{1,9},{9,1},{2,10},{10,2},{3,11},{11,3},{4,12},{12,4},... | collective-permute-start | bytes 2359304 | tf_op jit(solution)/shard_map/gather/ppermute | solution.py:40
  82.0 22.5 %collective-permute-start.7 = (bf16[256,1536]{1,0:T(8,128)(2,1)S(1)}, bf16[256,1536]{1,0:T(8,128)(2,1)S(1)}, u32[]{:S(2)}, u32[]{:S(2)}) collective-permute-start(bf16[256,1536]{1,0:T(8,128)(2,1)S(1)} %convolution_convert_fusion), channel_id=1, source_target_pairs={{0,8},{8,0},{1,9},{9,1},{2,10},{10,2},{3,11},{11,3},{4,12},{12,4},... | collective-permute-start | bytes 2359304 | tf_op jit(solution)/shard_map/sum/ppermute | solution.py:40
  105.8 15.4 %all-to-all-start.5 = ((bf16[4,64,1536]{2,1,0:T(8,128)(2,1)}), bf16[4,64,1536]{2,1,0:T(8,128)(2,1)S(1)}, u32[]{:S(2)}, u32[]{:S(2)}) async-start(bf16[4,64,1536]{2,1,0:T(8,128)(2,1)} %bitcast.19), calls=%async_computation.5 | async-start | bytes 1572864 | tf_op jit(solution)/shard_map/sum/all_to_all | solution.py:26
  110.3 11.7 %collective-permute-start.8 = (bf16[16,1536]{1,0:T(8,128)(2,1)S(1)}, bf16[16,1536]{1,0:T(8,128)(2,1)S(1)}, u32[]{:S(2)}, u32[]{:S(2)}) collective-permute-start(bf16[16,1536]{1,0:T(8,128)(2,1)S(1)} %get-tuple-element.66), channel_id=1, source_target_pairs={{0,64},{64,128},{128,192},{192,0},{1,65},{65,129},{129,193},{193,1... | collective-permute-start | bytes 147464 | tf_op jit(solution)/shard_map/sum/ppermute | solution.py:40
  122.0 19.3 %all-to-all-start.6 = ((bf16[4,16,1536]{2,1,0:T(8,128)(2,1)}), bf16[4,16,1536]{2,1,0:T(8,128)(2,1)S(1)}, u32[]{:S(2)}, u32[]{:S(2)}) async-start(bf16[4,16,1536]{2,1,0:T(8,128)(2,1)} %bitcast.21), calls=%async_computation.6 | async-start | bytes 393216 | tf_op jit(solution)/shard_map/sum/all_to_all | solution.py:26
  127.8 13.8 %collective-permute-start.9 = (bf16[16,1536]{1,0:T(8,128)(2,1)S(1)}, bf16[16,1536]{1,0:T(8,128)(2,1)S(1)}, u32[]{:S(2)}, u32[]{:S(2)}) collective-permute-start(bf16[16,1536]{1,0:T(8,128)(2,1)S(1)} %get-tuple-element.64), channel_id=1, source_target_pairs={{0,128},{64,192},{128,0},{192,64},{1,129},{65,193},{129,1},{193,65... | collective-permute-start | bytes 147464 | tf_op jit(solution)/shard_map/sum/ppermute | solution.py:40
  135.4 9.4 %collective-permute-start.10 = (bf16[16,1536]{1,0:T(8,128)(2,1)S(1)}, bf16[16,1536]{1,0:T(8,128)(2,1)S(1)}, u32[]{:S(2)}, u32[]{:S(2)}) collective-permute-start(bf16[16,1536]{1,0:T(8,128)(2,1)S(1)} %get-tuple-element.65), channel_id=1, source_target_pairs={{0,192},{64,0},{128,64},{192,128},{1,193},{65,1},{129,65},{193,129... | collective-permute-start | bytes 147464 | tf_op jit(solution)/shard_map/sum/ppermute | solution.py:40
  146.3 23.6 %all-to-all-start.7 = ((bf16[32,2,16,384]{3,2,1,0:T(8,128)(2,1)}), bf16[32,2,16,384]{3,2,1,0:T(8,128)(2,1)S(1)}, u32[]{:S(2)}, u32[]{:S(2)}) async-start(bf16[32,2,16,384]{3,2,1,0:T(8,128)(2,1)} %bitcast.23), calls=%async_computation.7 | async-start | bytes 1572864 | tf_op jit(solution)/shard_map/head_grads/all_to_all | solution.py:26
  184.8 20.2 %all-to-all-start.9 = ((bf16[4,96,384]{2,1,0:T(8,128)(2,1)}), bf16[4,96,384]{2,1,0:T(8,128)(2,1)S(1)}, u32[]{:S(2)}, u32[]{:S(2)}) async-start(bf16[4,96,384]{2,1,0:T(8,128)(2,1)} %broadcast_in_dim.16), calls=%async_computation.9 | async-start | bytes 589824 | tf_op jit(solution)/shard_map/weight_grads/all_to_all | solution.py:26
  192.5 5.5 %collective-permute-start.11 = (bf16[2,2,128,192]{2,3,1,0:T(8,128)(2,1)S(1)}, bf16[2,2,128,192]{2,3,1,0:T(8,128)(2,1)S(1)}, u32[]{:S(2)}, u32[]{:S(2)}) collective-permute-start(bf16[2,2,128,192]{2,3,1,0:T(8,128)(2,1)S(1)} %fusion.23), channel_id=1, source_target_pairs={{0,8},{8,0},{1,9},{9,1},{2,10},{10,2},{3,11},{11,3},{4,12},{12,4},... | collective-permute-start | bytes 589832 | tf_op jit(solution)/shard_map/input_grads/ppermute | solution.py:40
  205.9 21.7 %all-to-all-start.10 = ((bf16[8,96,384]{2,1,0:T(8,128)(2,1)}), bf16[8,96,384]{2,1,0:T(8,128)(2,1)S(1)}, u32[]{:S(2)}, u32[]{:S(2)}) async-start(bf16[8,96,384]{2,1,0:T(8,128)(2,1)} %broadcast_in_dim.17), calls=%async_computation.10 | async-start | bytes 1179648 | tf_op jit(solution)/shard_map/weight_grads/all_to_all | solution.py:26
  215.0 10.4 %collective-permute-start.12 = (bf16[2,128,192]{1,2,0:T(8,128)(2,1)S(1)}, bf16[2,128,192]{1,2,0:T(8,128)(2,1)S(1)}, u32[]{:S(2)}, u32[]{:S(2)}) collective-permute-start(bf16[2,128,192]{1,2,0:T(8,128)(2,1)S(1)} %fusion.44), channel_id=1, source_target_pairs={{0,16},{16,0},{1,17},{17,1},{2,18},{18,2},{3,19},{19,3},{4,20},{20... | collective-permute-start | bytes 294920 | tf_op jit(solution)/shard_map/weight_grads/ppermute | solution.py:40
  228.4 8.9 %collective-permute-start.13 = (bf16[2,192,768]{2,1,0:T(8,128)(2,1)S(1)}, bf16[2,192,768]{2,1,0:T(8,128)(2,1)S(1)}, u32[]{:S(2)}, u32[]{:S(2)}) collective-permute-start(bf16[2,192,768]{2,1,0:T(8,128)(2,1)S(1)} %reshape.242), channel_id=1, source_target_pairs={{0,8},{8,0},{1,9},{9,1},{2,10},{10,2},{3,11},{11,3},{4,12},{12,4},... | collective-permute-start | bytes 1769480 | tf_op jit(solution)/shard_map/weight_grads/ppermute | solution.py:40
  237.4 1.0 copy-start
  237.4 1.4 copy-start.1

commit v18 on v15

--- a/solution.py
+++ b/solution.py
@@ -11,6 +11,7 @@
 PARTS = {"xl": 2, "zh": 4, "zm": 2, "z0": 2, "c": 2, "y": 4, "xh": 2}
 DP = ("xl", "zh", "zm", "z0", "c")
 ZL = ("zm", "z0")
+RING = (1, 3, 2)
 MP = ("y", "xh")
 
 
@@ -42,15 +43,15 @@
 
 def ring_gather(rows, axis):
     n = count(axis)
-    return jnp.concatenate([rows] + [shifted(rows, axis, n - k) for k in range(1, n)], axis=0)
+    return jnp.concatenate([rows] + [shifted(rows, axis, n - k) for k in RING], axis=0)
 
 
 def ring_scatter_sum(total, axis):
     n = count(axis)
     blocks = split_rows(total, n)
     own = blocks[0]
-    for k in range(1, n):
-        own = own + shifted(blocks[k].astype(BF16), axis, k).astype(F32)
+    for block, k in zip(blocks[1:], RING):
+        own = own + shifted(block.astype(BF16), axis, k).astype(F32)
     return own
 
 

time: 218 us -> 218 us (level)
  waiting for transfers between devices: 41.9 us -> 38.8 us
  starting transfers between devices: 139 us -> 142 us
    all_to_all x8, starting transfers between devices: 63.3 us -> 65.7 us  [exchange(): return lax.all_to_all(blocks, axes, split_axis=0, concat_axis=0, tiled=True)]
  transfers between devices with their start and end apart: 28 -> 28, of which waited for: 14 -> 14; matrix products, arithmetic and copies ran while one was open for 4% -> 3% of each run, Pallas kernels for 0% -> 0%
where the time goes in v18:
time: 218 us; the launch traced here: 216 us
  starting transfers between devices  142 us (65%)
  waiting for transfers between devices  38.8 us (18%)
  blocking collectives  13 us (6%)
  local copies, waits for them, and re-layouts  8.22 us (4%)
  matrix products  6.18 us (3%)
  between operations  3.29 us (2%)
  Pallas kernels  2.59 us (1%)
  other arithmetic  2.44 us (1%)
    ppermute x19, starting transfers between devices, shifted(): return lax.ppermute(value, axis, [(i, (i + by) % n) for i in range(n)])  71.5 us
    all_to_all x8, starting transfers between devices, exchange(): return lax.all_to_all(blocks, axes, split_axis=0, concat_axis=0, tiled=True)  65.7 us
    all_to_all x8, waiting for transfers between devices, exchange(): return lax.all_to_all(blocks, axes, split_axis=0, concat_axis=0, tiled=True)  28.7 us
    all_to_all x1, blocking collectives, exchange(): return lax.all_to_all(blocks, axes, split_axis=0, concat_axis=0, tiled=True)  13 us
    ppermute x19, waiting for transfers between devices, shifted(): return lax.ppermute(value, axis, [(i, (i + by) % n) for i in range(n)])  10.2 us
    ppermute x1, starting transfers between devices, on_device(): lax.ppermute(features, ('z0', 'c'), [(i, 3 - i) for i in range(4)])  4.39 us
  transfers between devices with their start and end apart: 28, of which 14 were waited for; matrix products, arithmetic and copies ran while one was open for 3% of the time, Pallas kernels for 0%

profile of v18, /device:TPU:1, one launch (start us, length us, event | category | flops | bytes accessed | tf_op | source)
XLA Modules:
  0.0 216.2 jit_solution(14699271675665655038)
XLA Ops:
  0.6 2.6 %heads.1 = bf16[128,3072]{1,0:T(8,128)(2,1)} custom-call(bf16[192,128]{1,0:T(8,128)(2,1)} %bitcast.126, bf16[192,1536]{1,0:T(8,128)(2,1)} %refs_1_.1, bf16[192,128]{1,0:T(8,128)(2,1)} %bitcast.129, bf16[192,1536]{1,0:T(8,128)(2,1)} %refs_3_.1), custom_call_target="tpu_custom_call" | custom-call | flops 150994944 | bytes 2064384 | tf_op jit(solution)/shard_map/heads/pallas_call | solution.py:77
  3.2 7.6 %all-to-all-start = ((bf16[8,16,3072]{2,1,0:T(8,128)(2,1)}), bf16[8,16,3072]{2,1,0:T(8,128)(2,1)S(1)}, u32[]{:S(2)}, u32[]{:S(2)}) async-start(bf16[8,16,3072]{2,1,0:T(8,128)(2,1)} %bitcast.118), calls=%async_computation | async-start | bytes 1572864 | tf_op jit(solution)/shard_map/heads/all_to_all | solution.py:27
  10.9 4.4 %collective-permute-start.2 = (bf16[2,192,128]{2,1,0:T(8,128)(2,1)S(1)}, bf16[2,192,128]{2,1,0:T(8,128)(2,1)S(1)}, u32[]{:S(2)}, u32[]{:S(2)}) collective-permute-start(bf16[2,192,128]{2,1,0:T(8,128)(2,1)S(1)} %pad_maximum_fusion.4), channel_id=1, source_target_pairs={{0,24},{8,16},{16,8},{24,0},{1,25},{9,17},{17,9},{25,1},{2,26},{10... | collective-permute-start | bytes 294920 | tf_op jit(solution)/shard_map/heads/ppermute | solution.py:163
  15.3 3.7 %collective-permute-start.1 = (bf16[2,192,128]{2,1,0:T(8,128)(2,1)S(1)}, bf16[2,192,128]{2,1,0:T(8,128)(2,1)S(1)}, u32[]{:S(2)}, u32[]{:S(2)}) collective-permute-start(bf16[2,192,128]{2,1,0:T(8,128)(2,1)S(1)} %pad_maximum_fusion.4), channel_id=1, source_target_pairs={{0,16},{16,0},{1,17},{17,1},{2,18},{18,2},{3,19},{19,3},{4,20},{20... | collective-permute-start | bytes 294920 | tf_op jit(solution)/shard_map/heads/ppermute | solution.py:41
  19.1 1.9 collective-permute-start
  21.0 0.9 collective-permute-done.1
  21.9 0.4 collective-permute-done
  22.6 0.7 broadcast_in_dim.12
  23.3 16.6 %all-to-all-start.1 = ((bf16[4,16,1536]{2,1,0:T(8,128)(2,1)}), bf16[4,16,1536]{2,1,0:T(8,128)(2,1)S(1)}, u32[]{:S(2)}, u32[]{:S(2)}) async-start(bf16[4,16,1536]{2,1,0:T(8,128)(2,1)} %broadcast_in_dim.12), calls=%async_computation.1 | async-start | bytes 393216 | tf_op jit(solution)/shard_map/gather_texts/all_to_all | solution.py:27
  40.0 3.1 %collective-permute-start.5 = (bf16[16,1536]{1,0:T(8,128)(2,1)S(1)}, bf16[16,1536]{1,0:T(8,128)(2,1)S(1)}, u32[]{:S(2)}, u32[]{:S(2)}) collective-permute-start(bf16[16,1536]{1,0:T(8,128)(2,1)S(1)} %get-tuple-element.29), channel_id=1, source_target_pairs={{0,32},{16,48},{32,0},{48,16},{1,33},{17,49},{33,1},{49,17},{2,34}... | collective-permute-start | bytes 147464 | tf_op jit(solution)/shard_map/gather_images/ppermute | solution.py:41
  43.1 2.7 %collective-permute-start.4 = (bf16[16,1536]{1,0:T(8,128)(2,1)S(1)}, bf16[16,1536]{1,0:T(8,128)(2,1)S(1)}, u32[]{:S(2)}, u32[]{:S(2)}) collective-permute-start(bf16[16,1536]{1,0:T(8,128)(2,1)S(1)} %get-tuple-element.29), channel_id=1, source_target_pairs={{0,16},{16,32},{32,48},{48,0},{1,17},{17,33},{33,49},{49,1},{2,18}... | collective-permute-start | bytes 147464 | tf_op jit(solution)/shard_map/gather_images/ppermute | solution.py:41
  45.8 4.4 %collective-permute-start.3 = (bf16[16,1536]{1,0:T(8,128)(2,1)S(1)}, bf16[16,1536]{1,0:T(8,128)(2,1)S(1)}, u32[]{:S(2)}, u32[]{:S(2)}) collective-permute-start(bf16[16,1536]{1,0:T(8,128)(2,1)S(1)} %get-tuple-element.29), channel_id=1, source_target_pairs={{0,48},{16,0},{32,16},{48,32},{1,49},{17,1},{33,17},{49,33},{2,50}... | collective-permute-start | bytes 147464 | tf_op jit(solution)/shard_map/gather_images/ppermute | solution.py:41
  52.2 0.5 all-to-all-done.1
  52.7 0.9 broadcast_in_dim.14
  53.7 3.5 %all-to-all-start.2 = ((bf16[4,64,1536]{2,1,0:T(8,128)(2,1)}), bf16[4,64,1536]{2,1,0:T(8,128)(2,1)S(1)}, u32[]{:S(2)}, u32[]{:S(2)}) async-start(bf16[4,64,1536]{2,1,0:T(8,128)(2,1)} %broadcast_in_dim.14), calls=%async_computation.2 | async-start | bytes 1572864 | tf_op jit(solution)/shard_map/gather_texts/all_to_all | solution.py:27
  57.2 2.8 %collective-permute-start.8 = (bf16[64,1536]{1,0:T(8,128)(2,1)S(1)}, bf16[64,1536]{1,0:T(8,128)(2,1)S(1)}, u32[]{:S(2)}, u32[]{:S(2)}) collective-permute-start(bf16[64,1536]{1,0:T(8,128)(2,1)S(1)} %pad_maximum_fusion.3), channel_id=1, source_target_pairs={{0,4},{2,6},{4,0},{6,2},{1,5},{3,7},{5,1},{7,3},{8,12},{10,14},{12... | collective-permute-start | bytes 589832 | tf_op jit(solution)/shard_map/gather_images/ppermute | solution.py:41
  60.0 2.5 %collective-permute-start.7 = (bf16[64,1536]{1,0:T(8,128)(2,1)S(1)}, bf16[64,1536]{1,0:T(8,128)(2,1)S(1)}, u32[]{:S(2)}, u32[]{:S(2)}) collective-permute-start(bf16[64,1536]{1,0:T(8,128)(2,1)S(1)} %pad_maximum_fusion.3), channel_id=1, source_target_pairs={{0,2},{2,4},{4,6},{6,0},{1,3},{3,5},{5,7},{7,1},{8,10},{10,12},{12... | collective-permute-start | bytes 589832 | tf_op jit(solution)/shard_map/gather_images/ppermute | solution.py:41
  62.5 4.0 %collective-permute-start.6 = (bf16[64,1536]{1,0:T(8,128)(2,1)S(1)}, bf16[64,1536]{1,0:T(8,128)(2,1)S(1)}, u32[]{:S(2)}, u32[]{:S(2)}) collective-permute-start(bf16[64,1536]{1,0:T(8,128)(2,1)S(1)} %pad_maximum_fusion.3), channel_id=1, source_target_pairs={{0,6},{2,0},{4,2},{6,4},{1,7},{3,1},{5,3},{7,5},{8,14},{10,8},{12,... | collective-permute-start | bytes 589832 | tf_op jit(solution)/shard_map/gather_images/ppermute | solution.py:41
  66.6 10.0 %collective-permute-start.9 = (bf16[256,1536]{1,0:T(8,128)(2,1)S(1)}, bf16[256,1536]{1,0:T(8,128)(2,1)S(1)}, u32[]{:S(2)}, u32[]{:S(2)}) collective-permute-start(bf16[256,1536]{1,0:T(8,128)(2,1)S(1)} %bitcast.115), channel_id=1, source_target_pairs={{0,8},{8,0},{1,9},{9,1},{2,10},{10,2},{3,11},{11,3},{4,12},{12,4},... | collective-permute-start | bytes 2359304 | tf_op jit(solution)/shard_map/gather_texts/ppermute | solution.py:41
  76.7 1.8 collective-permute-done.9
  78.5 0.4 fusion.14
  78.9 0.4 convolution_convert_fusion
  79.3 2.3 %collective-permute-start.16 = (bf16[256,1536]{1,0:T(8,128)(2,1)S(1)}, bf16[256,1536]{1,0:T(8,128)(2,1)S(1)}, u32[]{:S(2)}, u32[]{:S(2)}) collective-permute-start(bf16[256,1536]{1,0:T(8,128)(2,1)S(1)} %convolution_convert_fusion), channel_id=1, source_target_pairs={{0,8},{8,0},{1,9},{9,1},{2,10},{10,2},{3,11},{11,3},{4,12},{12,4},... | collective-permute-start | bytes 2359304 | tf_op jit(solution)/shard_map/sum_texts/ppermute | solution.py:41
  81.6 0.4 fusion.15
  82.0 0.4 fusion.63
  82.4 0.4 fusion.62
  82.8 0.7 collective-permute-done.16
  83.5 1.3 fusion
  84.7 4.5 %all-to-all-start.3 = ((bf16[4,64,1536]{2,1,0:T(8,128)(2,1)}), bf16[4,64,1536]{2,1,0:T(8,128)(2,1)S(1)}, u32[]{:S(2)}, u32[]{:S(2)}) async-start(bf16[4,64,1536]{2,1,0:T(8,128)(2,1)} %bitcast.18), calls=%async_computation.3 | async-start | bytes 1572864 | tf_op jit(solution)/shard_map/sum_texts/all_to_all | solution.py:27
  89.2 0.8 fusion.60
  90.0 2.1 collective-permute-start.10
  92.1 5.3 %collective-permute-start.12 = (bf16[64,1536]{1,0:T(8,128)(2,1)}, bf16[64,1536]{1,0:T(8,128)(2,1)S(1)}, u32[]{:S(2)}, u32[]{:S(2)}) collective-permute-start(bf16[64,1536]{1,0:T(8,128)(2,1)} %get-tuple-element.33), channel_id=1, source_target_pairs={{0,4},{2,6},{4,0},{6,2},{1,5},{3,7},{5,1},{7,3},{8,12},{10,14},{12... | collective-permute-start | bytes 589832 | tf_op jit(solution)/shard_map/sum_images/ppermute | solution.py:41
  97.4 1.9 collective-permute-start.11
  99.4 1.6 all-to-all-done.3
  100.9 0.8 reduce_sum.97
  101.8 6.8 %all-to-all-start.4 = ((bf16[4,16,1536]{2,1,0:T(8,128)(2,1)}), bf16[4,16,1536]{2,1,0:T(8,128)(2,1)S(1)}, u32[]{:S(2)}, u32[]{:S(2)}) async-start(bf16[4,16,1536]{2,1,0:T(8,128)(2,1)} %bitcast.19), calls=%async_computation.4 | async-start | bytes 393216 | tf_op jit(solution)/shard_map/sum_texts/all_to_all | solution.py:27
  108.7 1.9 collective-permute-start.13
  110.7 2.0 collective-permute-start.15
  112.7 5.1 %collective-permute-start.14 = (bf16[16,1536]{1,0:T(8,128)(2,1)S(1)}, bf16[16,1536]{1,0:T(8,128)(2,1)S(1)}, u32[]{:S(2)}, u32[]{:S(2)}) collective-permute-start(bf16[16,1536]{1,0:T(8,128)(2,1)S(1)} %get-tuple-element.57), channel_id=1, source_target_pairs={{0,48},{16,0},{32,16},{48,32},{1,49},{17,1},{33,17},{49,33},{2,50}... | collective-permute-start | bytes 147464 | tf_op jit(solution)/shard_map/sum_images/ppermute | solution.py:41
  117.8 3.4 %all-to-all-done.4 = bf16[4,16,1536]{2,1,0:T(8,128)(2,1)S(1)} async-done(((bf16[4,16,1536]{2,1,0:T(8,128)(2,1)}), bf16[4,16,1536]{2,1,0:T(8,128)(2,1)S(1)}, u32[]{:S(2)}, u32[]{:S(2)}) %all-to-all-start.4) | async-done | bytes 196640 | tf_op jit(solution)/shard_map/sum_texts/all_to_all | solution.py:27
  122.0 1.0 broadcast_in_dim.15
  122.9 10.4 %all-to-all-start.5 = ((bf16[32,2,16,384]{3,2,1,0:T(8,128)(2,1)}), bf16[32,2,16,384]{3,2,1,0:T(8,128)(2,1)S(1)}, u32[]{:S(2)}, u32[]{:S(2)}) async-start(bf16[32,2,16,384]{3,2,1,0:T(8,128)(2,1)} %bitcast.21), calls=%async_computation.5 | async-start | bytes 1572864 | tf_op jit(solution)/shard_map/head_grads/all_to_all | solution.py:27
  133.5 14.0 %all-to-all-done.5 = bf16[32,2,16,384]{3,2,1,0:T(8,128)(2,1)S(1)} async-done(((bf16[32,2,16,384]{3,2,1,0:T(8,128)(2,1)}), bf16[32,2,16,384]{3,2,1,0:T(8,128)(2,1)S(1)}, u32[]{:S(2)}, u32[]{:S(2)}) %all-to-all-start.5) | async-done | bytes 786464 | tf_op jit(solution)/shard_map/head_grads/all_to_all | solution.py:27
  147.6 0.3 fusion.16
  148.2 13.0 %all_to_all.45 = bf16[4,96,384]{2,1,0:T(8,128)(2,1)S(1)} all-to-all(bf16[4,96,384]{2,1,0:T(8,128)(2,1)S(1)} %bitcast.124), channel_id=1, replica_groups=mesh['xl'=2,'zh'=4,'zm'=2,'z0'=2,'c'=2,'y'=4,'xh'=2] {'xl','zm'}, dimensions={0} | all-to-all | bytes 589824 | tf_op jit(solution)/shard_map/weight_grads/all_to_all | solution.py:27
  161.3 0.7 broadcast_in_dim.16
  162.0 9.2 %all-to-all-start.7 = ((bf16[4,96,384]{2,1,0:T(8,128)(2,1)}), bf16[4,96,384]{2,1,0:T(8,128)(2,1)S(1)}, u32[]{:S(2)}, u32[]{:S(2)}) async-start(bf16[4,96,384]{2,1,0:T(8,128)(2,1)} %broadcast_in_dim.16), calls=%async_computation.7 | async-start | bytes 589824 | tf_op jit(solution)/shard_map/weight_grads/all_to_all | solution.py:27
  171.2 1.2 convolution_bitcast_fusion
  172.4 1.2 convolution_bitcast_fusion.1
  173.7 3.9 %collective-permute-start.17 = (bf16[2,2,128,192]{2,3,1,0:T(8,128)(2,1)S(1)}, bf16[2,2,128,192]{2,3,1,0:T(8,128)(2,1)S(1)}, u32[]{:S(2)}, u32[]{:S(2)}) collective-permute-start(bf16[2,2,128,192]{2,3,1,0:T(8,128)(2,1)S(1)} %fusion.26), channel_id=1, source_target_pairs={{0,8},{8,0},{1,9},{9,1},{2,10},{10,2},{3,11},{11,3},{4,12},{12,4},... | collective-permute-start | bytes 589832 | tf_op jit(solution)/shard_map/input_grads/ppermute | solution.py:41
  177.6 1.0 collective-permute-done.17
  178.7 5.8 %all-to-all-done.7 = bf16[4,96,384]{2,1,0:T(8,128)(2,1)S(1)} async-done(((bf16[4,96,384]{2,1,0:T(8,128)(2,1)}), bf16[4,96,384]{2,1,0:T(8,128)(2,1)S(1)}, u32[]{:S(2)}, u32[]{:S(2)}) %all-to-all-start.7) | async-done | bytes 294944 | tf_op jit(solution)/shard_map/weight_grads/all_to_all | solution.py:27
  184.6 0.9 broadcast_in_dim.17
  185.4 7.1 %all-to-all-start.8 = ((bf16[8,96,384]{2,1,0:T(8,128)(2,1)}), bf16[8,96,384]{2,1,0:T(8,128)(2,1)S(1)}, u32[]{:S(2)}, u32[]{:S(2)}) async-start(bf16[8,96,384]{2,1,0:T(8,128)(2,1)} %broadcast_in_dim.17), calls=%async_computation.8 | async-start | bytes 1179648 | tf_op jit(solution)/shard_map/weight_grads/all_to_all | solution.py:27
  192.5 3.4 %collective-permute-start.18 = (bf16[2,128,192]{1,2,0:T(8,128)(2,1)S(1)}, bf16[2,128,192]{1,2,0:T(8,128)(2,1)S(1)}, u32[]{:S(2)}, u32[]{:S(2)}) collective-permute-start(bf16[2,128,192]{1,2,0:T(8,128)(2,1)S(1)} %fusion.47), channel_id=1, source_target_pairs={{0,16},{16,0},{1,17},{17,1},{2,18},{18,2},{3,19},{19,3},{4,20},{20... | collective-permute-start | bytes 294920 | tf_op jit(solution)/shard_map/weight_grads/ppermute | solution.py:41
  195.9 3.9 %collective-permute-done.18 = bf16[2,128,192]{1,2,0:T(8,128)(2,1)S(1)} collective-permute-done((bf16[2,128,192]{1,2,0:T(8,128)(2,1)S(1)}, bf16[2,128,192]{1,2,0:T(8,128)(2,1)S(1)}, u32[]{:S(2)}, u32[]{:S(2)}) %collective-permute-start.18) | collective-permute-done | bytes 98336 | tf_op jit(solution)/shard_map/weight_grads/ppermute | solution.py:41
  199.8 0.7 slice_bitcast_fusion.4
  200.5 3.3 %all-to-all-done.8 = bf16[8,96,384]{2,1,0:T(8,128)(2,1)S(1)} async-done(((bf16[8,96,384]{2,1,0:T(8,128)(2,1)}), bf16[8,96,384]{2,1,0:T(8,128)(2,1)S(1)}, u32[]{:S(2)}, u32[]{:S(2)}) %all-to-all-start.8) | async-done | bytes 589856 | tf_op jit(solution)/shard_map/weight_grads/all_to_all | solution.py:27
  203.8 0.5 copy.18
  204.2 0.4 reshape.237
  204.6 8.4 %collective-permute-start.19 = (bf16[2,192,768]{2,1,0:T(8,128)(2,1)S(1)}, bf16[2,192,768]{2,1,0:T(8,128)(2,1)S(1)}, u32[]{:S(2)}, u32[]{:S(2)}) collective-permute-start(bf16[2,192,768]{2,1,0:T(8,128)(2,1)S(1)} %reshape.237), channel_id=1, source_target_pairs={{0,8},{8,0},{1,9},{9,1},{2,10},{10,2},{3,11},{11,3},{4,12},{12,4},... | collective-permute-start | bytes 1769480 | tf_op jit(solution)/shard_map/weight_grads/ppermute | solution.py:41
  213.3 1.4 collective-permute-done.19
  214.8 1.0 copy-done
  215.8 0.4 copy-done.1
  (74 shorter events, 2.4 us)
Async XLA Ops:
  3.2 7.7 %copy-start.2 = (bf16[128,192]{0,1:T(8,128)(2,1)S(1)}, bf16[128,192]{0,1:T(8,128)(2,1)}, u32[]{:S(2)}) copy-start(bf16[128,192]{0,1:T(8,128)(2,1)} %param.7) | copy-start | bytes 147460
  3.2 7.6 %copy-start.3 = (bf16[128,192]{0,1:T(8,128)(2,1)S(1)}, bf16[128,192]{0,1:T(8,128)(2,1)}, u32[]{:S(2)}) copy-start(bf16[128,192]{0,1:T(8,128)(2,1)} %param.8) | copy-start | bytes 147460
  3.2 19.0 %all-to-all-start = ((bf16[8,16,3072]{2,1,0:T(8,128)(2,1)}), bf16[8,16,3072]{2,1,0:T(8,128)(2,1)S(1)}, u32[]{:S(2)}, u32[]{:S(2)}) async-start(bf16[8,16,3072]{2,1,0:T(8,128)(2,1)} %bitcast.118), calls=%async_computation | async-start | bytes 1572864 | tf_op jit(solution)/shard_map/heads/all_to_all | solution.py:27
  10.9 10.1 %collective-permute-start.2 = (bf16[2,192,128]{2,1,0:T(8,128)(2,1)S(1)}, bf16[2,192,128]{2,1,0:T(8,128)(2,1)S(1)}, u32[]{:S(2)}, u32[]{:S(2)}) collective-permute-start(bf16[2,192,128]{2,1,0:T(8,128)(2,1)S(1)} %pad_maximum_fusion.4), channel_id=1, source_target_pairs={{0,24},{8,16},{16,8},{24,0},{1,25},{9,17},{17,9},{25,1},{2,26},{10... | collective-permute-start | bytes 294920 | tf_op jit(solution)/shard_map/heads/ppermute | solution.py:163
  15.3 6.6 %collective-permute-start.1 = (bf16[2,192,128]{2,1,0:T(8,128)(2,1)S(1)}, bf16[2,192,128]{2,1,0:T(8,128)(2,1)S(1)}, u32[]{:S(2)}, u32[]{:S(2)}) collective-permute-start(bf16[2,192,128]{2,1,0:T(8,128)(2,1)S(1)} %pad_maximum_fusion.4), channel_id=1, source_target_pairs={{0,16},{16,0},{1,17},{17,1},{2,18},{18,2},{3,19},{19,3},{4,20},{20... | collective-permute-start | bytes 294920 | tf_op jit(solution)/shard_map/heads/ppermute | solution.py:41
  19.1 3.2 %collective-permute-start = (bf16[2,192,128]{2,1,0:T(8,128)(2,1)S(1)}, bf16[2,192,128]{2,1,0:T(8,128)(2,1)S(1)}, u32[]{:S(2)}, u32[]{:S(2)}) collective-permute-start(bf16[2,192,128]{2,1,0:T(8,128)(2,1)S(1)} %pad_maximum_fusion.4), channel_id=1, source_target_pairs={{0,8},{8,0},{1,9},{9,1},{2,10},{10,2},{3,11},{11,3},{4,12},{12,4},... | collective-permute-start | bytes 294920 | tf_op jit(solution)/shard_map/heads/ppermute | solution.py:41
  21.0 2.3 %copy-start.4 = (bf16[2,192,128]{2,1,0:T(8,128)(2,1)}, bf16[2,192,128]{2,1,0:T(8,128)(2,1)S(1)}, u32[]{:S(2)}) copy-start(bf16[2,192,128]{2,1,0:T(8,128)(2,1)S(1)} %collective-permute-done.2) | copy-start | bytes 294916
  21.9 31.8 %copy-start.6 = (bf16[2,192,128]{2,1,0:T(8,128)(2,1)}, bf16[2,192,128]{2,1,0:T(8,128)(2,1)S(1)}, u32[]{:S(2)}) copy-start(bf16[2,192,128]{2,1,0:T(8,128)(2,1)S(1)} %collective-permute-done.1) | copy-start | bytes 294916
  22.2 31.4 %copy-start.8 = (bf16[2,192,128]{2,1,0:T(8,128)(2,1)}, bf16[2,192,128]{2,1,0:T(8,128)(2,1)S(1)}, u32[]{:S(2)}) copy-start(bf16[2,192,128]{2,1,0:T(8,128)(2,1)S(1)} %collective-permute-done) | copy-start | bytes 294916
  23.3 29.4 %all-to-all-start.1 = ((bf16[4,16,1536]{2,1,0:T(8,128)(2,1)}), bf16[4,16,1536]{2,1,0:T(8,128)(2,1)S(1)}, u32[]{:S(2)}, u32[]{:S(2)}) async-start(bf16[4,16,1536]{2,1,0:T(8,128)(2,1)} %broadcast_in_dim.12), calls=%async_computation.1 | async-start | bytes 393216 | tf_op jit(solution)/shard_map/gather_texts/all_to_all | solution.py:27
  40.0 17.2 %collective-permute-start.5 = (bf16[16,1536]{1,0:T(8,128)(2,1)S(1)}, bf16[16,1536]{1,0:T(8,128)(2,1)S(1)}, u32[]{:S(2)}, u32[]{:S(2)}) collective-permute-start(bf16[16,1536]{1,0:T(8,128)(2,1)S(1)} %get-tuple-element.29), channel_id=1, source_target_pairs={{0,32},{16,48},{32,0},{48,16},{1,33},{17,49},{33,1},{49,17},{2,34}... | collective-permute-start | bytes 147464 | tf_op jit(solution)/shard_map/gather_images/ppermute | solution.py:41
  43.1 14.1 %collective-permute-start.4 = (bf16[16,1536]{1,0:T(8,128)(2,1)S(1)}, bf16[16,1536]{1,0:T(8,128)(2,1)S(1)}, u32[]{:S(2)}, u32[]{:S(2)}) collective-permute-start(bf16[16,1536]{1,0:T(8,128)(2,1)S(1)} %get-tuple-element.29), channel_id=1, source_target_pairs={{0,16},{16,32},{32,48},{48,0},{1,17},{17,33},{33,49},{49,1},{2,18}... | collective-permute-start | bytes 147464 | tf_op jit(solution)/shard_map/gather_images/ppermute | solution.py:41
  45.8 11.4 %collective-permute-start.3 = (bf16[16,1536]{1,0:T(8,128)(2,1)S(1)}, bf16[16,1536]{1,0:T(8,128)(2,1)S(1)}, u32[]{:S(2)}, u32[]{:S(2)}) collective-permute-start(bf16[16,1536]{1,0:T(8,128)(2,1)S(1)} %get-tuple-element.29), channel_id=1, source_target_pairs={{0,48},{16,0},{32,16},{48,32},{1,49},{17,1},{33,17},{49,33},{2,50}... | collective-permute-start | bytes 147464 | tf_op jit(solution)/shard_map/gather_images/ppermute | solution.py:41
  53.7 12.9 %all-to-all-start.2 = ((bf16[4,64,1536]{2,1,0:T(8,128)(2,1)}), bf16[4,64,1536]{2,1,0:T(8,128)(2,1)S(1)}, u32[]{:S(2)}, u32[]{:S(2)}) async-start(bf16[4,64,1536]{2,1,0:T(8,128)(2,1)} %broadcast_in_dim.14), calls=%async_computation.2 | async-start | bytes 1572864 | tf_op jit(solution)/shard_map/gather_texts/all_to_all | solution.py:27
  57.2 19.5 %collective-permute-start.8 = (bf16[64,1536]{1,0:T(8,128)(2,1)S(1)}, bf16[64,1536]{1,0:T(8,128)(2,1)S(1)}, u32[]{:S(2)}, u32[]{:S(2)}) collective-permute-start(bf16[64,1536]{1,0:T(8,128)(2,1)S(1)} %pad_maximum_fusion.3), channel_id=1, source_target_pairs={{0,4},{2,6},{4,0},{6,2},{1,5},{3,7},{5,1},{7,3},{8,12},{10,14},{12... | collective-permute-start | bytes 589832 | tf_op jit(solution)/shard_map/gather_images/ppermute | solution.py:41
  60.0 16.6 %collective-permute-start.7 = (bf16[64,1536]{1,0:T(8,128)(2,1)S(1)}, bf16[64,1536]{1,0:T(8,128)(2,1)S(1)}, u32[]{:S(2)}, u32[]{:S(2)}) collective-permute-start(bf16[64,1536]{1,0:T(8,128)(2,1)S(1)} %pad_maximum_fusion.3), channel_id=1, source_target_pairs={{0,2},{2,4},{4,6},{6,0},{1,3},{3,5},{5,7},{7,1},{8,10},{10,12},{12... | collective-permute-start | bytes 589832 | tf_op jit(solution)/shard_map/gather_images/ppermute | solution.py:41
  62.5 14.1 %collective-permute-start.6 = (bf16[64,1536]{1,0:T(8,128)(2,1)S(1)}, bf16[64,1536]{1,0:T(8,128)(2,1)S(1)}, u32[]{:S(2)}, u32[]{:S(2)}) collective-permute-start(bf16[64,1536]{1,0:T(8,128)(2,1)S(1)} %pad_maximum_fusion.3), channel_id=1, source_target_pairs={{0,6},{2,0},{4,2},{6,4},{1,7},{3,1},{5,3},{7,5},{8,14},{10,8},{12,... | collective-permute-start | bytes 589832 | tf_op jit(solution)/shard_map/gather_images/ppermute | solution.py:41
  66.6 11.9 %collective-permute-start.9 = (bf16[256,1536]{1,0:T(8,128)(2,1)S(1)}, bf16[256,1536]{1,0:T(8,128)(2,1)S(1)}, u32[]{:S(2)}, u32[]{:S(2)}) collective-permute-start(bf16[256,1536]{1,0:T(8,128)(2,1)S(1)} %bitcast.115), channel_id=1, source_target_pairs={{0,8},{8,0},{1,9},{9,1},{2,10},{10,2},{3,11},{11,3},{4,12},{12,4},... | collective-permute-start | bytes 2359304 | tf_op jit(solution)/shard_map/gather_texts/ppermute | solution.py:41
  79.3 4.2 %collective-permute-start.16 = (bf16[256,1536]{1,0:T(8,128)(2,1)S(1)}, bf16[256,1536]{1,0:T(8,128)(2,1)S(1)}, u32[]{:S(2)}, u32[]{:S(2)}) collective-permute-start(bf16[256,1536]{1,0:T(8,128)(2,1)S(1)} %convolution_convert_fusion), channel_id=1, source_target_pairs={{0,8},{8,0},{1,9},{9,1},{2,10},{10,2},{3,11},{11,3},{4,12},{12,4},... | collective-permute-start | bytes 2359304 | tf_op jit(solution)/shard_map/sum_texts/ppermute | solution.py:41
  84.7 16.2 %all-to-all-start.3 = ((bf16[4,64,1536]{2,1,0:T(8,128)(2,1)}), bf16[4,64,1536]{2,1,0:T(8,128)(2,1)S(1)}, u32[]{:S(2)}, u32[]{:S(2)}) async-start(bf16[4,64,1536]{2,1,0:T(8,128)(2,1)} %bitcast.18), calls=%async_computation.3 | async-start | bytes 1572864 | tf_op jit(solution)/shard_map/sum_texts/all_to_all | solution.py:27
  90.0 18.6 %collective-permute-start.10 = (bf16[64,1536]{1,0:T(8,128)(2,1)}, bf16[64,1536]{1,0:T(8,128)(2,1)S(1)}, u32[]{:S(2)}, u32[]{:S(2)}) collective-permute-start(bf16[64,1536]{1,0:T(8,128)(2,1)} %get-tuple-element.32), channel_id=1, source_target_pairs={{0,2},{2,4},{4,6},{6,0},{1,3},{3,5},{5,7},{7,1},{8,10},{10,12},{12... | collective-permute-start | bytes 589832 | tf_op jit(solution)/shard_map/sum_images/ppermute | solution.py:41
  92.1 16.5 %collective-permute-start.12 = (bf16[64,1536]{1,0:T(8,128)(2,1)}, bf16[64,1536]{1,0:T(8,128)(2,1)S(1)}, u32[]{:S(2)}, u32[]{:S(2)}) collective-permute-start(bf16[64,1536]{1,0:T(8,128)(2,1)} %get-tuple-element.33), channel_id=1, source_target_pairs={{0,4},{2,6},{4,0},{6,2},{1,5},{3,7},{5,1},{7,3},{8,12},{10,14},{12... | collective-permute-start | bytes 589832 | tf_op jit(solution)/shard_map/sum_images/ppermute | solution.py:41
  97.4 11.2 %collective-permute-start.11 = (bf16[64,1536]{1,0:T(8,128)(2,1)S(1)}, bf16[64,1536]{1,0:T(8,128)(2,1)S(1)}, u32[]{:S(2)}, u32[]{:S(2)}) collective-permute-start(bf16[64,1536]{1,0:T(8,128)(2,1)S(1)} %get-tuple-element.34), channel_id=1, source_target_pairs={{0,6},{2,0},{4,2},{6,4},{1,7},{3,1},{5,3},{7,5},{8,14},{10,8},{12,... | collective-permute-start | bytes 589832 | tf_op jit(solution)/shard_map/sum_images/ppermute | solution.py:41
  101.8 19.4 %all-to-all-start.4 = ((bf16[4,16,1536]{2,1,0:T(8,128)(2,1)}), bf16[4,16,1536]{2,1,0:T(8,128)(2,1)S(1)}, u32[]{:S(2)}, u32[]{:S(2)}) async-start(bf16[4,16,1536]{2,1,0:T(8,128)(2,1)} %bitcast.19), calls=%async_computation.4 | async-start | bytes 393216 | tf_op jit(solution)/shard_map/sum_texts/all_to_all | solution.py:27
  108.7 12.4 %collective-permute-start.13 = (bf16[16,1536]{1,0:T(8,128)(2,1)S(1)}, bf16[16,1536]{1,0:T(8,128)(2,1)S(1)}, u32[]{:S(2)}, u32[]{:S(2)}) collective-permute-start(bf16[16,1536]{1,0:T(8,128)(2,1)S(1)} %get-tuple-element.55), channel_id=1, source_target_pairs={{0,16},{16,32},{32,48},{48,0},{1,17},{17,33},{33,49},{49,1},{2,18}... | collective-permute-start | bytes 147464 | tf_op jit(solution)/shard_map/sum_images/ppermute | solution.py:41
  110.7 10.5 %collective-permute-start.15 = (bf16[16,1536]{1,0:T(8,128)(2,1)S(1)}, bf16[16,1536]{1,0:T(8,128)(2,1)S(1)}, u32[]{:S(2)}, u32[]{:S(2)}) collective-permute-start(bf16[16,1536]{1,0:T(8,128)(2,1)S(1)} %get-tuple-element.56), channel_id=1, source_target_pairs={{0,32},{16,48},{32,0},{48,16},{1,33},{17,49},{33,1},{49,17},{2,34}... | collective-permute-start | bytes 147464 | tf_op jit(solution)/shard_map/sum_images/ppermute | solution.py:41
  112.7 8.7 %collective-permute-start.14 = (bf16[16,1536]{1,0:T(8,128)(2,1)S(1)}, bf16[16,1536]{1,0:T(8,128)(2,1)S(1)}, u32[]{:S(2)}, u32[]{:S(2)}) collective-permute-start(bf16[16,1536]{1,0:T(8,128)(2,1)S(1)} %get-tuple-element.57), channel_id=1, source_target_pairs={{0,48},{16,0},{32,16},{48,32},{1,49},{17,1},{33,17},{49,33},{2,50}... | collective-permute-start | bytes 147464 | tf_op jit(solution)/shard_map/sum_images/ppermute | solution.py:41
  121.9 11.4 %copy-start.5 = (bf16[2,192,128]{2,1,0:T(8,128)(2,1)S(1)}, bf16[2,192,128]{2,1,0:T(8,128)(2,1)}, u32[]{:S(2)}) copy-start(bf16[2,192,128]{2,1,0:T(8,128)(2,1)} %copy-done.4) | copy-start | bytes 294916
  121.9 11.4 %copy-start.7 = (bf16[2,192,128]{2,1,0:T(8,128)(2,1)S(1)}, bf16[2,192,128]{2,1,0:T(8,128)(2,1)}, u32[]{:S(2)}) copy-start(bf16[2,192,128]{2,1,0:T(8,128)(2,1)} %copy-done.6) | copy-start | bytes 294916
  122.0 11.4 %copy-start.9 = (bf16[2,192,128]{2,1,0:T(8,128)(2,1)S(1)}, bf16[2,192,128]{2,1,0:T(8,128)(2,1)}, u32[]{:S(2)}) copy-start(bf16[2,192,128]{2,1,0:T(8,128)(2,1)} %copy-done.8) | copy-start | bytes 294916
  122.9 24.6 %all-to-all-start.5 = ((bf16[32,2,16,384]{3,2,1,0:T(8,128)(2,1)}), bf16[32,2,16,384]{3,2,1,0:T(8,128)(2,1)S(1)}, u32[]{:S(2)}, u32[]{:S(2)}) async-start(bf16[32,2,16,384]{3,2,1,0:T(8,128)(2,1)} %bitcast.21), calls=%async_computation.5 | async-start | bytes 1572864 | tf_op jit(solution)/shard_map/head_grads/all_to_all | solution.py:27
  162.0 22.5 %all-to-all-start.7 = ((bf16[4,96,384]{2,1,0:T(8,128)(2,1)}), bf16[4,96,384]{2,1,0:T(8,128)(2,1)S(1)}, u32[]{:S(2)}, u32[]{:S(2)}) async-start(bf16[4,96,384]{2,1,0:T(8,128)(2,1)} %broadcast_in_dim.16), calls=%async_computation.7 | async-start | bytes 589824 | tf_op jit(solution)/shard_map/weight_grads/all_to_all | solution.py:27
  173.7 5.0 %collective-permute-start.17 = (bf16[2,2,128,192]{2,3,1,0:T(8,128)(2,1)S(1)}, bf16[2,2,128,192]{2,3,1,0:T(8,128)(2,1)S(1)}, u32[]{:S(2)}, u32[]{:S(2)}) collective-permute-start(bf16[2,2,128,192]{2,3,1,0:T(8,128)(2,1)S(1)} %fusion.26), channel_id=1, source_target_pairs={{0,8},{8,0},{1,9},{9,1},{2,10},{10,2},{3,11},{11,3},{4,12},{12,4},... | collective-permute-start | bytes 589832 | tf_op jit(solution)/shard_map/input_grads/ppermute | solution.py:41
  185.4 18.3 %all-to-all-start.8 = ((bf16[8,96,384]{2,1,0:T(8,128)(2,1)}), bf16[8,96,384]{2,1,0:T(8,128)(2,1)S(1)}, u32[]{:S(2)}, u32[]{:S(2)}) async-start(bf16[8,96,384]{2,1,0:T(8,128)(2,1)} %broadcast_in_dim.17), calls=%async_computation.8 | async-start | bytes 1179648 | tf_op jit(solution)/shard_map/weight_grads/all_to_all | solution.py:27
  192.5 7.2 %collective-permute-start.18 = (bf16[2,128,192]{1,2,0:T(8,128)(2,1)S(1)}, bf16[2,128,192]{1,2,0:T(8,128)(2,1)S(1)}, u32[]{:S(2)}, u32[]{:S(2)}) collective-permute-start(bf16[2,128,192]{1,2,0:T(8,128)(2,1)S(1)} %fusion.47), channel_id=1, source_target_pairs={{0,16},{16,0},{1,17},{17,1},{2,18},{18,2},{3,19},{19,3},{4,20},{20... | collective-permute-start | bytes 294920 | tf_op jit(solution)/shard_map/weight_grads/ppermute | solution.py:41
  204.6 10.0 %collective-permute-start.19 = (bf16[2,192,768]{2,1,0:T(8,128)(2,1)S(1)}, bf16[2,192,768]{2,1,0:T(8,128)(2,1)S(1)}, u32[]{:S(2)}, u32[]{:S(2)}) collective-permute-start(bf16[2,192,768]{2,1,0:T(8,128)(2,1)S(1)} %reshape.237), channel_id=1, source_target_pairs={{0,8},{8,0},{1,9},{9,1},{2,10},{10,2},{3,11},{11,3},{4,12},{12,4},... | collective-permute-start | bytes 1769480 | tf_op jit(solution)/shard_map/weight_grads/ppermute | solution.py:41
  214.8 1.0 copy-start
  214.8 1.4 copy-start.1
